TPU v7x, 32 devices: a whole 2x2x4 slice. The times are simulated.
32 devices in a mesh: slab: 8 (over z, y), face: 4 (over x, core).
Axes of the slice: x: 2, y: 2, z: 4, core: 2. Of those that a mesh axis runs over, the one named last changes fastest.
Arguments:
- rhs: bfloat16 [4, 8, 128, 4096], P(None, 'slab', None, 'face'), may hold values from -6 to 6
- inflow: bfloat16 [8, 128, 1024], P('slab', None, 'face'), may hold values from -6 to 6
- diag_tiles: bfloat16 [8, 32, 128, 128], P('slab', 'face')
- off_tiles: bfloat16 [8, 32, 4, 128, 128], P('slab', 'face'), may hold values from -0.5 to 0.5
- cols: int32 [8, 32, 4], P('slab', 'face'), may hold values from 0 to 31, as said below
- inverse_tiles: bfloat16 [8, 32, 128, 128], P('slab', 'face')
- coupling: bfloat16 [8, 8, 128, 128], P('slab', 'face'), may hold values from -1 to 1
- iface: int32 [8], P('face'), may hold values from 0 to 7, as said below
Outputs:
- solution: bfloat16 [4, 8, 128, 4096], P(None, 'slab', None, 'face')
Inputs may be any that keep to these rules, and one draw needn't show every extreme that they name: `cols`: each column index lies within 2 tile rows of the block of 8 tile rows that holds its row; a block's first tile row reaches the tile row 2 before the block and its last reaches the tile row 2 after the block, wherever the slab has them. The 2 entries of one block of iface are distinct.
All inputs are finite; a program needn't handle non-finite values.
Results may differ from a plain program's by a relative error of at most 0.01.
Values may be sent and summed in bfloat16 or wider, within the bound.
No kernel may reach another device: no remote copies, remote signals or barrier semaphores. Data moves between devices by JAX's collectives and lax.ppermute only.
A program may use at most 64 MiB of HBM per device.

v0:
```python
import jax
import jax.numpy as jnp
from jax import lax
from jax.sharding import PartitionSpec as P

HALO_T = 2


def padded(value, sides, width):
    for axis, dim in sides:
        size, length = (lax.axis_size(axis), value.shape[dim])
        up = [(i, (i + 1) % size) for i in range(size - 1)]
        down = [(j, i) for i, j in up]
        last = lax.slice_in_dim(value, length - width, length, axis=dim)
        leading = lax.slice_in_dim(value, 0, width, axis=dim)
        before = lax.ppermute(last, axis, up)
        after = lax.ppermute(leading, axis, down)
        value = jnp.concatenate([before, value, after], axis=dim)
    return value


def from_behind(block, axis, distance):
    devices = range(lax.axis_size(axis))
    route = [(i - distance, i) for i in devices if i - distance in devices]
    return lax.ppermute(block, axis, route)


def tile_apply(tiles, values):
    return jnp.einsum("rij,srj->sri", tiles, values, preferred_element_type=jnp.float32)


def on_device(rhs, inflow, diag_tiles, off_tiles, cols, inverse_tiles, coupling, iface):
    face_index = lax.axis_index("face")
    diagonal = diag_tiles[0]
    neighbours = off_tiles[0]
    inverse = inverse_tiles[0]
    couple = coupling[0]
    count = diagonal.shape[0]
    width = diagonal.shape[1]
    iface_count = couple.shape[0]
    local_cols = cols[0] - (face_index * count - HALO_T)
    selector = (iface[None, :] == jnp.arange(count, dtype=jnp.int32)[:, None]).astype(jnp.float32)
    rhs_local = rhs[:, 0]
    inflow_local = inflow[0]
    incoming = inflow_local
    results = []
    total = rhs_local.shape[0]
    for tick in range(total):
        rhs_tick = rhs_local[tick]
        sources = rhs_tick.shape[0]
        inbound = incoming.reshape(sources, iface_count, width)
        coupled = jnp.einsum("qij,sqj->sqi", couple, inbound, preferred_element_type=jnp.float32)
        placed = jnp.einsum("rq,sqi->sri", selector, coupled)
        right = (rhs_tick.reshape(sources, count, width).astype(jnp.float32) - placed).astype(
            jnp.bfloat16
        )
        advance_field = tile_apply(inverse, right).astype(jnp.bfloat16)
        for sweep in range(2):
            extended = padded(advance_field, (("face", 1),), HALO_T)
            gathered = jnp.take(extended, local_cols, axis=1)
            product = tile_apply(diagonal, advance_field) + jnp.einsum(
                "rkij,srkj->sri", neighbours, gathered, preferred_element_type=jnp.float32
            )
            correction = (right.astype(jnp.float32) - product).astype(jnp.bfloat16)
            advance_field = (
                advance_field.astype(jnp.float32) + tile_apply(inverse, correction)
            ).astype(jnp.bfloat16)
        sent = jnp.take(advance_field, iface, axis=1).reshape(sources, iface_count * width)
        field, sent = (advance_field.reshape(sources, count * width), sent)
        results.append(field)
        if tick + 1 < total:
            incoming = from_behind(sent, "slab", 1)
    solution = jnp.stack(results)
    return solution[:, None]


def solution(mesh):
    placed = (
        P(None, "slab", None, "face"),
        P("slab", None, "face"),
        P("slab", "face", None, None),
        P("slab", "face", None, None, None),
        P("slab", "face", None),
        P("slab", "face", None, None),
        P("slab", "face", None, None),
        P("face"),
    )
    return jax.shard_map(
        on_device,
        mesh=mesh,
        in_specs=placed,
        out_specs=P(None, "slab", None, "face"),
        check_vma=False,
    )
```

profile of v0, /device:TPU:9, one launch (start us, length us, event | category | flops | bytes accessed | tf_op | source)
XLA Modules:
  0.0 132.6 jit_solution(6187747821180489170)
XLA Ops:
  0.0 2.6 %convert_bitcast_fusion.3 = (f32[16,8,8,128]{3,1,2,0:T(8,128)S(1)}, f32[16,8,8,128]{3,1,2,0:T(8,128)}, f32[16,8,8,128]{3,1,2,0:T(8,128)}, f32[16,8,8,128]{3,1,2,0:T(8,128)}) fusion(bf16[4,1,128,1024]{3,2,1,0:T(8,128)(2,1)} %param.12), kind=kLoop, calls=%fused_computation.131 | loop fusion | flops 524288 | bytes 3145728
  6.3 2.7 %collective-permute-start.1 = (bf16[128,2,128]{0,2,1:T(8,128)(2,1)S(1)}, bf16[128,2,128]{0,2,1:T(8,128)(2,1)S(1)}, u32[]{:S(2)}, u32[]{:S(2)}) collective-permute-start(bf16[128,2,128]{0,2,1:T(8,128)(2,1)S(1)} %get-tuple-element.28), channel_id=1, source_target_pairs={{1,0},{2,1},{3,2},{5,4},{6,5},{7,6},{9,8},{10,9},{11,10},{13,12},{... | collective-permute-start | bytes 196616 | tf_op jit(solution)/shard_map/ppermute | solution.py:17
  9.1 3.0 %collective-permute-start = (bf16[128,2,128]{0,2,1:T(8,128)(2,1)S(1)}, bf16[128,2,128]{0,2,1:T(8,128)(2,1)S(1)}, u32[]{:S(2)}, u32[]{:S(2)}) collective-permute-start(bf16[128,2,128]{0,2,1:T(8,128)(2,1)S(1)} %get-tuple-element.27), channel_id=1, source_target_pairs={{0,1},{1,2},{2,3},{4,5},{5,6},{6,7},{8,9},{9,10},{10,11},{12,13},{... | collective-permute-start | bytes 196616 | tf_op jit(solution)/shard_map/ppermute | solution.py:16
  17.9 1.9 %collective-permute-start.3 = (bf16[128,2,128]{0,2,1:T(8,128)(2,1)S(1)}, bf16[128,2,128]{0,2,1:T(8,128)(2,1)S(1)}, u32[]{:S(2)}, u32[]{:S(2)}) collective-permute-start(bf16[128,2,128]{0,2,1:T(8,128)(2,1)S(1)} %get-tuple-element.26), channel_id=1, source_target_pairs={{1,0},{2,1},{3,2},{5,4},{6,5},{7,6},{9,8},{10,9},{11,10},{13,12},{... | collective-permute-start | bytes 196616 | tf_op jit(solution)/shard_map/ppermute | solution.py:17
  19.8 4.2 %collective-permute-start.2 = (bf16[128,2,128]{0,2,1:T(8,128)(2,1)S(1)}, bf16[128,2,128]{0,2,1:T(8,128)(2,1)S(1)}, u32[]{:S(2)}, u32[]{:S(2)}) collective-permute-start(bf16[128,2,128]{0,2,1:T(8,128)(2,1)S(1)} %get-tuple-element.25), channel_id=1, source_target_pairs={{0,1},{1,2},{2,3},{4,5},{5,6},{6,7},{8,9},{9,10},{10,11},{12,13},{... | collective-permute-start | bytes 196616 | tf_op jit(solution)/shard_map/ppermute | solution.py:16
  27.1 1.8 %fusion.40 = f32[8,128,128,1]{2,1,3,0:T(8,128)S(1)} fusion(bf16[1,8,4,128,128]{4,3,2,1,0:T(8,128)(2,1)S(1)} %copy-done, bf16[8,4,128,128]{2,3,1,0:T(8,128)(2,1)} %bitcast.310, pred[8,4]{1,0:T(8,128)(4,1)S(1)} %copy.42), kind=kOutput, calls=%fused_computation.68 | convolution fusion | flops 134742016 | bytes 2621472 | tf_op jit(solution)/shard_map/rkij,srkj->sri/dot_general | solution.py:61
  30.4 3.1 %collective-permute-start.4 = (bf16[128,256]{0,1:T(8,128)(2,1)S(1)}, bf16[128,256]{0,1:T(8,128)(2,1)S(1)}, u32[]{:S(2)}, u32[]{:S(2)}) collective-permute-start(bf16[128,256]{0,1:T(8,128)(2,1)S(1)} %bitcast.321), channel_id=1, source_target_pairs={{0,4},{4,8},{8,12},{12,16},{16,20},{20,24},{24,28},{1,5},{5,9},{9,... | collective-permute-start | bytes 196616 | tf_op jit(solution)/shard_map/ppermute | solution.py:25
  33.7 2.6 %collective-permute-done.4 = bf16[128,256]{0,1:T(8,128)(2,1)S(1)} collective-permute-done((bf16[128,256]{0,1:T(8,128)(2,1)S(1)}, bf16[128,256]{0,1:T(8,128)(2,1)S(1)}, u32[]{:S(2)}, u32[]{:S(2)}) %collective-permute-start.4) | collective-permute-done | bytes 65568 | tf_op jit(solution)/shard_map/ppermute | solution.py:25
  37.2 1.9 %collective-permute-start.6 = (bf16[128,2,128]{0,2,1:T(8,128)(2,1)S(1)}, bf16[128,2,128]{0,2,1:T(8,128)(2,1)S(1)}, u32[]{:S(2)}, u32[]{:S(2)}) collective-permute-start(bf16[128,2,128]{0,2,1:T(8,128)(2,1)S(1)} %get-tuple-element.24), channel_id=1, source_target_pairs={{1,0},{2,1},{3,2},{5,4},{6,5},{7,6},{9,8},{10,9},{11,10},{13,12},{... | collective-permute-start | bytes 196616 | tf_op jit(solution)/shard_map/ppermute | solution.py:17
  39.1 5.4 %collective-permute-start.5 = (bf16[128,2,128]{0,2,1:T(8,128)(2,1)S(1)}, bf16[128,2,128]{0,2,1:T(8,128)(2,1)S(1)}, u32[]{:S(2)}, u32[]{:S(2)}) collective-permute-start(bf16[128,2,128]{0,2,1:T(8,128)(2,1)S(1)} %get-tuple-element.23), channel_id=1, source_target_pairs={{0,1},{1,2},{2,3},{4,5},{5,6},{6,7},{8,9},{9,10},{10,11},{12,13},{... | collective-permute-start | bytes 196616 | tf_op jit(solution)/shard_map/ppermute | solution.py:16
  48.2 1.8 %fusion.38 = f32[8,128,128,1]{2,1,3,0:T(8,128)S(1)} fusion(bf16[1,8,4,128,128]{4,3,2,1,0:T(8,128)(2,1)S(1)} %copy-done, bf16[8,4,128,128]{2,3,1,0:T(8,128)(2,1)} %bitcast.311, pred[8,4]{1,0:T(8,128)(4,1)S(1)} %copy-done.18), kind=kOutput, calls=%fused_computation.66 | convolution fusion | flops 134742016 | bytes 2621472 | tf_op jit(solution)/shard_map/rkij,srkj->sri/dot_general | solution.py:61
  51.0 1.9 %collective-permute-start.8 = (bf16[128,2,128]{0,2,1:T(8,128)(2,1)S(1)}, bf16[128,2,128]{0,2,1:T(8,128)(2,1)S(1)}, u32[]{:S(2)}, u32[]{:S(2)}) collective-permute-start(bf16[128,2,128]{0,2,1:T(8,128)(2,1)S(1)} %get-tuple-element.22), channel_id=1, source_target_pairs={{1,0},{2,1},{3,2},{5,4},{6,5},{7,6},{9,8},{10,9},{11,10},{13,12},{... | collective-permute-start | bytes 196616 | tf_op jit(solution)/shard_map/ppermute | solution.py:17
  52.9 4.3 %collective-permute-start.7 = (bf16[128,2,128]{0,2,1:T(8,128)(2,1)S(1)}, bf16[128,2,128]{0,2,1:T(8,128)(2,1)S(1)}, u32[]{:S(2)}, u32[]{:S(2)}) collective-permute-start(bf16[128,2,128]{0,2,1:T(8,128)(2,1)S(1)} %get-tuple-element.21), channel_id=1, source_target_pairs={{0,1},{1,2},{2,3},{4,5},{5,6},{6,7},{8,9},{9,10},{10,11},{12,13},{... | collective-permute-start | bytes 196616 | tf_op jit(solution)/shard_map/ppermute | solution.py:16
  64.2 2.2 %collective-permute-start.9 = (bf16[128,256]{0,1:T(8,128)(2,1)S(1)}, bf16[128,256]{0,1:T(8,128)(2,1)S(1)}, u32[]{:S(2)}, u32[]{:S(2)}) collective-permute-start(bf16[128,256]{0,1:T(8,128)(2,1)S(1)} %bitcast.322), channel_id=1, source_target_pairs={{0,4},{4,8},{8,12},{12,16},{16,20},{20,24},{24,28},{1,5},{5,9},{9,... | collective-permute-start | bytes 196616 | tf_op jit(solution)/shard_map/ppermute | solution.py:25
  66.6 3.5 %collective-permute-done.9 = bf16[128,256]{0,1:T(8,128)(2,1)S(1)} collective-permute-done((bf16[128,256]{0,1:T(8,128)(2,1)S(1)}, bf16[128,256]{0,1:T(8,128)(2,1)S(1)}, u32[]{:S(2)}, u32[]{:S(2)}) %collective-permute-start.9) | collective-permute-done | bytes 65568 | tf_op jit(solution)/shard_map/ppermute | solution.py:25
  71.0 1.9 %collective-permute-start.11 = (bf16[128,2,128]{0,2,1:T(8,128)(2,1)S(1)}, bf16[128,2,128]{0,2,1:T(8,128)(2,1)S(1)}, u32[]{:S(2)}, u32[]{:S(2)}) collective-permute-start(bf16[128,2,128]{0,2,1:T(8,128)(2,1)S(1)} %get-tuple-element.20), channel_id=1, source_target_pairs={{1,0},{2,1},{3,2},{5,4},{6,5},{7,6},{9,8},{10,9},{11,10},{13,12},{... | collective-permute-start | bytes 196616 | tf_op jit(solution)/shard_map/ppermute | solution.py:17
  72.9 5.4 %collective-permute-start.10 = (bf16[128,2,128]{0,2,1:T(8,128)(2,1)S(1)}, bf16[128,2,128]{0,2,1:T(8,128)(2,1)S(1)}, u32[]{:S(2)}, u32[]{:S(2)}) collective-permute-start(bf16[128,2,128]{0,2,1:T(8,128)(2,1)S(1)} %get-tuple-element.19), channel_id=1, source_target_pairs={{0,1},{1,2},{2,3},{4,5},{5,6},{6,7},{8,9},{9,10},{10,11},{12,13},{... | collective-permute-start | bytes 196616 | tf_op jit(solution)/shard_map/ppermute | solution.py:16
  84.8 1.9 %collective-permute-start.13 = (bf16[128,2,128]{0,2,1:T(8,128)(2,1)S(1)}, bf16[128,2,128]{0,2,1:T(8,128)(2,1)S(1)}, u32[]{:S(2)}, u32[]{:S(2)}) collective-permute-start(bf16[128,2,128]{0,2,1:T(8,128)(2,1)S(1)} %get-tuple-element.18), channel_id=1, source_target_pairs={{1,0},{2,1},{3,2},{5,4},{6,5},{7,6},{9,8},{10,9},{11,10},{13,12},{... | collective-permute-start | bytes 196616 | tf_op jit(solution)/shard_map/ppermute | solution.py:17
  86.7 4.4 %collective-permute-start.12 = (bf16[128,2,128]{0,2,1:T(8,128)(2,1)S(1)}, bf16[128,2,128]{0,2,1:T(8,128)(2,1)S(1)}, u32[]{:S(2)}, u32[]{:S(2)}) collective-permute-start(bf16[128,2,128]{0,2,1:T(8,128)(2,1)S(1)} %get-tuple-element.17), channel_id=1, source_target_pairs={{0,1},{1,2},{2,3},{4,5},{5,6},{6,7},{8,9},{9,10},{10,11},{12,13},{... | collective-permute-start | bytes 196616 | tf_op jit(solution)/shard_map/ppermute | solution.py:16
  98.0 1.9 %collective-permute-start.14 = (bf16[128,256]{0,1:T(8,128)(2,1)S(1)}, bf16[128,256]{0,1:T(8,128)(2,1)S(1)}, u32[]{:S(2)}, u32[]{:S(2)}) collective-permute-start(bf16[128,256]{0,1:T(8,128)(2,1)S(1)} %bitcast.320), channel_id=1, source_target_pairs={{0,4},{4,8},{8,12},{12,16},{16,20},{20,24},{24,28},{1,5},{5,9},{9,... | collective-permute-start | bytes 196616 | tf_op jit(solution)/shard_map/ppermute | solution.py:25
  104.8 1.9 %collective-permute-start.16 = (bf16[128,2,128]{0,2,1:T(8,128)(2,1)S(1)}, bf16[128,2,128]{0,2,1:T(8,128)(2,1)S(1)}, u32[]{:S(2)}, u32[]{:S(2)}) collective-permute-start(bf16[128,2,128]{0,2,1:T(8,128)(2,1)S(1)} %get-tuple-element.16), channel_id=1, source_target_pairs={{1,0},{2,1},{3,2},{5,4},{6,5},{7,6},{9,8},{10,9},{11,10},{13,12},{... | collective-permute-start | bytes 196616 | tf_op jit(solution)/shard_map/ppermute | solution.py:17
  106.7 5.4 %collective-permute-start.15 = (bf16[128,2,128]{0,2,1:T(8,128)(2,1)S(1)}, bf16[128,2,128]{0,2,1:T(8,128)(2,1)S(1)}, u32[]{:S(2)}, u32[]{:S(2)}) collective-permute-start(bf16[128,2,128]{0,2,1:T(8,128)(2,1)S(1)} %get-tuple-element.15), channel_id=1, source_target_pairs={{0,1},{1,2},{2,3},{4,5},{5,6},{6,7},{8,9},{9,10},{10,11},{12,13},{... | collective-permute-start | bytes 196616 | tf_op jit(solution)/shard_map/ppermute | solution.py:16
  118.6 1.9 %collective-permute-start.18 = (bf16[128,2,128]{0,2,1:T(8,128)(2,1)S(1)}, bf16[128,2,128]{0,2,1:T(8,128)(2,1)S(1)}, u32[]{:S(2)}, u32[]{:S(2)}) collective-permute-start(bf16[128,2,128]{0,2,1:T(8,128)(2,1)S(1)} %get-tuple-element.14), channel_id=1, source_target_pairs={{1,0},{2,1},{3,2},{5,4},{6,5},{7,6},{9,8},{10,9},{11,10},{13,12},{... | collective-permute-start | bytes 196616 | tf_op jit(solution)/shard_map/ppermute | solution.py:17
  120.5 4.3 %collective-permute-start.17 = (bf16[128,2,128]{0,2,1:T(8,128)(2,1)S(1)}, bf16[128,2,128]{0,2,1:T(8,128)(2,1)S(1)}, u32[]{:S(2)}, u32[]{:S(2)}) collective-permute-start(bf16[128,2,128]{0,2,1:T(8,128)(2,1)S(1)} %get-tuple-element.13), channel_id=1, source_target_pairs={{0,1},{1,2},{2,3},{4,5},{5,6},{6,7},{8,9},{9,10},{10,11},{12,13},{... | collective-permute-start | bytes 196616 | tf_op jit(solution)/shard_map/ppermute | solution.py:16
  (153 shorter events, 59.7 us)
Async XLA Ops:
  0.0 15.2 %copy-start = (bf16[1,8,4,128,128]{4,3,2,1,0:T(8,128)(2,1)S(1)}, bf16[1,8,4,128,128]{4,3,2,1,0:T(8,128)(2,1)}, u32[]{:S(2)}) copy-start(bf16[1,8,4,128,128]{4,3,2,1,0:T(8,128)(2,1)} %param.15) | copy-start | bytes 3145732
  6.3 6.8 %copy-start.2 = (bf16[1,8,128,128]{3,2,1,0:T(8,128)(2,1)S(1)}, bf16[1,8,128,128]{3,2,1,0:T(8,128)(2,1)}, u32[]{:S(2)}) copy-start(bf16[1,8,128,128]{3,2,1,0:T(8,128)(2,1)} %param.14) | copy-start | bytes 786436
  6.3 7.1 %collective-permute-start.1 = (bf16[128,2,128]{0,2,1:T(8,128)(2,1)S(1)}, bf16[128,2,128]{0,2,1:T(8,128)(2,1)S(1)}, u32[]{:S(2)}, u32[]{:S(2)}) collective-permute-start(bf16[128,2,128]{0,2,1:T(8,128)(2,1)S(1)} %get-tuple-element.28), channel_id=1, source_target_pairs={{1,0},{2,1},{3,2},{5,4},{6,5},{7,6},{9,8},{10,9},{11,10},{13,12},{... | collective-permute-start | bytes 196616 | tf_op jit(solution)/shard_map/ppermute | solution.py:17
  9.1 4.4 %collective-permute-start = (bf16[128,2,128]{0,2,1:T(8,128)(2,1)S(1)}, bf16[128,2,128]{0,2,1:T(8,128)(2,1)S(1)}, u32[]{:S(2)}, u32[]{:S(2)}) collective-permute-start(bf16[128,2,128]{0,2,1:T(8,128)(2,1)S(1)} %get-tuple-element.27), channel_id=1, source_target_pairs={{0,1},{1,2},{2,3},{4,5},{5,6},{6,7},{8,9},{9,10},{10,11},{12,13},{... | collective-permute-start | bytes 196616 | tf_op jit(solution)/shard_map/ppermute | solution.py:16
  13.1 14.0 %copy-start.17 = (pred[8,4]{1,0:T(8,128)(4,1)}, pred[8,4]{1,0:T(8,128)(4,1)S(1)}, u32[]{:S(2)}) copy-start(pred[8,4]{1,0:T(8,128)(4,1)S(1)} %copy.42) | copy-start | bytes 100
  17.9 6.5 %collective-permute-start.3 = (bf16[128,2,128]{0,2,1:T(8,128)(2,1)S(1)}, bf16[128,2,128]{0,2,1:T(8,128)(2,1)S(1)}, u32[]{:S(2)}, u32[]{:S(2)}) collective-permute-start(bf16[128,2,128]{0,2,1:T(8,128)(2,1)S(1)} %get-tuple-element.26), channel_id=1, source_target_pairs={{1,0},{2,1},{3,2},{5,4},{6,5},{7,6},{9,8},{10,9},{11,10},{13,12},{... | collective-permute-start | bytes 196616 | tf_op jit(solution)/shard_map/ppermute | solution.py:17
  19.8 5.5 %collective-permute-start.2 = (bf16[128,2,128]{0,2,1:T(8,128)(2,1)S(1)}, bf16[128,2,128]{0,2,1:T(8,128)(2,1)S(1)}, u32[]{:S(2)}, u32[]{:S(2)}) collective-permute-start(bf16[128,2,128]{0,2,1:T(8,128)(2,1)S(1)} %get-tuple-element.25), channel_id=1, source_target_pairs={{0,1},{1,2},{2,3},{4,5},{5,6},{6,7},{8,9},{9,10},{10,11},{12,13},{... | collective-permute-start | bytes 196616 | tf_op jit(solution)/shard_map/ppermute | solution.py:16
  29.4 4.1 %copy-start.5 = (f32[16,8,8,128]{3,1,2,0:T(8,128)S(1)}, f32[16,8,8,128]{3,1,2,0:T(8,128)}, u32[]{:S(2)}) copy-start(f32[16,8,8,128]{3,1,2,0:T(8,128)} %get-tuple-element.10) | copy-start | bytes 1572868
  30.4 5.9 %collective-permute-start.4 = (bf16[128,256]{0,1:T(8,128)(2,1)S(1)}, bf16[128,256]{0,1:T(8,128)(2,1)S(1)}, u32[]{:S(2)}, u32[]{:S(2)}) collective-permute-start(bf16[128,256]{0,1:T(8,128)(2,1)S(1)} %bitcast.321), channel_id=1, source_target_pairs={{0,4},{4,8},{8,12},{12,16},{16,20},{20,24},{24,28},{1,5},{5,9},{9,... | collective-permute-start | bytes 196616 | tf_op jit(solution)/shard_map/ppermute | solution.py:25
  37.2 7.7 %collective-permute-start.6 = (bf16[128,2,128]{0,2,1:T(8,128)(2,1)S(1)}, bf16[128,2,128]{0,2,1:T(8,128)(2,1)S(1)}, u32[]{:S(2)}, u32[]{:S(2)}) collective-permute-start(bf16[128,2,128]{0,2,1:T(8,128)(2,1)S(1)} %get-tuple-element.24), channel_id=1, source_target_pairs={{1,0},{2,1},{3,2},{5,4},{6,5},{7,6},{9,8},{10,9},{11,10},{13,12},{... | collective-permute-start | bytes 196616 | tf_op jit(solution)/shard_map/ppermute | solution.py:17
  39.1 6.7 %collective-permute-start.5 = (bf16[128,2,128]{0,2,1:T(8,128)(2,1)S(1)}, bf16[128,2,128]{0,2,1:T(8,128)(2,1)S(1)}, u32[]{:S(2)}, u32[]{:S(2)}) collective-permute-start(bf16[128,2,128]{0,2,1:T(8,128)(2,1)S(1)} %get-tuple-element.23), channel_id=1, source_target_pairs={{0,1},{1,2},{2,3},{4,5},{5,6},{6,7},{8,9},{9,10},{10,11},{12,13},{... | collective-permute-start | bytes 196616 | tf_op jit(solution)/shard_map/ppermute | solution.py:16
  51.0 6.5 %collective-permute-start.8 = (bf16[128,2,128]{0,2,1:T(8,128)(2,1)S(1)}, bf16[128,2,128]{0,2,1:T(8,128)(2,1)S(1)}, u32[]{:S(2)}, u32[]{:S(2)}) collective-permute-start(bf16[128,2,128]{0,2,1:T(8,128)(2,1)S(1)} %get-tuple-element.22), channel_id=1, source_target_pairs={{1,0},{2,1},{3,2},{5,4},{6,5},{7,6},{9,8},{10,9},{11,10},{13,12},{... | collective-permute-start | bytes 196616 | tf_op jit(solution)/shard_map/ppermute | solution.py:17
  52.9 5.6 %collective-permute-start.7 = (bf16[128,2,128]{0,2,1:T(8,128)(2,1)S(1)}, bf16[128,2,128]{0,2,1:T(8,128)(2,1)S(1)}, u32[]{:S(2)}, u32[]{:S(2)}) collective-permute-start(bf16[128,2,128]{0,2,1:T(8,128)(2,1)S(1)} %get-tuple-element.21), channel_id=1, source_target_pairs={{0,1},{1,2},{2,3},{4,5},{5,6},{6,7},{8,9},{9,10},{10,11},{12,13},{... | collective-permute-start | bytes 196616 | tf_op jit(solution)/shard_map/ppermute | solution.py:16
  64.2 5.9 %collective-permute-start.9 = (bf16[128,256]{0,1:T(8,128)(2,1)S(1)}, bf16[128,256]{0,1:T(8,128)(2,1)S(1)}, u32[]{:S(2)}, u32[]{:S(2)}) collective-permute-start(bf16[128,256]{0,1:T(8,128)(2,1)S(1)} %bitcast.322), channel_id=1, source_target_pairs={{0,4},{4,8},{8,12},{12,16},{16,20},{20,24},{24,28},{1,5},{5,9},{9,... | collective-permute-start | bytes 196616 | tf_op jit(solution)/shard_map/ppermute | solution.py:25
  66.5 3.6 %copy-start.10 = (bf16[1,2,128,128]{3,2,1,0:T(8,128)(2,1)S(1)}, bf16[1,2,128,128]{3,2,1,0:T(8,128)(2,1)}, u32[]{:S(2)}) copy-start(bf16[1,2,128,128]{3,2,1,0:T(8,128)(2,1)} %param.18) | copy-start | bytes 196612
  71.0 7.7 %collective-permute-start.11 = (bf16[128,2,128]{0,2,1:T(8,128)(2,1)S(1)}, bf16[128,2,128]{0,2,1:T(8,128)(2,1)S(1)}, u32[]{:S(2)}, u32[]{:S(2)}) collective-permute-start(bf16[128,2,128]{0,2,1:T(8,128)(2,1)S(1)} %get-tuple-element.20), channel_id=1, source_target_pairs={{1,0},{2,1},{3,2},{5,4},{6,5},{7,6},{9,8},{10,9},{11,10},{13,12},{... | collective-permute-start | bytes 196616 | tf_op jit(solution)/shard_map/ppermute | solution.py:17
  72.9 6.7 %collective-permute-start.10 = (bf16[128,2,128]{0,2,1:T(8,128)(2,1)S(1)}, bf16[128,2,128]{0,2,1:T(8,128)(2,1)S(1)}, u32[]{:S(2)}, u32[]{:S(2)}) collective-permute-start(bf16[128,2,128]{0,2,1:T(8,128)(2,1)S(1)} %get-tuple-element.19), channel_id=1, source_target_pairs={{0,1},{1,2},{2,3},{4,5},{5,6},{6,7},{8,9},{9,10},{10,11},{12,13},{... | collective-permute-start | bytes 196616 | tf_op jit(solution)/shard_map/ppermute | solution.py:16
  84.8 6.7 %collective-permute-start.13 = (bf16[128,2,128]{0,2,1:T(8,128)(2,1)S(1)}, bf16[128,2,128]{0,2,1:T(8,128)(2,1)S(1)}, u32[]{:S(2)}, u32[]{:S(2)}) collective-permute-start(bf16[128,2,128]{0,2,1:T(8,128)(2,1)S(1)} %get-tuple-element.18), channel_id=1, source_target_pairs={{1,0},{2,1},{3,2},{5,4},{6,5},{7,6},{9,8},{10,9},{11,10},{13,12},{... | collective-permute-start | bytes 196616 | tf_op jit(solution)/shard_map/ppermute | solution.py:17
  86.7 5.6 %collective-permute-start.12 = (bf16[128,2,128]{0,2,1:T(8,128)(2,1)S(1)}, bf16[128,2,128]{0,2,1:T(8,128)(2,1)S(1)}, u32[]{:S(2)}, u32[]{:S(2)}) collective-permute-start(bf16[128,2,128]{0,2,1:T(8,128)(2,1)S(1)} %get-tuple-element.17), channel_id=1, source_target_pairs={{0,1},{1,2},{2,3},{4,5},{5,6},{6,7},{8,9},{9,10},{10,11},{12,13},{... | collective-permute-start | bytes 196616 | tf_op jit(solution)/shard_map/ppermute | solution.py:16
  98.0 5.9 %collective-permute-start.14 = (bf16[128,256]{0,1:T(8,128)(2,1)S(1)}, bf16[128,256]{0,1:T(8,128)(2,1)S(1)}, u32[]{:S(2)}, u32[]{:S(2)}) collective-permute-start(bf16[128,256]{0,1:T(8,128)(2,1)S(1)} %bitcast.320), channel_id=1, source_target_pairs={{0,4},{4,8},{8,12},{12,16},{16,20},{20,24},{24,28},{1,5},{5,9},{9,... | collective-permute-start | bytes 196616 | tf_op jit(solution)/shard_map/ppermute | solution.py:25
  104.8 7.7 %collective-permute-start.16 = (bf16[128,2,128]{0,2,1:T(8,128)(2,1)S(1)}, bf16[128,2,128]{0,2,1:T(8,128)(2,1)S(1)}, u32[]{:S(2)}, u32[]{:S(2)}) collective-permute-start(bf16[128,2,128]{0,2,1:T(8,128)(2,1)S(1)} %get-tuple-element.16), channel_id=1, source_target_pairs={{1,0},{2,1},{3,2},{5,4},{6,5},{7,6},{9,8},{10,9},{11,10},{13,12},{... | collective-permute-start | bytes 196616 | tf_op jit(solution)/shard_map/ppermute | solution.py:17
  106.7 6.7 %collective-permute-start.15 = (bf16[128,2,128]{0,2,1:T(8,128)(2,1)S(1)}, bf16[128,2,128]{0,2,1:T(8,128)(2,1)S(1)}, u32[]{:S(2)}, u32[]{:S(2)}) collective-permute-start(bf16[128,2,128]{0,2,1:T(8,128)(2,1)S(1)} %get-tuple-element.15), channel_id=1, source_target_pairs={{0,1},{1,2},{2,3},{4,5},{5,6},{6,7},{8,9},{9,10},{10,11},{12,13},{... | collective-permute-start | bytes 196616 | tf_op jit(solution)/shard_map/ppermute | solution.py:16
  118.6 6.5 %collective-permute-start.18 = (bf16[128,2,128]{0,2,1:T(8,128)(2,1)S(1)}, bf16[128,2,128]{0,2,1:T(8,128)(2,1)S(1)}, u32[]{:S(2)}, u32[]{:S(2)}) collective-permute-start(bf16[128,2,128]{0,2,1:T(8,128)(2,1)S(1)} %get-tuple-element.14), channel_id=1, source_target_pairs={{1,0},{2,1},{3,2},{5,4},{6,5},{7,6},{9,8},{10,9},{11,10},{13,12},{... | collective-permute-start | bytes 196616 | tf_op jit(solution)/shard_map/ppermute | solution.py:17
  120.5 5.6 %collective-permute-start.17 = (bf16[128,2,128]{0,2,1:T(8,128)(2,1)S(1)}, bf16[128,2,128]{0,2,1:T(8,128)(2,1)S(1)}, u32[]{:S(2)}, u32[]{:S(2)}) collective-permute-start(bf16[128,2,128]{0,2,1:T(8,128)(2,1)S(1)} %get-tuple-element.13), channel_id=1, source_target_pairs={{0,1},{1,2},{2,3},{4,5},{5,6},{6,7},{8,9},{9,10},{10,11},{12,13},{... | collective-permute-start | bytes 196616 | tf_op jit(solution)/shard_map/ppermute | solution.py:16
  (18 other events, 24.1 us)
where the time goes:
time: 134 us; the launch traced here: 133 us
  starting transfers between devices  59.9 us (45%)
  local copies, waits for them, and re-layouts  26.2 us (20%)
  matrix products  22.7 us (17%)
  waiting for transfers between devices  14 us (10%)
  other arithmetic  9.08 us (7%)
    ppermute x8, starting transfers between devices, padded(): before = lax.ppermute(last, axis, up)  36.4 us
    ppermute x8, starting transfers between devices, padded(): after = lax.ppermute(leading, axis, down)  16.2 us
    dot_general x8, matrix products, on_device(): jnp.einsum('rkij,srkj->sri', neighbours, gathered, preferred_element_type...  14.2 us
    gather x8, local copies, waits for them, and re-layouts, on_device(): gathered = jnp.take(extended, local_cols, axis=1)  13.2 us
    unnamed x50, local copies, waits for them, and re-layouts  8.94 us
    ppermute x3, waiting for transfers between devices, from_behind(): return lax.ppermute(block, axis, route)  7.37 us
    ppermute x3, starting transfers between devices, from_behind(): return lax.ppermute(block, axis, route)  7.28 us
    ppermute x8, waiting for transfers between devices, padded(): before = lax.ppermute(last, axis, up)  6.65 us
  transfers between devices with their start and end apart: 19, of which 10 were waited for; matrix products, arithmetic and copies ran while one was open for 4% of the time, Pallas kernels for 0%

commit v1 on v0

v1 whole, which is shorter than its diff:
```python
import functools

import jax
import jax.numpy as jnp
from jax import lax
from jax.experimental import pallas as pl
from jax.experimental.pallas import tpu as pltpu
from jax.sharding import PartitionSpec as P

HALO = 2
BF = jnp.bfloat16
F32 = jnp.float32


def dot_nt(a, b):
    return lax.dot_general(a, b, (((1,), (1,)), ((), ())), preferred_element_type=F32)


def dot_nn(a, b):
    return lax.dot_general(a, b, (((1,), (0,)), ((), ())), preferred_element_type=F32)


class Dims:
    def __init__(self, ticks, sources, count, neigh, width, nq, faces):
        self.ticks, self.sources, self.count, self.neigh = ticks, sources, count, neigh
        self.width, self.nq, self.faces = width, nq, faces
        self.batch = ticks * sources
        self.group = nq * width
        self.slots = max(4, min(faces, 5))
        self.shifts = None if faces <= 4 else (-2, -1, 0, 1, 2)
        self.hops = 4 if faces <= 4 else 5
        self.ext = count + 2 * HALO
        self.at_iface = count * neigh
        self.at_face = self.at_iface + nq

    def source_face(self, face, hop):
        return face ^ hop if self.shifts is None else face + self.shifts[hop]

    def slot(self, face):
        return lax.rem(face + 2 * self.slots, self.slots)


def sweep_rows(d, meta, right_at, ext, diag, off, inv, store, starts, rows):
    def one(r, carry):
        w = jnp.concatenate([diag[r]] + [off[r, k] for k in range(d.neigh)], axis=1)
        inverse = inv[r]
        c = [meta[r * d.neigh + k] for k in range(d.neigh)]
        for s in starts:
            span = pl.ds(s, rows)
            own = ext[r + HALO, span, :]
            x = jnp.concatenate([own] + [ext[c[k], span, :] for k in range(d.neigh)], axis=1)
            correction = (right_at(r, span).astype(F32) - dot_nt(x, w)).astype(BF)
            store(r, span, (own.astype(F32) + dot_nt(correction, inverse)).astype(BF))
        return carry

    lax.fori_loop(0, d.count, one, 0)


def edge_rows(d, parity):
    last = d.count - HALO
    return last * (1 - parity), last * parity


def place_halo(d, parity, ext, pair, cross, span, source):
    up = d.count + HALO
    ext[pl.ds(up * (1 - parity), HALO), span, :] = pair[:, source, :]
    ext[pl.ds(up * parity, HALO), span, :] = cross[:, source, :]


def first_kernel(d, meta, rhs, inflow, inv, coupling, right, field, grows, gfield, pair, cross):
    face = meta[d.at_face]
    parity = lax.rem(face, 2)
    w = d.width
    for t in range(d.ticks):
        for r in range(d.count):
            right[r, t * d.sources : (t + 1) * d.sources, :] = rhs[t, :, r * w : (r + 1) * w]
    for q in range(d.nq):
        row = meta[d.at_iface + q]
        coupled = dot_nt(inflow[:, q * w : (q + 1) * w], coupling[q])
        right[row, 0 : d.sources, :] = (right[row, 0 : d.sources, :].astype(F32) - coupled).astype(BF)
        turned = coupling[q].astype(F32).T.astype(BF)
        grows[q] = turned
        gfield[q] = dot_nt(turned, inv[row]).astype(BF)

    def one(r, carry):
        field[r] = dot_nt(right[r], inv[r]).astype(BF)
        return carry

    lax.fori_loop(0, d.count, one, 0)
    for start, buffer in zip(edge_rows(d, parity), (pair, cross)):
        for e in range(HALO):
            buffer[e, 0 : d.batch, :] = field[start + e]
            for q in range(d.nq):
                hit = meta[d.at_iface + q] == start + e
                buffer[e, d.batch + q * w : d.batch + (q + 1) * w, :] = jnp.where(hit, gfield[q], jnp.zeros((w, w), BF))


def batch_kernel(d, last, meta, right, field, pair_in, cross_in, diag, off, inv, *rest):
    if last:
        out, faces_out, sent, ext = rest
    else:
        out, pair, cross, ext = rest
    parity = lax.rem(meta[d.at_face], 2)
    span = pl.ds(0, d.batch)
    ext[HALO : HALO + d.count] = field[...]
    place_halo(d, parity, ext, pair_in, cross_in, span, span)

    def store(r, span, value):
        out[r, span, :] = value

    sweep_rows(
        d, meta, lambda r, span: right[r, span, :], ext, diag, off, inv, store, range(0, d.batch, d.group), d.group
    )
    if last:
        for q in range(d.nq):
            row = meta[d.at_iface + q]
            for t in range(d.ticks):
                faces_out[t, q] = out[row, t * d.sources : (t + 1) * d.sources, :]
            sent[q] = out[row, 0 : d.sources, :]
    else:
        for start, buffer in zip(edge_rows(d, parity), (pair, cross)):
            buffer[...] = out[pl.ds(start, HALO)]


def group_start(d, face):
    return pl.multiple_of(d.slot(face) * d.group, d.group)


def fill_grows(d, meta, grows, gright, face):
    gright[...] = jnp.zeros_like(gright)
    for q in range(d.nq):
        row = meta[d.at_iface + q]
        gright[row, pl.ds(group_start(d, face) + q * d.width, d.width), :] = grows[q]


def coupling_first_kernel(d, meta, grows, gfield, pair_in, cross_in, diag, off, inv, out, pair, cross, ext, gright):
    face = meta[d.at_face]
    parity = lax.rem(face, 2)
    fill_grows(d, meta, grows, gright, face)
    ext[...] = jnp.zeros_like(ext)
    out[...] = jnp.zeros_like(out)
    for q in range(d.nq):
        row = meta[d.at_iface + q] + HALO
        ext[row, pl.ds(group_start(d, face) + q * d.width, d.width), :] = gfield[q]
    up = d.count + HALO
    source = pl.ds(d.batch, d.group)
    pair_face, cross_face = face + 1 - 2 * parity, face - 1 + 2 * parity
    ext[pl.ds(up * (1 - parity), HALO), pl.ds(group_start(d, pair_face), d.group), :] = pair_in[:, source, :]
    ext[pl.ds(up * parity, HALO), pl.ds(group_start(d, cross_face), d.group), :] = cross_in[:, source, :]

    def store(r, span, value):
        out[r, span, :] = value

    starts = [group_start(d, face + shift) for shift in (-1, 0, 1)]
    sweep_rows(d, meta, lambda r, span: gright[r, span, :], ext, diag, off, inv, store, starts, d.group)
    for start, buffer in zip(edge_rows(d, parity), (pair, cross)):
        for i, s in enumerate(starts):
            buffer[:, i * d.group : (i + 1) * d.group, :] = out[pl.ds(start, HALO), pl.ds(s, d.group), :]


def coupling_last_kernel(d, meta, grows, gfirst, pair_in, cross_in, diag, off, inv, out, chain, ext, gright):
    face = meta[d.at_face]
    parity = lax.rem(face, 2)
    fill_grows(d, meta, grows, gright, face)
    ext[...] = jnp.zeros_like(ext)
    ext[HALO : HALO + d.count] = gfirst[...]
    up = d.count + HALO
    neighbours = ((up * (1 - parity), face + 1 - 2 * parity, pair_in), (up * parity, face - 1 + 2 * parity, cross_in))
    for start, other, block in neighbours:
        for i, shift in enumerate((-1, 0, 1)):
            ext[pl.ds(start, HALO), pl.ds(group_start(d, other + shift), d.group), :] = block[
                :, i * d.group : (i + 1) * d.group, :
            ]

    def store(r, span, value):
        out[span, pl.ds(pl.multiple_of(r * d.width, d.width), d.width)] = value

    starts = range(0, d.slots * d.group, d.group)
    sweep_rows(d, meta, lambda r, span: gright[r, span, :], ext, diag, off, inv, store, starts, d.group)
    for q in range(d.nq):
        lane = pl.multiple_of(meta[d.at_iface + q] * d.width, d.width)
        chain[:, q * d.width : (q + 1) * d.width] = out[:, pl.ds(lane, d.width)]


def chain_kernel(d, tick, meta, chain, faces_out, *rest):
    arrived, sent = rest[:-1], rest[-1]
    face = meta[d.at_face]
    total = jnp.zeros((d.sources, d.group), F32)
    for hop, block in enumerate(arrived):
        x = jnp.concatenate([block[q] for q in range(d.nq)], axis=1)
        total += dot_nn(x, chain[pl.ds(group_start(d, d.source_face(face, hop)), d.group), :])
    for q in range(d.nq):
        sent[q] = (faces_out[tick, q].astype(F32) - total[:, q * d.width : (q + 1) * d.width]).astype(BF)


def final_kernel(d, meta, fields, coupled, *rest):
    arrived, out = rest[:-1], rest[-1]
    face = meta[d.at_face]
    w = d.width
    for r in range(d.count):
        out[0, :, r * w : (r + 1) * w] = fields[r, 0 : d.sources, :]
    for t in range(1, d.ticks):
        blocks = arrived[(t - 1) * d.hops : t * d.hops]
        total = jnp.zeros((d.sources, d.count * w), F32)
        for hop, block in enumerate(blocks):
            x = jnp.concatenate([block[q] for q in range(d.nq)], axis=1)
            total += dot_nn(x, coupled[pl.ds(group_start(d, d.source_face(face, hop)), d.group), :])
        for r in range(d.count):
            base = fields[r, t * d.sources : (t + 1) * d.sources, :].astype(F32)
            out[t, :, r * w : (r + 1) * w] = (base - total[:, r * w : (r + 1) * w]).astype(BF)


def call(body, name, inputs, outs, scratch=(), flops=0):
    smem = pl.BlockSpec(memory_space=pltpu.SMEM)
    vmem = pl.BlockSpec(memory_space=pltpu.VMEM)
    moved = sum(x.size * x.dtype.itemsize for x in inputs) + sum(2 * functools.reduce(lambda a, b: a * b, s) for s in outs)
    return pl.pallas_call(
        body,
        name=name,
        out_shape=[jax.ShapeDtypeStruct(s, BF) for s in outs],
        in_specs=[smem] + [vmem] * (len(inputs) - 1),
        out_specs=[vmem] * len(outs),
        scratch_shapes=[pltpu.VMEM(s, BF) for s in scratch],
        compiler_params=pltpu.CompilerParams(vmem_limit_bytes=32 * 1024 * 1024),
        cost_estimate=pl.CostEstimate(flops=flops, bytes_accessed=moved, transcendentals=0),
    )(*inputs)


def on_device(rhs, inflow, diag_tiles, off_tiles, cols, inverse_tiles, coupling, iface):
    faces, slabs = lax.axis_size("face"), lax.axis_size("slab")
    ticks, _, sources, _ = rhs.shape
    _, count, neigh, width, _ = off_tiles.shape
    nq = coupling.shape[1]
    d = Dims(ticks, sources, count, neigh, width, nq, faces)
    diag, off, inv, couple = diag_tiles[0], off_tiles[0], inverse_tiles[0], coupling[0]
    face = lax.axis_index("face").astype(jnp.int32)
    local = cols[0].reshape(-1) - (face * count - HALO)
    meta = jnp.concatenate([local, iface, face[None]])
    tile = width * width

    pairing = [(i, i ^ 1) for i in range(faces) if i ^ 1 < faces]
    crossing = [(i, ((i + 1) ^ 1) - 1) for i in range(faces) if 0 <= ((i + 1) ^ 1) - 1 < faces]

    def exchange(pair, cross):
        got = lax.ppermute(cross, "face", crossing)
        return lax.ppermute(pair, "face", pairing), got

    def onward(block):
        got = []
        for hop in range(d.hops):
            route = []
            for s in range(1, slabs):
                for f in range(faces):
                    g = d.source_face(f, hop)
                    if 0 <= g < faces:
                        route.append(((s - 1) * faces + g, s * faces + f))
            got.append(lax.ppermute(block, ("slab", "face"), route))
        return got

    batch, group, ext, wide = d.batch, d.group, d.ext, d.slots * d.group
    right, field, grows, gfield, pair, cross = call(
        functools.partial(first_kernel, d),
        "first",
        [meta, rhs[:, 0], inflow[0], inv, couple],
        [(count, batch, width)] * 2 + [(nq, width, width)] * 2 + [(HALO, batch + group, width)] * 2,
        flops=2 * batch * count * tile,
    )
    pair0, cross0 = exchange(pair, cross)
    field, pair, cross = call(
        functools.partial(batch_kernel, d, False),
        "second",
        [meta, right, field, pair0, cross0, diag, off, inv],
        [(count, batch, width)] + [(HALO, batch, width)] * 2,
        [(ext, batch, width)],
        flops=2 * batch * count * tile * (neigh + 2),
    )
    pair1, cross1 = exchange(pair, cross)
    gfirst, gpair, gcross = call(
        functools.partial(coupling_first_kernel, d),
        "coupling_first",
        [meta, grows, gfield, pair0, cross0, diag, off, inv],
        [(count, wide, width)] + [(HALO, 3 * group, width)] * 2,
        [(ext, wide, width), (count, wide, width)],
        flops=2 * 3 * group * count * tile * (neigh + 2),
    )
    gpair, gcross = exchange(gpair, gcross)
    fields, faces_out, sent = call(
        functools.partial(batch_kernel, d, True),
        "third",
        [meta, right, field, pair1, cross1, diag, off, inv],
        [(count, batch, width), (ticks, nq, sources, width), (nq, sources, width)],
        [(ext, batch, width)],
        flops=2 * batch * count * tile * (neigh + 2),
    )
    arrived = onward(sent)
    coupled, chain = call(
        functools.partial(coupling_last_kernel, d),
        "coupling_last",
        [meta, grows, gfirst, gpair, gcross, diag, off, inv],
        [(wide, count * width), (wide, group)],
        [(ext, wide, width), (count, wide, width)],
        flops=2 * wide * count * tile * (neigh + 2),
    )
    everything = list(arrived)
    for tick in range(1, ticks - 1):
        (sent,) = call(
            functools.partial(chain_kernel, d, tick),
            "chain",
            [meta, chain, faces_out] + arrived,
            [(nq, sources, width)],
            flops=2 * sources * wide * group,
        )
        arrived = onward(sent)
        everything += arrived
    (out,) = call(
        functools.partial(final_kernel, d),
        "final",
        [meta, fields, coupled] + everything,
        [(ticks, sources, count * width)],
        flops=2 * (ticks - 1) * sources * wide * count * width,
    )
    return out[:, None]


def solution(mesh):
    placed = (
        P(None, "slab", None, "face"),
        P("slab", None, "face"),
        P("slab", "face", None, None),
        P("slab", "face", None, None, None),
        P("slab", "face", None),
        P("slab", "face", None, None),
        P("slab", "face", None, None),
        P("face"),
    )
    return jax.shard_map(
        on_device,
        mesh=mesh,
        in_specs=placed,
        out_specs=P(None, "slab", None, "face"),
        check_vma=False,
    )
```

time: 134 us -> 113 us (0.84)
  Pallas kernels: 0 us -> 38.8 us
  matrix products: 22.7 us -> 0 us
  local copies, waits for them, and re-layouts: 26.2 us -> 7.15 us
  starting transfers between devices: 59.9 us -> 41.3 us
  waiting for transfers between devices: 14 us -> 22.6 us
  other arithmetic: 9.08 us -> 1.42 us
    pallas_call x0 -> x8, Pallas kernels: none -> 38.8 us  [call(): pl.pallas_call(body, name=name, out_shape=[jax.ShapeDtypeStruct(s, BF) fo...]
    dot_general x36 -> x0, matrix products: 22.7 us -> none  [the longest x8 14.2 us: on_device(): jnp.einsum('rkij,srkj->sri', neighbours, gathered, preferred_element_type...]
    ppermute x19 -> x18, starting transfers between devices: 59.9 us -> 41.3 us  [the longest x12 31.8 us: onward(): got.append(lax.ppermute(block, ('slab', 'face'), route))]
    gather x11 -> x0, local copies, waits for them, and re-layouts: 14.9 us -> none  [the longest x8 13.2 us: on_device(): gathered = jnp.take(extended, local_cols, axis=1)]
    ppermute x19 -> x18, waiting for transfers between devices: 14 us -> 22.6 us  [the longest x12 11.4 us: onward(): got.append(lax.ppermute(block, ('slab', 'face'), route))]
    convert_element_type x8 -> x0, other arithmetic: 4.76 us -> none  [on_device(): correction = (right.astype(jnp.float32) - product).astype(jnp.bfloat16)]
    unnamed x1 -> x0, other arithmetic: 2.55 us -> none
    another operation x5 -> x0, local copies, waits for them, and re-layouts: 2 us -> none  [the longest x4 1.98 us: on_device(): solution = jnp.stack(results)]
  transfers between devices with their start and end apart: 19 -> 18, of which waited for: 10 -> 7; matrix products, arithmetic and copies ran while one was open for 4% -> 0% of each run, Pallas kernels for 0% -> 21%
where the time goes in v1:
time: 113 us; the launch traced here: 112 us
  starting transfers between devices  41.3 us (37%)
  Pallas kernels  38.8 us (34%)
  waiting for transfers between devices  22.6 us (20%)
  local copies, waits for them, and re-layouts  7.15 us (6%)
  other arithmetic  1.42 us (1%)
    pallas_call x8, Pallas kernels, call(): pl.pallas_call(body, name=name, out_shape=[jax.ShapeDtypeStruct(s, BF) fo...  38.8 us
    ppermute x12, starting transfers between devices, onward(): got.append(lax.ppermute(block, ('slab', 'face'), route))  31.8 us
    ppermute x12, waiting for transfers between devices, onward(): got.append(lax.ppermute(block, ('slab', 'face'), route))  11.4 us
    ppermute x3, waiting for transfers between devices, exchange(): got = lax.ppermute(cross, 'face', crossing)  11.2 us
    ppermute x3, starting transfers between devices, exchange(): got = lax.ppermute(cross, 'face', crossing)  8.58 us
    unnamed x18, local copies, waits for them, and re-layouts  6.98 us
  transfers between devices with their start and end apart: 18, of which 7 were waited for; matrix products, arithmetic and copies ran while one was open for 0% of the time, Pallas kernels for 21%

profile of v1, /device:TPU:9, one launch (start us, length us, event | category | flops | bytes accessed | tf_op | source)
XLA Modules:
  0.0 111.5 jit_solution(9410299402910327609)
XLA Ops:
  5.4 2.4 %first.1 = (bf16[8,512,128]{2,1,0:T(8,128)(2,1)S(1)}, bf16[8,512,128]{2,1,0:T(8,128)(2,1)S(1)}, bf16[2,128,128]{2,1,0:T(8,128)(2,1)S(1)}, bf16[2,128,128]{2,1,0:...) custom-call(s32[35]{0:T(128)S(1)} %pad_add_fusion.meta, ...), custom_call_target="tpu_custom_call" | custom-call | flops 134217728 | bytes 4456588 | tf_op jit(solution)/shard_map/first/pallas_call | solution.py:217
  8.6 3.0 %collective-permute-start.1 = (bf16[2,768,128]{2,1,0:T(8,128)(2,1)S(1)}, bf16[2,768,128]{2,1,0:T(8,128)(2,1)S(1)}, u32[]{:S(2)}, u32[]{:S(2)}) collective-permute-start(bf16[2,768,128]{2,1,0:T(8,128)(2,1)S(1)} %get-tuple-element.25), channel_id=1, source_target_pairs={{1,2},{2,1},{5,6},{6,5},{9,10},{10,9},{13,14},{14,13},{17,18},{18,... | collective-permute-start | bytes 1179656 | tf_op jit(solution)/shard_map/ppermute | solution.py:245
  11.6 6.0 %collective-permute-done.1.cross_in = bf16[2,768,128]{2,1,0:T(8,128)(2,1)S(1)} collective-permute-done((bf16[2,768,128]{2,1,0:T(8,128)(2,1)S(1)}, bf16[2,768,128]{2,1,0:T(8,128)(2,1)S(1)}, u32[]{:S(2)}, u32[]{:S(2)}) %collective-permute-start.1) | collective-permute-done | bytes 393248 | tf_op jit(solution)/shard_map/ppermute | solution.py:245
  20.8 8.9 %coupling_first.1 = (bf16[8,1024,128]{2,1,0:T(8,128)(2,1)S(1)}, bf16[2,768,128]{2,1,0:T(8,128)(2,1)S(1)}, bf16[2,768,128]{2,1,0:T(8,128)(2,1)S(1)}) custom-call(s32[35]{0:T(128)S(1)} %pad_add_fusion.meta, bf16[2,128,128]{2,1,0:T(8,128)(2,1)S(1)} %get-tuple-element.30.grows, bf16[2,128,128]{2,1,0:T(8,128)(2,1)S(1)} %get-tuple-element.31.gfield, ...), custom_call_target="tpu_custom_call" | custom-call | flops 1207959552 | bytes 5374092 | tf_op jit(solution)/shard_map/coupling_first/pallas_call | solution.py:217
  29.8 3.0 %collective-permute-start.5 = (bf16[2,768,128]{2,1,0:T(8,128)(2,1)S(1)}, bf16[2,768,128]{2,1,0:T(8,128)(2,1)S(1)}, u32[]{:S(2)}, u32[]{:S(2)}) collective-permute-start(bf16[2,768,128]{2,1,0:T(8,128)(2,1)S(1)} %get-tuple-element.34), channel_id=1, source_target_pairs={{1,2},{2,1},{5,6},{6,5},{9,10},{10,9},{13,14},{14,13},{17,18},{18,... | collective-permute-start | bytes 1179656 | tf_op jit(solution)/shard_map/ppermute | solution.py:245
  32.8 6.1 %second.1 = (bf16[8,512,128]{2,1,0:T(8,128)(2,1)S(1)}, bf16[2,512,128]{2,1,0:T(8,128)(2,1)S(1)}, bf16[2,512,128]{2,1,0:T(8,128)(2,1)S(1)}) custom-call(s32[35]{0:T(128)S(1)} %pad_add_fusion.meta, bf16[8,512,128]{2,1,0:T(8,128)(2,1)S(1)} %get-tuple-element.22.right, bf16[8,512,128]{2,1,0:T(8,128)(2,1)S(1)} %get-tuple-element.23.field, ...), custom_call_target="tpu_custom_call" | custom-call | flops 805306368 | bytes 6029452 | tf_op jit(solution)/shard_map/second/pallas_call | solution.py:217
  39.1 2.5 %collective-permute-start.3 = (bf16[2,512,128]{2,1,0:T(8,128)(2,1)S(1)}, bf16[2,512,128]{2,1,0:T(8,128)(2,1)S(1)}, u32[]{:S(2)}, u32[]{:S(2)}) collective-permute-start(bf16[2,512,128]{2,1,0:T(8,128)(2,1)S(1)} %get-tuple-element.28), channel_id=1, source_target_pairs={{1,2},{2,1},{5,6},{6,5},{9,10},{10,9},{13,14},{14,13},{17,18},{18,... | collective-permute-start | bytes 786440 | tf_op jit(solution)/shard_map/ppermute | solution.py:245
  41.6 5.1 %collective-permute-done.3.cross_in = bf16[2,512,128]{2,1,0:T(8,128)(2,1)S(1)} collective-permute-done((bf16[2,512,128]{2,1,0:T(8,128)(2,1)S(1)}, bf16[2,512,128]{2,1,0:T(8,128)(2,1)S(1)}, u32[]{:S(2)}, u32[]{:S(2)}) %collective-permute-start.3) | collective-permute-done | bytes 262176 | tf_op jit(solution)/shard_map/ppermute | solution.py:245
  46.7 6.1 %third.1 = (bf16[8,512,128]{2,1,0:T(8,128)(2,1)S(1)}, bf16[4,2,128,128]{3,2,1,0:T(8,128)(2,1)S(1)}, bf16[2,128,128]{2,1,0:T(8,128)(2,1)S(1)}) custom-call(s32[35]{0:T(128)S(1)} %pad_add_fusion.meta, bf16[8,512,128]{2,1,0:T(8,128)(2,1)S(1)} %get-tuple-element.22.right, bf16[8,512,128]{2,1,0:T(8,128)(2,1)S(1)} %get-tuple-element.26.field, ...), custom_call_target="tpu_custom_call" | custom-call | flops 805306368 | bytes 5570700 | tf_op jit(solution)/shard_map/third/pallas_call | solution.py:217
  52.9 3.1 %collective-permute-start.6 = (bf16[2,128,128]{2,1,0:T(8,128)(2,1)S(1)}, bf16[2,128,128]{2,1,0:T(8,128)(2,1)S(1)}, u32[]{:S(2)}, u32[]{:S(2)}) collective-permute-start(bf16[2,128,128]{2,1,0:T(8,128)(2,1)S(1)} %get-tuple-element.36), channel_id=1, source_target_pairs={{0,4},{1,5},{2,6},{3,7},{4,8},{5,9},{6,10},{7,11},{8,12},{9,13},{1... | collective-permute-start | bytes 196616 | tf_op jit(solution)/shard_map/ppermute | solution.py:257
  56.0 1.9 %collective-permute-start.7 = (bf16[2,128,128]{2,1,0:T(8,128)(2,1)S(1)}, bf16[2,128,128]{2,1,0:T(8,128)(2,1)S(1)}, u32[]{:S(2)}, u32[]{:S(2)}) collective-permute-start(bf16[2,128,128]{2,1,0:T(8,128)(2,1)S(1)} %get-tuple-element.36), channel_id=1, source_target_pairs={{1,4},{0,5},{3,6},{2,7},{5,8},{4,9},{7,10},{6,11},{9,12},{8,13},{1... | collective-permute-start | bytes 196616 | tf_op jit(solution)/shard_map/ppermute | solution.py:257
  58.0 5.0 %collective-permute-start.8 = (bf16[2,128,128]{2,1,0:T(8,128)(2,1)S(1)}, bf16[2,128,128]{2,1,0:T(8,128)(2,1)S(1)}, u32[]{:S(2)}, u32[]{:S(2)}) collective-permute-start(bf16[2,128,128]{2,1,0:T(8,128)(2,1)S(1)} %get-tuple-element.36), channel_id=1, source_target_pairs={{2,4},{3,5},{0,6},{1,7},{6,8},{7,9},{4,10},{5,11},{10,12},{11,13},... | collective-permute-start | bytes 196616 | tf_op jit(solution)/shard_map/ppermute | solution.py:257
  63.0 4.0 %collective-permute-start.9 = (bf16[2,128,128]{2,1,0:T(8,128)(2,1)S(1)}, bf16[2,128,128]{2,1,0:T(8,128)(2,1)S(1)}, u32[]{:S(2)}, u32[]{:S(2)}) collective-permute-start(bf16[2,128,128]{2,1,0:T(8,128)(2,1)S(1)} %get-tuple-element.36), channel_id=1, source_target_pairs={{3,4},{2,5},{1,6},{0,7},{7,8},{6,9},{5,10},{4,11},{11,12},{10,13},... | collective-permute-start | bytes 196616 | tf_op jit(solution)/shard_map/ppermute | solution.py:257
  67.0 11.1 %coupling_last.1 = (bf16[1024,1024]{1,0:T(8,128)(2,1)S(1)}, bf16[1024,256]{1,0:T(8,128)(2,1)S(1)}) custom-call(s32[35]{0:T(128)S(1)} %pad_add_fusion.meta, bf16[2,128,128]{2,1,0:T(8,128)(2,1)S(1)} %get-tuple-element.30.grows, bf16[8,1024,128]{2,1,0:T(8,128)(2,1)S(1)} %get-tuple-element.32.gfirst, bf16[2,768,128]{2,1,0:T(8,128)(2,1)S(1)} %collective-permute-done.4.pair_in, ...), custom_call_target="tpu_custom_call" | custom-call | flops 1610612736 | bytes 7143564 | tf_op jit(solution)/shard_map/coupling_last/pallas_call | solution.py:217
  78.9 3.1 %collective-permute-start.10 = (bf16[2,128,128]{2,1,0:T(8,128)(2,1)S(1)}, bf16[2,128,128]{2,1,0:T(8,128)(2,1)S(1)}, u32[]{:S(2)}, u32[]{:S(2)}) collective-permute-start(bf16[2,128,128]{2,1,0:T(8,128)(2,1)S(1)} %chain.2), channel_id=1, source_target_pairs={{0,4},{1,5},{2,6},{3,7},{4,8},{5,9},{6,10},{7,11},{8,12},{9,13},{1... | collective-permute-start | bytes 196616 | tf_op jit(solution)/shard_map/ppermute | solution.py:257
  82.1 1.9 %collective-permute-start.11 = (bf16[2,128,128]{2,1,0:T(8,128)(2,1)S(1)}, bf16[2,128,128]{2,1,0:T(8,128)(2,1)S(1)}, u32[]{:S(2)}, u32[]{:S(2)}) collective-permute-start(bf16[2,128,128]{2,1,0:T(8,128)(2,1)S(1)} %chain.2), channel_id=1, source_target_pairs={{1,4},{0,5},{3,6},{2,7},{5,8},{4,9},{7,10},{6,11},{9,12},{8,13},{1... | collective-permute-start | bytes 196616 | tf_op jit(solution)/shard_map/ppermute | solution.py:257
  84.0 2.3 %collective-permute-start.12 = (bf16[2,128,128]{2,1,0:T(8,128)(2,1)S(1)}, bf16[2,128,128]{2,1,0:T(8,128)(2,1)S(1)}, u32[]{:S(2)}, u32[]{:S(2)}) collective-permute-start(bf16[2,128,128]{2,1,0:T(8,128)(2,1)S(1)} %chain.2), channel_id=1, source_target_pairs={{2,4},{3,5},{0,6},{1,7},{6,8},{7,9},{4,10},{5,11},{10,12},{11,13},... | collective-permute-start | bytes 196616 | tf_op jit(solution)/shard_map/ppermute | solution.py:257
  86.3 2.5 %collective-permute-start.13 = (bf16[2,128,128]{2,1,0:T(8,128)(2,1)S(1)}, bf16[2,128,128]{2,1,0:T(8,128)(2,1)S(1)}, u32[]{:S(2)}, u32[]{:S(2)}) collective-permute-start(bf16[2,128,128]{2,1,0:T(8,128)(2,1)S(1)} %chain.2), channel_id=1, source_target_pairs={{3,4},{2,5},{1,6},{0,7},{7,8},{6,9},{5,10},{4,11},{11,12},{10,13},... | collective-permute-start | bytes 196616 | tf_op jit(solution)/shard_map/ppermute | solution.py:257
  88.8 2.0 %collective-permute-done.12.rest_2_.rest_6_ = bf16[2,128,128]{2,1,0:T(8,128)(2,1)S(1)} collective-permute-done((bf16[2,128,128]{2,1,0:T(8,128)(2,1)S(1)}, bf16[2,128,128]{2,1,0:T(8,128)(2,1)S(1)}, u32[]{:S(2)}, u32[]{:S(2)}) %collective-permute-start.12) | collective-permute-done | bytes 65568 | tf_op jit(solution)/shard_map/ppermute | solution.py:257
  90.8 3.8 %collective-permute-done.13.rest_3_.rest_7_ = bf16[2,128,128]{2,1,0:T(8,128)(2,1)S(1)} collective-permute-done((bf16[2,128,128]{2,1,0:T(8,128)(2,1)S(1)}, bf16[2,128,128]{2,1,0:T(8,128)(2,1)S(1)}, u32[]{:S(2)}, u32[]{:S(2)}) %collective-permute-start.13) | collective-permute-done | bytes 65568 | tf_op jit(solution)/shard_map/ppermute | solution.py:257
  95.4 1.9 %collective-permute-start.14 = (bf16[2,128,128]{2,1,0:T(8,128)(2,1)S(1)}, bf16[2,128,128]{2,1,0:T(8,128)(2,1)S(1)}, u32[]{:S(2)}, u32[]{:S(2)}) collective-permute-start(bf16[2,128,128]{2,1,0:T(8,128)(2,1)S(1)} %chain.3), channel_id=1, source_target_pairs={{0,4},{1,5},{2,6},{3,7},{4,8},{5,9},{6,10},{7,11},{8,12},{9,13},{1... | collective-permute-start | bytes 196616 | tf_op jit(solution)/shard_map/ppermute | solution.py:257
  101.2 2.2 %collective-permute-start.17 = (bf16[2,128,128]{2,1,0:T(8,128)(2,1)S(1)}, bf16[2,128,128]{2,1,0:T(8,128)(2,1)S(1)}, u32[]{:S(2)}, u32[]{:S(2)}) collective-permute-start(bf16[2,128,128]{2,1,0:T(8,128)(2,1)S(1)} %chain.3), channel_id=1, source_target_pairs={{3,4},{2,5},{1,6},{0,7},{7,8},{6,9},{5,10},{4,11},{11,12},{10,13},... | collective-permute-start | bytes 196616 | tf_op jit(solution)/shard_map/ppermute | solution.py:257
  106.1 2.9 %collective-permute-done.17.rest_11_ = bf16[2,128,128]{2,1,0:T(8,128)(2,1)S(1)} collective-permute-done((bf16[2,128,128]{2,1,0:T(8,128)(2,1)S(1)}, bf16[2,128,128]{2,1,0:T(8,128)(2,1)S(1)}, u32[]{:S(2)}, u32[]{:S(2)}) %collective-permute-start.17) | collective-permute-done | bytes 65568 | tf_op jit(solution)/shard_map/ppermute | solution.py:257
  109.0 2.5 %final.1 = bf16[4,128,1024]{2,1,0:T(8,128)(2,1)} custom-call(s32[35]{0:T(128)S(1)} %pad_add_fusion.meta, bf16[8,512,128]{2,1,0:T(8,128)(2,1)S(1)} %get-tuple-element.29.fields, bf16[1024,1024]{1,0:T(8,128)(2,1)S(1)} %get-tuple-element.35.coupled, bf16[2,128,128]{2,1,0:T(8,128)(2,1)S(1)} %collective-permute-done.6.rest_0_, ...), custom_call_target="tpu_custom_call" | custom-call | flops 805306368 | bytes 4980876 | tf_op jit(solution)/shard_map/final/pallas_call | solution.py:217
  (42 shorter events, 17.6 us)
Async XLA Ops:
  1.6 1.0 copy-start.2
  2.5 1.2 %copy-start.6 = (bf16[4,1,128,1024]{3,2,1,0:T(8,128)(2,1)S(1)}, bf16[4,1,128,1024]{3,2,1,0:T(8,128)(2,1)}, u32[]{:S(2)}) copy-start(bf16[4,1,128,1024]{3,2,1,0:T(8,128)(2,1)} %param.8) | copy-start | bytes 3145732
  7.8 3.8 %collective-permute-start = (bf16[2,768,128]{2,1,0:T(8,128)(2,1)S(1)}, bf16[2,768,128]{2,1,0:T(8,128)(2,1)S(1)}, u32[]{:S(2)}, u32[]{:S(2)}) collective-permute-start(bf16[2,768,128]{2,1,0:T(8,128)(2,1)S(1)} %get-tuple-element.24), channel_id=1, source_target_pairs={{0,1},{1,0},{2,3},{3,2},{4,5},{5,4},{6,7},{7,6},{8,9},{9,8},{10,11... | collective-permute-start | bytes 1179656 | tf_op jit(solution)/shard_map/ppermute | solution.py:246
  8.6 9.1 %collective-permute-start.1 = (bf16[2,768,128]{2,1,0:T(8,128)(2,1)S(1)}, bf16[2,768,128]{2,1,0:T(8,128)(2,1)S(1)}, u32[]{:S(2)}, u32[]{:S(2)}) collective-permute-start(bf16[2,768,128]{2,1,0:T(8,128)(2,1)S(1)} %get-tuple-element.25), channel_id=1, source_target_pairs={{1,2},{2,1},{5,6},{6,5},{9,10},{10,9},{13,14},{14,13},{17,18},{18,... | collective-permute-start | bytes 1179656 | tf_op jit(solution)/shard_map/ppermute | solution.py:245
  17.6 1.2 %copy-start = (bf16[1,8,4,128,128]{4,3,2,1,0:T(8,128)(2,1)S(1)}, bf16[1,8,4,128,128]{4,3,2,1,0:T(8,128)(2,1)}, u32[]{:S(2)}) copy-start(bf16[1,8,4,128,128]{4,3,2,1,0:T(8,128)(2,1)} %param.11) | copy-start | bytes 3145732
  18.9 0.9 copy-start.3
  20.8 12.0 %copy-start.1 = (bf16[1,8,4,128,128]{4,3,2,1,0:T(8,128)(2,1)S(1)}, bf16[1,8,4,128,128]{4,3,2,1,0:T(8,128)(2,1)}, u32[]{:S(2)}) copy-start(bf16[1,8,4,128,128]{4,3,2,1,0:T(8,128)(2,1)} %param.11) | copy-start | bytes 3145732
  20.8 12.0 %copy-start.5 = (bf16[1,8,128,128]{3,2,1,0:T(8,128)(2,1)S(1)}, bf16[1,8,128,128]{3,2,1,0:T(8,128)(2,1)}, u32[]{:S(2)}) copy-start(bf16[1,8,128,128]{3,2,1,0:T(8,128)(2,1)} %param.10) | copy-start | bytes 786436
  29.7 33.3 %collective-permute-start.4 = (bf16[2,768,128]{2,1,0:T(8,128)(2,1)S(1)}, bf16[2,768,128]{2,1,0:T(8,128)(2,1)S(1)}, u32[]{:S(2)}, u32[]{:S(2)}) collective-permute-start(bf16[2,768,128]{2,1,0:T(8,128)(2,1)S(1)} %get-tuple-element.33), channel_id=1, source_target_pairs={{0,1},{1,0},{2,3},{3,2},{4,5},{5,4},{6,7},{7,6},{8,9},{9,8},{10,11... | collective-permute-start | bytes 1179656 | tf_op jit(solution)/shard_map/ppermute | solution.py:246
  29.8 37.2 %collective-permute-start.5 = (bf16[2,768,128]{2,1,0:T(8,128)(2,1)S(1)}, bf16[2,768,128]{2,1,0:T(8,128)(2,1)S(1)}, u32[]{:S(2)}, u32[]{:S(2)}) collective-permute-start(bf16[2,768,128]{2,1,0:T(8,128)(2,1)S(1)} %get-tuple-element.34), channel_id=1, source_target_pairs={{1,2},{2,1},{5,6},{6,5},{9,10},{10,9},{13,14},{14,13},{17,18},{18,... | collective-permute-start | bytes 1179656 | tf_op jit(solution)/shard_map/ppermute | solution.py:245
  39.0 2.6 %collective-permute-start.2 = (bf16[2,512,128]{2,1,0:T(8,128)(2,1)S(1)}, bf16[2,512,128]{2,1,0:T(8,128)(2,1)S(1)}, u32[]{:S(2)}, u32[]{:S(2)}) collective-permute-start(bf16[2,512,128]{2,1,0:T(8,128)(2,1)S(1)} %get-tuple-element.27), channel_id=1, source_target_pairs={{0,1},{1,0},{2,3},{3,2},{4,5},{5,4},{6,7},{7,6},{8,9},{9,8},{10,11... | collective-permute-start | bytes 786440 | tf_op jit(solution)/shard_map/ppermute | solution.py:246
  39.1 7.7 %collective-permute-start.3 = (bf16[2,512,128]{2,1,0:T(8,128)(2,1)S(1)}, bf16[2,512,128]{2,1,0:T(8,128)(2,1)S(1)}, u32[]{:S(2)}, u32[]{:S(2)}) collective-permute-start(bf16[2,512,128]{2,1,0:T(8,128)(2,1)S(1)} %get-tuple-element.28), channel_id=1, source_target_pairs={{1,2},{2,1},{5,6},{6,5},{9,10},{10,9},{13,14},{14,13},{17,18},{18,... | collective-permute-start | bytes 786440 | tf_op jit(solution)/shard_map/ppermute | solution.py:245
  52.9 25.2 %collective-permute-start.6 = (bf16[2,128,128]{2,1,0:T(8,128)(2,1)S(1)}, bf16[2,128,128]{2,1,0:T(8,128)(2,1)S(1)}, u32[]{:S(2)}, u32[]{:S(2)}) collective-permute-start(bf16[2,128,128]{2,1,0:T(8,128)(2,1)S(1)} %get-tuple-element.36), channel_id=1, source_target_pairs={{0,4},{1,5},{2,6},{3,7},{4,8},{5,9},{6,10},{7,11},{8,12},{9,13},{1... | collective-permute-start | bytes 196616 | tf_op jit(solution)/shard_map/ppermute | solution.py:257
  56.0 22.0 %collective-permute-start.7 = (bf16[2,128,128]{2,1,0:T(8,128)(2,1)S(1)}, bf16[2,128,128]{2,1,0:T(8,128)(2,1)S(1)}, u32[]{:S(2)}, u32[]{:S(2)}) collective-permute-start(bf16[2,128,128]{2,1,0:T(8,128)(2,1)S(1)} %get-tuple-element.36), channel_id=1, source_target_pairs={{1,4},{0,5},{3,6},{2,7},{5,8},{4,9},{7,10},{6,11},{9,12},{8,13},{1... | collective-permute-start | bytes 196616 | tf_op jit(solution)/shard_map/ppermute | solution.py:257
  58.0 20.1 %collective-permute-start.8 = (bf16[2,128,128]{2,1,0:T(8,128)(2,1)S(1)}, bf16[2,128,128]{2,1,0:T(8,128)(2,1)S(1)}, u32[]{:S(2)}, u32[]{:S(2)}) collective-permute-start(bf16[2,128,128]{2,1,0:T(8,128)(2,1)S(1)} %get-tuple-element.36), channel_id=1, source_target_pairs={{2,4},{3,5},{0,6},{1,7},{6,8},{7,9},{4,10},{5,11},{10,12},{11,13},... | collective-permute-start | bytes 196616 | tf_op jit(solution)/shard_map/ppermute | solution.py:257
  63.0 15.1 %collective-permute-start.9 = (bf16[2,128,128]{2,1,0:T(8,128)(2,1)S(1)}, bf16[2,128,128]{2,1,0:T(8,128)(2,1)S(1)}, u32[]{:S(2)}, u32[]{:S(2)}) collective-permute-start(bf16[2,128,128]{2,1,0:T(8,128)(2,1)S(1)} %get-tuple-element.36), channel_id=1, source_target_pairs={{3,4},{2,5},{1,6},{0,7},{7,8},{6,9},{5,10},{4,11},{11,12},{10,13},... | collective-permute-start | bytes 196616 | tf_op jit(solution)/shard_map/ppermute | solution.py:257
  78.9 9.8 %collective-permute-start.10 = (bf16[2,128,128]{2,1,0:T(8,128)(2,1)S(1)}, bf16[2,128,128]{2,1,0:T(8,128)(2,1)S(1)}, u32[]{:S(2)}, u32[]{:S(2)}) collective-permute-start(bf16[2,128,128]{2,1,0:T(8,128)(2,1)S(1)} %chain.2), channel_id=1, source_target_pairs={{0,4},{1,5},{2,6},{3,7},{4,8},{5,9},{6,10},{7,11},{8,12},{9,13},{1... | collective-permute-start | bytes 196616 | tf_op jit(solution)/shard_map/ppermute | solution.py:257
  82.1 6.7 %collective-permute-start.11 = (bf16[2,128,128]{2,1,0:T(8,128)(2,1)S(1)}, bf16[2,128,128]{2,1,0:T(8,128)(2,1)S(1)}, u32[]{:S(2)}, u32[]{:S(2)}) collective-permute-start(bf16[2,128,128]{2,1,0:T(8,128)(2,1)S(1)} %chain.2), channel_id=1, source_target_pairs={{1,4},{0,5},{3,6},{2,7},{5,8},{4,9},{7,10},{6,11},{9,12},{8,13},{1... | collective-permute-start | bytes 196616 | tf_op jit(solution)/shard_map/ppermute | solution.py:257
  84.0 6.8 %collective-permute-start.12 = (bf16[2,128,128]{2,1,0:T(8,128)(2,1)S(1)}, bf16[2,128,128]{2,1,0:T(8,128)(2,1)S(1)}, u32[]{:S(2)}, u32[]{:S(2)}) collective-permute-start(bf16[2,128,128]{2,1,0:T(8,128)(2,1)S(1)} %chain.2), channel_id=1, source_target_pairs={{2,4},{3,5},{0,6},{1,7},{6,8},{7,9},{4,10},{5,11},{10,12},{11,13},... | collective-permute-start | bytes 196616 | tf_op jit(solution)/shard_map/ppermute | solution.py:257
  86.3 8.3 %collective-permute-start.13 = (bf16[2,128,128]{2,1,0:T(8,128)(2,1)S(1)}, bf16[2,128,128]{2,1,0:T(8,128)(2,1)S(1)}, u32[]{:S(2)}, u32[]{:S(2)}) collective-permute-start(bf16[2,128,128]{2,1,0:T(8,128)(2,1)S(1)} %chain.2), channel_id=1, source_target_pairs={{3,4},{2,5},{1,6},{0,7},{7,8},{6,9},{5,10},{4,11},{11,12},{10,13},... | collective-permute-start | bytes 196616 | tf_op jit(solution)/shard_map/ppermute | solution.py:257
  95.4 8.0 %collective-permute-start.14 = (bf16[2,128,128]{2,1,0:T(8,128)(2,1)S(1)}, bf16[2,128,128]{2,1,0:T(8,128)(2,1)S(1)}, u32[]{:S(2)}, u32[]{:S(2)}) collective-permute-start(bf16[2,128,128]{2,1,0:T(8,128)(2,1)S(1)} %chain.3), channel_id=1, source_target_pairs={{0,4},{1,5},{2,6},{3,7},{4,8},{5,9},{6,10},{7,11},{8,12},{9,13},{1... | collective-permute-start | bytes 196616 | tf_op jit(solution)/shard_map/ppermute | solution.py:257
  97.3 6.9 %collective-permute-start.15 = (bf16[2,128,128]{2,1,0:T(8,128)(2,1)S(1)}, bf16[2,128,128]{2,1,0:T(8,128)(2,1)S(1)}, u32[]{:S(2)}, u32[]{:S(2)}) collective-permute-start(bf16[2,128,128]{2,1,0:T(8,128)(2,1)S(1)} %chain.3), channel_id=1, source_target_pairs={{1,4},{0,5},{3,6},{2,7},{5,8},{4,9},{7,10},{6,11},{9,12},{8,13},{1... | collective-permute-start | bytes 196616 | tf_op jit(solution)/shard_map/ppermute | solution.py:257
  99.3 6.8 %collective-permute-start.16 = (bf16[2,128,128]{2,1,0:T(8,128)(2,1)S(1)}, bf16[2,128,128]{2,1,0:T(8,128)(2,1)S(1)}, u32[]{:S(2)}, u32[]{:S(2)}) collective-permute-start(bf16[2,128,128]{2,1,0:T(8,128)(2,1)S(1)} %chain.3), channel_id=1, source_target_pairs={{2,4},{3,5},{0,6},{1,7},{6,8},{7,9},{4,10},{5,11},{10,12},{11,13},... | collective-permute-start | bytes 196616 | tf_op jit(solution)/shard_map/ppermute | solution.py:257
  101.2 7.8 %collective-permute-start.17 = (bf16[2,128,128]{2,1,0:T(8,128)(2,1)S(1)}, bf16[2,128,128]{2,1,0:T(8,128)(2,1)S(1)}, u32[]{:S(2)}, u32[]{:S(2)}) collective-permute-start(bf16[2,128,128]{2,1,0:T(8,128)(2,1)S(1)} %chain.3), channel_id=1, source_target_pairs={{3,4},{2,5},{1,6},{0,7},{7,8},{6,9},{5,10},{4,11},{11,12},{10,13},... | collective-permute-start | bytes 196616 | tf_op jit(solution)/shard_map/ppermute | solution.py:257
  (3 other events, 2.6 us)

commit v2 on v1

v2 whole, which is shorter than its diff:
```python
import functools
import math

import jax
import jax.numpy as jnp
from jax import lax
from jax.experimental import pallas as pl
from jax.experimental.pallas import tpu as pltpu
from jax.sharding import PartitionSpec as P

HALO = 2
BF = jnp.bfloat16
F32 = jnp.float32


def dot_nt(a, b):
    return lax.dot_general(a, b, (((1,), (1,)), ((), ())), preferred_element_type=F32)


def dot_nn(a, b):
    return lax.dot_general(a, b, (((1,), (0,)), ((), ())), preferred_element_type=F32)


class Dims:
    def __init__(self, ticks, sources, count, neigh, width, nq, faces):
        self.ticks, self.sources, self.count, self.neigh = ticks, sources, count, neigh
        self.width, self.nq, self.faces = width, nq, faces
        self.batch = ticks * sources
        self.group = nq * width
        self.ext = count + 2 * HALO
        self.depth = (1 + neigh) * width
        self.slots = 4 if faces <= 4 else 6
        self.wide = self.slots * self.group
        self.last = count - HALO
        self.up = count + HALO

    def start(self, face):
        return pl.multiple_of(lax.rem(face + 2 * self.slots, self.slots) * self.group, self.group)

    def first_col(self, face):
        return face * self.count - HALO


def edge_rows(d, parity):
    return d.last * (1 - parity), d.last * parity


def first_kernel(d, face_ref, iface, rhs, inflow, inv, coupling, field, gfield, pair, cross, right, flow, tiles, couple, sems):
    w = d.width
    copies = [
        pltpu.make_async_copy(inv, tiles, sems.at[0]),
        pltpu.make_async_copy(coupling, couple, sems.at[1]),
        pltpu.make_async_copy(inflow, flow, sems.at[2]),
    ]
    copies += [
        pltpu.make_async_copy(rhs.at[:, :, pl.ds(r * w, w)], right.at[r], sems.at[3 + r]) for r in range(d.count)
    ]
    for copy in copies:
        copy.start()
    parity = lax.rem(face_ref[0], 2)
    for copy in copies[:3]:
        copy.wait()
    coupled = []
    for q in range(d.nq):
        coupled.append(dot_nt(flow[:, q * w : (q + 1) * w], couple[q]))
        turned = couple[q].astype(F32).T.astype(BF)
        gfield[q] = dot_nt(turned, tiles[iface[q]]).astype(BF)
    for r in range(d.count):
        copies[3 + r].wait()
        field[r] = dot_nt(right[r].reshape(d.batch, w), tiles[r]).astype(BF)
    for q in range(d.nq):
        row = iface[q]
        corrected = (right[row, 0].astype(F32) - coupled[q]).astype(BF)
        field[row, 0 : d.sources, :] = dot_nt(corrected, tiles[row]).astype(BF)
    for start, buffer in zip(edge_rows(d, parity), (pair, cross)):
        for e in range(HALO):
            buffer[e, 0 : d.batch, :] = field[start + e]
            for q in range(d.nq):
                hit = iface[q] == start + e
                buffer[e, d.batch + q * w : d.batch + (q + 1) * w, :] = jnp.where(hit, gfield[q], jnp.zeros((w, w), BF))


def fold_kernel(d, after, diag, off, inv, folded):
    w = d.width
    for r in range(d.count):
        tiles = jnp.concatenate([diag[r]] + [off[r, k] for k in range(d.neigh)], axis=1)
        product = dot_nn(inv[r], tiles)
        rows = lax.broadcasted_iota(jnp.int32, (w, w), 0)
        unit = (rows == lax.broadcasted_iota(jnp.int32, (w, w), 1)).astype(F32)
        for k in range(1 + d.neigh):
            part = product[:, k * w : (k + 1) * w].T
            folded[r, k * w : (k + 1) * w, :] = ((unit if k == 0 else 0.0) - part).astype(BF)


def sweep(d, cols, face, ext, span, r, folded):
    x = [ext[r + HALO, span, :]] + [ext[cols[r, k] - d.first_col(face), span, :] for k in range(d.neigh)]
    return dot_nn(jnp.concatenate(x, axis=1), folded[r])


def batch_kernel(d, last, face_ref, iface, cols, field, base, pair_in, cross_in, folded, *rest):
    if last:
        out, faces_out, sent, ext = rest
    else:
        out, pair, cross, ext = rest
    face = face_ref[0]
    parity = lax.rem(face, 2)
    ext[HALO : HALO + d.count] = field[...]
    ext[pl.ds(d.up * (1 - parity), HALO)] = pair_in[:, 0 : d.batch, :]
    ext[pl.ds(d.up * parity, HALO)] = cross_in[:, 0 : d.batch, :]
    for r in range(d.count):
        for s in range(0, d.batch, d.group):
            span = pl.ds(s, d.group)
            out[r, span, :] = (base[r, span, :].astype(F32) + sweep(d, cols, face, ext, span, r, folded)).astype(BF)
    if last:
        for q in range(d.nq):
            row = iface[q]
            for t in range(d.ticks):
                faces_out[t, q] = out[row, t * d.sources : (t + 1) * d.sources, :]
            sent[q] = out[row, 0 : d.sources, :]
    else:
        for start, buffer in zip(edge_rows(d, parity), (pair, cross)):
            buffer[...] = out[pl.ds(start, HALO)]


def coupling_first_kernel(d, face_ref, iface, cols, gfield, pair_in, cross_in, folded, after, out, pair, cross, met):
    face = face_ref[0]
    parity = lax.rem(face, 2)
    w = d.width
    met[...] = jnp.zeros_like(met)
    for r in range(d.count):
        lanes = slice(r * w, (r + 1) * w)
        for q in range(d.nq):
            met[2 * HALO + q, :, lanes] = jnp.where(iface[q] == r, folded[r, 0:w, :], jnp.zeros((w, w), BF))
        for k in range(d.neigh):
            c = cols[r, k] - d.first_col(face)
            inside = jnp.logical_and(c >= HALO, c < d.up)
            at = jnp.where(c < HALO, c, c - d.count)
            hit = jnp.logical_not(inside)
            for q in range(d.nq):
                here = c == iface[q] + HALO
                at = jnp.where(here, 2 * HALO + q, at)
                hit = jnp.logical_or(hit, here)

            @pl.when(hit)
            def _():
                met[at, :, lanes] += folded[r, (1 + k) * w : (2 + k) * w, :]

    out[...] = jnp.zeros_like(out)

    def put(start, rows, value):
        for r in range(d.count):
            out[r, pl.ds(start, rows), :] = value[:, r * w : (r + 1) * w].astype(BF)

    pair_face, cross_face = face + 1 - 2 * parity, face - 1 + 2 * parity
    for at, other, block in ((HALO * (1 - parity), pair_face, pair_in), (HALO * parity, cross_face, cross_in)):
        x = jnp.concatenate([block[e, d.batch : d.batch + d.group, :] for e in range(HALO)], axis=1)
        tiles = jnp.concatenate([met[at + e] for e in range(HALO)], axis=0)
        put(d.start(other), d.group, dot_nn(x, tiles))
    for q in range(d.nq):
        start = d.start(face) + q * w
        put(start, w, dot_nn(gfield[q], met[2 * HALO + q]))
        row = iface[q]
        span = pl.ds(pl.multiple_of(start, w), w)
        out[row, span, :] = (out[row, span, :].astype(F32) + gfield[q].astype(F32)).astype(BF)
    for start, buffer in zip(edge_rows(d, parity), (pair, cross)):
        for i, shift in enumerate((-1, 0, 1)):
            buffer[:, i * d.group : (i + 1) * d.group, :] = out[pl.ds(start, HALO), pl.ds(d.start(face + shift), d.group), :]


def coupling_last_kernel(d, face_ref, iface, cols, gfield, gfirst, pair_in, cross_in, folded, out, chain, ext):
    face = face_ref[0]
    parity = lax.rem(face, 2)
    w = d.width
    ext[0:HALO] = jnp.zeros((HALO, d.wide, w), BF)
    ext[d.up : d.ext] = jnp.zeros((HALO, d.wide, w), BF)
    ext[HALO : HALO + d.count] = gfirst[...]
    neighbours = ((d.up * (1 - parity), face + 1 - 2 * parity, pair_in), (d.up * parity, face - 1 + 2 * parity, cross_in))
    for start, other, block in neighbours:
        for i, shift in enumerate((-1, 0, 1)):
            ext[pl.ds(start, HALO), pl.ds(d.start(other + shift), d.group), :] = block[:, i * d.group : (i + 1) * d.group, :]
    for r in range(d.count):
        for s in range(0, d.wide, d.group):
            span = pl.ds(s, d.group)
            out[span, r * w : (r + 1) * w] = sweep(d, cols, face, ext, span, r, folded).astype(BF)
    for q in range(d.nq):
        lane = pl.ds(pl.multiple_of(iface[q] * w, w), w)
        span = pl.ds(pl.multiple_of(d.start(face) + q * w, w), w)
        out[span, lane] = (out[span, lane].astype(F32) + gfield[q].astype(F32)).astype(BF)
        chain[:, q * w : (q + 1) * w] = out[:, lane]


def arrived_blocks(d, face, own, other):
    parity = lax.rem(face, 2)
    shifts = chip_shifts(d.faces)
    for k, shift in enumerate(shifts):
        there = face + 2 * shift if len(shifts) != 2 else face ^ (2 * shift)
        for block, source in ((own, there), (other, there + 1 - 2 * parity)):
            yield jnp.concatenate([block(k, q) for q in range(d.nq)], axis=1), d.start(source)


def chip_shifts(faces):
    return (0,) if faces <= 2 else (0, 1) if faces <= 4 else (0, -1, 1)


def chain_kernel(d, tick, face_ref, chain, faces_out, other, *rest):
    own, sent = rest[:-1], rest[-1]
    total = jnp.zeros((d.sources, d.group), F32)
    for x, start in arrived_blocks(d, face_ref[0], lambda k, q: own[k][q], lambda k, q: other[k, q]):
        total += dot_nn(x, chain[pl.ds(start, d.group), :])
    for q in range(d.nq):
        sent[q] = (faces_out[tick, q].astype(F32) - total[:, q * d.width : (q + 1) * d.width]).astype(BF)


def final_kernel(d, face_ref, fields, coupled, *rest):
    arrived, out = rest[:-1], rest[-1]
    w = d.width
    hops = len(chip_shifts(d.faces))
    for r in range(d.count):
        out[0, :, r * w : (r + 1) * w] = fields[r, 0 : d.sources, :]
    for t in range(1, d.ticks):
        other, *own = arrived[(t - 1) * (hops + 1) : t * (hops + 1)]
        total = jnp.zeros((d.sources, d.count * w), F32)
        for x, start in arrived_blocks(d, face_ref[0], lambda k, q: own[k][q], lambda k, q: other[k, q]):
            total += dot_nn(x, coupled[pl.ds(start, d.group), :])
        for r in range(d.count):
            base = fields[r, t * d.sources : (t + 1) * d.sources, :].astype(F32)
            out[t, :, r * w : (r + 1) * w] = (base - total[:, r * w : (r + 1) * w]).astype(BF)


def call(body, name, smem, inputs, outs, scratch=(), flops=0, anywhere=(), sems=0):
    vmem = pl.BlockSpec(memory_space=pltpu.VMEM)
    moved = sum(x.size * x.dtype.itemsize for x in inputs) + sum(2 * math.prod(s) for s in outs)
    specs = [pl.BlockSpec(memory_space=pl.ANY) if i in anywhere else vmem for i in range(len(inputs))]
    return pl.pallas_call(
        body,
        name=name,
        out_shape=[jax.ShapeDtypeStruct(s, BF) for s in outs],
        in_specs=[pl.BlockSpec(memory_space=pltpu.SMEM)] * len(smem) + specs,
        out_specs=[vmem] * len(outs),
        scratch_shapes=[pltpu.VMEM(s, BF) for s in scratch] + ([pltpu.SemaphoreType.DMA((sems,))] if sems else []),
        compiler_params=pltpu.CompilerParams(vmem_limit_bytes=32 * 1024 * 1024),
        cost_estimate=pl.CostEstimate(flops=flops, bytes_accessed=moved, transcendentals=0),
    )(*smem, *inputs)


def on_device(rhs, inflow, diag_tiles, off_tiles, cols, inverse_tiles, coupling, iface):
    faces, slabs = lax.axis_size("face"), lax.axis_size("slab")
    ticks, _, sources, _ = rhs.shape
    _, count, neigh, width, _ = off_tiles.shape
    nq = coupling.shape[1]
    d = Dims(ticks, sources, count, neigh, width, nq, faces)
    diag, off, inv, couple, cols = diag_tiles[0], off_tiles[0], inverse_tiles[0], coupling[0], cols[0]
    face = lax.axis_index("face").astype(jnp.int32)[None]
    face, iface, cols = (pltpu.with_memory_space_constraint(x, pltpu.SMEM) for x in (face, iface, cols))
    tile = width * width

    pairing = [(i, i ^ 1) for i in range(faces) if i ^ 1 < faces]
    crossing = [(i, ((i + 1) ^ 1) - 1) for i in range(faces) if 0 <= ((i + 1) ^ 1) - 1 < faces]

    def exchange(pair, cross):
        got = lax.ppermute(cross, "face", crossing)
        return lax.ppermute(pair, "face", pairing), got

    def onward(block):
        shifts = chip_shifts(faces)
        own = []
        for shift in shifts:
            route = []
            for s in range(1, slabs):
                for f in range(faces):
                    g = f ^ (2 * shift) if len(shifts) == 2 else f + 2 * shift
                    if 0 <= g < faces:
                        route.append(((s - 1) * faces + g, s * faces + f))
            own.append(lax.ppermute(block, ("slab", "face"), route))
        return [lax.ppermute(jnp.stack(own), "face", pairing)] + own

    batch, group, ext, wide = d.batch, d.group, d.ext, d.wide
    field, gfield, pair, cross = call(
        functools.partial(first_kernel, d),
        "first",
        [face, iface],
        [pltpu.with_memory_space_constraint(x, pltpu.HBM) for x in (rhs[:, 0], inflow[0], inv, couple)],
        [(count, batch, width), (nq, width, width)] + [(HALO, batch + group, width)] * 2,
        [(count, ticks, sources, width), (sources, group), (count, width, width), (nq, width, width)],
        flops=2 * batch * count * tile,
        anywhere=(0, 1, 2, 3),
        sems=3 + count,
    )
    (folded,) = call(
        functools.partial(fold_kernel, d),
        "fold",
        [],
        [gfield, diag, off, inv],
        [(count, d.depth, width)],
        flops=2 * width * count * tile * (neigh + 1),
        anywhere=(0,),
    )
    pair0, cross0 = exchange(pair, cross)
    once, pair, cross = call(
        functools.partial(batch_kernel, d, False),
        "second",
        [face, iface, cols],
        [field, field, pair0, cross0, folded],
        [(count, batch, width)] + [(HALO, batch, width)] * 2,
        [(ext, batch, width)],
        flops=2 * batch * count * tile * (neigh + 1),
    )
    pair1, cross1 = exchange(pair, cross)
    gfirst, gpair, gcross = call(
        functools.partial(coupling_first_kernel, d),
        "coupling_first",
        [face, iface, cols],
        [gfield, pair0, cross0, folded, once],
        [(count, wide, width)] + [(HALO, 3 * group, width)] * 2,
        [(2 * HALO + nq, width, count * width)],
        flops=2 * (2 * HALO + nq) * width * count * tile,
        anywhere=(4,),
    )
    gpair, gcross = exchange(gpair, gcross)
    fields, faces_out, sent = call(
        functools.partial(batch_kernel, d, True),
        "third",
        [face, iface, cols],
        [once, field, pair1, cross1, folded],
        [(count, batch, width), (ticks, nq, sources, width), (nq, sources, width)],
        [(ext, batch, width)],
        flops=2 * batch * count * tile * (neigh + 1),
    )
    arrived = onward(sent)
    coupled, chain = call(
        functools.partial(coupling_last_kernel, d),
        "coupling_last",
        [face, iface, cols],
        [gfield, gfirst, gpair, gcross, folded],
        [(wide, count * width), (wide, group)],
        [(ext, wide, width)],
        flops=2 * wide * count * tile * (neigh + 1),
    )
    everything = list(arrived)
    for tick in range(1, ticks - 1):
        (sent,) = call(
            functools.partial(chain_kernel, d, tick),
            "chain",
            [face],
            [chain, faces_out] + arrived,
            [(nq, sources, width)],
            flops=2 * sources * wide * group,
        )
        arrived = onward(sent)
        everything += arrived
    (out,) = call(
        functools.partial(final_kernel, d),
        "final",
        [face],
        [fields, coupled] + everything,
        [(ticks, sources, count * width)],
        flops=2 * (ticks - 1) * sources * wide * count * width,
    )
    return out[:, None]


def solution(mesh):
    placed = (
        P(None, "slab", None, "face"),
        P("slab", None, "face"),
        P("slab", "face", None, None),
        P("slab", "face", None, None, None),
        P("slab", "face", None),
        P("slab", "face", None, None),
        P("slab", "face", None, None),
        P("face"),
    )
    return jax.shard_map(
        on_device,
        mesh=mesh,
        in_specs=placed,
        out_specs=P(None, "slab", None, "face"),
        check_vma=False,
    )
```

time: 113 us -> 69.4 us (0.61)
  Pallas kernels: 38.8 us -> 18.5 us
  waiting for transfers between devices: 22.6 us -> 13.6 us
  starting transfers between devices: 41.3 us -> 33.2 us
  local copies, waits for them, and re-layouts: 7.15 us -> 3.41 us
  other arithmetic: 1.42 us -> 0.04 us
    pallas_call x8 -> x9, Pallas kernels: 38.8 us -> 18.5 us  [call(): pl.pallas_call(body, name=name, out_shape=[jax.ShapeDtypeStruct(s, BF) fo...]
    ppermute x3, waiting for transfers between devices: 11.2 us -> 2.47 us  [exchange(): got = lax.ppermute(cross, 'face', crossing)]
    ppermute x12 -> x9, starting transfers between devices: 31.8 us -> 23.8 us  [the longest x6 17.3 us: onward(): own.append(lax.ppermute(block, ('slab', 'face'), route))]
    unnamed x18 -> x10, local copies, waits for them, and re-layouts: 6.98 us -> 2.65 us
    ppermute x12 -> x9, waiting for transfers between devices: 11.4 us -> 11.2 us  [the longest x6 9.19 us: onward(): own.append(lax.ppermute(block, ('slab', 'face'), route))]
  transfers between devices with their start and end apart: 18 -> 15, of which waited for: 7 -> 8; matrix products, arithmetic and copies ran while one was open for 0% -> 1% of each run, Pallas kernels for 21% -> 13%
where the time goes in v2:
time: 69.4 us; the launch traced here: 69 us
  starting transfers between devices  33.2 us (48%)
  Pallas kernels  18.5 us (27%)
  waiting for transfers between devices  13.6 us (20%)
  local copies, waits for them, and re-layouts  3.41 us (5%)
    pallas_call x9, Pallas kernels, call(): pl.pallas_call(body, name=name, out_shape=[jax.ShapeDtypeStruct(s, BF) fo...  18.5 us
    ppermute x6, starting transfers between devices, onward(): own.append(lax.ppermute(block, ('slab', 'face'), route))  17.3 us
    ppermute x6, waiting for transfers between devices, onward(): own.append(lax.ppermute(block, ('slab', 'face'), route))  9.19 us
    ppermute x3, starting transfers between devices, exchange(): got = lax.ppermute(cross, 'face', crossing)  8.52 us
    ppermute x3, starting transfers between devices, onward(): return [lax.ppermute(jnp.stack(own), 'face', pairing)] + own  6.47 us
    unnamed x10, local copies, waits for them, and re-layouts  2.65 us
    ppermute x3, waiting for transfers between devices, exchange(): got = lax.ppermute(cross, 'face', crossing)  2.47 us
    ppermute x3, waiting for transfers between devices, onward(): return [lax.ppermute(jnp.stack(own), 'face', pairing)] + own  1.98 us
  transfers between devices with their start and end apart: 15, of which 8 were waited for; matrix products, arithmetic and copies ran while one was open for 1% of the time, Pallas kernels for 13%

profile of v2, /device:TPU:9, one launch (start us, length us, event | category | flops | bytes accessed | tf_op | source)
XLA Modules:
  0.0 69.0 jit_solution(257206441808378052)
XLA Ops:
  0.7 4.4 %first.1 = (bf16[8,512,128]{2,1,0:T(8,128)(2,1)S(1)}, bf16[2,128,128]{2,1,0:T(8,128)(2,1)S(1)}, bf16[2,768,128]{2,1,0:T(8,128)(2,1)}, bf16[2,768,128]{2,1,0:T(8,128)(2,1)S(1)}) custom-call(s32[1]{0:T(128)} %bitcast.face_ref, s32[2]{0:T(128)S(1)} %copy-done.3, bf16[4,128,1024]{2,1,0:T(8,128)(2,1)} %bitcast.27, bf16[128,256]{1,0:T(8,128)(2,1)} %bitcast.28, ...), custom_call_target="tpu_custom_call" | custom-call | flops 134217728 | bytes 3342336 | tf_op jit(solution)/shard_map/first/pallas_call | solution.py:234
  5.9 3.0 %collective-permute-start.1 = (bf16[2,768,128]{2,1,0:T(8,128)(2,1)S(1)}, bf16[2,768,128]{2,1,0:T(8,128)(2,1)S(1)}, u32[]{:S(2)}, u32[]{:S(2)}) collective-permute-start(bf16[2,768,128]{2,1,0:T(8,128)(2,1)S(1)} %get-tuple-element.22), channel_id=1, source_target_pairs={{1,2},{2,1},{5,6},{6,5},{9,10},{10,9},{13,14},{14,13},{17,18},{18,... | collective-permute-start | bytes 1179656 | tf_op jit(solution)/shard_map/ppermute | solution.py:261
  12.5 2.5 %collective-permute-done.1.cross_in = bf16[2,768,128]{2,1,0:T(8,128)(2,1)S(1)} collective-permute-done((bf16[2,768,128]{2,1,0:T(8,128)(2,1)S(1)}, bf16[2,768,128]{2,1,0:T(8,128)(2,1)S(1)}, u32[]{:S(2)}, u32[]{:S(2)}) %collective-permute-start.1) | collective-permute-done | bytes 393248 | tf_op jit(solution)/shard_map/ppermute | solution.py:261
  15.0 2.3 %second.1 = (bf16[8,512,128]{2,1,0:T(8,128)(2,1)S(1)}, bf16[2,512,128]{2,1,0:T(8,128)(2,1)S(1)}, bf16[2,512,128]{2,1,0:T(8,128)(2,1)S(1)}) custom-call(s32[1]{0:T(128)} %bitcast.face_ref, s32[2]{0:T(128)S(1)} %copy-done.4, s32[8,4]{1,0:T(8,128)S(1)} %copy.10.cols, bf16[8,512,128]{2,1,0:T(8,128)(2,1)S(1)} %get-tuple-element.20.field.base, ...), custom_call_target="tpu_custom_call" | custom-call | flops 671088640 | bytes 5767168 | tf_op jit(solution)/shard_map/second/pallas_call | solution.py:234
  17.3 3.0 %collective-permute-start.3 = (bf16[2,512,128]{2,1,0:T(8,128)(2,1)S(1)}, bf16[2,512,128]{2,1,0:T(8,128)(2,1)S(1)}, u32[]{:S(2)}, u32[]{:S(2)}) collective-permute-start(bf16[2,512,128]{2,1,0:T(8,128)(2,1)S(1)} %get-tuple-element.26), channel_id=1, source_target_pairs={{1,2},{2,1},{5,6},{6,5},{9,10},{10,9},{13,14},{14,13},{17,18},{18,... | collective-permute-start | bytes 786440 | tf_op jit(solution)/shard_map/ppermute | solution.py:261
  20.4 2.1 %coupling_first.1 = (bf16[8,1024,128]{2,1,0:T(8,128)(2,1)S(1)}, bf16[2,768,128]{2,1,0:T(8,128)(2,1)S(1)}, bf16[2,768,128]{2,1,0:T(8,128)(2,1)S(1)}) custom-call(s32[1]{0:T(128)} %bitcast.face_ref, s32[2]{0:T(128)S(1)} %copy-done.4, s32[8,4]{1,0:T(8,128)S(1)} %copy.10.cols, bf16[2,128,128]{2,1,0:T(8,128)(2,1)S(1)} %get-tuple-element.23.after.gfield, ...), custom_call_target="tpu_custom_call" | custom-call | flops 201326592 | bytes 6094848 | tf_op jit(solution)/shard_map/coupling_first/pallas_call | solution.py:234
  22.6 2.5 %collective-permute-start.5 = (bf16[2,768,128]{2,1,0:T(8,128)(2,1)S(1)}, bf16[2,768,128]{2,1,0:T(8,128)(2,1)S(1)}, u32[]{:S(2)}, u32[]{:S(2)}) collective-permute-start(bf16[2,768,128]{2,1,0:T(8,128)(2,1)S(1)} %get-tuple-element.30), channel_id=1, source_target_pairs={{1,2},{2,1},{5,6},{6,5},{9,10},{10,9},{13,14},{14,13},{17,18},{18,... | collective-permute-start | bytes 1179656 | tf_op jit(solution)/shard_map/ppermute | solution.py:261
  25.1 2.3 %third.1 = (bf16[8,512,128]{2,1,0:T(8,128)(2,1)S(1)}, bf16[4,2,128,128]{3,2,1,0:T(8,128)(2,1)S(1)}, bf16[2,128,128]{2,1,0:T(8,128)(2,1)S(1)}) custom-call(s32[1]{0:T(128)} %bitcast.face_ref, s32[2]{0:T(128)S(1)} %copy-done.4, s32[8,4]{1,0:T(8,128)S(1)} %copy.10.cols, bf16[8,512,128]{2,1,0:T(8,128)(2,1)S(1)} %get-tuple-element.24.field.after, ...), custom_call_target="tpu_custom_call" | custom-call | flops 671088640 | bytes 5308416 | tf_op jit(solution)/shard_map/third/pallas_call | solution.py:234
  27.3 1.9 %collective-permute-start.7 = (bf16[2,128,128]{2,1,0:T(8,128)(2,1)S(1)}, bf16[2,128,128]{2,1,0:T(8,128)(2,1)S(1)}, u32[]{:S(2)}, u32[]{:S(2)}) collective-permute-start(bf16[2,128,128]{2,1,0:T(8,128)(2,1)S(1)} %get-tuple-element.32), channel_id=1, source_target_pairs={{2,4},{3,5},{0,6},{1,7},{6,8},{7,9},{4,10},{5,11},{10,12},{11,13},... | collective-permute-start | bytes 196616 | tf_op jit(solution)/shard_map/ppermute | solution.py:274
  29.3 3.2 %collective-permute-start.6 = (bf16[2,128,128]{2,1,0:T(8,128)(2,1)S(1)}, bf16[2,128,128]{2,1,0:T(8,128)(2,1)S(1)}, u32[]{:S(2)}, u32[]{:S(2)}) collective-permute-start(bf16[2,128,128]{2,1,0:T(8,128)(2,1)S(1)} %get-tuple-element.32), channel_id=1, source_target_pairs={{0,4},{1,5},{2,6},{3,7},{4,8},{5,9},{6,10},{7,11},{8,12},{9,13},{1... | collective-permute-start | bytes 196616 | tf_op jit(solution)/shard_map/ppermute | solution.py:274
  32.5 1.7 %collective-permute-done.7.rest_1_.rest_2_ = bf16[2,128,128]{2,1,0:T(8,128)(2,1)S(1)} collective-permute-done((bf16[2,128,128]{2,1,0:T(8,128)(2,1)S(1)}, bf16[2,128,128]{2,1,0:T(8,128)(2,1)S(1)}, u32[]{:S(2)}, u32[]{:S(2)}) %collective-permute-start.7) | collective-permute-done | bytes 65568 | tf_op jit(solution)/shard_map/ppermute | solution.py:274
  34.2 1.3 %collective-permute-done.6.rest_0_.rest_1_ = bf16[2,128,128]{2,1,0:T(8,128)(2,1)S(1)} collective-permute-done((bf16[2,128,128]{2,1,0:T(8,128)(2,1)S(1)}, bf16[2,128,128]{2,1,0:T(8,128)(2,1)S(1)}, u32[]{:S(2)}, u32[]{:S(2)}) %collective-permute-start.6) | collective-permute-done | bytes 65568 | tf_op jit(solution)/shard_map/ppermute | solution.py:274
  35.4 3.5 %collective-permute-start.8 = (bf16[2,2,128,128]{3,2,1,0:T(8,128)(2,1)S(1)}, bf16[2,2,128,128]{3,2,1,0:T(8,128)(2,1)S(1)}, u32[]{:S(2)}, u32[]{:S(2)}) collective-permute-start(bf16[2,2,128,128]{3,2,1,0:T(8,128)(2,1)S(1)} %pad_maximum_fusion), channel_id=1, source_target_pairs={{0,1},{1,0},{2,3},{3,2},{4,5},{5,4},{6,7},{7,6},{8,9},{9,8},{10,11... | collective-permute-start | bytes 393224 | tf_op jit(solution)/shard_map/ppermute | solution.py:275
  38.9 4.0 %coupling_last.1 = (bf16[1024,1024]{1,0:T(8,128)(2,1)S(1)}, bf16[1024,256]{1,0:T(8,128)(2,1)S(1)}) custom-call(s32[1]{0:T(128)} %bitcast.face_ref, s32[2]{0:T(128)S(1)} %copy-done.4, s32[8,4]{1,0:T(8,128)S(1)} %copy.10.cols, bf16[2,128,128]{2,1,0:T(8,128)(2,1)S(1)} %get-tuple-element.23.after.gfield, bf16[8,1024,128]{2,1,0:T(8,128)(2,1)S(1)} %get-tuple-element.28.gfirst, ...), custom_call_target="tpu_custom_call" | custom-call | flops 1342177280 | bytes 6881280 | tf_op jit(solution)/shard_map/coupling_last/pallas_call | solution.py:234
  43.2 1.9 %collective-permute-start.10 = (bf16[2,128,128]{2,1,0:T(8,128)(2,1)S(1)}, bf16[2,128,128]{2,1,0:T(8,128)(2,1)S(1)}, u32[]{:S(2)}, u32[]{:S(2)}) collective-permute-start(bf16[2,128,128]{2,1,0:T(8,128)(2,1)S(1)} %chain.2), channel_id=1, source_target_pairs={{2,4},{3,5},{0,6},{1,7},{6,8},{7,9},{4,10},{5,11},{10,12},{11,13},... | collective-permute-start | bytes 196616 | tf_op jit(solution)/shard_map/ppermute | solution.py:274
  45.1 3.1 %collective-permute-start.9 = (bf16[2,128,128]{2,1,0:T(8,128)(2,1)S(1)}, bf16[2,128,128]{2,1,0:T(8,128)(2,1)S(1)}, u32[]{:S(2)}, u32[]{:S(2)}) collective-permute-start(bf16[2,128,128]{2,1,0:T(8,128)(2,1)S(1)} %chain.2), channel_id=1, source_target_pairs={{0,4},{1,5},{2,6},{3,7},{4,8},{5,9},{6,10},{7,11},{8,12},{9,13},{1... | collective-permute-start | bytes 196616 | tf_op jit(solution)/shard_map/ppermute | solution.py:274
  48.2 2.3 %collective-permute-done.10.rest_1_.rest_5_ = bf16[2,128,128]{2,1,0:T(8,128)(2,1)S(1)} collective-permute-done((bf16[2,128,128]{2,1,0:T(8,128)(2,1)S(1)}, bf16[2,128,128]{2,1,0:T(8,128)(2,1)S(1)}, u32[]{:S(2)}, u32[]{:S(2)}) %collective-permute-start.10) | collective-permute-done | bytes 65568 | tf_op jit(solution)/shard_map/ppermute | solution.py:274
  50.6 1.1 %collective-permute-done.9.rest_0_.rest_4_ = bf16[2,128,128]{2,1,0:T(8,128)(2,1)S(1)} collective-permute-done((bf16[2,128,128]{2,1,0:T(8,128)(2,1)S(1)}, bf16[2,128,128]{2,1,0:T(8,128)(2,1)S(1)}, u32[]{:S(2)}, u32[]{:S(2)}) %collective-permute-start.9) | collective-permute-done | bytes 65568 | tf_op jit(solution)/shard_map/ppermute | solution.py:274
  51.7 1.2 %collective-permute-start.11 = (bf16[2,2,128,128]{3,2,1,0:T(8,128)(2,1)S(1)}, bf16[2,2,128,128]{3,2,1,0:T(8,128)(2,1)S(1)}, u32[]{:S(2)}, u32[]{:S(2)}) collective-permute-start(bf16[2,2,128,128]{3,2,1,0:T(8,128)(2,1)S(1)} %pad_maximum_fusion.1), channel_id=1, source_target_pairs={{0,1},{1,0},{2,3},{3,2},{4,5},{5,4},{6,7},{7,6},{8,9},{9,8},{10,11... | collective-permute-start | bytes 393224 | tf_op jit(solution)/shard_map/ppermute | solution.py:275
  54.1 4.1 %collective-permute-start.13 = (bf16[2,128,128]{2,1,0:T(8,128)(2,1)S(1)}, bf16[2,128,128]{2,1,0:T(8,128)(2,1)S(1)}, u32[]{:S(2)}, u32[]{:S(2)}) collective-permute-start(bf16[2,128,128]{2,1,0:T(8,128)(2,1)S(1)} %chain.3), channel_id=1, source_target_pairs={{2,4},{3,5},{0,6},{1,7},{6,8},{7,9},{4,10},{5,11},{10,12},{11,13},... | collective-permute-start | bytes 196616 | tf_op jit(solution)/shard_map/ppermute | solution.py:274
  58.2 3.1 %collective-permute-start.12 = (bf16[2,128,128]{2,1,0:T(8,128)(2,1)S(1)}, bf16[2,128,128]{2,1,0:T(8,128)(2,1)S(1)}, u32[]{:S(2)}, u32[]{:S(2)}) collective-permute-start(bf16[2,128,128]{2,1,0:T(8,128)(2,1)S(1)} %chain.3), channel_id=1, source_target_pairs={{0,4},{1,5},{2,6},{3,7},{4,8},{5,9},{6,10},{7,11},{8,12},{9,13},{1... | collective-permute-start | bytes 196616 | tf_op jit(solution)/shard_map/ppermute | solution.py:274
  61.3 2.8 %collective-permute-done.12.rest_7_ = bf16[2,128,128]{2,1,0:T(8,128)(2,1)S(1)} collective-permute-done((bf16[2,128,128]{2,1,0:T(8,128)(2,1)S(1)}, bf16[2,128,128]{2,1,0:T(8,128)(2,1)S(1)}, u32[]{:S(2)}, u32[]{:S(2)}) %collective-permute-start.12) | collective-permute-done | bytes 65568 | tf_op jit(solution)/shard_map/ppermute | solution.py:274
  64.1 1.9 %collective-permute-start.14 = (bf16[2,2,128,128]{3,2,1,0:T(8,128)(2,1)S(1)}, bf16[2,2,128,128]{3,2,1,0:T(8,128)(2,1)S(1)}, u32[]{:S(2)}, u32[]{:S(2)}) collective-permute-start(bf16[2,2,128,128]{3,2,1,0:T(8,128)(2,1)S(1)} %pad_maximum_fusion.2), channel_id=1, source_target_pairs={{0,1},{1,0},{2,3},{3,2},{4,5},{5,4},{6,7},{7,6},{8,9},{9,8},{10,11... | collective-permute-start | bytes 393224 | tf_op jit(solution)/shard_map/ppermute | solution.py:275
  66.9 2.0 %final.1 = bf16[4,128,1024]{2,1,0:T(8,128)(2,1)} custom-call(s32[1]{0:T(128)} %bitcast.face_ref, bf16[8,512,128]{2,1,0:T(8,128)(2,1)S(1)} %get-tuple-element.27.fields, bf16[1024,1024]{1,0:T(8,128)(2,1)S(1)} %get-tuple-element.31.coupled, bf16[2,2,128,128]{3,2,1,0:T(8,128)(2,1)S(1)} %collective-permute-done.8.other.rest_0_, ...), custom_call_target="tpu_custom_call" | custom-call | flops 805306368 | bytes 4980736 | tf_op jit(solution)/shard_map/final/pallas_call | solution.py:234
  (29 shorter events, 7.7 us)
Async XLA Ops:
  0.0 9.7 %copy-start = (bf16[1,8,4,128,128]{4,3,2,1,0:T(8,128)(2,1)S(1)}, bf16[1,8,4,128,128]{4,3,2,1,0:T(8,128)(2,1)}, u32[]{:S(2)}) copy-start(bf16[1,8,4,128,128]{4,3,2,1,0:T(8,128)(2,1)} %param.11) | copy-start | bytes 3145732
  0.0 0.7 %copy-start.3 = (s32[2]{0:T(128)S(1)}, s32[2]{0:T(128)}, u32[]{:S(2)}) copy-start(s32[2]{0:T(128)} %iface.9) | copy-start | bytes 28
  0.7 14.2 %copy-start.4 = (s32[2]{0:T(128)S(1)}, s32[2]{0:T(128)}, u32[]{:S(2)}) copy-start(s32[2]{0:T(128)} %iface.9) | copy-start | bytes 28
  5.1 7.3 %collective-permute-start = (bf16[2,768,128]{2,1,0:T(8,128)(2,1)}, bf16[2,768,128]{2,1,0:T(8,128)(2,1)S(1)}, u32[]{:S(2)}, u32[]{:S(2)}) collective-permute-start(bf16[2,768,128]{2,1,0:T(8,128)(2,1)} %get-tuple-element.21), channel_id=1, source_target_pairs={{0,1},{1,0},{2,3},{3,2},{4,5},{5,4},{6,7},{7,6},{8,9},{9,8},{10,11... | collective-permute-start | bytes 1179656 | tf_op jit(solution)/shard_map/ppermute | solution.py:262
  5.9 9.1 %collective-permute-start.1 = (bf16[2,768,128]{2,1,0:T(8,128)(2,1)S(1)}, bf16[2,768,128]{2,1,0:T(8,128)(2,1)S(1)}, u32[]{:S(2)}, u32[]{:S(2)}) collective-permute-start(bf16[2,768,128]{2,1,0:T(8,128)(2,1)S(1)} %get-tuple-element.22), channel_id=1, source_target_pairs={{1,2},{2,1},{5,6},{6,5},{9,10},{10,9},{13,14},{14,13},{17,18},{18,... | collective-permute-start | bytes 1179656 | tf_op jit(solution)/shard_map/ppermute | solution.py:261
  9.7 1.0 %copy-start.1 = (bf16[1,8,128,128]{3,2,1,0:T(8,128)(2,1)S(1)}, bf16[1,8,128,128]{3,2,1,0:T(8,128)(2,1)}, u32[]{:S(2)}) copy-start(bf16[1,8,128,128]{3,2,1,0:T(8,128)(2,1)} %param.13) | copy-start | bytes 786436
  10.6 0.9 %copy-start.2 = (bf16[1,8,128,128]{3,2,1,0:T(8,128)(2,1)S(1)}, bf16[1,8,128,128]{3,2,1,0:T(8,128)(2,1)}, u32[]{:S(2)}) copy-start(bf16[1,8,128,128]{3,2,1,0:T(8,128)(2,1)} %param.10) | copy-start | bytes 786436
  17.3 7.8 %collective-permute-start.2 = (bf16[2,512,128]{2,1,0:T(8,128)(2,1)S(1)}, bf16[2,512,128]{2,1,0:T(8,128)(2,1)S(1)}, u32[]{:S(2)}, u32[]{:S(2)}) collective-permute-start(bf16[2,512,128]{2,1,0:T(8,128)(2,1)S(1)} %get-tuple-element.25), channel_id=1, source_target_pairs={{0,1},{1,0},{2,3},{3,2},{4,5},{5,4},{6,7},{7,6},{8,9},{9,8},{10,11... | collective-permute-start | bytes 786440 | tf_op jit(solution)/shard_map/ppermute | solution.py:262
  17.3 7.7 %collective-permute-start.3 = (bf16[2,512,128]{2,1,0:T(8,128)(2,1)S(1)}, bf16[2,512,128]{2,1,0:T(8,128)(2,1)S(1)}, u32[]{:S(2)}, u32[]{:S(2)}) collective-permute-start(bf16[2,512,128]{2,1,0:T(8,128)(2,1)S(1)} %get-tuple-element.26), channel_id=1, source_target_pairs={{1,2},{2,1},{5,6},{6,5},{9,10},{10,9},{13,14},{14,13},{17,18},{18,... | collective-permute-start | bytes 786440 | tf_op jit(solution)/shard_map/ppermute | solution.py:261
  22.5 16.4 %collective-permute-start.4 = (bf16[2,768,128]{2,1,0:T(8,128)(2,1)S(1)}, bf16[2,768,128]{2,1,0:T(8,128)(2,1)S(1)}, u32[]{:S(2)}, u32[]{:S(2)}) collective-permute-start(bf16[2,768,128]{2,1,0:T(8,128)(2,1)S(1)} %get-tuple-element.29), channel_id=1, source_target_pairs={{0,1},{1,0},{2,3},{3,2},{4,5},{5,4},{6,7},{7,6},{8,9},{9,8},{10,11... | collective-permute-start | bytes 1179656 | tf_op jit(solution)/shard_map/ppermute | solution.py:262
  22.6 16.3 %collective-permute-start.5 = (bf16[2,768,128]{2,1,0:T(8,128)(2,1)S(1)}, bf16[2,768,128]{2,1,0:T(8,128)(2,1)S(1)}, u32[]{:S(2)}, u32[]{:S(2)}) collective-permute-start(bf16[2,768,128]{2,1,0:T(8,128)(2,1)S(1)} %get-tuple-element.30), channel_id=1, source_target_pairs={{1,2},{2,1},{5,6},{6,5},{9,10},{10,9},{13,14},{14,13},{17,18},{18,... | collective-permute-start | bytes 1179656 | tf_op jit(solution)/shard_map/ppermute | solution.py:261
  27.3 6.8 %collective-permute-start.7 = (bf16[2,128,128]{2,1,0:T(8,128)(2,1)S(1)}, bf16[2,128,128]{2,1,0:T(8,128)(2,1)S(1)}, u32[]{:S(2)}, u32[]{:S(2)}) collective-permute-start(bf16[2,128,128]{2,1,0:T(8,128)(2,1)S(1)} %get-tuple-element.32), channel_id=1, source_target_pairs={{2,4},{3,5},{0,6},{1,7},{6,8},{7,9},{4,10},{5,11},{10,12},{11,13},... | collective-permute-start | bytes 196616 | tf_op jit(solution)/shard_map/ppermute | solution.py:274
  29.3 6.2 %collective-permute-start.6 = (bf16[2,128,128]{2,1,0:T(8,128)(2,1)S(1)}, bf16[2,128,128]{2,1,0:T(8,128)(2,1)S(1)}, u32[]{:S(2)}, u32[]{:S(2)}) collective-permute-start(bf16[2,128,128]{2,1,0:T(8,128)(2,1)S(1)} %get-tuple-element.32), channel_id=1, source_target_pairs={{0,4},{1,5},{2,6},{3,7},{4,8},{5,9},{6,10},{7,11},{8,12},{9,13},{1... | collective-permute-start | bytes 196616 | tf_op jit(solution)/shard_map/ppermute | solution.py:274
  35.4 7.4 %collective-permute-start.8 = (bf16[2,2,128,128]{3,2,1,0:T(8,128)(2,1)S(1)}, bf16[2,2,128,128]{3,2,1,0:T(8,128)(2,1)S(1)}, u32[]{:S(2)}, u32[]{:S(2)}) collective-permute-start(bf16[2,2,128,128]{3,2,1,0:T(8,128)(2,1)S(1)} %pad_maximum_fusion), channel_id=1, source_target_pairs={{0,1},{1,0},{2,3},{3,2},{4,5},{5,4},{6,7},{7,6},{8,9},{9,8},{10,11... | collective-permute-start | bytes 393224 | tf_op jit(solution)/shard_map/ppermute | solution.py:275
  43.2 7.4 %collective-permute-start.10 = (bf16[2,128,128]{2,1,0:T(8,128)(2,1)S(1)}, bf16[2,128,128]{2,1,0:T(8,128)(2,1)S(1)}, u32[]{:S(2)}, u32[]{:S(2)}) collective-permute-start(bf16[2,128,128]{2,1,0:T(8,128)(2,1)S(1)} %chain.2), channel_id=1, source_target_pairs={{2,4},{3,5},{0,6},{1,7},{6,8},{7,9},{4,10},{5,11},{10,12},{11,13},... | collective-permute-start | bytes 196616 | tf_op jit(solution)/shard_map/ppermute | solution.py:274
  45.1 6.6 %collective-permute-start.9 = (bf16[2,128,128]{2,1,0:T(8,128)(2,1)S(1)}, bf16[2,128,128]{2,1,0:T(8,128)(2,1)S(1)}, u32[]{:S(2)}, u32[]{:S(2)}) collective-permute-start(bf16[2,128,128]{2,1,0:T(8,128)(2,1)S(1)} %chain.2), channel_id=1, source_target_pairs={{0,4},{1,5},{2,6},{3,7},{4,8},{5,9},{6,10},{7,11},{8,12},{9,13},{1... | collective-permute-start | bytes 196616 | tf_op jit(solution)/shard_map/ppermute | solution.py:274
  51.7 2.2 %collective-permute-start.11 = (bf16[2,2,128,128]{3,2,1,0:T(8,128)(2,1)S(1)}, bf16[2,2,128,128]{3,2,1,0:T(8,128)(2,1)S(1)}, u32[]{:S(2)}, u32[]{:S(2)}) collective-permute-start(bf16[2,2,128,128]{3,2,1,0:T(8,128)(2,1)S(1)} %pad_maximum_fusion.1), channel_id=1, source_target_pairs={{0,1},{1,0},{2,3},{3,2},{4,5},{5,4},{6,7},{7,6},{8,9},{9,8},{10,11... | collective-permute-start | bytes 393224 | tf_op jit(solution)/shard_map/ppermute | solution.py:275
  54.1 7.2 %collective-permute-start.13 = (bf16[2,128,128]{2,1,0:T(8,128)(2,1)S(1)}, bf16[2,128,128]{2,1,0:T(8,128)(2,1)S(1)}, u32[]{:S(2)}, u32[]{:S(2)}) collective-permute-start(bf16[2,128,128]{2,1,0:T(8,128)(2,1)S(1)} %chain.3), channel_id=1, source_target_pairs={{2,4},{3,5},{0,6},{1,7},{6,8},{7,9},{4,10},{5,11},{10,12},{11,13},... | collective-permute-start | bytes 196616 | tf_op jit(solution)/shard_map/ppermute | solution.py:274
  58.2 5.9 %collective-permute-start.12 = (bf16[2,128,128]{2,1,0:T(8,128)(2,1)S(1)}, bf16[2,128,128]{2,1,0:T(8,128)(2,1)S(1)}, u32[]{:S(2)}, u32[]{:S(2)}) collective-permute-start(bf16[2,128,128]{2,1,0:T(8,128)(2,1)S(1)} %chain.3), channel_id=1, source_target_pairs={{0,4},{1,5},{2,6},{3,7},{4,8},{5,9},{6,10},{7,11},{8,12},{9,13},{1... | collective-permute-start | bytes 196616 | tf_op jit(solution)/shard_map/ppermute | solution.py:274
  64.1 2.8 %collective-permute-start.14 = (bf16[2,2,128,128]{3,2,1,0:T(8,128)(2,1)S(1)}, bf16[2,2,128,128]{3,2,1,0:T(8,128)(2,1)S(1)}, u32[]{:S(2)}, u32[]{:S(2)}) collective-permute-start(bf16[2,2,128,128]{3,2,1,0:T(8,128)(2,1)S(1)} %pad_maximum_fusion.2), channel_id=1, source_target_pairs={{0,1},{1,0},{2,3},{3,2},{4,5},{5,4},{6,7},{7,6},{8,9},{9,8},{10,11... | collective-permute-start | bytes 393224 | tf_op jit(solution)/shard_map/ppermute | solution.py:275

commit v3 on v2

--- a/solution.py
+++ b/solution.py
@@ -45,33 +45,26 @@
     return d.last * (1 - parity), d.last * parity
 
 
-def first_kernel(d, face_ref, iface, rhs, inflow, inv, coupling, field, gfield, pair, cross, right, flow, tiles, couple, sems):
-    w = d.width
-    copies = [
-        pltpu.make_async_copy(inv, tiles, sems.at[0]),
-        pltpu.make_async_copy(coupling, couple, sems.at[1]),
-        pltpu.make_async_copy(inflow, flow, sems.at[2]),
-    ]
-    copies += [
-        pltpu.make_async_copy(rhs.at[:, :, pl.ds(r * w, w)], right.at[r], sems.at[3 + r]) for r in range(d.count)
-    ]
+def first_kernel(d, face_ref, iface_hbm, rhs, inflow, inv, coupling, field, gfield, pair, cross, iface, right, flow, tiles, couple, sems):
+    w = d.width
+    moves = [(inv, tiles)] + [(rhs.at[t], right.at[t]) for t in range(d.ticks)]
+    moves += [(iface_hbm, iface), (coupling, couple), (inflow, flow)]
+    copies = [pltpu.make_async_copy(a, b, sems.at[i]) for i, (a, b) in enumerate(moves)]
     for copy in copies:
         copy.start()
+    for copy in copies:
+        copy.wait()
     parity = lax.rem(face_ref[0], 2)
-    for copy in copies[:3]:
-        copy.wait()
-    coupled = []
-    for q in range(d.nq):
-        coupled.append(dot_nt(flow[:, q * w : (q + 1) * w], couple[q]))
-        turned = couple[q].astype(F32).T.astype(BF)
-        gfield[q] = dot_nt(turned, tiles[iface[q]]).astype(BF)
     for r in range(d.count):
-        copies[3 + r].wait()
-        field[r] = dot_nt(right[r].reshape(d.batch, w), tiles[r]).astype(BF)
+        x = jnp.concatenate([right[t, :, r * w : (r + 1) * w] for t in range(d.ticks)], axis=0)
+        field[r] = dot_nt(x, tiles[r]).astype(BF)
     for q in range(d.nq):
         row = iface[q]
-        corrected = (right[row, 0].astype(F32) - coupled[q]).astype(BF)
-        field[row, 0 : d.sources, :] = dot_nt(corrected, tiles[row]).astype(BF)
+        turned = couple[q].astype(F32).T.astype(BF)
+        gfield[q] = dot_nt(turned, tiles[row]).astype(BF)
+        coupled = dot_nn(flow[:, q * w : (q + 1) * w], turned)
+        corrected = right[0, :, pl.ds(pl.multiple_of(row * w, w), w)].astype(F32) - coupled
+        field[row, 0 : d.sources, :] = dot_nt(corrected.astype(BF), tiles[row]).astype(BF)
     for start, buffer in zip(edge_rows(d, parity), (pair, cross)):
         for e in range(HALO):
             buffer[e, 0 : d.batch, :] = field[start + e]
@@ -99,7 +92,7 @@
 
 def batch_kernel(d, last, face_ref, iface, cols, field, base, pair_in, cross_in, folded, *rest):
     if last:
-        out, faces_out, sent, ext = rest
+        out, faces_out, ext = rest
     else:
         out, pair, cross, ext = rest
     face = face_ref[0]
@@ -114,9 +107,8 @@
     if last:
         for q in range(d.nq):
             row = iface[q]
-            for t in range(d.ticks):
+            for t in range(d.ticks - 1):
                 faces_out[t, q] = out[row, t * d.sources : (t + 1) * d.sources, :]
-            sent[q] = out[row, 0 : d.sources, :]
     else:
         for start, buffer in zip(edge_rows(d, parity), (pair, cross)):
             buffer[...] = out[pl.ds(start, HALO)]
@@ -167,17 +159,34 @@
             buffer[:, i * d.group : (i + 1) * d.group, :] = out[pl.ds(start, HALO), pl.ds(d.start(face + shift), d.group), :]
 
 
-def coupling_last_kernel(d, face_ref, iface, cols, gfield, gfirst, pair_in, cross_in, folded, out, chain, ext):
-    face = face_ref[0]
+def coupling_ext(d, face, gfirst, pair_in, cross_in, ext):
     parity = lax.rem(face, 2)
-    w = d.width
-    ext[0:HALO] = jnp.zeros((HALO, d.wide, w), BF)
-    ext[d.up : d.ext] = jnp.zeros((HALO, d.wide, w), BF)
+    ext[0:HALO] = jnp.zeros((HALO, d.wide, d.width), BF)
+    ext[d.up : d.ext] = jnp.zeros((HALO, d.wide, d.width), BF)
     ext[HALO : HALO + d.count] = gfirst[...]
     neighbours = ((d.up * (1 - parity), face + 1 - 2 * parity, pair_in), (d.up * parity, face - 1 + 2 * parity, cross_in))
     for start, other, block in neighbours:
         for i, shift in enumerate((-1, 0, 1)):
             ext[pl.ds(start, HALO), pl.ds(d.start(other + shift), d.group), :] = block[:, i * d.group : (i + 1) * d.group, :]
+
+
+def coupling_chain_kernel(d, face_ref, iface, cols, gfield, gfirst, pair_in, cross_in, folded, after, chain, ext):
+    face = face_ref[0]
+    w = d.width
+    coupling_ext(d, face, gfirst, pair_in, cross_in, ext)
+    for q in range(d.nq):
+        lanes = slice(q * w, (q + 1) * w)
+        for s in range(0, d.wide, d.group):
+            span = pl.ds(s, d.group)
+            chain[span, lanes] = sweep(d, cols, face, ext, span, iface[q], folded).astype(BF)
+        span = pl.ds(pl.multiple_of(d.start(face) + q * w, w), w)
+        chain[span, lanes] = (chain[span, lanes].astype(F32) + gfield[q].astype(F32)).astype(BF)
+
+
+def coupling_last_kernel(d, face_ref, iface, cols, gfield, gfirst, pair_in, cross_in, folded, after, out, ext):
+    face = face_ref[0]
+    w = d.width
+    coupling_ext(d, face, gfirst, pair_in, cross_in, ext)
     for r in range(d.count):
         for s in range(0, d.wide, d.group):
             span = pl.ds(s, d.group)
@@ -186,58 +195,84 @@
         lane = pl.ds(pl.multiple_of(iface[q] * w, w), w)
         span = pl.ds(pl.multiple_of(d.start(face) + q * w, w), w)
         out[span, lane] = (out[span, lane].astype(F32) + gfield[q].astype(F32)).astype(BF)
-        chain[:, q * w : (q + 1) * w] = out[:, lane]
+
+
+def chip_hops(faces):
+    return [(0, None)] if faces <= 2 else [(0, 1)] if faces <= 4 else [(0, 1), (-1, None)]
+
+
+def hop_face(faces, face, hop):
+    return face ^ (2 * hop) if faces <= 4 else face + 2 * hop
 
 
 def arrived_blocks(d, face, own, other):
     parity = lax.rem(face, 2)
-    shifts = chip_shifts(d.faces)
-    for k, shift in enumerate(shifts):
-        there = face + 2 * shift if len(shifts) != 2 else face ^ (2 * shift)
-        for block, source in ((own, there), (other, there + 1 - 2 * parity)):
-            yield jnp.concatenate([block(k, q) for q in range(d.nq)], axis=1), d.start(source)
-
-
-def chip_shifts(faces):
-    return (0,) if faces <= 2 else (0, 1) if faces <= 4 else (0, -1, 1)
-
-
-def chain_kernel(d, tick, face_ref, chain, faces_out, other, *rest):
-    own, sent = rest[:-1], rest[-1]
-    total = jnp.zeros((d.sources, d.group), F32)
-    for x, start in arrived_blocks(d, face_ref[0], lambda k, q: own[k][q], lambda k, q: other[k, q]):
-        total += dot_nn(x, chain[pl.ds(start, d.group), :])
+    for i, hops in enumerate(chip_hops(d.faces)):
+        starts = [0 if hop is None else d.start(hop_face(d.faces, face - parity, hop)) for hop in hops]
+        for block, odd in ((own[i], parity), (other[i], 1 - parity)):
+            start = pl.multiple_of(jnp.where(odd == 1, starts[1], starts[0]), d.group)
+            yield jnp.concatenate([block[j] for j in range(2 * d.nq)], axis=1), start
+
+
+def chain_kernel(d, tick, face_ref, own_chain, other_chain, own_faces, other_faces, *rest):
+    arrived, sent = rest[:-1], rest[-1]
+    face = face_ref[0]
+    parity = lax.rem(face, 2)
+    half = len(arrived) // 2
+    blocks = list(arrived_blocks(d, face, arrived[:half], arrived[half:]))
+    for chain, base, odd in ((own_chain, own_faces, parity), (other_chain, other_faces, 1 - parity)):
+        total = jnp.zeros((d.sources, d.group), F32)
+        for x, start in blocks:
+            total += dot_nn(x, chain[pl.ds(start, 2 * d.group), :])
+        for q in range(d.nq):
+            value = base[tick, q].astype(F32) - total[:, q * d.width : (q + 1) * d.width]
+            sent[odd * d.nq + q] = value.astype(BF)
+
+
+def merge_kernel(d, face_ref, own, other, sent):
+    parity = lax.rem(face_ref[0], 2)
     for q in range(d.nq):
-        sent[q] = (faces_out[tick, q].astype(F32) - total[:, q * d.width : (q + 1) * d.width]).astype(BF)
-
-
-def final_kernel(d, face_ref, fields, coupled, *rest):
-    arrived, out = rest[:-1], rest[-1]
-    w = d.width
-    hops = len(chip_shifts(d.faces))
-    for r in range(d.count):
-        out[0, :, r * w : (r + 1) * w] = fields[r, 0 : d.sources, :]
-    for t in range(1, d.ticks):
-        other, *own = arrived[(t - 1) * (hops + 1) : t * (hops + 1)]
-        total = jnp.zeros((d.sources, d.count * w), F32)
-        for x, start in arrived_blocks(d, face_ref[0], lambda k, q: own[k][q], lambda k, q: other[k, q]):
-            total += dot_nn(x, coupled[pl.ds(start, d.group), :])
+        sent[parity * d.nq + q] = own[0, q]
+        sent[(1 - parity) * d.nq + q] = other[0, q]
+
+
+def output_kernel(d, ticks, face_ref, fields, coupled, *rest):
+    *arrived, out, held, sems = rest
+    w = d.width
+    face = face_ref[0]
+    each = 2 * len(chip_hops(d.faces))
+    copies = []
+    arrived = arrived[len(arrived) % each :]
+    for i, t in enumerate(ticks):
+        total = None
+        if t:
+            mine, arrived = arrived[:each], arrived[each:]
+            total = jnp.zeros((d.sources, d.count * w), F32)
+            for x, start in arrived_blocks(d, face, mine[: each // 2], mine[each // 2 :]):
+                total += dot_nn(x, coupled[pl.ds(start, 2 * d.group), :])
         for r in range(d.count):
-            base = fields[r, t * d.sources : (t + 1) * d.sources, :].astype(F32)
-            out[t, :, r * w : (r + 1) * w] = (base - total[:, r * w : (r + 1) * w]).astype(BF)
-
-
-def call(body, name, smem, inputs, outs, scratch=(), flops=0, anywhere=(), sems=0):
-    vmem = pl.BlockSpec(memory_space=pltpu.VMEM)
+            value = fields[r, t * d.sources : (t + 1) * d.sources, :]
+            if t:
+                value = (value.astype(F32) - total[:, r * w : (r + 1) * w]).astype(BF)
+            held[i, :, r * w : (r + 1) * w] = value
+        copies.append(pltpu.make_async_copy(held.at[i], out.at[t], sems.at[i]))
+        copies[-1].start()
+    for copy in copies:
+        copy.wait()
+
+
+def call(body, name, smem, inputs, outs, scratch=(), flops=0, anywhere=(), sems=0, place=pltpu.VMEM, aliases=None):
     moved = sum(x.size * x.dtype.itemsize for x in inputs) + sum(2 * math.prod(s) for s in outs)
-    specs = [pl.BlockSpec(memory_space=pl.ANY) if i in anywhere else vmem for i in range(len(inputs))]
+    specs = [pl.BlockSpec(memory_space=pl.ANY if i in anywhere else pltpu.VMEM) for i in range(len(inputs))]
     return pl.pallas_call(
         body,
         name=name,
         out_shape=[jax.ShapeDtypeStruct(s, BF) for s in outs],
         in_specs=[pl.BlockSpec(memory_space=pltpu.SMEM)] * len(smem) + specs,
-        out_specs=[vmem] * len(outs),
-        scratch_shapes=[pltpu.VMEM(s, BF) for s in scratch] + ([pltpu.SemaphoreType.DMA((sems,))] if sems else []),
+        out_specs=[pl.BlockSpec(memory_space=place)] * len(outs),
+        scratch_shapes=[pltpu.VMEM(s, BF) if isinstance(s, tuple) else s for s in scratch]
+        + ([pltpu.SemaphoreType.DMA((sems,))] if sems else []),
+        input_output_aliases=aliases or {},
         compiler_params=pltpu.CompilerParams(vmem_limit_bytes=32 * 1024 * 1024),
         cost_estimate=pl.CostEstimate(flops=flops, bytes_accessed=moved, transcendentals=0),
     )(*smem, *inputs)
@@ -251,7 +286,6 @@
     d = Dims(ticks, sources, count, neigh, width, nq, faces)
     diag, off, inv, couple, cols = diag_tiles[0], off_tiles[0], inverse_tiles[0], coupling[0], cols[0]
     face = lax.axis_index("face").astype(jnp.int32)[None]
-    face, iface, cols = (pltpu.with_memory_space_constraint(x, pltpu.SMEM) for x in (face, iface, cols))
     tile = width * width
 
     pairing = [(i, i ^ 1) for i in range(faces) if i ^ 1 < faces]
@@ -261,30 +295,42 @@
         got = lax.ppermute(cross, "face", crossing)
         return lax.ppermute(pair, "face", pairing), got
 
-    def onward(block):
-        shifts = chip_shifts(faces)
+    def swap(block):
+        return lax.ppermute(block, "face", pairing)
+
+    def onward(block, beside=lambda: None):
         own = []
-        for shift in shifts:
+        for hops in chip_hops(faces):
             route = []
             for s in range(1, slabs):
                 for f in range(faces):
-                    g = f ^ (2 * shift) if len(shifts) == 2 else f + 2 * shift
+                    hop = hops[f % 2]
+                    g = -1 if hop is None else hop_face(faces, f, hop)
                     if 0 <= g < faces:
                         route.append(((s - 1) * faces + g, s * faces + f))
             own.append(lax.ppermute(block, ("slab", "face"), route))
-        return [lax.ppermute(jnp.stack(own), "face", pairing)] + own
+        made = beside()
+        if made is not None:
+            *own, made = lax.optimization_barrier((*own, made))
+        return own + [swap(x) for x in own], made
 
     batch, group, ext, wide = d.batch, d.group, d.ext, d.wide
     field, gfield, pair, cross = call(
         functools.partial(first_kernel, d),
         "first",
-        [face, iface],
-        [pltpu.with_memory_space_constraint(x, pltpu.HBM) for x in (rhs[:, 0], inflow[0], inv, couple)],
+        [face],
+        [pltpu.with_memory_space_constraint(x, pltpu.HBM) for x in (iface, rhs[:, 0], inflow[0], inv, couple)],
         [(count, batch, width), (nq, width, width)] + [(HALO, batch + group, width)] * 2,
-        [(count, ticks, sources, width), (sources, group), (count, width, width), (nq, width, width)],
+        [
+            pltpu.SMEM(iface.shape, jnp.int32),
+            (ticks, sources, count * width),
+            (sources, group),
+            (count, width, width),
+            (nq, width, width),
+        ],
         flops=2 * batch * count * tile,
-        anywhere=(0, 1, 2, 3),
-        sems=3 + count,
+        anywhere=(0, 1, 2, 3, 4),
+        sems=4 + ticks,
     )
     (folded,) = call(
         functools.partial(fold_kernel, d),
@@ -310,52 +356,94 @@
         functools.partial(coupling_first_kernel, d),
         "coupling_first",
         [face, iface, cols],
-        [gfield, pair0, cross0, folded, once],
+        [gfield, pair0, cross0, folded, pair1],
         [(count, wide, width)] + [(HALO, 3 * group, width)] * 2,
         [(2 * HALO + nq, width, count * width)],
         flops=2 * (2 * HALO + nq) * width * count * tile,
         anywhere=(4,),
     )
+    cross1, gfirst = lax.optimization_barrier((cross1, gfirst))
     gpair, gcross = exchange(gpair, gcross)
-    fields, faces_out, sent = call(
+    fields, faces_out = call(
         functools.partial(batch_kernel, d, True),
         "third",
         [face, iface, cols],
         [once, field, pair1, cross1, folded],
-        [(count, batch, width), (ticks, nq, sources, width), (nq, sources, width)],
+        [(count, batch, width), (ticks - 1, nq, sources, width)],
         [(ext, batch, width)],
         flops=2 * batch * count * tile * (neigh + 1),
     )
-    arrived = onward(sent)
-    coupled, chain = call(
-        functools.partial(coupling_last_kernel, d),
-        "coupling_last",
-        [face, iface, cols],
-        [gfield, gfirst, gpair, gcross, folded],
-        [(wide, count * width), (wide, group)],
-        [(ext, wide, width)],
-        flops=2 * wide * count * tile * (neigh + 1),
-    )
-    everything = list(arrived)
-    for tick in range(1, ticks - 1):
+    other_faces = swap(faces_out)
+    (sent,) = call(
+        functools.partial(merge_kernel, d),
+        "merge",
+        [face],
+        [faces_out, other_faces],
+        [(2 * nq, sources, width)],
+    )
+
+    def operator_rows():
+        return call(
+            functools.partial(coupling_chain_kernel, d),
+            "coupling_chain",
+            [face, iface, cols],
+            [gfield, gfirst, gpair, gcross, folded, sent],
+            [(wide, group)],
+            [(ext, wide, width)],
+            flops=2 * wide * nq * tile * (neigh + 1),
+            anywhere=(5,),
+        )[0]
+
+    arrived, chain = onward(sent, operator_rows)
+    other_chain = swap(chain)
+    whole = (ticks, sources, count * width)
+
+    def operator():
+        return call(
+            functools.partial(coupling_last_kernel, d),
+            "coupling_last",
+            [face, iface, cols],
+            [gfield, gfirst, gpair, gcross, folded, chain],
+            [(wide, count * width)],
+            [(ext, wide, width)],
+            flops=2 * wide * count * tile * (neigh + 1),
+            anywhere=(5,),
+        )[0]
+
+    def output(which, blocks, earlier):
+        return call(
+            functools.partial(output_kernel, d, which),
+            "output",
+            [face],
+            [fields, coupled] + earlier + blocks,
+            [whole],
+            [(len(which), sources, count * width)],
+            flops=2 * len(which) * sources * wide * count * width,
+            anywhere=(2,) if earlier else (),
+            sems=len(which),
+            place=pl.ANY,
+            aliases={3: 0} if earlier else None,
+        )[0]
+
+    everything = []
+    coupled = most = None
+    for tick in range(1, ticks):
+        everything += arrived
+        if tick == ticks - 1:
+            break
         (sent,) = call(
             functools.partial(chain_kernel, d, tick),
             "chain",
             [face],
-            [chain, faces_out] + arrived,
-            [(nq, sources, width)],
-            flops=2 * sources * wide * group,
+            [chain, other_chain, faces_out, other_faces] + arrived,
+            [(2 * nq, sources, width)],
+            flops=4 * sources * wide * group,
         )
-        arrived = onward(sent)
-        everything += arrived
-    (out,) = call(
-        functools.partial(final_kernel, d),
-        "final",
-        [face],
-        [fields, coupled] + everything,
-        [(ticks, sources, count * width)],
-        flops=2 * (ticks - 1) * sources * wide * count * width,
-    )
+        if tick == 1:
+            arrived, coupled = onward(sent, operator)
+        else:
+            arrived, most = onward(sent, lambda: output(tuple(range(ticks - 1)), everything, []))
+    out = output((ticks - 1,), arrived, [most])
     return out[:, None]
 
 

time: 69.4 us -> 61.2 us (0.88)
  starting transfers between devices: 33.2 us -> 20.5 us
  waiting for transfers between devices: 13.6 us -> 17.9 us
  Pallas kernels: 18.5 us -> 19.4 us
  local copies, waits for them, and re-layouts: 3.41 us -> 2.67 us
    ppermute x6 -> x3, starting transfers between devices: 17.3 us -> 8.95 us  [onward(): own.append(lax.ppermute(block, ('slab', 'face'), route))]
    ppermute x3 -> x5, starting transfers between devices: 6.47 us -> 2.04 us  [swap(): return lax.ppermute(block, 'face', pairing)]
    ppermute x3 -> x5, waiting for transfers between devices: 1.98 us -> 5.12 us  [swap(): return lax.ppermute(block, 'face', pairing)]
    ppermute x6 -> x3, waiting for transfers between devices: 9.19 us -> 10.3 us  [onward(): own.append(lax.ppermute(block, ('slab', 'face'), route))]
    pallas_call x9 -> x12, Pallas kernels: 18.5 us -> 19.4 us  [call(): pl.pallas_call(body, name=name, out_shape=[jax.ShapeDtypeStruct(s, BF) fo...]
    unnamed x10 -> x8, local copies, waits for them, and re-layouts: 2.65 us -> 1.91 us
  transfers between devices with their start and end apart: 15 -> 14, of which waited for: 8 -> 8; matrix products, arithmetic and copies ran while one was open for 1% -> 1% of each run, Pallas kernels for 13% -> 20%
where the time goes in v3:
time: 61.2 us; the launch traced here: 60.8 us
  starting transfers between devices  20.5 us (33%)
  Pallas kernels  19.4 us (32%)
  waiting for transfers between devices  17.9 us (29%)
  local copies, waits for them, and re-layouts  2.67 us (4%)
    pallas_call x12, Pallas kernels, call(): pl.pallas_call(body, name=name, out_shape=[jax.ShapeDtypeStruct(s, BF) fo...  19.4 us
    ppermute x3, waiting for transfers between devices, onward(): own.append(lax.ppermute(block, ('slab', 'face'), route))  10.3 us
    ppermute x3, starting transfers between devices, onward(): own.append(lax.ppermute(block, ('slab', 'face'), route))  8.95 us
    ppermute x3, starting transfers between devices, exchange(): got = lax.ppermute(cross, 'face', crossing)  8.63 us
    ppermute x5, waiting for transfers between devices, swap(): return lax.ppermute(block, 'face', pairing)  5.12 us
    ppermute x3, waiting for transfers between devices, exchange(): got = lax.ppermute(cross, 'face', crossing)  2.47 us
    ppermute x5, starting transfers between devices, swap(): return lax.ppermute(block, 'face', pairing)  2.04 us
    unnamed x8, local copies, waits for them, and re-layouts  1.91 us
  transfers between devices with their start and end apart: 14, of which 8 were waited for; matrix products, arithmetic and copies ran while one was open for 1% of the time, Pallas kernels for 20%

profile of v3, /device:TPU:9, one launch (start us, length us, event | category | flops | bytes accessed | tf_op | source)
XLA Modules:
  0.0 60.8 jit_solution(14253663327341370923)
XLA Ops:
  0.0 2.9 %first.1 = (bf16[8,512,128]{2,1,0:T(8,128)(2,1)S(1)}, bf16[2,128,128]{2,1,0:T(8,128)(2,1)S(1)}, bf16[2,768,128]{2,1,0:T(8,128)(2,1)}, bf16[2,768,128]{2,1,0:T(8,128)(2,1)S(1)}) custom-call(s32[1]{0:T(128)} %bitcast.face_ref, s32[2]{0:T(128)} %iface.9, bf16[4,128,1024]{2,1,0:T(8,128)(2,1)} %bitcast.15, bf16[128,256]{1,0:T(8,128)(2,1)} %bitcast.16, ...), custom_call_target="tpu_custom_call" | custom-call | flops 134217728 | bytes 3342344 | tf_op jit(solution)/shard_map/first/pallas_call | solution.py:267
  3.7 3.0 %collective-permute-start.1 = (bf16[2,768,128]{2,1,0:T(8,128)(2,1)S(1)}, bf16[2,768,128]{2,1,0:T(8,128)(2,1)S(1)}, u32[]{:S(2)}, u32[]{:S(2)}) collective-permute-start(bf16[2,768,128]{2,1,0:T(8,128)(2,1)S(1)} %get-tuple-element.27), channel_id=1, source_target_pairs={{1,2},{2,1},{5,6},{6,5},{9,10},{10,9},{13,14},{14,13},{17,18},{18,... | collective-permute-start | bytes 1179656 | tf_op jit(solution)/shard_map/ppermute | solution.py:295
  7.5 0.9 %copy-done.1 = bf16[1,8,128,128]{3,2,1,0:T(8,128)(2,1)S(1)} copy-done((bf16[1,8,128,128]{3,2,1,0:T(8,128)(2,1)S(1)}, bf16[1,8,128,128]{3,2,1,0:T(8,128)(2,1)}, u32[]{:S(2)}) %copy-start.1) | copy-done | bytes 262168
  8.4 0.9 %copy-done.2 = bf16[1,8,128,128]{3,2,1,0:T(8,128)(2,1)S(1)} copy-done((bf16[1,8,128,128]{3,2,1,0:T(8,128)(2,1)S(1)}, bf16[1,8,128,128]{3,2,1,0:T(8,128)(2,1)}, u32[]{:S(2)}) %copy-start.2) | copy-done | bytes 262168
  10.3 2.5 %collective-permute-done.1.cross_in = bf16[2,768,128]{2,1,0:T(8,128)(2,1)S(1)} collective-permute-done((bf16[2,768,128]{2,1,0:T(8,128)(2,1)S(1)}, bf16[2,768,128]{2,1,0:T(8,128)(2,1)S(1)}, u32[]{:S(2)}, u32[]{:S(2)}) %collective-permute-start.1) | collective-permute-done | bytes 393248 | tf_op jit(solution)/shard_map/ppermute | solution.py:295
  12.8 2.3 %second.1 = (bf16[8,512,128]{2,1,0:T(8,128)(2,1)S(1)}, bf16[2,512,128]{2,1,0:T(8,128)(2,1)S(1)}, bf16[2,512,128]{2,1,0:T(8,128)(2,1)S(1)}) custom-call(s32[1]{0:T(128)} %bitcast.face_ref, s32[2]{0:T(128)S(1)} %copy-done.3, s32[8,4]{1,0:T(8,128)S(1)} %copy.12.cols, bf16[8,512,128]{2,1,0:T(8,128)(2,1)S(1)} %get-tuple-element.25.field.base, ...), custom_call_target="tpu_custom_call" | custom-call | flops 671088640 | bytes 5767168 | tf_op jit(solution)/shard_map/second/pallas_call | solution.py:267
  15.1 3.0 %collective-permute-start.3 = (bf16[2,512,128]{2,1,0:T(8,128)(2,1)S(1)}, bf16[2,512,128]{2,1,0:T(8,128)(2,1)S(1)}, u32[]{:S(2)}, u32[]{:S(2)}) collective-permute-start(bf16[2,512,128]{2,1,0:T(8,128)(2,1)S(1)} %get-tuple-element.31), channel_id=1, source_target_pairs={{1,2},{2,1},{5,6},{6,5},{9,10},{10,9},{13,14},{14,13},{17,18},{18,... | collective-permute-start | bytes 786440 | tf_op jit(solution)/shard_map/ppermute | solution.py:295
  18.2 2.1 %coupling_first.1 = (bf16[8,1024,128]{2,1,0:T(8,128)(2,1)S(1)}, bf16[2,768,128]{2,1,0:T(8,128)(2,1)S(1)}, bf16[2,768,128]{2,1,0:T(8,128)(2,1)S(1)}) custom-call(s32[1]{0:T(128)} %bitcast.face_ref, s32[2]{0:T(128)S(1)} %copy-done.3, s32[8,4]{1,0:T(8,128)S(1)} %copy.12.cols, bf16[2,128,128]{2,1,0:T(8,128)(2,1)S(1)} %get-tuple-element.28.after.gfield, ...), custom_call_target="tpu_custom_call" | custom-call | flops 201326592 | bytes 5308416 | tf_op jit(solution)/shard_map/coupling_first/pallas_call | solution.py:267
  20.3 2.6 %collective-permute-start.7 = (bf16[2,768,128]{2,1,0:T(8,128)(2,1)S(1)}, bf16[2,768,128]{2,1,0:T(8,128)(2,1)S(1)}, u32[]{:S(2)}, u32[]{:S(2)}) collective-permute-start(bf16[2,768,128]{2,1,0:T(8,128)(2,1)S(1)} %get-tuple-element.38), channel_id=1, source_target_pairs={{1,2},{2,1},{5,6},{6,5},{9,10},{10,9},{13,14},{14,13},{17,18},{18,... | collective-permute-start | bytes 1179656 | tf_op jit(solution)/shard_map/ppermute | solution.py:295
  22.9 2.2 %third.1 = (bf16[8,512,128]{2,1,0:T(8,128)(2,1)S(1)}, bf16[3,2,128,128]{3,2,1,0:T(8,128)(2,1)S(1)}) custom-call(s32[1]{0:T(128)} %bitcast.face_ref, s32[2]{0:T(128)S(1)} %copy-done.3, s32[8,4]{1,0:T(8,128)S(1)} %copy.12.cols, bf16[8,512,128]{2,1,0:T(8,128)(2,1)S(1)} %get-tuple-element.29.field, bf16[8,512,128]{2,1,0:T(8,128)(2,1)S(1)} %get-tuple-element.25.field.base, ...), custom_call_target="tpu_custom_call" | custom-call | flops 671088640 | bytes 5177344 | tf_op jit(solution)/shard_map/third/pallas_call | solution.py:267
  25.3 1.4 %collective-permute-done.4.other.other_faces = bf16[3,2,128,128]{3,2,1,0:T(8,128)(2,1)S(1)} collective-permute-done((bf16[3,2,128,128]{3,2,1,0:T(8,128)(2,1)S(1)}, bf16[3,2,128,128]{3,2,1,0:T(8,128)(2,1)S(1)}, u32[]{:S(2)}, u32[]{:S(2)}) %collective-permute-start.4) | collective-permute-done | bytes 196640 | tf_op jit(solution)/shard_map/ppermute | solution.py:299
  26.7 3.7 %collective-permute-start.5 = (bf16[4,128,128]{2,1,0:T(8,128)(2,1)S(1)}, bf16[4,128,128]{2,1,0:T(8,128)(2,1)S(1)}, u32[]{:S(2)}, u32[]{:S(2)}) collective-permute-start(bf16[4,128,128]{2,1,0:T(8,128)(2,1)S(1)} %merge.1.after), channel_id=1, source_target_pairs={{0,4},{3,5},{2,6},{1,7},{4,8},{7,9},{6,10},{5,11},{8,12},{11,13},{... | collective-permute-start | bytes 393224 | tf_op jit(solution)/shard_map/ppermute | solution.py:311
  30.4 1.8 %coupling_chain.1.own_chain.after = bf16[1024,256]{1,0:T(8,128)(2,1)S(1)} custom-call(s32[1]{0:T(128)} %bitcast.face_ref, s32[2]{0:T(128)S(1)} %copy-done.3, s32[8,4]{1,0:T(8,128)S(1)} %copy.12.cols, bf16[2,128,128]{2,1,0:T(8,128)(2,1)S(1)} %get-tuple-element.28.after.gfield, bf16[8,1024,128]{2,1,0:T(8,128)(2,1)S(1)} %get-tuple-element.36.gfirst, ...), custom_call_target="tpu_custom_call" | custom-call | flops 335544320 | bytes 4915200 | tf_op jit(solution)/shard_map/coupling_chain/pallas_call | solution.py:267
  32.2 3.2 %collective-permute-done.5.rest_0_ = bf16[4,128,128]{2,1,0:T(8,128)(2,1)S(1)} collective-permute-done((bf16[4,128,128]{2,1,0:T(8,128)(2,1)S(1)}, bf16[4,128,128]{2,1,0:T(8,128)(2,1)S(1)}, u32[]{:S(2)}, u32[]{:S(2)}) %collective-permute-start.5) | collective-permute-done | bytes 131104 | tf_op jit(solution)/shard_map/ppermute | solution.py:311
  36.2 1.7 %collective-permute-done.9.rest_1_ = bf16[4,128,128]{2,1,0:T(8,128)(2,1)S(1)} collective-permute-done((bf16[4,128,128]{2,1,0:T(8,128)(2,1)S(1)}, bf16[4,128,128]{2,1,0:T(8,128)(2,1)S(1)}, u32[]{:S(2)}, u32[]{:S(2)}) %collective-permute-start.9) | collective-permute-done | bytes 131104 | tf_op jit(solution)/shard_map/ppermute | solution.py:299
  38.2 3.1 %collective-permute-start.10 = (bf16[4,128,128]{2,1,0:T(8,128)(2,1)S(1)}, bf16[4,128,128]{2,1,0:T(8,128)(2,1)S(1)}, u32[]{:S(2)}, u32[]{:S(2)}) collective-permute-start(bf16[4,128,128]{2,1,0:T(8,128)(2,1)S(1)} %chain.2), channel_id=1, source_target_pairs={{0,4},{3,5},{2,6},{1,7},{4,8},{7,9},{6,10},{5,11},{8,12},{11,13},{... | collective-permute-start | bytes 393224 | tf_op jit(solution)/shard_map/ppermute | solution.py:311
  41.3 3.8 %coupling_last.1.coupled = bf16[1024,1024]{1,0:T(8,128)(2,1)S(1)} custom-call(s32[1]{0:T(128)} %bitcast.face_ref, s32[2]{0:T(128)S(1)} %copy-done.3, s32[8,4]{1,0:T(8,128)S(1)} %copy.12.cols, bf16[2,128,128]{2,1,0:T(8,128)(2,1)S(1)} %get-tuple-element.28.after.gfield, bf16[8,1024,128]{2,1,0:T(8,128)(2,1)S(1)} %get-tuple-element.36.gfirst, ...), custom_call_target="tpu_custom_call" | custom-call | flops 1342177280 | bytes 6881280 | tf_op jit(solution)/shard_map/coupling_last/pallas_call | solution.py:267
  45.1 1.9 %collective-permute-done.10.rest_0_.rest_2_ = bf16[4,128,128]{2,1,0:T(8,128)(2,1)S(1)} collective-permute-done((bf16[4,128,128]{2,1,0:T(8,128)(2,1)S(1)}, bf16[4,128,128]{2,1,0:T(8,128)(2,1)S(1)}, u32[]{:S(2)}, u32[]{:S(2)}) %collective-permute-start.10) | collective-permute-done | bytes 131104 | tf_op jit(solution)/shard_map/ppermute | solution.py:311
  47.7 1.0 %collective-permute-done.11.rest_1_.rest_3_ = bf16[4,128,128]{2,1,0:T(8,128)(2,1)S(1)} collective-permute-done((bf16[4,128,128]{2,1,0:T(8,128)(2,1)S(1)}, bf16[4,128,128]{2,1,0:T(8,128)(2,1)S(1)}, u32[]{:S(2)}, u32[]{:S(2)}) %collective-permute-start.11) | collective-permute-done | bytes 131104 | tf_op jit(solution)/shard_map/ppermute | solution.py:299
  49.0 2.2 %collective-permute-start.12 = (bf16[4,128,128]{2,1,0:T(8,128)(2,1)S(1)}, bf16[4,128,128]{2,1,0:T(8,128)(2,1)S(1)}, u32[]{:S(2)}, u32[]{:S(2)}) collective-permute-start(bf16[4,128,128]{2,1,0:T(8,128)(2,1)S(1)} %chain.3), channel_id=1, source_target_pairs={{0,4},{3,5},{2,6},{1,7},{4,8},{7,9},{6,10},{5,11},{8,12},{11,13},{... | collective-permute-start | bytes 393224 | tf_op jit(solution)/shard_map/ppermute | solution.py:311
  51.1 1.6 %output.2.rest_0_ = bf16[4,128,1024]{2,1,0:T(8,128)(2,1)} custom-call(s32[1]{0:T(128)} %bitcast.face_ref, bf16[8,512,128]{2,1,0:T(8,128)(2,1)S(1)} %get-tuple-element.34.fields, bf16[1024,1024]{1,0:T(8,128)(2,1)S(1)} %coupling_last.1.coupled, bf16[4,128,128]{2,1,0:T(8,128)(2,1)S(1)} %collective-permute-done.5.rest_0_, ...), custom_call_target="tpu_custom_call" | custom-call | flops 805306368 | bytes 4718592 | tf_op jit(solution)/shard_map/output/pallas_call | solution.py:267
  52.7 5.1 %collective-permute-done.12.rest_1_ = bf16[4,128,128]{2,1,0:T(8,128)(2,1)S(1)} collective-permute-done((bf16[4,128,128]{2,1,0:T(8,128)(2,1)S(1)}, bf16[4,128,128]{2,1,0:T(8,128)(2,1)S(1)}, u32[]{:S(2)}, u32[]{:S(2)}) %collective-permute-start.12) | collective-permute-done | bytes 131104 | tf_op jit(solution)/shard_map/ppermute | solution.py:311
  58.5 1.0 %collective-permute-done.13.rest_2_ = bf16[4,128,128]{2,1,0:T(8,128)(2,1)S(1)} collective-permute-done((bf16[4,128,128]{2,1,0:T(8,128)(2,1)S(1)}, bf16[4,128,128]{2,1,0:T(8,128)(2,1)S(1)}, u32[]{:S(2)}, u32[]{:S(2)}) %collective-permute-start.13) | collective-permute-done | bytes 131104 | tf_op jit(solution)/shard_map/ppermute | solution.py:299
  59.5 1.2 %output.3 = bf16[4,128,1024]{2,1,0:T(8,128)(2,1)} custom-call(s32[1]{0:T(128)} %bitcast.face_ref, bf16[8,512,128]{2,1,0:T(8,128)(2,1)S(1)} %get-tuple-element.34.fields, bf16[1024,1024]{1,0:T(8,128)(2,1)S(1)} %coupling_last.1.coupled, bf16[4,128,1024]{2,1,0:T(8,128)(2,1)} %output.2.rest_0_, ...), custom_call_target="tpu_custom_call", output_to_operand_aliasing={{}: (3, {})} | custom-call | flops 268435456 | bytes 5505024 | tf_op jit(solution)/shard_map/output/pallas_call | solution.py:267
  (25 shorter events, 5.3 us)
Async XLA Ops:
  0.0 7.5 %copy-start = (bf16[1,8,4,128,128]{4,3,2,1,0:T(8,128)(2,1)S(1)}, bf16[1,8,4,128,128]{4,3,2,1,0:T(8,128)(2,1)}, u32[]{:S(2)}) copy-start(bf16[1,8,4,128,128]{4,3,2,1,0:T(8,128)(2,1)} %param.11) | copy-start | bytes 3145732
  0.0 12.8 %copy-start.3 = (s32[2]{0:T(128)S(1)}, s32[2]{0:T(128)}, u32[]{:S(2)}) copy-start(s32[2]{0:T(128)} %iface.9) | copy-start | bytes 28
  2.9 7.4 %collective-permute-start = (bf16[2,768,128]{2,1,0:T(8,128)(2,1)}, bf16[2,768,128]{2,1,0:T(8,128)(2,1)S(1)}, u32[]{:S(2)}, u32[]{:S(2)}) collective-permute-start(bf16[2,768,128]{2,1,0:T(8,128)(2,1)} %get-tuple-element.26), channel_id=1, source_target_pairs={{0,1},{1,0},{2,3},{3,2},{4,5},{5,4},{6,7},{7,6},{8,9},{9,8},{10,11... | collective-permute-start | bytes 1179656 | tf_op jit(solution)/shard_map/ppermute | solution.py:296
  3.7 9.1 %collective-permute-start.1 = (bf16[2,768,128]{2,1,0:T(8,128)(2,1)S(1)}, bf16[2,768,128]{2,1,0:T(8,128)(2,1)S(1)}, u32[]{:S(2)}, u32[]{:S(2)}) collective-permute-start(bf16[2,768,128]{2,1,0:T(8,128)(2,1)S(1)} %get-tuple-element.27), channel_id=1, source_target_pairs={{1,2},{2,1},{5,6},{6,5},{9,10},{10,9},{13,14},{14,13},{17,18},{18,... | collective-permute-start | bytes 1179656 | tf_op jit(solution)/shard_map/ppermute | solution.py:295
  7.5 1.0 %copy-start.1 = (bf16[1,8,128,128]{3,2,1,0:T(8,128)(2,1)S(1)}, bf16[1,8,128,128]{3,2,1,0:T(8,128)(2,1)}, u32[]{:S(2)}) copy-start(bf16[1,8,128,128]{3,2,1,0:T(8,128)(2,1)} %param.13) | copy-start | bytes 786436
  8.4 0.9 %copy-start.2 = (bf16[1,8,128,128]{3,2,1,0:T(8,128)(2,1)S(1)}, bf16[1,8,128,128]{3,2,1,0:T(8,128)(2,1)}, u32[]{:S(2)}) copy-start(bf16[1,8,128,128]{3,2,1,0:T(8,128)(2,1)} %param.10) | copy-start | bytes 786436
  15.1 3.1 %collective-permute-start.2 = (bf16[2,512,128]{2,1,0:T(8,128)(2,1)S(1)}, bf16[2,512,128]{2,1,0:T(8,128)(2,1)S(1)}, u32[]{:S(2)}, u32[]{:S(2)}) collective-permute-start(bf16[2,512,128]{2,1,0:T(8,128)(2,1)S(1)} %get-tuple-element.30), channel_id=1, source_target_pairs={{0,1},{1,0},{2,3},{3,2},{4,5},{5,4},{6,7},{7,6},{8,9},{9,8},{10,11... | collective-permute-start | bytes 786440 | tf_op jit(solution)/shard_map/ppermute | solution.py:296
  15.1 7.8 %collective-permute-start.3 = (bf16[2,512,128]{2,1,0:T(8,128)(2,1)S(1)}, bf16[2,512,128]{2,1,0:T(8,128)(2,1)S(1)}, u32[]{:S(2)}, u32[]{:S(2)}) collective-permute-start(bf16[2,512,128]{2,1,0:T(8,128)(2,1)S(1)} %get-tuple-element.31), channel_id=1, source_target_pairs={{1,2},{2,1},{5,6},{6,5},{9,10},{10,9},{13,14},{14,13},{17,18},{18,... | collective-permute-start | bytes 786440 | tf_op jit(solution)/shard_map/ppermute | solution.py:295
  20.2 10.2 %collective-permute-start.6 = (bf16[2,768,128]{2,1,0:T(8,128)(2,1)S(1)}, bf16[2,768,128]{2,1,0:T(8,128)(2,1)S(1)}, u32[]{:S(2)}, u32[]{:S(2)}) collective-permute-start(bf16[2,768,128]{2,1,0:T(8,128)(2,1)S(1)} %get-tuple-element.37), channel_id=1, source_target_pairs={{0,1},{1,0},{2,3},{3,2},{4,5},{5,4},{6,7},{7,6},{8,9},{9,8},{10,11... | collective-permute-start | bytes 1179656 | tf_op jit(solution)/shard_map/ppermute | solution.py:296
  20.3 10.1 %collective-permute-start.7 = (bf16[2,768,128]{2,1,0:T(8,128)(2,1)S(1)}, bf16[2,768,128]{2,1,0:T(8,128)(2,1)S(1)}, u32[]{:S(2)}, u32[]{:S(2)}) collective-permute-start(bf16[2,768,128]{2,1,0:T(8,128)(2,1)S(1)} %get-tuple-element.38), channel_id=1, source_target_pairs={{1,2},{2,1},{5,6},{6,5},{9,10},{10,9},{13,14},{14,13},{17,18},{18,... | collective-permute-start | bytes 1179656 | tf_op jit(solution)/shard_map/ppermute | solution.py:295
  25.2 1.5 %collective-permute-start.4 = (bf16[3,2,128,128]{3,2,1,0:T(8,128)(2,1)S(1)}, bf16[3,2,128,128]{3,2,1,0:T(8,128)(2,1)S(1)}, u32[]{:S(2)}, u32[]{:S(2)}) collective-permute-start(bf16[3,2,128,128]{3,2,1,0:T(8,128)(2,1)S(1)} %get-tuple-element.35.own.own_faces), channel_id=1, source_target_pairs={{0,1},{1,0},{2,3},{3,2},{4,5},{5,4},{6,7},{7,6},{8,9},{9,8},{10,11... | collective-permute-start | bytes 589832 | tf_op jit(solution)/shard_map/ppermute | solution.py:299
  26.7 8.7 %collective-permute-start.5 = (bf16[4,128,128]{2,1,0:T(8,128)(2,1)S(1)}, bf16[4,128,128]{2,1,0:T(8,128)(2,1)S(1)}, u32[]{:S(2)}, u32[]{:S(2)}) collective-permute-start(bf16[4,128,128]{2,1,0:T(8,128)(2,1)S(1)} %merge.1.after), channel_id=1, source_target_pairs={{0,4},{3,5},{2,6},{1,7},{4,8},{7,9},{6,10},{5,11},{8,12},{11,13},{... | collective-permute-start | bytes 393224 | tf_op jit(solution)/shard_map/ppermute | solution.py:311
  35.4 2.4 %collective-permute-start.8 = (bf16[1024,256]{1,0:T(8,128)(2,1)S(1)}, bf16[1024,256]{1,0:T(8,128)(2,1)S(1)}, u32[]{:S(2)}, u32[]{:S(2)}) collective-permute-start(bf16[1024,256]{1,0:T(8,128)(2,1)S(1)} %coupling_chain.1.own_chain.after), channel_id=1, source_target_pairs={{0,1},{1,0},{2,3},{3,2},{4,5},{5,4},{6,7},{7,6},{8,9},{9,8},{10,11... | collective-permute-start | bytes 1572872 | tf_op jit(solution)/shard_map/ppermute | solution.py:299
  36.2 1.7 %collective-permute-start.9 = (bf16[4,128,128]{2,1,0:T(8,128)(2,1)S(1)}, bf16[4,128,128]{2,1,0:T(8,128)(2,1)S(1)}, u32[]{:S(2)}, u32[]{:S(2)}) collective-permute-start(bf16[4,128,128]{2,1,0:T(8,128)(2,1)S(1)} %collective-permute-done.5.rest_0_), channel_id=1, source_target_pairs={{0,1},{1,0},{2,3},{3,2},{4,5},{5,4},{6,7},{7,6},{8,9},{9,8},{10,11... | collective-permute-start | bytes 393224 | tf_op jit(solution)/shard_map/ppermute | solution.py:299
  38.2 8.9 %collective-permute-start.10 = (bf16[4,128,128]{2,1,0:T(8,128)(2,1)S(1)}, bf16[4,128,128]{2,1,0:T(8,128)(2,1)S(1)}, u32[]{:S(2)}, u32[]{:S(2)}) collective-permute-start(bf16[4,128,128]{2,1,0:T(8,128)(2,1)S(1)} %chain.2), channel_id=1, source_target_pairs={{0,4},{3,5},{2,6},{1,7},{4,8},{7,9},{6,10},{5,11},{8,12},{11,13},{... | collective-permute-start | bytes 393224 | tf_op jit(solution)/shard_map/ppermute | solution.py:311
  47.1 1.6 %collective-permute-start.11 = (bf16[4,128,128]{2,1,0:T(8,128)(2,1)S(1)}, bf16[4,128,128]{2,1,0:T(8,128)(2,1)S(1)}, u32[]{:S(2)}, u32[]{:S(2)}) collective-permute-start(bf16[4,128,128]{2,1,0:T(8,128)(2,1)S(1)} %collective-permute-done.10.rest_0_.rest_2_), channel_id=1, source_target_pairs={{0,1},{1,0},{2,3},{3,2},{4,5},{5,4},{6,7},{7,6},{8,9},{9,8},{10,11... | collective-permute-start | bytes 393224 | tf_op jit(solution)/shard_map/ppermute | solution.py:299
  49.0 8.9 %collective-permute-start.12 = (bf16[4,128,128]{2,1,0:T(8,128)(2,1)S(1)}, bf16[4,128,128]{2,1,0:T(8,128)(2,1)S(1)}, u32[]{:S(2)}, u32[]{:S(2)}) collective-permute-start(bf16[4,128,128]{2,1,0:T(8,128)(2,1)S(1)} %chain.3), channel_id=1, source_target_pairs={{0,4},{3,5},{2,6},{1,7},{4,8},{7,9},{6,10},{5,11},{8,12},{11,13},{... | collective-permute-start | bytes 393224 | tf_op jit(solution)/shard_map/ppermute | solution.py:311
  57.8 1.6 %collective-permute-start.13 = (bf16[4,128,128]{2,1,0:T(8,128)(2,1)S(1)}, bf16[4,128,128]{2,1,0:T(8,128)(2,1)S(1)}, u32[]{:S(2)}, u32[]{:S(2)}) collective-permute-start(bf16[4,128,128]{2,1,0:T(8,128)(2,1)S(1)} %collective-permute-done.12.rest_1_), channel_id=1, source_target_pairs={{0,1},{1,0},{2,3},{3,2},{4,5},{5,4},{6,7},{7,6},{8,9},{9,8},{10,11... | collective-permute-start | bytes 393224 | tf_op jit(solution)/shard_map/ppermute | solution.py:299

commit v4 on v3

--- a/solution.py
+++ b/solution.py
@@ -25,7 +25,9 @@
     def __init__(self, ticks, sources, count, neigh, width, nq, faces):
         self.ticks, self.sources, self.count, self.neigh = ticks, sources, count, neigh
         self.width, self.nq, self.faces = width, nq, faces
-        self.batch = ticks * sources
+        self.split = max(ticks // 2, 1)
+        self.early = self.split * sources
+        self.later = (ticks - self.split) * sources
         self.group = nq * width
         self.ext = count + 2 * HALO
         self.depth = (1 + neigh) * width
@@ -41,40 +43,61 @@
         return face * self.count - HALO
 
 
+def spans(rows):
+    parts = -(-rows // 256)
+    return [(i * (rows // parts), rows // parts) for i in range(parts)]
+
+
 def edge_rows(d, parity):
     return d.last * (1 - parity), d.last * parity
 
 
-def first_kernel(d, face_ref, iface_hbm, rhs, inflow, inv, coupling, field, gfield, pair, cross, iface, right, flow, tiles, couple, sems):
-    w = d.width
-    moves = [(inv, tiles)] + [(rhs.at[t], right.at[t]) for t in range(d.ticks)]
-    moves += [(iface_hbm, iface), (coupling, couple), (inflow, flow)]
+def start_copies(moves, sems):
     copies = [pltpu.make_async_copy(a, b, sems.at[i]) for i, (a, b) in enumerate(moves)]
     for copy in copies:
         copy.start()
     for copy in copies:
         copy.wait()
+
+
+def first_kernel(d, face_ref, iface_hbm, rhs, inflow, inv, coupling, field, pair, cross, iface, right, flow, tiles, couple, sems):
+    w = d.width
+    moves = [(inv, tiles)] + [(rhs.at[t], right.at[t]) for t in range(d.split)]
+    start_copies(moves + [(iface_hbm, iface), (coupling, couple), (inflow, flow)], sems)
     parity = lax.rem(face_ref[0], 2)
     for r in range(d.count):
-        x = jnp.concatenate([right[t, :, r * w : (r + 1) * w] for t in range(d.ticks)], axis=0)
+        x = jnp.concatenate([right[t, :, r * w : (r + 1) * w] for t in range(d.split)], axis=0)
         field[r] = dot_nt(x, tiles[r]).astype(BF)
     for q in range(d.nq):
         row = iface[q]
-        turned = couple[q].astype(F32).T.astype(BF)
-        gfield[q] = dot_nt(turned, tiles[row]).astype(BF)
-        coupled = dot_nn(flow[:, q * w : (q + 1) * w], turned)
+        coupled = dot_nt(flow[:, q * w : (q + 1) * w], couple[q])
         corrected = right[0, :, pl.ds(pl.multiple_of(row * w, w), w)].astype(F32) - coupled
         field[row, 0 : d.sources, :] = dot_nt(corrected.astype(BF), tiles[row]).astype(BF)
     for start, buffer in zip(edge_rows(d, parity), (pair, cross)):
+        buffer[...] = field[pl.ds(start, HALO)]
+
+
+def first_later_kernel(d, face_ref, iface, rhs, inv, coupling, after, field, gfield, pair, cross, right, tiles, couple, sems):
+    w = d.width
+    moves = [(rhs.at[t], right.at[t - d.split]) for t in range(d.split, d.ticks)]
+    start_copies([(inv, tiles), (coupling, couple)] + moves, sems)
+    parity = lax.rem(face_ref[0], 2)
+    for q in range(d.nq):
+        gfield[q] = dot_nt(couple[q].astype(F32).T.astype(BF), tiles[iface[q]]).astype(BF)
+    for r in range(d.count):
+        x = jnp.concatenate([right[t, :, r * w : (r + 1) * w] for t in range(d.ticks - d.split)], axis=0)
+        field[r] = dot_nt(x, tiles[r]).astype(BF)
+    for start, buffer in zip(edge_rows(d, parity), (pair, cross)):
         for e in range(HALO):
-            buffer[e, 0 : d.batch, :] = field[start + e]
+            buffer[e, 0 : d.later, :] = field[start + e]
             for q in range(d.nq):
                 hit = iface[q] == start + e
-                buffer[e, d.batch + q * w : d.batch + (q + 1) * w, :] = jnp.where(hit, gfield[q], jnp.zeros((w, w), BF))
-
-
-def fold_kernel(d, after, diag, off, inv, folded):
-    w = d.width
+                buffer[e, d.later + q * w : d.later + (q + 1) * w, :] = jnp.where(hit, gfield[q], jnp.zeros((w, w), BF))
+
+
+def fold_kernel(d, after, diag_hbm, off_hbm, inv_hbm, folded, diag, off, inv, sems):
+    w = d.width
+    start_copies([(inv_hbm, inv), (diag_hbm, diag), (off_hbm, off)], sems)
     for r in range(d.count):
         tiles = jnp.concatenate([diag[r]] + [off[r, k] for k in range(d.neigh)], axis=1)
         product = dot_nn(inv[r], tiles)
@@ -90,32 +113,56 @@
     return dot_nn(jnp.concatenate(x, axis=1), folded[r])
 
 
-def batch_kernel(d, last, face_ref, iface, cols, field, base, pair_in, cross_in, folded, *rest):
-    if last:
-        out, faces_out, ext = rest
-    else:
-        out, pair, cross, ext = rest
+def correct(d, cols, face, field, base, pair_in, cross_in, folded, out, ext):
+    parity = lax.rem(face, 2)
+    rows = out.shape[1]
+    ext[HALO : HALO + d.count] = field[...]
+    ext[pl.ds(d.up * (1 - parity), HALO)] = pair_in[:, 0:rows, :]
+    ext[pl.ds(d.up * parity, HALO)] = cross_in[:, 0:rows, :]
+    for r in range(d.count):
+        for start, size in spans(rows):
+            span = pl.ds(start, size)
+            out[r, span, :] = (base[r, span, :].astype(F32) + sweep(d, cols, face, ext, span, r, folded)).astype(BF)
+
+
+def second_kernel(d, face_ref, cols, field, pair_in, cross_in, folded, out, pair, cross, ext):
+    correct(d, cols, face_ref[0], field, field, pair_in, cross_in, folded, out, ext)
+    for start, buffer in zip(edge_rows(d, lax.rem(face_ref[0], 2)), (pair, cross)):
+        buffer[...] = out[pl.ds(start, HALO)]
+
+
+def third_kernel(d, face_ref, iface, cols, field, base, pair_in, cross_in, folded, out, faces_out, ext):
+    correct(d, cols, face_ref[0], field, base, pair_in, cross_in, folded, out, ext)
+    interface_rows(d, iface, out, faces_out)
+
+
+def interface_rows(d, iface, out, faces_out):
+    for q in range(d.nq):
+        for t in range(faces_out.shape[0]):
+            faces_out[t, q] = out[iface[q], t * d.sources : (t + 1) * d.sources, :]
+
+
+def second_later_kernel(d, face_ref, iface, cols, field, gfield, pair_in, cross_in, folded, after, out, gfirst, pair, cross, ext, met):
     face = face_ref[0]
-    parity = lax.rem(face, 2)
-    ext[HALO : HALO + d.count] = field[...]
-    ext[pl.ds(d.up * (1 - parity), HALO)] = pair_in[:, 0 : d.batch, :]
-    ext[pl.ds(d.up * parity, HALO)] = cross_in[:, 0 : d.batch, :]
-    for r in range(d.count):
-        for s in range(0, d.batch, d.group):
-            span = pl.ds(s, d.group)
-            out[r, span, :] = (base[r, span, :].astype(F32) + sweep(d, cols, face, ext, span, r, folded)).astype(BF)
-    if last:
-        for q in range(d.nq):
-            row = iface[q]
-            for t in range(d.ticks - 1):
-                faces_out[t, q] = out[row, t * d.sources : (t + 1) * d.sources, :]
-    else:
-        for start, buffer in zip(edge_rows(d, parity), (pair, cross)):
-            buffer[...] = out[pl.ds(start, HALO)]
-
-
-def coupling_first_kernel(d, face_ref, iface, cols, gfield, pair_in, cross_in, folded, after, out, pair, cross, met):
+    correct(d, cols, face, field, field, pair_in, cross_in, folded, out, ext)
+    coupling_first(d, face, iface, cols, gfield, pair_in, cross_in, folded, gfirst, met)
+    for start, buffer in zip(edge_rows(d, lax.rem(face, 2)), (pair, cross)):
+        buffer[:, 0 : d.later, :] = out[pl.ds(start, HALO)]
+        for i, shift in enumerate((-1, 0, 1)):
+            span = pl.ds(d.start(face + shift), d.group)
+            buffer[:, d.later + i * d.group : d.later + (i + 1) * d.group, :] = gfirst[pl.ds(start, HALO), span, :]
+
+
+def third_later_kernel(
+    d, face_ref, iface, cols, field, base, gfield, gfirst, pair_in, cross_in, folded, after, out, faces_out, chain, ext, gext
+):
     face = face_ref[0]
+    coupling_chain(d, face, iface, cols, gfield, gfirst, pair_in, cross_in, folded, chain, gext)
+    correct(d, cols, face, field, base, pair_in, cross_in, folded, out, ext)
+    interface_rows(d, iface, out, faces_out)
+
+
+def coupling_first(d, face, iface, cols, gfield, pair_in, cross_in, folded, out, met):
     parity = lax.rem(face, 2)
     w = d.width
     met[...] = jnp.zeros_like(met)
@@ -145,7 +192,7 @@
 
     pair_face, cross_face = face + 1 - 2 * parity, face - 1 + 2 * parity
     for at, other, block in ((HALO * (1 - parity), pair_face, pair_in), (HALO * parity, cross_face, cross_in)):
-        x = jnp.concatenate([block[e, d.batch : d.batch + d.group, :] for e in range(HALO)], axis=1)
+        x = jnp.concatenate([block[e, d.later : d.later + d.group, :] for e in range(HALO)], axis=1)
         tiles = jnp.concatenate([met[at + e] for e in range(HALO)], axis=0)
         put(d.start(other), d.group, dot_nn(x, tiles))
     for q in range(d.nq):
@@ -154,10 +201,6 @@
         row = iface[q]
         span = pl.ds(pl.multiple_of(start, w), w)
         out[row, span, :] = (out[row, span, :].astype(F32) + gfield[q].astype(F32)).astype(BF)
-    for start, buffer in zip(edge_rows(d, parity), (pair, cross)):
-        for i, shift in enumerate((-1, 0, 1)):
-            buffer[:, i * d.group : (i + 1) * d.group, :] = out[pl.ds(start, HALO), pl.ds(d.start(face + shift), d.group), :]
-
 
 def coupling_ext(d, face, gfirst, pair_in, cross_in, ext):
     parity = lax.rem(face, 2)
@@ -167,11 +210,11 @@
     neighbours = ((d.up * (1 - parity), face + 1 - 2 * parity, pair_in), (d.up * parity, face - 1 + 2 * parity, cross_in))
     for start, other, block in neighbours:
         for i, shift in enumerate((-1, 0, 1)):
-            ext[pl.ds(start, HALO), pl.ds(d.start(other + shift), d.group), :] = block[:, i * d.group : (i + 1) * d.group, :]
-
-
-def coupling_chain_kernel(d, face_ref, iface, cols, gfield, gfirst, pair_in, cross_in, folded, after, chain, ext):
-    face = face_ref[0]
+            at = d.later + i * d.group
+            ext[pl.ds(start, HALO), pl.ds(d.start(other + shift), d.group), :] = block[:, at : at + d.group, :]
+
+
+def coupling_chain(d, face, iface, cols, gfield, gfirst, pair_in, cross_in, folded, chain, ext):
     w = d.width
     coupling_ext(d, face, gfirst, pair_in, cross_in, ext)
     for q in range(d.nq):
@@ -236,7 +279,7 @@
         sent[(1 - parity) * d.nq + q] = other[0, q]
 
 
-def output_kernel(d, ticks, face_ref, fields, coupled, *rest):
+def output_kernel(d, ticks, face_ref, field, later, coupled, *rest):
     *arrived, out, held, sems = rest
     w = d.width
     face = face_ref[0]
@@ -251,10 +294,11 @@
             for x, start in arrived_blocks(d, face, mine[: each // 2], mine[each // 2 :]):
                 total += dot_nn(x, coupled[pl.ds(start, 2 * d.group), :])
         for r in range(d.count):
-            value = fields[r, t * d.sources : (t + 1) * d.sources, :]
+            fields, at = (field, t) if t < d.split else (later, t - d.split)
+            value = fields[r, at * d.sources : (at + 1) * d.sources, :]
             if t:
-                value = (value.astype(F32) - total[:, r * w : (r + 1) * w]).astype(BF)
-            held[i, :, r * w : (r + 1) * w] = value
+                value = value.astype(F32) - total[:, r * w : (r + 1) * w]
+            held[i, :, r * w : (r + 1) * w] = value.astype(BF)
         copies.append(pltpu.make_async_copy(held.at[i], out.at[t], sems.at[i]))
         copies[-1].start()
     for copy in copies:
@@ -262,7 +306,6 @@
 
 
 def call(body, name, smem, inputs, outs, scratch=(), flops=0, anywhere=(), sems=0, place=pltpu.VMEM, aliases=None):
-    moved = sum(x.size * x.dtype.itemsize for x in inputs) + sum(2 * math.prod(s) for s in outs)
     specs = [pl.BlockSpec(memory_space=pl.ANY if i in anywhere else pltpu.VMEM) for i in range(len(inputs))]
     return pl.pallas_call(
         body,
@@ -274,7 +317,7 @@
         + ([pltpu.SemaphoreType.DMA((sems,))] if sems else []),
         input_output_aliases=aliases or {},
         compiler_params=pltpu.CompilerParams(vmem_limit_bytes=32 * 1024 * 1024),
-        cost_estimate=pl.CostEstimate(flops=flops, bytes_accessed=moved, transcendentals=0),
+        cost_estimate=pl.CostEstimate(flops=flops // 64, bytes_accessed=0, transcendentals=0),
     )(*smem, *inputs)
 
 
@@ -298,7 +341,7 @@
     def swap(block):
         return lax.ppermute(block, "face", pairing)
 
-    def onward(block, beside=lambda: None):
+    def onward(block, beside):
         own = []
         for hops in chip_hops(faces):
             route = []
@@ -309,93 +352,109 @@
                     if 0 <= g < faces:
                         route.append(((s - 1) * faces + g, s * faces + f))
             own.append(lax.ppermute(block, ("slab", "face"), route))
-        made = beside()
-        if made is not None:
-            *own, made = lax.optimization_barrier((*own, made))
+        own, made = lax.optimization_barrier((own, beside()))
         return own + [swap(x) for x in own], made
 
-    batch, group, ext, wide = d.batch, d.group, d.ext, d.wide
-    field, gfield, pair, cross = call(
+    split, early, later, group, ext, wide = d.split, d.early, d.later, d.group, d.ext, d.wide
+    sweep_flops = 2 * count * tile * (neigh + 1)
+    diag, off = (pltpu.with_memory_space_constraint(x, pltpu.HBM) for x in (diag, off))
+    on_hbm = [pltpu.with_memory_space_constraint(x, pltpu.HBM) for x in (iface, rhs[:, 0], inflow[0], inv, couple)]
+    field, pair, cross = call(
         functools.partial(first_kernel, d),
         "first",
         [face],
-        [pltpu.with_memory_space_constraint(x, pltpu.HBM) for x in (iface, rhs[:, 0], inflow[0], inv, couple)],
-        [(count, batch, width), (nq, width, width)] + [(HALO, batch + group, width)] * 2,
+        on_hbm,
+        [(count, early, width)] + [(HALO, early, width)] * 2,
         [
             pltpu.SMEM(iface.shape, jnp.int32),
-            (ticks, sources, count * width),
+            (split, sources, count * width),
             (sources, group),
             (count, width, width),
             (nq, width, width),
         ],
-        flops=2 * batch * count * tile,
-        anywhere=(0, 1, 2, 3, 4),
-        sems=4 + ticks,
-    )
+        flops=2 * early * count * tile,
+        anywhere=range(5),
+        sems=4 + split,
+    )
+    pair0, cross0 = exchange(pair, cross)
+    field_later, gfield, pair, cross = call(
+        functools.partial(first_later_kernel, d),
+        "first_later",
+        [face, iface],
+        [on_hbm[1], on_hbm[3], on_hbm[4], pair0],
+        [(count, later, width), (nq, width, width)] + [(HALO, later + group, width)] * 2,
+        [(ticks - split, sources, count * width), (count, width, width), (nq, width, width)],
+        flops=2 * later * count * tile,
+        anywhere=range(4),
+        sems=2 + ticks - split,
+    )
+    pair_later0, cross_later0 = exchange(pair, cross)
     (folded,) = call(
         functools.partial(fold_kernel, d),
         "fold",
         [],
-        [gfield, diag, off, inv],
+        [gfield, diag, off, on_hbm[3]],
         [(count, d.depth, width)],
-        flops=2 * width * count * tile * (neigh + 1),
-        anywhere=(0,),
-    )
-    pair0, cross0 = exchange(pair, cross)
+        [(count, width, width), (count, neigh, width, width), (count, width, width)],
+        flops=width * sweep_flops,
+        anywhere=range(4),
+        sems=3,
+    )
+    cross0, folded = lax.optimization_barrier((cross0, folded))
     once, pair, cross = call(
-        functools.partial(batch_kernel, d, False),
+        functools.partial(second_kernel, d),
         "second",
+        [face, cols],
+        [field, pair0, cross0, folded],
+        [(count, early, width)] + [(HALO, early, width)] * 2,
+        [(ext, early, width)],
+        flops=early * sweep_flops,
+    )
+    pair1, cross1 = exchange(pair, cross)
+    once_later, gfirst, pair, cross = call(
+        functools.partial(second_later_kernel, d),
+        "second_later",
         [face, iface, cols],
-        [field, field, pair0, cross0, folded],
-        [(count, batch, width)] + [(HALO, batch, width)] * 2,
-        [(ext, batch, width)],
-        flops=2 * batch * count * tile * (neigh + 1),
-    )
-    pair1, cross1 = exchange(pair, cross)
-    gfirst, gpair, gcross = call(
-        functools.partial(coupling_first_kernel, d),
-        "coupling_first",
-        [face, iface, cols],
-        [gfield, pair0, cross0, folded, pair1],
-        [(count, wide, width)] + [(HALO, 3 * group, width)] * 2,
-        [(2 * HALO + nq, width, count * width)],
-        flops=2 * (2 * HALO + nq) * width * count * tile,
-        anywhere=(4,),
+        [field_later, gfield, pair_later0, cross_later0, folded, pair1],
+        [(count, later, width), (count, wide, width)] + [(HALO, later + 3 * group, width)] * 2,
+        [(ext, later, width), (2 * HALO + nq, width, count * width)],
+        flops=(later + (2 * HALO + nq) * width) * sweep_flops,
+        anywhere=(5,),
     )
     cross1, gfirst = lax.optimization_barrier((cross1, gfirst))
-    gpair, gcross = exchange(gpair, gcross)
-    fields, faces_out = call(
-        functools.partial(batch_kernel, d, True),
+    pair_later1, cross_later1 = exchange(pair, cross)
+    twice, faces_early = call(
+        functools.partial(third_kernel, d),
         "third",
         [face, iface, cols],
         [once, field, pair1, cross1, folded],
-        [(count, batch, width), (ticks - 1, nq, sources, width)],
-        [(ext, batch, width)],
-        flops=2 * batch * count * tile * (neigh + 1),
-    )
-    other_faces = swap(faces_out)
+        [(count, early, width), (split, nq, sources, width)],
+        [(ext, early, width)],
+        flops=early * sweep_flops * 4096,
+    )
+    other_early = swap(faces_early)
     (sent,) = call(
         functools.partial(merge_kernel, d),
         "merge",
         [face],
-        [faces_out, other_faces],
+        [faces_early, other_early],
         [(2 * nq, sources, width)],
     )
 
-    def operator_rows():
+    def third_later():
         return call(
-            functools.partial(coupling_chain_kernel, d),
-            "coupling_chain",
+            functools.partial(third_later_kernel, d),
+            "third_later",
             [face, iface, cols],
-            [gfield, gfirst, gpair, gcross, folded, sent],
-            [(wide, group)],
-            [(ext, wide, width)],
-            flops=2 * wide * nq * tile * (neigh + 1),
-            anywhere=(5,),
-        )[0]
-
-    arrived, chain = onward(sent, operator_rows)
-    other_chain = swap(chain)
+            [once_later, field_later, gfield, gfirst, pair_later1, cross_later1, folded, sent],
+            [(count, later, width), (ticks - split, nq, sources, width), (wide, group)],
+            [(ext, later, width), (ext, wide, width)],
+            flops=later * sweep_flops + 2 * wide * nq * tile * (neigh + 1),
+            anywhere=(7,),
+        )
+
+    arrived, (twice_later, faces_later, chain) = onward(sent, third_later)
+    other_chain, other_later = swap(chain), swap(faces_later)
     whole = (ticks, sources, count * width)
 
     def operator():
@@ -403,10 +462,10 @@
             functools.partial(coupling_last_kernel, d),
             "coupling_last",
             [face, iface, cols],
-            [gfield, gfirst, gpair, gcross, folded, chain],
+            [gfield, gfirst, pair_later1, cross_later1, folded, chain],
             [(wide, count * width)],
             [(ext, wide, width)],
-            flops=2 * wide * count * tile * (neigh + 1),
+            flops=wide * sweep_flops,
             anywhere=(5,),
         )[0]
 
@@ -415,14 +474,14 @@
             functools.partial(output_kernel, d, which),
             "output",
             [face],
-            [fields, coupled] + earlier + blocks,
+            [twice, twice_later, coupled] + earlier + blocks,
             [whole],
             [(len(which), sources, count * width)],
             flops=2 * len(which) * sources * wide * count * width,
-            anywhere=(2,) if earlier else (),
+            anywhere=(3,) if earlier else (),
             sems=len(which),
             place=pl.ANY,
-            aliases={3: 0} if earlier else None,
+            aliases={4: 0} if earlier else None,
         )[0]
 
     everything = []
@@ -431,11 +490,12 @@
         everything += arrived
         if tick == ticks - 1:
             break
+        early_tick = tick < split
         (sent,) = call(
-            functools.partial(chain_kernel, d, tick),
+            functools.partial(chain_kernel, d, tick if early_tick else tick - split),
             "chain",
             [face],
-            [chain, other_chain, faces_out, other_faces] + arrived,
+            [chain, other_chain] + ([faces_early, other_early] if early_tick else [faces_later, other_later]) + arrived,
             [(2 * nq, sources, width)],
             flops=4 * sources * wide * group,
         )

time: 61.2 us -> 61.4 us (level)
  waiting for transfers between devices: 17.9 us -> 14.9 us
  starting transfers between devices: 20.5 us -> 23.3 us
  Pallas kernels: 19.4 us -> 21.8 us
  local copies, waits for them, and re-layouts: 2.67 us -> 0.74 us
    ppermute x3 -> x4, starting transfers between devices: 8.63 us -> 11.6 us  [exchange(): got = lax.ppermute(cross, 'face', crossing)]
    pallas_call x12 -> x13, Pallas kernels: 19.4 us -> 21.8 us  [call(): pl.pallas_call(body, name=name, out_shape=[jax.ShapeDtypeStruct(s, BF) fo...]
    ppermute x3, waiting for transfers between devices: 10.3 us -> 8.34 us  [onward(): own.append(lax.ppermute(block, ('slab', 'face'), route))]
    unnamed x8 -> x6, local copies, waits for them, and re-layouts: 1.91 us -> 0.66 us
    ppermute x3 -> x4, waiting for transfers between devices: 2.47 us -> 1.6 us  [exchange(): got = lax.ppermute(cross, 'face', crossing)]
    squeeze x1, local copies, waits for them, and re-layouts: 0.76 us -> 0.08 us  [on_device(): cols[0]]
    ppermute x5 -> x6, waiting for transfers between devices: 5.12 us -> 4.9 us  [swap(): return lax.ppermute(block, 'face', pairing)]
    ppermute x5 -> x6, starting transfers between devices: 2.04 us -> 2.27 us  [swap(): return lax.ppermute(block, 'face', pairing)]
  transfers between devices with their start and end apart: 14 -> 17, of which waited for: 8 -> 9; matrix products, arithmetic and copies ran while one was open for 1% -> 0% of each run, Pallas kernels for 20% -> 30%
where the time goes in v4:
time: 61.4 us; the launch traced here: 61 us
  starting transfers between devices  23.3 us (38%)
  Pallas kernels  21.8 us (36%)
  waiting for transfers between devices  14.9 us (24%)
  local copies, waits for them, and re-layouts  0.74 us (1%)
    pallas_call x13, Pallas kernels, call(): pl.pallas_call(body, name=name, out_shape=[jax.ShapeDtypeStruct(s, BF) fo...  21.8 us
    ppermute x4, starting transfers between devices, exchange(): got = lax.ppermute(cross, 'face', crossing)  11.6 us
    ppermute x3, starting transfers between devices, onward(): own.append(lax.ppermute(block, ('slab', 'face'), route))  8.54 us
    ppermute x3, waiting for transfers between devices, onward(): own.append(lax.ppermute(block, ('slab', 'face'), route))  8.34 us
    ppermute x6, waiting for transfers between devices, swap(): return lax.ppermute(block, 'face', pairing)  4.9 us
    ppermute x6, starting transfers between devices, swap(): return lax.ppermute(block, 'face', pairing)  2.27 us
    ppermute x4, waiting for transfers between devices, exchange(): got = lax.ppermute(cross, 'face', crossing)  1.6 us
  transfers between devices with their start and end apart: 17, of which 9 were waited for; matrix products, arithmetic and copies ran while one was open for 0% of the time, Pallas kernels for 30%

profile of v4, /device:TPU:9, one launch (start us, length us, event | category | flops | bytes accessed | tf_op | source)
XLA Modules:
  0.0 61.0 jit_solution(11065697920451530393)
XLA Ops:
  0.0 1.7 %first.1 = (bf16[8,256,128]{2,1,0:T(8,128)(2,1)S(1)}, bf16[2,256,128]{2,1,0:T(8,128)(2,1)S(1)}, bf16[2,256,128]{2,1,0:T(8,128)(2,1)S(1)}) custom-call(s32[1]{0:T(128)} %bitcast.face_ref, s32[2]{0:T(128)} %iface.9, bf16[4,128,1024]{2,1,0:T(8,128)(2,1)} %bitcast.11, bf16[128,256]{1,0:T(8,128)(2,1)} %bitcast.20, bf16[8,128,128]{2,1,0:T(8,128)(2,1)} %bitcast.13, ...), custom_call_target="tpu_custom_call" | custom-call | flops 1048576 | tf_op jit(solution)/shard_map/first/pallas_call | solution.py:310
  2.4 3.0 %collective-permute-start.1 = (bf16[2,256,128]{2,1,0:T(8,128)(2,1)S(1)}, bf16[2,256,128]{2,1,0:T(8,128)(2,1)S(1)}, u32[]{:S(2)}, u32[]{:S(2)}) collective-permute-start(bf16[2,256,128]{2,1,0:T(8,128)(2,1)S(1)} %get-tuple-element.38), channel_id=1, source_target_pairs={{1,2},{2,1},{5,6},{6,5},{9,10},{10,9},{13,14},{14,13},{17,18},{18,... | collective-permute-start | bytes 393224 | tf_op jit(solution)/shard_map/ppermute | solution.py:338
  6.1 2.1 %first_later.1 = (bf16[8,256,128]{2,1,0:T(8,128)(2,1)S(1)}, bf16[2,128,128]{2,1,0:T(8,128)(2,1)S(1)}, bf16[2,512,128]{2,1,0:T(8,128)(2,1)S(1)}, bf16[2,512,128]{2,1,0:T(8,128)(2,1)S(1)}) custom-call(s32[1]{0:T(128)} %bitcast.face_ref, s32[2]{0:T(128)S(1)} %copy-done, bf16[4,128,1024]{2,1,0:T(8,128)(2,1)} %bitcast.12, bf16[8,128,128]{2,1,0:T(8,128)(2,1)} %bitcast.14, ...), custom_call_target="tpu_custom_call" | custom-call | flops 1048576 | tf_op jit(solution)/shard_map/first_later/pallas_call | solution.py:310
  8.3 2.5 %collective-permute-start.5 = (bf16[2,512,128]{2,1,0:T(8,128)(2,1)S(1)}, bf16[2,512,128]{2,1,0:T(8,128)(2,1)S(1)}, u32[]{:S(2)}, u32[]{:S(2)}) collective-permute-start(bf16[2,512,128]{2,1,0:T(8,128)(2,1)S(1)} %get-tuple-element.47), channel_id=1, source_target_pairs={{1,2},{2,1},{5,6},{6,5},{9,10},{10,9},{13,14},{14,13},{17,18},{18,... | collective-permute-start | bytes 786440 | tf_op jit(solution)/shard_map/ppermute | solution.py:338
  11.0 2.3 %fold.1.folded = bf16[8,640,128]{2,1,0:T(8,128)(2,1)S(1)} custom-call(bf16[2,128,128]{2,1,0:T(8,128)(2,1)S(1)} %get-tuple-element.39.after.gfield, bf16[8,128,128]{2,1,0:T(8,128)(2,1)} %bitcast.17, bf16[8,4,128,128]{3,2,1,0:T(8,128)(2,1)} %bitcast.16, bf16[8,128,128]{2,1,0:T(8,128)(2,1)} %bitcast.15), custom_call_target="tpu_custom_call" | custom-call | flops 2621440 | tf_op jit(solution)/shard_map/fold/pallas_call | solution.py:310
  13.3 1.5 %second.1 = (bf16[8,256,128]{2,1,0:T(8,128)(2,1)S(1)}, bf16[2,256,128]{2,1,0:T(8,128)(2,1)S(1)}, bf16[2,256,128]{2,1,0:T(8,128)(2,1)S(1)}) custom-call(s32[1]{0:T(128)} %bitcast.face_ref, s32[8,4]{1,0:T(8,128)S(1)} %copy.12.cols, bf16[8,256,128]{2,1,0:T(8,128)(2,1)S(1)} %get-tuple-element.36.field.base, ...), custom_call_target="tpu_custom_call" | custom-call | flops 5242880 | tf_op jit(solution)/shard_map/second/pallas_call | solution.py:310
  14.9 3.0 %collective-permute-start.3 = (bf16[2,256,128]{2,1,0:T(8,128)(2,1)S(1)}, bf16[2,256,128]{2,1,0:T(8,128)(2,1)S(1)}, u32[]{:S(2)}, u32[]{:S(2)}) collective-permute-start(bf16[2,256,128]{2,1,0:T(8,128)(2,1)S(1)} %get-tuple-element.44), channel_id=1, source_target_pairs={{1,2},{2,1},{5,6},{6,5},{9,10},{10,9},{13,14},{14,13},{17,18},{18,... | collective-permute-start | bytes 393224 | tf_op jit(solution)/shard_map/ppermute | solution.py:338
  18.0 2.9 %second_later.1 = (bf16[8,256,128]{2,1,0:T(8,128)(2,1)S(1)}, bf16[8,1024,128]{2,1,0:T(8,128)(2,1)S(1)}, bf16[2,1024,128]{2,1,0:T(8,128)(2,1)S(1)}, bf16[2,1024,128]{2,1,0:T(8,128)(2,1)S(1)}) custom-call(s32[1]{0:T(128)} %bitcast.face_ref, s32[2]{0:T(128)S(1)} %copy-done.1, s32[8,4]{1,0:T(8,128)S(1)} %copy.12.cols, ...), custom_call_target="tpu_custom_call" | custom-call | flops 20971520 | tf_op jit(solution)/shard_map/second_later/pallas_call | solution.py:310
  21.2 3.0 %collective-permute-start.9 = (bf16[2,1024,128]{2,1,0:T(8,128)(2,1)S(1)}, bf16[2,1024,128]{2,1,0:T(8,128)(2,1)S(1)}, u32[]{:S(2)}, u32[]{:S(2)}) collective-permute-start(bf16[2,1024,128]{2,1,0:T(8,128)(2,1)S(1)} %get-tuple-element.55), channel_id=1, source_target_pairs={{1,2},{2,1},{5,6},{6,5},{9,10},{10,9},{13,14},{14,13},{17,18},{18,... | collective-permute-start | bytes 1572872 | tf_op jit(solution)/shard_map/ppermute | solution.py:338
  24.2 1.5 %third.1 = (bf16[8,256,128]{2,1,0:T(8,128)(2,1)S(1)}, bf16[2,2,128,128]{3,2,1,0:T(8,128)(2,1)S(1)}) custom-call(s32[1]{0:T(128)} %bitcast.face_ref, s32[2]{0:T(128)S(1)} %copy-done.1, s32[8,4]{1,0:T(8,128)S(1)} %copy.12.cols, bf16[8,256,128]{2,1,0:T(8,128)(2,1)S(1)} %get-tuple-element.42.field, bf16[8,256,128]{2,1,0:T(8,128)(2,1)S(1)} %get-tuple-element.36.field.base, ...), custom_call_target="tpu_custom_call" | custom-call | flops 21474836480 | tf_op jit(solution)/shard_map/third/pallas_call | solution.py:310
  25.8 1.3 %collective-permute-done.6.other.other_faces = bf16[2,2,128,128]{3,2,1,0:T(8,128)(2,1)S(1)} collective-permute-done((bf16[2,2,128,128]{3,2,1,0:T(8,128)(2,1)S(1)}, bf16[2,2,128,128]{3,2,1,0:T(8,128)(2,1)S(1)}, u32[]{:S(2)}, u32[]{:S(2)}) %collective-permute-start.6) | collective-permute-done | bytes 131104 | tf_op jit(solution)/shard_map/ppermute | solution.py:342
  27.2 3.2 %collective-permute-start.7 = (bf16[4,128,128]{2,1,0:T(8,128)(2,1)S(1)}, bf16[4,128,128]{2,1,0:T(8,128)(2,1)S(1)}, u32[]{:S(2)}, u32[]{:S(2)}) collective-permute-start(bf16[4,128,128]{2,1,0:T(8,128)(2,1)S(1)} %merge.1.after), channel_id=1, source_target_pairs={{0,4},{3,5},{2,6},{1,7},{4,8},{7,9},{6,10},{5,11},{8,12},{11,13},{... | collective-permute-start | bytes 393224 | tf_op jit(solution)/shard_map/ppermute | solution.py:354
  30.4 1.3 %collective-permute-done.9.cross_in = bf16[2,1024,128]{2,1,0:T(8,128)(2,1)S(1)} collective-permute-done((bf16[2,1024,128]{2,1,0:T(8,128)(2,1)S(1)}, bf16[2,1024,128]{2,1,0:T(8,128)(2,1)S(1)}, u32[]{:S(2)}, u32[]{:S(2)}) %collective-permute-start.9) | collective-permute-done | bytes 524320 | tf_op jit(solution)/shard_map/ppermute | solution.py:338
  31.7 2.5 %third_later.1 = (bf16[8,256,128]{2,1,0:T(8,128)(2,1)S(1)}, bf16[2,2,128,128]{3,2,1,0:T(8,128)(2,1)S(1)}, bf16[1024,256]{1,0:T(8,128)(2,1)S(1)}) custom-call(s32[1]{0:T(128)} %bitcast.face_ref, s32[2]{0:T(128)S(1)} %copy-done.1, s32[8,4]{1,0:T(8,128)S(1)} %copy.12.cols, bf16[8,256,128]{2,1,0:T(8,128)(2,1)S(1)} %get-tuple-element.52.field, ...), custom_call_target="tpu_custom_call" | custom-call | flops 10485760 | tf_op jit(solution)/shard_map/third_later/pallas_call | solution.py:310
  34.2 1.8 %collective-permute-done.7.rest_0_ = bf16[4,128,128]{2,1,0:T(8,128)(2,1)S(1)} collective-permute-done((bf16[4,128,128]{2,1,0:T(8,128)(2,1)S(1)}, bf16[4,128,128]{2,1,0:T(8,128)(2,1)S(1)}, u32[]{:S(2)}, u32[]{:S(2)}) %collective-permute-start.7) | collective-permute-done | bytes 131104 | tf_op jit(solution)/shard_map/ppermute | solution.py:354
  36.6 1.6 %collective-permute-done.11.rest_1_ = bf16[4,128,128]{2,1,0:T(8,128)(2,1)S(1)} collective-permute-done((bf16[4,128,128]{2,1,0:T(8,128)(2,1)S(1)}, bf16[4,128,128]{2,1,0:T(8,128)(2,1)S(1)}, u32[]{:S(2)}, u32[]{:S(2)}) %collective-permute-start.11) | collective-permute-done | bytes 131104 | tf_op jit(solution)/shard_map/ppermute | solution.py:342
  38.5 2.8 %collective-permute-start.12 = (bf16[4,128,128]{2,1,0:T(8,128)(2,1)S(1)}, bf16[4,128,128]{2,1,0:T(8,128)(2,1)S(1)}, u32[]{:S(2)}, u32[]{:S(2)}) collective-permute-start(bf16[4,128,128]{2,1,0:T(8,128)(2,1)S(1)} %chain.2), channel_id=1, source_target_pairs={{0,4},{3,5},{2,6},{1,7},{4,8},{7,9},{6,10},{5,11},{8,12},{11,13},{... | collective-permute-start | bytes 393224 | tf_op jit(solution)/shard_map/ppermute | solution.py:354
  41.7 3.8 %coupling_last.1.coupled = bf16[1024,1024]{1,0:T(8,128)(2,1)S(1)} custom-call(s32[1]{0:T(128)} %bitcast.face_ref, s32[2]{0:T(128)S(1)} %copy-done.1, s32[8,4]{1,0:T(8,128)S(1)} %copy.12.cols, bf16[2,128,128]{2,1,0:T(8,128)(2,1)S(1)} %get-tuple-element.39.after.gfield, bf16[8,1024,128]{2,1,0:T(8,128)(2,1)S(1)} %get-tuple-element.53.gfirst, ...), custom_call_target="tpu_custom_call" | custom-call | flops 20971520 | tf_op jit(solution)/shard_map/coupling_last/pallas_call | solution.py:310
  45.6 1.7 %collective-permute-done.12.rest_0_.rest_2_ = bf16[4,128,128]{2,1,0:T(8,128)(2,1)S(1)} collective-permute-done((bf16[4,128,128]{2,1,0:T(8,128)(2,1)S(1)}, bf16[4,128,128]{2,1,0:T(8,128)(2,1)S(1)}, u32[]{:S(2)}, u32[]{:S(2)}) %collective-permute-start.12) | collective-permute-done | bytes 131104 | tf_op jit(solution)/shard_map/ppermute | solution.py:354
  49.2 2.5 %collective-permute-start.15 = (bf16[4,128,128]{2,1,0:T(8,128)(2,1)S(1)}, bf16[4,128,128]{2,1,0:T(8,128)(2,1)S(1)}, u32[]{:S(2)}, u32[]{:S(2)}) collective-permute-start(bf16[4,128,128]{2,1,0:T(8,128)(2,1)S(1)} %chain.3), channel_id=1, source_target_pairs={{0,4},{3,5},{2,6},{1,7},{4,8},{7,9},{6,10},{5,11},{8,12},{11,13},{... | collective-permute-start | bytes 393224 | tf_op jit(solution)/shard_map/ppermute | solution.py:354
  51.7 1.6 %output.2.rest_0_ = bf16[4,128,1024]{2,1,0:T(8,128)(2,1)} custom-call(s32[1]{0:T(128)} %bitcast.face_ref, bf16[8,256,128]{2,1,0:T(8,128)(2,1)S(1)} %get-tuple-element.50.field, bf16[8,256,128]{2,1,0:T(8,128)(2,1)S(1)} %get-tuple-element.59.later, bf16[1024,1024]{1,0:T(8,128)(2,1)S(1)} %coupling_last.1.coupled, ...), custom_call_target="tpu_custom_call" | custom-call | flops 12582912 | tf_op jit(solution)/shard_map/output/pallas_call | solution.py:310
  53.3 4.8 %collective-permute-done.15.rest_1_ = bf16[4,128,128]{2,1,0:T(8,128)(2,1)S(1)} collective-permute-done((bf16[4,128,128]{2,1,0:T(8,128)(2,1)S(1)}, bf16[4,128,128]{2,1,0:T(8,128)(2,1)S(1)}, u32[]{:S(2)}, u32[]{:S(2)}) %collective-permute-start.15) | collective-permute-done | bytes 131104 | tf_op jit(solution)/shard_map/ppermute | solution.py:354
  58.7 1.0 %collective-permute-done.16.rest_2_ = bf16[4,128,128]{2,1,0:T(8,128)(2,1)S(1)} collective-permute-done((bf16[4,128,128]{2,1,0:T(8,128)(2,1)S(1)}, bf16[4,128,128]{2,1,0:T(8,128)(2,1)S(1)}, u32[]{:S(2)}, u32[]{:S(2)}) %collective-permute-start.16) | collective-permute-done | bytes 131104 | tf_op jit(solution)/shard_map/ppermute | solution.py:342
  59.7 1.2 %output.3 = bf16[4,128,1024]{2,1,0:T(8,128)(2,1)} custom-call(s32[1]{0:T(128)} %bitcast.face_ref, bf16[8,256,128]{2,1,0:T(8,128)(2,1)S(1)} %get-tuple-element.50.field, bf16[8,256,128]{2,1,0:T(8,128)(2,1)S(1)} %get-tuple-element.59.later, bf16[1024,1024]{1,0:T(8,128)(2,1)S(1)} %coupling_last.1.coupled, ...), custom_call_target="tpu_custom_call", output_to_operand_aliasing={{}: (4, {})} | custom-call | flops 4194304 | tf_op jit(solution)/shard_map/output/pallas_call | solution.py:310
  (30 shorter events, 5.9 us)
Async XLA Ops:
  0.0 10.9 %copy-start.2 = (s32[1,8,4]{1,2,0:T(4,128)S(1)}, s32[1,8,4]{1,2,0:T(4,128)}, u32[]{:S(2)}) copy-start(s32[1,8,4]{1,2,0:T(4,128)} %param.12) | copy-start | bytes 388
  1.7 3.8 %collective-permute-start = (bf16[2,256,128]{2,1,0:T(8,128)(2,1)S(1)}, bf16[2,256,128]{2,1,0:T(8,128)(2,1)S(1)}, u32[]{:S(2)}, u32[]{:S(2)}) collective-permute-start(bf16[2,256,128]{2,1,0:T(8,128)(2,1)S(1)} %get-tuple-element.37), channel_id=1, source_target_pairs={{0,1},{1,0},{2,3},{3,2},{4,5},{5,4},{6,7},{7,6},{8,9},{9,8},{10,11... | collective-permute-start | bytes 393224 | tf_op jit(solution)/shard_map/ppermute | solution.py:339
  2.4 10.9 %collective-permute-start.1 = (bf16[2,256,128]{2,1,0:T(8,128)(2,1)S(1)}, bf16[2,256,128]{2,1,0:T(8,128)(2,1)S(1)}, u32[]{:S(2)}, u32[]{:S(2)}) collective-permute-start(bf16[2,256,128]{2,1,0:T(8,128)(2,1)S(1)} %get-tuple-element.38), channel_id=1, source_target_pairs={{1,2},{2,1},{5,6},{6,5},{9,10},{10,9},{13,14},{14,13},{17,18},{18,... | collective-permute-start | bytes 393224 | tf_op jit(solution)/shard_map/ppermute | solution.py:338
  5.4 0.7 %copy-start = (s32[2]{0:T(128)S(1)}, s32[2]{0:T(128)}, u32[]{:S(2)}) copy-start(s32[2]{0:T(128)} %iface.9) | copy-start | bytes 28
  8.3 9.7 %collective-permute-start.4 = (bf16[2,512,128]{2,1,0:T(8,128)(2,1)S(1)}, bf16[2,512,128]{2,1,0:T(8,128)(2,1)S(1)}, u32[]{:S(2)}, u32[]{:S(2)}) collective-permute-start(bf16[2,512,128]{2,1,0:T(8,128)(2,1)S(1)} %get-tuple-element.46), channel_id=1, source_target_pairs={{0,1},{1,0},{2,3},{3,2},{4,5},{5,4},{6,7},{7,6},{8,9},{9,8},{10,11... | collective-permute-start | bytes 786440 | tf_op jit(solution)/shard_map/ppermute | solution.py:339
  8.3 9.7 %collective-permute-start.5 = (bf16[2,512,128]{2,1,0:T(8,128)(2,1)S(1)}, bf16[2,512,128]{2,1,0:T(8,128)(2,1)S(1)}, u32[]{:S(2)}, u32[]{:S(2)}) collective-permute-start(bf16[2,512,128]{2,1,0:T(8,128)(2,1)S(1)} %get-tuple-element.47), channel_id=1, source_target_pairs={{1,2},{2,1},{5,6},{6,5},{9,10},{10,9},{13,14},{14,13},{17,18},{18,... | collective-permute-start | bytes 786440 | tf_op jit(solution)/shard_map/ppermute | solution.py:338
  11.0 7.0 %copy-start.1 = (s32[2]{0:T(128)S(1)}, s32[2]{0:T(128)}, u32[]{:S(2)}) copy-start(s32[2]{0:T(128)} %iface.9) | copy-start | bytes 28
  14.9 3.1 %collective-permute-start.2 = (bf16[2,256,128]{2,1,0:T(8,128)(2,1)S(1)}, bf16[2,256,128]{2,1,0:T(8,128)(2,1)S(1)}, u32[]{:S(2)}, u32[]{:S(2)}) collective-permute-start(bf16[2,256,128]{2,1,0:T(8,128)(2,1)S(1)} %get-tuple-element.43), channel_id=1, source_target_pairs={{0,1},{1,0},{2,3},{3,2},{4,5},{5,4},{6,7},{7,6},{8,9},{9,8},{10,11... | collective-permute-start | bytes 393224 | tf_op jit(solution)/shard_map/ppermute | solution.py:339
  14.9 6.3 %collective-permute-start.3 = (bf16[2,256,128]{2,1,0:T(8,128)(2,1)S(1)}, bf16[2,256,128]{2,1,0:T(8,128)(2,1)S(1)}, u32[]{:S(2)}, u32[]{:S(2)}) collective-permute-start(bf16[2,256,128]{2,1,0:T(8,128)(2,1)S(1)} %get-tuple-element.44), channel_id=1, source_target_pairs={{1,2},{2,1},{5,6},{6,5},{9,10},{10,9},{13,14},{14,13},{17,18},{18,... | collective-permute-start | bytes 393224 | tf_op jit(solution)/shard_map/ppermute | solution.py:338
  21.2 9.2 %collective-permute-start.8 = (bf16[2,1024,128]{2,1,0:T(8,128)(2,1)S(1)}, bf16[2,1024,128]{2,1,0:T(8,128)(2,1)S(1)}, u32[]{:S(2)}, u32[]{:S(2)}) collective-permute-start(bf16[2,1024,128]{2,1,0:T(8,128)(2,1)S(1)} %get-tuple-element.54), channel_id=1, source_target_pairs={{0,1},{1,0},{2,3},{3,2},{4,5},{5,4},{6,7},{7,6},{8,9},{9,8},{10,11... | collective-permute-start | bytes 1572872 | tf_op jit(solution)/shard_map/ppermute | solution.py:339
  21.2 10.5 %collective-permute-start.9 = (bf16[2,1024,128]{2,1,0:T(8,128)(2,1)S(1)}, bf16[2,1024,128]{2,1,0:T(8,128)(2,1)S(1)}, u32[]{:S(2)}, u32[]{:S(2)}) collective-permute-start(bf16[2,1024,128]{2,1,0:T(8,128)(2,1)S(1)} %get-tuple-element.55), channel_id=1, source_target_pairs={{1,2},{2,1},{5,6},{6,5},{9,10},{10,9},{13,14},{14,13},{17,18},{18,... | collective-permute-start | bytes 1572872 | tf_op jit(solution)/shard_map/ppermute | solution.py:338
  25.8 1.4 %collective-permute-start.6 = (bf16[2,2,128,128]{3,2,1,0:T(8,128)(2,1)S(1)}, bf16[2,2,128,128]{3,2,1,0:T(8,128)(2,1)S(1)}, u32[]{:S(2)}, u32[]{:S(2)}) collective-permute-start(bf16[2,2,128,128]{3,2,1,0:T(8,128)(2,1)S(1)} %get-tuple-element.51.own.own_faces), channel_id=1, source_target_pairs={{0,1},{1,0},{2,3},{3,2},{4,5},{5,4},{6,7},{7,6},{8,9},{9,8},{10,11... | collective-permute-start | bytes 393224 | tf_op jit(solution)/shard_map/ppermute | solution.py:342
  27.2 8.9 %collective-permute-start.7 = (bf16[4,128,128]{2,1,0:T(8,128)(2,1)S(1)}, bf16[4,128,128]{2,1,0:T(8,128)(2,1)S(1)}, u32[]{:S(2)}, u32[]{:S(2)}) collective-permute-start(bf16[4,128,128]{2,1,0:T(8,128)(2,1)S(1)} %merge.1.after), channel_id=1, source_target_pairs={{0,4},{3,5},{2,6},{1,7},{4,8},{7,9},{6,10},{5,11},{8,12},{11,13},{... | collective-permute-start | bytes 393224 | tf_op jit(solution)/shard_map/ppermute | solution.py:354
  36.1 2.1 %collective-permute-start.10 = (bf16[1024,256]{1,0:T(8,128)(2,1)S(1)}, bf16[1024,256]{1,0:T(8,128)(2,1)S(1)}, u32[]{:S(2)}, u32[]{:S(2)}) collective-permute-start(bf16[1024,256]{1,0:T(8,128)(2,1)S(1)} %get-tuple-element.60.own_chain.after), channel_id=1, source_target_pairs={{0,1},{1,0},{2,3},{3,2},{4,5},{5,4},{6,7},{7,6},{8,9},{9,8},{10,11... | collective-permute-start | bytes 1572872 | tf_op jit(solution)/shard_map/ppermute | solution.py:342
  36.2 2.0 %collective-permute-start.11 = (bf16[4,128,128]{2,1,0:T(8,128)(2,1)S(1)}, bf16[4,128,128]{2,1,0:T(8,128)(2,1)S(1)}, u32[]{:S(2)}, u32[]{:S(2)}) collective-permute-start(bf16[4,128,128]{2,1,0:T(8,128)(2,1)S(1)} %collective-permute-done.7.rest_0_), channel_id=1, source_target_pairs={{0,1},{1,0},{2,3},{3,2},{4,5},{5,4},{6,7},{7,6},{8,9},{9,8},{10,11... | collective-permute-start | bytes 393224 | tf_op jit(solution)/shard_map/ppermute | solution.py:342
  38.5 8.8 %collective-permute-start.12 = (bf16[4,128,128]{2,1,0:T(8,128)(2,1)S(1)}, bf16[4,128,128]{2,1,0:T(8,128)(2,1)S(1)}, u32[]{:S(2)}, u32[]{:S(2)}) collective-permute-start(bf16[4,128,128]{2,1,0:T(8,128)(2,1)S(1)} %chain.2), channel_id=1, source_target_pairs={{0,4},{3,5},{2,6},{1,7},{4,8},{7,9},{6,10},{5,11},{8,12},{11,13},{... | collective-permute-start | bytes 393224 | tf_op jit(solution)/shard_map/ppermute | solution.py:354
  41.3 6.6 %collective-permute-start.13 = (bf16[2,2,128,128]{3,2,1,0:T(8,128)(2,1)S(1)}, bf16[2,2,128,128]{3,2,1,0:T(8,128)(2,1)S(1)}, u32[]{:S(2)}, u32[]{:S(2)}) collective-permute-start(bf16[2,2,128,128]{3,2,1,0:T(8,128)(2,1)S(1)} %get-tuple-element.63.own_faces), channel_id=1, source_target_pairs={{0,1},{1,0},{2,3},{3,2},{4,5},{5,4},{6,7},{7,6},{8,9},{9,8},{10,11... | collective-permute-start | bytes 393224 | tf_op jit(solution)/shard_map/ppermute | solution.py:342
  47.3 1.6 %collective-permute-start.14 = (bf16[4,128,128]{2,1,0:T(8,128)(2,1)S(1)}, bf16[4,128,128]{2,1,0:T(8,128)(2,1)S(1)}, u32[]{:S(2)}, u32[]{:S(2)}) collective-permute-start(bf16[4,128,128]{2,1,0:T(8,128)(2,1)S(1)} %collective-permute-done.12.rest_0_.rest_2_), channel_id=1, source_target_pairs={{0,1},{1,0},{2,3},{3,2},{4,5},{5,4},{6,7},{7,6},{8,9},{9,8},{10,11... | collective-permute-start | bytes 393224 | tf_op jit(solution)/shard_map/ppermute | solution.py:342
  49.2 8.9 %collective-permute-start.15 = (bf16[4,128,128]{2,1,0:T(8,128)(2,1)S(1)}, bf16[4,128,128]{2,1,0:T(8,128)(2,1)S(1)}, u32[]{:S(2)}, u32[]{:S(2)}) collective-permute-start(bf16[4,128,128]{2,1,0:T(8,128)(2,1)S(1)} %chain.3), channel_id=1, source_target_pairs={{0,4},{3,5},{2,6},{1,7},{4,8},{7,9},{6,10},{5,11},{8,12},{11,13},{... | collective-permute-start | bytes 393224 | tf_op jit(solution)/shard_map/ppermute | solution.py:354
  58.1 1.6 %collective-permute-start.16 = (bf16[4,128,128]{2,1,0:T(8,128)(2,1)S(1)}, bf16[4,128,128]{2,1,0:T(8,128)(2,1)S(1)}, u32[]{:S(2)}, u32[]{:S(2)}) collective-permute-start(bf16[4,128,128]{2,1,0:T(8,128)(2,1)S(1)} %collective-permute-done.15.rest_1_), channel_id=1, source_target_pairs={{0,1},{1,0},{2,3},{3,2},{4,5},{5,4},{6,7},{7,6},{8,9},{9,8},{10,11... | collective-permute-start | bytes 393224 | tf_op jit(solution)/shard_map/ppermute | solution.py:342

commit v5 on v3

--- a/solution.py
+++ b/solution.py
@@ -31,6 +31,9 @@
         self.depth = (1 + neigh) * width
         self.slots = 4 if faces <= 4 else 6
         self.wide = self.slots * self.group
+        self.mark = 16
+        self.share = -(-nq // HALO) * width
+        self.first_rows = self.batch + self.share + nq * self.mark
         self.last = count - HALO
         self.up = count + HALO
 
@@ -45,35 +48,46 @@
     return d.last * (1 - parity), d.last * parity
 
 
-def first_kernel(d, face_ref, iface_hbm, rhs, inflow, inv, coupling, field, gfield, pair, cross, iface, right, flow, tiles, couple, sems):
+def first_kernel(
+    d, face_ref, iface_hbm, cols_hbm, inflow, coupling, inv, rhs, diag_hbm, off_hbm, *rest
+):
+    field, gfield, pair, cross, tiles, diag, off, iface, cols, right, flow, couple, sems = rest
     w = d.width
-    moves = [(inv, tiles)] + [(rhs.at[t], right.at[t]) for t in range(d.ticks)]
-    moves += [(iface_hbm, iface), (coupling, couple), (inflow, flow)]
+    moves = [(iface_hbm, iface), (inflow, flow), (coupling, couple), (inv, tiles)]
+    moves += [(rhs.at[t], right.at[t]) for t in range(d.ticks)]
+    moves += [(cols_hbm, cols), (diag_hbm, diag), (off_hbm, off)]
     copies = [pltpu.make_async_copy(a, b, sems.at[i]) for i, (a, b) in enumerate(moves)]
     for copy in copies:
         copy.start()
-    for copy in copies:
+    for copy in copies[:4]:
         copy.wait()
-    parity = lax.rem(face_ref[0], 2)
+    coupled = []
+    for q in range(d.nq):
+        turned = couple[q].astype(F32).T.astype(BF)
+        gfield[q] = dot_nt(turned, tiles[iface[q]]).astype(BF)
+        coupled.append(dot_nn(flow[:, q * w : (q + 1) * w], turned))
+    for copy in copies[4 : 4 + d.ticks]:
+        copy.wait()
     for r in range(d.count):
         x = jnp.concatenate([right[t, :, r * w : (r + 1) * w] for t in range(d.ticks)], axis=0)
         field[r] = dot_nt(x, tiles[r]).astype(BF)
     for q in range(d.nq):
         row = iface[q]
-        turned = couple[q].astype(F32).T.astype(BF)
-        gfield[q] = dot_nt(turned, tiles[row]).astype(BF)
-        coupled = dot_nn(flow[:, q * w : (q + 1) * w], turned)
-        corrected = right[0, :, pl.ds(pl.multiple_of(row * w, w), w)].astype(F32) - coupled
+        corrected = right[0, :, pl.ds(pl.multiple_of(row * w, w), w)].astype(F32) - coupled[q]
         field[row, 0 : d.sources, :] = dot_nt(corrected.astype(BF), tiles[row]).astype(BF)
-    for start, buffer in zip(edge_rows(d, parity), (pair, cross)):
-        for e in range(HALO):
-            buffer[e, 0 : d.batch, :] = field[start + e]
-            for q in range(d.nq):
-                hit = iface[q] == start + e
-                buffer[e, d.batch + q * w : d.batch + (q + 1) * w, :] = jnp.where(hit, gfield[q], jnp.zeros((w, w), BF))
-
-
-def fold_kernel(d, after, diag, off, inv, folded):
+    for start, buffer in zip(edge_rows(d, lax.rem(face_ref[0], 2)), (pair, cross)):
+        buffer[:, 0 : d.batch, :] = field[pl.ds(start, HALO)]
+        for q in range(d.nq):
+            at = d.batch + q // HALO * w
+            buffer[q % HALO, at : at + w, :] = gfield[q]
+            at = d.batch + d.share + q * d.mark
+            for e in range(HALO):
+                buffer[e, at : at + d.mark, :] = jnp.full((d.mark, w), iface[q] == start + e).astype(F32).astype(BF)
+    for copy in copies[4 + d.ticks :]:
+        copy.wait()
+
+
+def fold_kernel(d, inv, diag, off, folded):
     w = d.width
     for r in range(d.count):
         tiles = jnp.concatenate([diag[r]] + [off[r, k] for k in range(d.neigh)], axis=1)
@@ -86,32 +100,58 @@
 
 
 def sweep(d, cols, face, ext, span, r, folded):
-    x = [ext[r + HALO, span, :]] + [ext[cols[r, k] - d.first_col(face), span, :] for k in range(d.neigh)]
+    x = [ext[r + HALO, span, :]] + [ext[cols[k, r] - d.first_col(face), span, :] for k in range(d.neigh)]
     return dot_nn(jnp.concatenate(x, axis=1), folded[r])
 
 
-def batch_kernel(d, last, face_ref, iface, cols, field, base, pair_in, cross_in, folded, *rest):
-    if last:
-        out, faces_out, ext = rest
-    else:
-        out, pair, cross, ext = rest
-    face = face_ref[0]
+def extend(d, face, field, pair_in, cross_in, ext):
     parity = lax.rem(face, 2)
-    ext[HALO : HALO + d.count] = field[...]
-    ext[pl.ds(d.up * (1 - parity), HALO)] = pair_in[:, 0 : d.batch, :]
-    ext[pl.ds(d.up * parity, HALO)] = cross_in[:, 0 : d.batch, :]
+    rows = pl.ds(0, ext.shape[1])
+    ext[HALO : HALO + d.count] = field[:, rows, :]
+    ext[pl.ds(d.up * (1 - parity), HALO)] = pair_in[:, rows, :]
+    ext[pl.ds(d.up * parity, HALO)] = cross_in[:, rows, :]
+
+
+def correct(d, cols, face, base, folded, out, ext):
     for r in range(d.count):
         for s in range(0, d.batch, d.group):
             span = pl.ds(s, d.group)
             out[r, span, :] = (base[r, span, :].astype(F32) + sweep(d, cols, face, ext, span, r, folded)).astype(BF)
-    if last:
-        for q in range(d.nq):
-            row = iface[q]
-            for t in range(d.ticks - 1):
-                faces_out[t, q] = out[row, t * d.sources : (t + 1) * d.sources, :]
-    else:
-        for start, buffer in zip(edge_rows(d, parity), (pair, cross)):
-            buffer[...] = out[pl.ds(start, HALO)]
+
+
+def second_kernel(d, face_ref, cols, field, pair_in, cross_in, folded, out, pair, cross, ext):
+    face = face_ref[0]
+    extend(d, face, field, pair_in, cross_in, ext)
+    correct(d, cols, face, field, folded, out, ext)
+    for start, buffer in zip(edge_rows(d, lax.rem(face, 2)), (pair, cross)):
+        buffer[...] = out[pl.ds(start, HALO)]
+
+
+def third_rows_kernel(d, face_ref, iface, cols, once, field, pair_in, cross_in, folded, faces_out, ext):
+    face = face_ref[0]
+    extend(d, face, once, pair_in, cross_in, ext)
+    for q in range(d.nq):
+        row = iface[q]
+        span = pl.ds(0, (d.ticks - 1) * d.sources)
+        value = (field[row, span, :].astype(F32) + sweep(d, cols, face, ext, span, row, folded)).astype(BF)
+        for t in range(d.ticks - 1):
+            faces_out[t, q] = value[t * d.sources : (t + 1) * d.sources, :]
+
+
+def third_kernel(d, face_ref, cols, once, field, pair_in, cross_in, folded, after, out, ext):
+    face = face_ref[0]
+    extend(d, face, once, pair_in, cross_in, ext)
+    correct(d, cols, face, field, folded, out, ext)
+
+
+def marked(d, block, e):
+    parts = []
+    for q in range(d.nq):
+        at = d.batch + q // HALO * d.width
+        mark = d.batch + d.share + q * d.mark
+        mark = block[e, mark : mark + d.mark, :]
+        parts.append(block[q % HALO, at : at + d.width, :] * jnp.concatenate([mark] * (d.width // d.mark), axis=0))
+    return jnp.concatenate(parts, axis=0)
 
 
 def coupling_first_kernel(d, face_ref, iface, cols, gfield, pair_in, cross_in, folded, after, out, pair, cross, met):
@@ -124,7 +164,7 @@
         for q in range(d.nq):
             met[2 * HALO + q, :, lanes] = jnp.where(iface[q] == r, folded[r, 0:w, :], jnp.zeros((w, w), BF))
         for k in range(d.neigh):
-            c = cols[r, k] - d.first_col(face)
+            c = cols[k, r] - d.first_col(face)
             inside = jnp.logical_and(c >= HALO, c < d.up)
             at = jnp.where(c < HALO, c, c - d.count)
             hit = jnp.logical_not(inside)
@@ -145,7 +185,7 @@
 
     pair_face, cross_face = face + 1 - 2 * parity, face - 1 + 2 * parity
     for at, other, block in ((HALO * (1 - parity), pair_face, pair_in), (HALO * parity, cross_face, cross_in)):
-        x = jnp.concatenate([block[e, d.batch : d.batch + d.group, :] for e in range(HALO)], axis=1)
+        x = jnp.concatenate([marked(d, block, e) for e in range(HALO)], axis=1)
         tiles = jnp.concatenate([met[at + e] for e in range(HALO)], axis=0)
         put(d.start(other), d.group, dot_nn(x, tiles))
     for q in range(d.nq):
@@ -262,19 +302,18 @@
 
 
 def call(body, name, smem, inputs, outs, scratch=(), flops=0, anywhere=(), sems=0, place=pltpu.VMEM, aliases=None):
-    moved = sum(x.size * x.dtype.itemsize for x in inputs) + sum(2 * math.prod(s) for s in outs)
+    outs = [x if isinstance(x, jax.ShapeDtypeStruct) else jax.ShapeDtypeStruct(x, BF) for x in outs]
     specs = [pl.BlockSpec(memory_space=pl.ANY if i in anywhere else pltpu.VMEM) for i in range(len(inputs))]
     return pl.pallas_call(
         body,
         name=name,
-        out_shape=[jax.ShapeDtypeStruct(s, BF) for s in outs],
+        out_shape=outs,
         in_specs=[pl.BlockSpec(memory_space=pltpu.SMEM)] * len(smem) + specs,
-        out_specs=[pl.BlockSpec(memory_space=place)] * len(outs),
-        scratch_shapes=[pltpu.VMEM(s, BF) if isinstance(s, tuple) else s for s in scratch]
-        + ([pltpu.SemaphoreType.DMA((sems,))] if sems else []),
+        out_specs=[pl.BlockSpec(memory_space=place if x.dtype == BF else pltpu.SMEM) for x in outs],
+        scratch_shapes=[pltpu.VMEM(s, BF) for s in scratch] + ([pltpu.SemaphoreType.DMA((sems,))] if sems else []),
         input_output_aliases=aliases or {},
         compiler_params=pltpu.CompilerParams(vmem_limit_bytes=32 * 1024 * 1024),
-        cost_estimate=pl.CostEstimate(flops=flops, bytes_accessed=moved, transcendentals=0),
+        cost_estimate=pl.CostEstimate(flops=flops, bytes_accessed=0, transcendentals=0),
     )(*smem, *inputs)
 
 
@@ -284,7 +323,7 @@
     _, count, neigh, width, _ = off_tiles.shape
     nq = coupling.shape[1]
     d = Dims(ticks, sources, count, neigh, width, nq, faces)
-    diag, off, inv, couple, cols = diag_tiles[0], off_tiles[0], inverse_tiles[0], coupling[0], cols[0]
+    diag, off, inv, couple, cols = diag_tiles[0], off_tiles[0], inverse_tiles[0], coupling[0], cols[0].T
     face = lax.axis_index("face").astype(jnp.int32)[None]
     tile = width * width
 
@@ -315,41 +354,37 @@
         return own + [swap(x) for x in own], made
 
     batch, group, ext, wide = d.batch, d.group, d.ext, d.wide
-    field, gfield, pair, cross = call(
+    sweep_flops = 2 * count * tile * (neigh + 1)
+    ints = [jax.ShapeDtypeStruct(x.shape, x.dtype) for x in (iface, cols)]
+    on_hbm = (iface, cols, inflow[0], couple, inv, rhs[:, 0], diag, off)
+    field, gfield, pair, cross, inv, diag, off, iface, cols = call(
         functools.partial(first_kernel, d),
         "first",
         [face],
-        [pltpu.with_memory_space_constraint(x, pltpu.HBM) for x in (iface, rhs[:, 0], inflow[0], inv, couple)],
-        [(count, batch, width), (nq, width, width)] + [(HALO, batch + group, width)] * 2,
-        [
-            pltpu.SMEM(iface.shape, jnp.int32),
-            (ticks, sources, count * width),
-            (sources, group),
-            (count, width, width),
-            (nq, width, width),
-        ],
+        [pltpu.with_memory_space_constraint(x, pltpu.HBM) for x in on_hbm],
+        [(count, batch, width), (nq, width, width)] + [(HALO, d.first_rows, width)] * 2 + [x.shape for x in (inv, diag, off)] + ints,
+        [(ticks, sources, count * width), (sources, group), (nq, width, width)],
         flops=2 * batch * count * tile,
-        anywhere=(0, 1, 2, 3, 4),
-        sems=4 + ticks,
-    )
+        anywhere=range(8),
+        sems=7 + ticks,
+    )
+    pair0, cross0 = exchange(pair, cross)
     (folded,) = call(
         functools.partial(fold_kernel, d),
         "fold",
         [],
-        [gfield, diag, off, inv],
+        [inv, diag, off],
         [(count, d.depth, width)],
-        flops=2 * width * count * tile * (neigh + 1),
-        anywhere=(0,),
-    )
-    pair0, cross0 = exchange(pair, cross)
+        flops=width * sweep_flops // 64,
+    )
     once, pair, cross = call(
-        functools.partial(batch_kernel, d, False),
+        functools.partial(second_kernel, d),
         "second",
-        [face, iface, cols],
-        [field, field, pair0, cross0, folded],
+        [face, cols],
+        [field, pair0, cross0, folded],
         [(count, batch, width)] + [(HALO, batch, width)] * 2,
         [(ext, batch, width)],
-        flops=2 * batch * count * tile * (neigh + 1),
+        flops=batch * sweep_flops // 64,
     )
     pair1, cross1 = exchange(pair, cross)
     gfirst, gpair, gcross = call(
@@ -364,14 +399,14 @@
     )
     cross1, gfirst = lax.optimization_barrier((cross1, gfirst))
     gpair, gcross = exchange(gpair, gcross)
-    fields, faces_out = call(
-        functools.partial(batch_kernel, d, True),
-        "third",
+    (faces_out,) = call(
+        functools.partial(third_rows_kernel, d),
+        "third_rows",
         [face, iface, cols],
         [once, field, pair1, cross1, folded],
-        [(count, batch, width), (ticks - 1, nq, sources, width)],
-        [(ext, batch, width)],
-        flops=2 * batch * count * tile * (neigh + 1),
+        [(ticks - 1, nq, sources, width)],
+        [(ext, (ticks - 1) * sources, width)],
+        flops=batch * sweep_flops,
     )
     other_faces = swap(faces_out)
     (sent,) = call(
@@ -381,7 +416,6 @@
         [faces_out, other_faces],
         [(2 * nq, sources, width)],
     )
-
     def operator_rows():
         return call(
             functools.partial(coupling_chain_kernel, d),
@@ -394,6 +428,18 @@
             anywhere=(5,),
         )[0]
 
+    def fields():
+        return call(
+            functools.partial(third_kernel, d),
+            "third",
+            [face, cols],
+            [once, field, pair1, cross1, folded, sent],
+            [(count, batch, width)],
+            [(ext, batch, width)],
+            flops=batch * sweep_flops,
+            anywhere=(5,),
+        )[0]
+
     arrived, chain = onward(sent, operator_rows)
     other_chain = swap(chain)
     whole = (ticks, sources, count * width)
@@ -406,7 +452,7 @@
             [gfield, gfirst, gpair, gcross, folded, chain],
             [(wide, count * width)],
             [(ext, wide, width)],
-            flops=2 * wide * count * tile * (neigh + 1),
+            flops=wide * sweep_flops,
             anywhere=(5,),
         )[0]
 
@@ -415,7 +461,7 @@
             functools.partial(output_kernel, d, which),
             "output",
             [face],
-            [fields, coupled] + earlier + blocks,
+            [twice, coupled] + earlier + blocks,
             [whole],
             [(len(which), sources, count * width)],
             flops=2 * len(which) * sources * wide * count * width,
@@ -442,6 +488,7 @@
         if tick == 1:
             arrived, coupled = onward(sent, operator)
         else:
+            twice = fields()
             arrived, most = onward(sent, lambda: output(tuple(range(ticks - 1)), everything, []))
     out = output((ticks - 1,), arrived, [most])
     return out[:, None]

time: 61.2 us -> 58.9 us (0.962)
  local copies, waits for them, and re-layouts: 2.67 us -> 0 us
    ppermute x3, waiting for transfers between devices: 10.3 us -> 7.77 us  [onward(): own.append(lax.ppermute(block, ('slab', 'face'), route))]
    ppermute x3, waiting for transfers between devices: 2.47 us -> 4.82 us  [exchange(): got = lax.ppermute(cross, 'face', crossing)]
    unnamed x8 -> x0, local copies, waits for them, and re-layouts: 1.91 us -> none
    squeeze x1 -> x0, local copies, waits for them, and re-layouts: 0.76 us -> none  [on_device(): cols[0]]
    pallas_call x12 -> x13, Pallas kernels: 19.4 us -> 20 us  [call(): pl.pallas_call(body, name=name, out_shape=outs, in_specs=[pl.BlockSpec(me...]
  transfers between devices with their start and end apart: 14 -> 14, of which waited for: 8 -> 9; matrix products, arithmetic and copies ran while one was open for 1% -> 0% of each run, Pallas kernels for 20% -> 23%
where the time goes in v5:
time: 58.9 us; the launch traced here: 58.6 us
  starting transfers between devices  20.5 us (35%)
  Pallas kernels  20 us (34%)
  waiting for transfers between devices  17.7 us (30%)
    pallas_call x13, Pallas kernels, call(): pl.pallas_call(body, name=name, out_shape=outs, in_specs=[pl.BlockSpec(me...  20 us
    ppermute x3, starting transfers between devices, onward(): own.append(lax.ppermute(block, ('slab', 'face'), route))  8.96 us
    ppermute x3, starting transfers between devices, exchange(): got = lax.ppermute(cross, 'face', crossing)  8.56 us
    ppermute x3, waiting for transfers between devices, onward(): own.append(lax.ppermute(block, ('slab', 'face'), route))  7.77 us
    ppermute x5, waiting for transfers between devices, swap(): return lax.ppermute(block, 'face', pairing)  5.12 us
    ppermute x3, waiting for transfers between devices, exchange(): got = lax.ppermute(cross, 'face', crossing)  4.82 us
    ppermute x5, starting transfers between devices, swap(): return lax.ppermute(block, 'face', pairing)  2.08 us
  transfers between devices with their start and end apart: 14, of which 9 were waited for; matrix products, arithmetic and copies ran while one was open for 0% of the time, Pallas kernels for 23%

profile of v5, /device:TPU:9, one launch (start us, length us, event | category | flops | bytes accessed | tf_op | source)
XLA Modules:
  0.0 58.6 jit_solution(3554526199558004157)
XLA Ops:
  0.0 2.6 %first.1 = (bf16[8,512,128]{2,1,0:T(8,128)(2,1)S(1)}, bf16[2,128,128]{2,1,0:T(8,128)(2,1)S(1)}, bf16[2,672,128]{2,1,0:T(8,128)(2,1)S(1)}, bf16[2,672,128]{2,1,0:...) custom-call(s32[1]{0:T(128)} %bitcast.face_ref, ...), custom_call_target="tpu_custom_call" | custom-call | flops 134217728 | tf_op jit(solution)/shard_map/first/pallas_call | solution.py:307
  3.3 3.0 %collective-permute-start.1 = (bf16[2,672,128]{2,1,0:T(8,128)(2,1)S(1)}, bf16[2,672,128]{2,1,0:T(8,128)(2,1)S(1)}, u32[]{:S(2)}, u32[]{:S(2)}) collective-permute-start(bf16[2,672,128]{2,1,0:T(8,128)(2,1)S(1)} %get-tuple-element.31), channel_id=1, source_target_pairs={{1,2},{2,1},{5,6},{6,5},{9,10},{10,9},{13,14},{14,13},{17,18},{18,... | collective-permute-start | bytes 1032200 | tf_op jit(solution)/shard_map/ppermute | solution.py:334
  6.4 0.9 %fold.1.folded = bf16[8,640,128]{2,1,0:T(8,128)(2,1)S(1)} custom-call(bf16[8,128,128]{2,1,0:T(8,128)(2,1)S(1)} %get-tuple-element.32.inv, bf16[8,128,128]{2,1,0:T(8,128)(2,1)S(1)} %get-tuple-element.33.diag, bf16[8,4,128,128]{3,2,1,0:T(8,128)(2,1)S(1)} %get-tuple-element.34.off), custom_call_target="tpu_custom_call" | custom-call | flops 2621440 | tf_op jit(solution)/shard_map/fold/pallas_call | solution.py:307
  7.3 4.6 %collective-permute-done.1.cross_in = bf16[2,672,128]{2,1,0:T(8,128)(2,1)S(1)} collective-permute-done((bf16[2,672,128]{2,1,0:T(8,128)(2,1)S(1)}, bf16[2,672,128]{2,1,0:T(8,128)(2,1)S(1)}, u32[]{:S(2)}, u32[]{:S(2)}) %collective-permute-start.1) | collective-permute-done | bytes 344096 | tf_op jit(solution)/shard_map/ppermute | solution.py:334
  11.9 2.3 %second.1 = (bf16[8,512,128]{2,1,0:T(8,128)(2,1)S(1)}, bf16[2,512,128]{2,1,0:T(8,128)(2,1)S(1)}, bf16[2,512,128]{2,1,0:T(8,128)(2,1)S(1)}) custom-call(s32[1]{0:T(128)} %bitcast.face_ref, s32[4,8]{1,0:T(4,128)S(1)} %get-tuple-element.28.cols, bf16[8,512,128]{2,1,0:T(8,128)(2,1)S(1)} %get-tuple-element.29.field, ...), custom_call_target="tpu_custom_call" | custom-call | flops 10485760 | tf_op jit(solution)/shard_map/second/pallas_call | solution.py:307
  14.2 3.0 %collective-permute-start.3 = (bf16[2,512,128]{2,1,0:T(8,128)(2,1)S(1)}, bf16[2,512,128]{2,1,0:T(8,128)(2,1)S(1)}, u32[]{:S(2)}, u32[]{:S(2)}) collective-permute-start(bf16[2,512,128]{2,1,0:T(8,128)(2,1)S(1)} %get-tuple-element.37), channel_id=1, source_target_pairs={{1,2},{2,1},{5,6},{6,5},{9,10},{10,9},{13,14},{14,13},{17,18},{18,... | collective-permute-start | bytes 786440 | tf_op jit(solution)/shard_map/ppermute | solution.py:334
  17.3 2.1 %coupling_first.1 = (bf16[8,1024,128]{2,1,0:T(8,128)(2,1)S(1)}, bf16[2,768,128]{2,1,0:T(8,128)(2,1)S(1)}, bf16[2,768,128]{2,1,0:T(8,128)(2,1)S(1)}) custom-call(s32[1]{0:T(128)} %bitcast.face_ref, s32[2]{0:T(128)S(1)} %get-tuple-element.38.iface, s32[4,8]{1,0:T(4,128)S(1)} %get-tuple-element.28.cols, bf16[2,128,128]{2,1,0:T(8,128)(2,1)S(1)} %get-tuple-element.39.gfield, ...), custom_call_target="tpu_custom_call" | custom-call | flops 201326592 | tf_op jit(solution)/shard_map/coupling_first/pallas_call | solution.py:307
  19.4 2.5 %collective-permute-start.7 = (bf16[2,768,128]{2,1,0:T(8,128)(2,1)S(1)}, bf16[2,768,128]{2,1,0:T(8,128)(2,1)S(1)}, u32[]{:S(2)}, u32[]{:S(2)}) collective-permute-start(bf16[2,768,128]{2,1,0:T(8,128)(2,1)S(1)} %get-tuple-element.44), channel_id=1, source_target_pairs={{1,2},{2,1},{5,6},{6,5},{9,10},{10,9},{13,14},{14,13},{17,18},{18,... | collective-permute-start | bytes 1179656 | tf_op jit(solution)/shard_map/ppermute | solution.py:334
  22.0 1.0 %third_rows.1.own.own_faces = bf16[3,2,128,128]{3,2,1,0:T(8,128)(2,1)S(1)} custom-call(s32[1]{0:T(128)} %bitcast.face_ref, s32[2]{0:T(128)S(1)} %get-tuple-element.38.iface, s32[4,8]{1,0:T(4,128)S(1)} %get-tuple-element.28.cols, bf16[8,512,128]{2,1,0:T(8,128)(2,1)S(1)} %get-tuple-element.35.once, bf16[8,512,128]{2,1,0:T(8,128)(2,1)S(1)} %get-tuple-element.29.field, ...), custom_call_target="tpu_custom_call" | custom-call | flops 671088640 | tf_op jit(solution)/shard_map/third_rows/pallas_call | solution.py:307
  23.1 1.4 %collective-permute-done.4.other.other_faces = bf16[3,2,128,128]{3,2,1,0:T(8,128)(2,1)S(1)} collective-permute-done((bf16[3,2,128,128]{3,2,1,0:T(8,128)(2,1)S(1)}, bf16[3,2,128,128]{3,2,1,0:T(8,128)(2,1)S(1)}, u32[]{:S(2)}, u32[]{:S(2)}) %collective-permute-start.4) | collective-permute-done | bytes 196640 | tf_op jit(solution)/shard_map/ppermute | solution.py:338
  24.5 3.7 %collective-permute-start.5 = (bf16[4,128,128]{2,1,0:T(8,128)(2,1)S(1)}, bf16[4,128,128]{2,1,0:T(8,128)(2,1)S(1)}, u32[]{:S(2)}, u32[]{:S(2)}) collective-permute-start(bf16[4,128,128]{2,1,0:T(8,128)(2,1)S(1)} %merge.1.after), channel_id=1, source_target_pairs={{0,4},{3,5},{2,6},{1,7},{4,8},{7,9},{6,10},{5,11},{8,12},{11,13},{... | collective-permute-start | bytes 393224 | tf_op jit(solution)/shard_map/ppermute | solution.py:350
  28.5 1.8 %coupling_chain.1.own_chain.after = bf16[1024,256]{1,0:T(8,128)(2,1)S(1)} custom-call(s32[1]{0:T(128)} %bitcast.face_ref, s32[2]{0:T(128)S(1)} %get-tuple-element.38.iface, s32[4,8]{1,0:T(4,128)S(1)} %get-tuple-element.28.cols, bf16[2,128,128]{2,1,0:T(8,128)(2,1)S(1)} %get-tuple-element.39.gfield, bf16[8,1024,128]{2,1,0:T(8,128)(2,1)S(1)} %get-tuple-element.42.gfirst, ...), custom_call_target="tpu_custom_call" | custom-call | flops 335544320 | tf_op jit(solution)/shard_map/coupling_chain/pallas_call | solution.py:307
  30.3 2.9 %collective-permute-done.5.rest_0_ = bf16[4,128,128]{2,1,0:T(8,128)(2,1)S(1)} collective-permute-done((bf16[4,128,128]{2,1,0:T(8,128)(2,1)S(1)}, bf16[4,128,128]{2,1,0:T(8,128)(2,1)S(1)}, u32[]{:S(2)}, u32[]{:S(2)}) %collective-permute-start.5) | collective-permute-done | bytes 131104 | tf_op jit(solution)/shard_map/ppermute | solution.py:350
  34.0 1.7 %collective-permute-done.9.rest_1_ = bf16[4,128,128]{2,1,0:T(8,128)(2,1)S(1)} collective-permute-done((bf16[4,128,128]{2,1,0:T(8,128)(2,1)S(1)}, bf16[4,128,128]{2,1,0:T(8,128)(2,1)S(1)}, u32[]{:S(2)}, u32[]{:S(2)}) %collective-permute-start.9) | collective-permute-done | bytes 131104 | tf_op jit(solution)/shard_map/ppermute | solution.py:338
  36.0 2.9 %collective-permute-start.10 = (bf16[4,128,128]{2,1,0:T(8,128)(2,1)S(1)}, bf16[4,128,128]{2,1,0:T(8,128)(2,1)S(1)}, u32[]{:S(2)}, u32[]{:S(2)}) collective-permute-start(bf16[4,128,128]{2,1,0:T(8,128)(2,1)S(1)} %chain.2), channel_id=1, source_target_pairs={{0,4},{3,5},{2,6},{1,7},{4,8},{7,9},{6,10},{5,11},{8,12},{11,13},{... | collective-permute-start | bytes 393224 | tf_op jit(solution)/shard_map/ppermute | solution.py:350
  39.0 3.8 %coupling_last.1.coupled = bf16[1024,1024]{1,0:T(8,128)(2,1)S(1)} custom-call(s32[1]{0:T(128)} %bitcast.face_ref, s32[2]{0:T(128)S(1)} %get-tuple-element.38.iface, s32[4,8]{1,0:T(4,128)S(1)} %get-tuple-element.28.cols, bf16[2,128,128]{2,1,0:T(8,128)(2,1)S(1)} %get-tuple-element.39.gfield, bf16[8,1024,128]{2,1,0:T(8,128)(2,1)S(1)} %get-tuple-element.42.gfirst, ...), custom_call_target="tpu_custom_call" | custom-call | flops 1342177280 | tf_op jit(solution)/shard_map/coupling_last/pallas_call | solution.py:307
  42.8 2.1 %collective-permute-done.10.rest_0_.rest_2_ = bf16[4,128,128]{2,1,0:T(8,128)(2,1)S(1)} collective-permute-done((bf16[4,128,128]{2,1,0:T(8,128)(2,1)S(1)}, bf16[4,128,128]{2,1,0:T(8,128)(2,1)S(1)}, u32[]{:S(2)}, u32[]{:S(2)}) %collective-permute-start.10) | collective-permute-done | bytes 131104 | tf_op jit(solution)/shard_map/ppermute | solution.py:350
  45.5 1.0 %collective-permute-done.11.rest_1_.rest_3_ = bf16[4,128,128]{2,1,0:T(8,128)(2,1)S(1)} collective-permute-done((bf16[4,128,128]{2,1,0:T(8,128)(2,1)S(1)}, bf16[4,128,128]{2,1,0:T(8,128)(2,1)S(1)}, u32[]{:S(2)}, u32[]{:S(2)}) %collective-permute-start.11) | collective-permute-done | bytes 131104 | tf_op jit(solution)/shard_map/ppermute | solution.py:338
  46.8 2.3 %collective-permute-start.12 = (bf16[4,128,128]{2,1,0:T(8,128)(2,1)S(1)}, bf16[4,128,128]{2,1,0:T(8,128)(2,1)S(1)}, u32[]{:S(2)}, u32[]{:S(2)}) collective-permute-start(bf16[4,128,128]{2,1,0:T(8,128)(2,1)S(1)} %chain.3.after), channel_id=1, source_target_pairs={{0,4},{3,5},{2,6},{1,7},{4,8},{7,9},{6,10},{5,11},{8,12},{11,13},{... | collective-permute-start | bytes 393224 | tf_op jit(solution)/shard_map/ppermute | solution.py:350
  49.1 2.2 %third.1.fields = bf16[8,512,128]{2,1,0:T(8,128)(2,1)S(1)} custom-call(s32[1]{0:T(128)} %bitcast.face_ref, s32[4,8]{1,0:T(4,128)S(1)} %get-tuple-element.28.cols, bf16[8,512,128]{2,1,0:T(8,128)(2,1)S(1)} %get-tuple-element.35.once, bf16[8,512,128]{2,1,0:T(8,128)(2,1)S(1)} %get-tuple-element.29.field, ...), custom_call_target="tpu_custom_call" | custom-call | flops 671088640 | tf_op jit(solution)/shard_map/third/pallas_call | solution.py:307
  51.3 1.6 %output.2.rest_0_ = bf16[4,128,1024]{2,1,0:T(8,128)(2,1)} custom-call(s32[1]{0:T(128)} %bitcast.face_ref, bf16[8,512,128]{2,1,0:T(8,128)(2,1)S(1)} %third.1.fields, bf16[1024,1024]{1,0:T(8,128)(2,1)S(1)} %coupling_last.1.coupled, bf16[4,128,128]{2,1,0:T(8,128)(2,1)S(1)} %collective-permute-done.5.rest_0_, ...), custom_call_target="tpu_custom_call" | custom-call | flops 805306368 | tf_op jit(solution)/shard_map/output/pallas_call | solution.py:307
  52.9 2.7 %collective-permute-done.12.rest_1_ = bf16[4,128,128]{2,1,0:T(8,128)(2,1)S(1)} collective-permute-done((bf16[4,128,128]{2,1,0:T(8,128)(2,1)S(1)}, bf16[4,128,128]{2,1,0:T(8,128)(2,1)S(1)}, u32[]{:S(2)}, u32[]{:S(2)}) %collective-permute-start.12) | collective-permute-done | bytes 131104 | tf_op jit(solution)/shard_map/ppermute | solution.py:350
  56.3 1.0 %collective-permute-done.13.rest_2_ = bf16[4,128,128]{2,1,0:T(8,128)(2,1)S(1)} collective-permute-done((bf16[4,128,128]{2,1,0:T(8,128)(2,1)S(1)}, bf16[4,128,128]{2,1,0:T(8,128)(2,1)S(1)}, u32[]{:S(2)}, u32[]{:S(2)}) %collective-permute-start.13) | collective-permute-done | bytes 131104 | tf_op jit(solution)/shard_map/ppermute | solution.py:338
  57.3 1.2 %output.3 = bf16[4,128,1024]{2,1,0:T(8,128)(2,1)} custom-call(s32[1]{0:T(128)} %bitcast.face_ref, bf16[8,512,128]{2,1,0:T(8,128)(2,1)S(1)} %third.1.fields, bf16[1024,1024]{1,0:T(8,128)(2,1)S(1)} %coupling_last.1.coupled, bf16[4,128,1024]{2,1,0:T(8,128)(2,1)} %output.2.rest_0_, ...), custom_call_target="tpu_custom_call", output_to_operand_aliasing={{}: (3, {})} | custom-call | flops 268435456 | tf_op jit(solution)/shard_map/output/pallas_call | solution.py:307
  (17 shorter events, 3.8 us)
Async XLA Ops:
  2.6 4.7 %collective-permute-start = (bf16[2,672,128]{2,1,0:T(8,128)(2,1)S(1)}, bf16[2,672,128]{2,1,0:T(8,128)(2,1)S(1)}, u32[]{:S(2)}, u32[]{:S(2)}) collective-permute-start(bf16[2,672,128]{2,1,0:T(8,128)(2,1)S(1)} %get-tuple-element.30), channel_id=1, source_target_pairs={{0,1},{1,0},{2,3},{3,2},{4,5},{5,4},{6,7},{7,6},{8,9},{9,8},{10,11... | collective-permute-start | bytes 1032200 | tf_op jit(solution)/shard_map/ppermute | solution.py:335
  3.3 8.6 %collective-permute-start.1 = (bf16[2,672,128]{2,1,0:T(8,128)(2,1)S(1)}, bf16[2,672,128]{2,1,0:T(8,128)(2,1)S(1)}, u32[]{:S(2)}, u32[]{:S(2)}) collective-permute-start(bf16[2,672,128]{2,1,0:T(8,128)(2,1)S(1)} %get-tuple-element.31), channel_id=1, source_target_pairs={{1,2},{2,1},{5,6},{6,5},{9,10},{10,9},{13,14},{14,13},{17,18},{18,... | collective-permute-start | bytes 1032200 | tf_op jit(solution)/shard_map/ppermute | solution.py:334
  14.2 3.1 %collective-permute-start.2 = (bf16[2,512,128]{2,1,0:T(8,128)(2,1)S(1)}, bf16[2,512,128]{2,1,0:T(8,128)(2,1)S(1)}, u32[]{:S(2)}, u32[]{:S(2)}) collective-permute-start(bf16[2,512,128]{2,1,0:T(8,128)(2,1)S(1)} %get-tuple-element.36), channel_id=1, source_target_pairs={{0,1},{1,0},{2,3},{3,2},{4,5},{5,4},{6,7},{7,6},{8,9},{9,8},{10,11... | collective-permute-start | bytes 786440 | tf_op jit(solution)/shard_map/ppermute | solution.py:335
  14.2 7.7 %collective-permute-start.3 = (bf16[2,512,128]{2,1,0:T(8,128)(2,1)S(1)}, bf16[2,512,128]{2,1,0:T(8,128)(2,1)S(1)}, u32[]{:S(2)}, u32[]{:S(2)}) collective-permute-start(bf16[2,512,128]{2,1,0:T(8,128)(2,1)S(1)} %get-tuple-element.37), channel_id=1, source_target_pairs={{1,2},{2,1},{5,6},{6,5},{9,10},{10,9},{13,14},{14,13},{17,18},{18,... | collective-permute-start | bytes 786440 | tf_op jit(solution)/shard_map/ppermute | solution.py:334
  19.3 8.9 %collective-permute-start.6 = (bf16[2,768,128]{2,1,0:T(8,128)(2,1)S(1)}, bf16[2,768,128]{2,1,0:T(8,128)(2,1)S(1)}, u32[]{:S(2)}, u32[]{:S(2)}) collective-permute-start(bf16[2,768,128]{2,1,0:T(8,128)(2,1)S(1)} %get-tuple-element.43), channel_id=1, source_target_pairs={{0,1},{1,0},{2,3},{3,2},{4,5},{5,4},{6,7},{7,6},{8,9},{9,8},{10,11... | collective-permute-start | bytes 1179656 | tf_op jit(solution)/shard_map/ppermute | solution.py:335
  19.4 9.1 %collective-permute-start.7 = (bf16[2,768,128]{2,1,0:T(8,128)(2,1)S(1)}, bf16[2,768,128]{2,1,0:T(8,128)(2,1)S(1)}, u32[]{:S(2)}, u32[]{:S(2)}) collective-permute-start(bf16[2,768,128]{2,1,0:T(8,128)(2,1)S(1)} %get-tuple-element.44), channel_id=1, source_target_pairs={{1,2},{2,1},{5,6},{6,5},{9,10},{10,9},{13,14},{14,13},{17,18},{18,... | collective-permute-start | bytes 1179656 | tf_op jit(solution)/shard_map/ppermute | solution.py:334
  23.0 1.5 %collective-permute-start.4 = (bf16[3,2,128,128]{3,2,1,0:T(8,128)(2,1)S(1)}, bf16[3,2,128,128]{3,2,1,0:T(8,128)(2,1)S(1)}, u32[]{:S(2)}, u32[]{:S(2)}) collective-permute-start(bf16[3,2,128,128]{3,2,1,0:T(8,128)(2,1)S(1)} %third_rows.1.own.own_faces), channel_id=1, source_target_pairs={{0,1},{1,0},{2,3},{3,2},{4,5},{5,4},{6,7},{7,6},{8,9},{9,8},{10,11... | collective-permute-start | bytes 589832 | tf_op jit(solution)/shard_map/ppermute | solution.py:338
  24.5 8.7 %collective-permute-start.5 = (bf16[4,128,128]{2,1,0:T(8,128)(2,1)S(1)}, bf16[4,128,128]{2,1,0:T(8,128)(2,1)S(1)}, u32[]{:S(2)}, u32[]{:S(2)}) collective-permute-start(bf16[4,128,128]{2,1,0:T(8,128)(2,1)S(1)} %merge.1.after), channel_id=1, source_target_pairs={{0,4},{3,5},{2,6},{1,7},{4,8},{7,9},{6,10},{5,11},{8,12},{11,13},{... | collective-permute-start | bytes 393224 | tf_op jit(solution)/shard_map/ppermute | solution.py:350
  33.2 2.5 %collective-permute-start.8 = (bf16[1024,256]{1,0:T(8,128)(2,1)S(1)}, bf16[1024,256]{1,0:T(8,128)(2,1)S(1)}, u32[]{:S(2)}, u32[]{:S(2)}) collective-permute-start(bf16[1024,256]{1,0:T(8,128)(2,1)S(1)} %coupling_chain.1.own_chain.after), channel_id=1, source_target_pairs={{0,1},{1,0},{2,3},{3,2},{4,5},{5,4},{6,7},{7,6},{8,9},{9,8},{10,11... | collective-permute-start | bytes 1572872 | tf_op jit(solution)/shard_map/ppermute | solution.py:338
  34.0 1.7 %collective-permute-start.9 = (bf16[4,128,128]{2,1,0:T(8,128)(2,1)S(1)}, bf16[4,128,128]{2,1,0:T(8,128)(2,1)S(1)}, u32[]{:S(2)}, u32[]{:S(2)}) collective-permute-start(bf16[4,128,128]{2,1,0:T(8,128)(2,1)S(1)} %collective-permute-done.5.rest_0_), channel_id=1, source_target_pairs={{0,1},{1,0},{2,3},{3,2},{4,5},{5,4},{6,7},{7,6},{8,9},{9,8},{10,11... | collective-permute-start | bytes 393224 | tf_op jit(solution)/shard_map/ppermute | solution.py:338
  36.0 8.9 %collective-permute-start.10 = (bf16[4,128,128]{2,1,0:T(8,128)(2,1)S(1)}, bf16[4,128,128]{2,1,0:T(8,128)(2,1)S(1)}, u32[]{:S(2)}, u32[]{:S(2)}) collective-permute-start(bf16[4,128,128]{2,1,0:T(8,128)(2,1)S(1)} %chain.2), channel_id=1, source_target_pairs={{0,4},{3,5},{2,6},{1,7},{4,8},{7,9},{6,10},{5,11},{8,12},{11,13},{... | collective-permute-start | bytes 393224 | tf_op jit(solution)/shard_map/ppermute | solution.py:350
  44.9 1.6 %collective-permute-start.11 = (bf16[4,128,128]{2,1,0:T(8,128)(2,1)S(1)}, bf16[4,128,128]{2,1,0:T(8,128)(2,1)S(1)}, u32[]{:S(2)}, u32[]{:S(2)}) collective-permute-start(bf16[4,128,128]{2,1,0:T(8,128)(2,1)S(1)} %collective-permute-done.10.rest_0_.rest_2_), channel_id=1, source_target_pairs={{0,1},{1,0},{2,3},{3,2},{4,5},{5,4},{6,7},{7,6},{8,9},{9,8},{10,11... | collective-permute-start | bytes 393224 | tf_op jit(solution)/shard_map/ppermute | solution.py:338
  46.8 8.8 %collective-permute-start.12 = (bf16[4,128,128]{2,1,0:T(8,128)(2,1)S(1)}, bf16[4,128,128]{2,1,0:T(8,128)(2,1)S(1)}, u32[]{:S(2)}, u32[]{:S(2)}) collective-permute-start(bf16[4,128,128]{2,1,0:T(8,128)(2,1)S(1)} %chain.3.after), channel_id=1, source_target_pairs={{0,4},{3,5},{2,6},{1,7},{4,8},{7,9},{6,10},{5,11},{8,12},{11,13},{... | collective-permute-start | bytes 393224 | tf_op jit(solution)/shard_map/ppermute | solution.py:350
  55.7 1.6 %collective-permute-start.13 = (bf16[4,128,128]{2,1,0:T(8,128)(2,1)S(1)}, bf16[4,128,128]{2,1,0:T(8,128)(2,1)S(1)}, u32[]{:S(2)}, u32[]{:S(2)}) collective-permute-start(bf16[4,128,128]{2,1,0:T(8,128)(2,1)S(1)} %collective-permute-done.12.rest_1_), channel_id=1, source_target_pairs={{0,1},{1,0},{2,3},{3,2},{4,5},{5,4},{6,7},{7,6},{8,9},{9,8},{10,11... | collective-permute-start | bytes 393224 | tf_op jit(solution)/shard_map/ppermute | solution.py:338

commit v6 on v5

--- a/solution.py
+++ b/solution.py
@@ -87,7 +87,7 @@
         copy.wait()
 
 
-def fold_kernel(d, inv, diag, off, folded):
+def fold_kernel(d, face_ref, iface, cols, inv, diag, off, folded, met):
     w = d.width
     for r in range(d.count):
         tiles = jnp.concatenate([diag[r]] + [off[r, k] for k in range(d.neigh)], axis=1)
@@ -97,74 +97,13 @@
         for k in range(1 + d.neigh):
             part = product[:, k * w : (k + 1) * w].T
             folded[r, k * w : (k + 1) * w, :] = ((unit if k == 0 else 0.0) - part).astype(BF)
-
-
-def sweep(d, cols, face, ext, span, r, folded):
-    x = [ext[r + HALO, span, :]] + [ext[cols[k, r] - d.first_col(face), span, :] for k in range(d.neigh)]
-    return dot_nn(jnp.concatenate(x, axis=1), folded[r])
-
-
-def extend(d, face, field, pair_in, cross_in, ext):
-    parity = lax.rem(face, 2)
-    rows = pl.ds(0, ext.shape[1])
-    ext[HALO : HALO + d.count] = field[:, rows, :]
-    ext[pl.ds(d.up * (1 - parity), HALO)] = pair_in[:, rows, :]
-    ext[pl.ds(d.up * parity, HALO)] = cross_in[:, rows, :]
-
-
-def correct(d, cols, face, base, folded, out, ext):
-    for r in range(d.count):
-        for s in range(0, d.batch, d.group):
-            span = pl.ds(s, d.group)
-            out[r, span, :] = (base[r, span, :].astype(F32) + sweep(d, cols, face, ext, span, r, folded)).astype(BF)
-
-
-def second_kernel(d, face_ref, cols, field, pair_in, cross_in, folded, out, pair, cross, ext):
-    face = face_ref[0]
-    extend(d, face, field, pair_in, cross_in, ext)
-    correct(d, cols, face, field, folded, out, ext)
-    for start, buffer in zip(edge_rows(d, lax.rem(face, 2)), (pair, cross)):
-        buffer[...] = out[pl.ds(start, HALO)]
-
-
-def third_rows_kernel(d, face_ref, iface, cols, once, field, pair_in, cross_in, folded, faces_out, ext):
-    face = face_ref[0]
-    extend(d, face, once, pair_in, cross_in, ext)
-    for q in range(d.nq):
-        row = iface[q]
-        span = pl.ds(0, (d.ticks - 1) * d.sources)
-        value = (field[row, span, :].astype(F32) + sweep(d, cols, face, ext, span, row, folded)).astype(BF)
-        for t in range(d.ticks - 1):
-            faces_out[t, q] = value[t * d.sources : (t + 1) * d.sources, :]
-
-
-def third_kernel(d, face_ref, cols, once, field, pair_in, cross_in, folded, after, out, ext):
-    face = face_ref[0]
-    extend(d, face, once, pair_in, cross_in, ext)
-    correct(d, cols, face, field, folded, out, ext)
-
-
-def marked(d, block, e):
-    parts = []
-    for q in range(d.nq):
-        at = d.batch + q // HALO * d.width
-        mark = d.batch + d.share + q * d.mark
-        mark = block[e, mark : mark + d.mark, :]
-        parts.append(block[q % HALO, at : at + d.width, :] * jnp.concatenate([mark] * (d.width // d.mark), axis=0))
-    return jnp.concatenate(parts, axis=0)
-
-
-def coupling_first_kernel(d, face_ref, iface, cols, gfield, pair_in, cross_in, folded, after, out, pair, cross, met):
-    face = face_ref[0]
-    parity = lax.rem(face, 2)
-    w = d.width
     met[...] = jnp.zeros_like(met)
     for r in range(d.count):
         lanes = slice(r * w, (r + 1) * w)
         for q in range(d.nq):
             met[2 * HALO + q, :, lanes] = jnp.where(iface[q] == r, folded[r, 0:w, :], jnp.zeros((w, w), BF))
         for k in range(d.neigh):
-            c = cols[k, r] - d.first_col(face)
+            c = cols[k, r] - d.first_col(face_ref[0])
             inside = jnp.logical_and(c >= HALO, c < d.up)
             at = jnp.where(c < HALO, c, c - d.count)
             hit = jnp.logical_not(inside)
@@ -177,7 +116,83 @@
             def _():
                 met[at, :, lanes] += folded[r, (1 + k) * w : (2 + k) * w, :]
 
-    out[...] = jnp.zeros_like(out)
+
+def sweep(d, cols, face, ext, span, r, folded):
+    x = [ext[r + HALO, span, :]] + [ext[cols[k, r] - d.first_col(face), span, :] for k in range(d.neigh)]
+    return dot_nn(jnp.concatenate(x, axis=1), folded[r])
+
+
+def place_halo(d, face, pair_in, cross_in, ext):
+    parity = lax.rem(face, 2)
+    rows = pl.ds(0, ext.shape[1])
+    ext[pl.ds(d.up * (1 - parity), HALO)] = pair_in[:, rows, :]
+    ext[pl.ds(d.up * parity, HALO)] = cross_in[:, rows, :]
+
+
+def extend(d, face, edges, inner, pair_in, cross_in, ext):
+    rows = pl.ds(0, ext.shape[1])
+    ext[HALO : 2 * HALO] = edges[0:HALO, rows, :]
+    ext[2 * HALO : d.count] = inner[:, rows, :]
+    ext[d.count : d.up] = edges[HALO : 2 * HALO, rows, :]
+    place_halo(d, face, pair_in, cross_in, ext)
+
+
+def correct(d, cols, face, base, folded, out, ext, rows, first=0):
+    for i, r in enumerate(rows):
+        for s in range(0, d.batch, d.group):
+            span = pl.ds(s, d.group)
+            value = base[r, span, :].astype(F32) + sweep(d, cols, face, ext, span, r, folded)
+            out[first + i, span, :] = value.astype(BF)
+
+
+def second_edges_kernel(d, face_ref, cols, field, pair_in, cross_in, folded, edges, pair, cross, ext):
+    face = face_ref[0]
+    ext[HALO : HALO + d.count] = field[...]
+    place_halo(d, face, pair_in, cross_in, ext)
+    correct(d, cols, face, field, folded, edges, ext, list(range(HALO)) + list(range(d.last, d.count)))
+    parity = lax.rem(face, 2)
+    pair[...] = edges[pl.ds(HALO * (1 - parity), HALO)]
+    cross[...] = edges[pl.ds(HALO * parity, HALO)]
+
+
+def second_inner_kernel(d, face_ref, cols, field, ext, folded, after, out):
+    correct(d, cols, face_ref[0], field, folded, out, ext, range(HALO, d.last))
+
+
+def third_rows_kernel(d, face_ref, iface, cols, edges, inner, field, pair_in, cross_in, folded, sent, ext):
+    face = face_ref[0]
+    extend(d, face, edges, inner, pair_in, cross_in, ext)
+    span = pl.ds(0, d.sources)
+    for q in range(d.nq):
+        row = iface[q]
+        sent[q] = (field[row, span, :].astype(F32) + sweep(d, cols, face, ext, span, row, folded)).astype(BF)
+
+
+def third_kernel(d, face_ref, iface, cols, edges, inner, field, pair_in, cross_in, folded, after, out, faces_out, ext):
+    face = face_ref[0]
+    extend(d, face, edges, inner, pair_in, cross_in, ext)
+    correct(d, cols, face, field, folded, out, ext, range(d.count))
+    for q in range(d.nq):
+        for t in range(1, d.ticks - 1):
+            faces_out[t - 1, q] = out[iface[q], t * d.sources : (t + 1) * d.sources, :]
+
+
+def marked(d, block, e):
+    parts = []
+    for q in range(d.nq):
+        at = d.batch + q // HALO * d.width
+        mark = d.batch + d.share + q * d.mark
+        mark = block[e, mark : mark + d.mark, :]
+        parts.append(block[q % HALO, at : at + d.width, :] * jnp.concatenate([mark] * (d.width // d.mark), axis=0))
+    return jnp.concatenate(parts, axis=0)
+
+
+def coupling_first_kernel(d, face_ref, iface, gfield, pair_in, cross_in, met, after, out, pair, cross):
+    face = face_ref[0]
+    parity = lax.rem(face, 2)
+    w = d.width
+    for shift in range(2, d.slots - 1):
+        out[:, pl.ds(d.start(face + shift), d.group), :] = jnp.zeros((d.count, d.group, w), BF)
 
     def put(start, rows, value):
         for r in range(d.count):
@@ -265,15 +280,15 @@
         for x, start in blocks:
             total += dot_nn(x, chain[pl.ds(start, 2 * d.group), :])
         for q in range(d.nq):
-            value = base[tick, q].astype(F32) - total[:, q * d.width : (q + 1) * d.width]
+            value = base[tick - 1, q].astype(F32) - total[:, q * d.width : (q + 1) * d.width]
             sent[odd * d.nq + q] = value.astype(BF)
 
 
 def merge_kernel(d, face_ref, own, other, sent):
     parity = lax.rem(face_ref[0], 2)
     for q in range(d.nq):
-        sent[parity * d.nq + q] = own[0, q]
-        sent[(1 - parity) * d.nq + q] = other[0, q]
+        sent[parity * d.nq + q] = own[q]
+        sent[(1 - parity) * d.nq + q] = other[q]
 
 
 def output_kernel(d, ticks, face_ref, fields, coupled, *rest):
@@ -283,20 +298,22 @@
     each = 2 * len(chip_hops(d.faces))
     copies = []
     arrived = arrived[len(arrived) % each :]
+    part = 2 * w
     for i, t in enumerate(ticks):
-        total = None
+        blocks = []
         if t:
             mine, arrived = arrived[:each], arrived[each:]
-            total = jnp.zeros((d.sources, d.count * w), F32)
-            for x, start in arrived_blocks(d, face, mine[: each // 2], mine[each // 2 :]):
-                total += dot_nn(x, coupled[pl.ds(start, 2 * d.group), :])
-        for r in range(d.count):
-            value = fields[r, t * d.sources : (t + 1) * d.sources, :]
-            if t:
-                value = (value.astype(F32) - total[:, r * w : (r + 1) * w]).astype(BF)
-            held[i, :, r * w : (r + 1) * w] = value
-        copies.append(pltpu.make_async_copy(held.at[i], out.at[t], sems.at[i]))
-        copies[-1].start()
+            blocks = list(arrived_blocks(d, face, mine[: each // 2], mine[each // 2 :]))
+        for c in range(0, d.count * w, part):
+            total = jnp.zeros((d.sources, part), F32)
+            for x, start in blocks:
+                total += dot_nn(x, coupled[pl.ds(start, 2 * d.group), c : c + part])
+            for j in range(0, part, w):
+                value = fields[(c + j) // w, t * d.sources : (t + 1) * d.sources, :].astype(F32)
+                held[i, :, c + j : c + j + w] = (value - total[:, j : j + w]).astype(BF)
+            here = held.at[i, :, c : c + part]
+            copies.append(pltpu.make_async_copy(here, out.at[t, :, c : c + part], sems.at[len(copies)]))
+            copies[-1].start()
     for copy in copies:
         copy.wait()
 
@@ -369,79 +386,84 @@
         sems=7 + ticks,
     )
     pair0, cross0 = exchange(pair, cross)
-    (folded,) = call(
+    folded, met = call(
         functools.partial(fold_kernel, d),
         "fold",
-        [],
+        [face, iface, cols],
         [inv, diag, off],
-        [(count, d.depth, width)],
+        [(count, d.depth, width), (2 * HALO + nq, width, count * width)],
         flops=width * sweep_flops // 64,
     )
-    once, pair, cross = call(
-        functools.partial(second_kernel, d),
-        "second",
+    edges, pair, cross, ext0 = call(
+        functools.partial(second_edges_kernel, d),
+        "second_edges",
         [face, cols],
         [field, pair0, cross0, folded],
-        [(count, batch, width)] + [(HALO, batch, width)] * 2,
-        [(ext, batch, width)],
+        [(2 * HALO, batch, width)] + [(HALO, batch, width)] * 2 + [(ext, batch, width)],
         flops=batch * sweep_flops // 64,
     )
     pair1, cross1 = exchange(pair, cross)
     gfirst, gpair, gcross = call(
         functools.partial(coupling_first_kernel, d),
         "coupling_first",
-        [face, iface, cols],
-        [gfield, pair0, cross0, folded, pair1],
+        [face, iface],
+        [gfield, pair0, cross0, met, pair1],
         [(count, wide, width)] + [(HALO, 3 * group, width)] * 2,
-        [(2 * HALO + nq, width, count * width)],
         flops=2 * (2 * HALO + nq) * width * count * tile,
         anywhere=(4,),
     )
-    cross1, gfirst = lax.optimization_barrier((cross1, gfirst))
-    gpair, gcross = exchange(gpair, gcross)
-    (faces_out,) = call(
+    gpair1, gcross1 = exchange(gpair, gcross)
+    (inner,) = call(
+        functools.partial(second_inner_kernel, d),
+        "second_inner",
+        [face, cols],
+        [field, ext0, folded, gfirst],
+        [(count - 2 * HALO, batch, width)],
+        flops=0,
+        anywhere=(3,),
+    )
+    cross1, inner = lax.optimization_barrier((cross1, inner))
+    (own_first,) = call(
         functools.partial(third_rows_kernel, d),
         "third_rows",
         [face, iface, cols],
-        [once, field, pair1, cross1, folded],
-        [(ticks - 1, nq, sources, width)],
-        [(ext, (ticks - 1) * sources, width)],
-        flops=batch * sweep_flops,
-    )
-    other_faces = swap(faces_out)
+        [edges, inner, field, pair1, cross1, folded],
+        [(nq, sources, width)],
+        [(ext, sources, width)],
+        flops=batch * sweep_flops * 5 // 2,
+    )
     (sent,) = call(
         functools.partial(merge_kernel, d),
         "merge",
         [face],
-        [faces_out, other_faces],
+        [own_first, swap(own_first)],
         [(2 * nq, sources, width)],
     )
+
     def operator_rows():
-        return call(
+        (chain,) = call(
             functools.partial(coupling_chain_kernel, d),
             "coupling_chain",
             [face, iface, cols],
-            [gfield, gfirst, gpair, gcross, folded, sent],
+            [gfield, gfirst, gpair1, gcross1, folded, sent],
             [(wide, group)],
             [(ext, wide, width)],
-            flops=2 * wide * nq * tile * (neigh + 1),
+            flops=0,
             anywhere=(5,),
-        )[0]
-
-    def fields():
-        return call(
+        )
+        return chain, *call(
             functools.partial(third_kernel, d),
             "third",
-            [face, cols],
-            [once, field, pair1, cross1, folded, sent],
-            [(count, batch, width)],
+            [face, iface, cols],
+            [edges, inner, field, pair1, cross1, folded, chain],
+            [(count, batch, width), (ticks - 2, nq, sources, width)],
             [(ext, batch, width)],
-            flops=batch * sweep_flops,
-            anywhere=(5,),
-        )[0]
-
-    arrived, chain = onward(sent, operator_rows)
-    other_chain = swap(chain)
+            flops=0,
+            anywhere=(6,),
+        )
+
+    arrived, (chain, twice, faces_out) = onward(sent, operator_rows)
+    other_chain, other_faces = swap(chain), swap(faces_out)
     whole = (ticks, sources, count * width)
 
     def operator():
@@ -449,7 +471,7 @@
             functools.partial(coupling_last_kernel, d),
             "coupling_last",
             [face, iface, cols],
-            [gfield, gfirst, gpair, gcross, folded, chain],
+            [gfield, gfirst, gpair1, gcross1, folded, chain],
             [(wide, count * width)],
             [(ext, wide, width)],
             flops=wide * sweep_flops,
@@ -466,7 +488,7 @@
             [(len(which), sources, count * width)],
             flops=2 * len(which) * sources * wide * count * width,
             anywhere=(2,) if earlier else (),
-            sems=len(which),
+            sems=len(which) * count,
             place=pl.ANY,
             aliases={3: 0} if earlier else None,
         )[0]
@@ -488,7 +510,6 @@
         if tick == 1:
             arrived, coupled = onward(sent, operator)
         else:
-            twice = fields()
             arrived, most = onward(sent, lambda: output(tuple(range(ticks - 1)), everything, []))
     out = output((ticks - 1,), arrived, [most])
     return out[:, None]

time: 58.9 us -> 58.6 us (level)
  waiting for transfers between devices: 17.7 us -> 15.8 us
  Pallas kernels: 20 us -> 21.1 us
  starting transfers between devices: 20.5 us -> 21.1 us
    ppermute x3, waiting for transfers between devices: 4.82 us -> 3.36 us  [exchange(): got = lax.ppermute(cross, 'face', crossing)]
    pallas_call x13 -> x14, Pallas kernels: 20 us -> 21.1 us  [call(): pl.pallas_call(body, name=name, out_shape=outs, in_specs=[pl.BlockSpec(me...]
    ppermute x5 -> x6, starting transfers between devices: 2.08 us -> 2.59 us  [swap(): return lax.ppermute(block, 'face', pairing)]
    ppermute x5 -> x6, waiting for transfers between devices: 5.12 us -> 4.62 us  [swap(): return lax.ppermute(block, 'face', pairing)]
  transfers between devices with their start and end apart: 14 -> 15, of which waited for: 9 -> 9; matrix products, arithmetic and copies ran while one was open for 0% -> 0% of each run, Pallas kernels for 23% -> 26%
where the time goes in v6:
time: 58.6 us; the launch traced here: 58.3 us
  Pallas kernels  21.1 us (36%)
  starting transfers between devices  21.1 us (36%)
  waiting for transfers between devices  15.8 us (27%)
    pallas_call x14, Pallas kernels, call(): pl.pallas_call(body, name=name, out_shape=outs, in_specs=[pl.BlockSpec(me...  21.1 us
    ppermute x3, starting transfers between devices, onward(): own.append(lax.ppermute(block, ('slab', 'face'), route))  9.01 us
    ppermute x3, starting transfers between devices, exchange(): got = lax.ppermute(cross, 'face', crossing)  8.58 us
    ppermute x3, waiting for transfers between devices, onward(): own.append(lax.ppermute(block, ('slab', 'face'), route))  7.84 us
    ppermute x6, waiting for transfers between devices, swap(): return lax.ppermute(block, 'face', pairing)  4.62 us
    ppermute x3, waiting for transfers between devices, exchange(): got = lax.ppermute(cross, 'face', crossing)  3.36 us
    ppermute x6, starting transfers between devices, swap(): return lax.ppermute(block, 'face', pairing)  2.59 us
  transfers between devices with their start and end apart: 15, of which 9 were waited for; matrix products, arithmetic and copies ran while one was open for 0% of the time, Pallas kernels for 26%

profile of v6, /device:TPU:9, one launch (start us, length us, event | category | flops | bytes accessed | tf_op | source)
XLA Modules:
  0.0 58.3 jit_solution(9216969934681547932)
XLA Ops:
  0.0 2.6 %first.1 = (bf16[8,512,128]{2,1,0:T(8,128)(2,1)S(1)}, bf16[2,128,128]{2,1,0:T(8,128)(2,1)S(1)}, bf16[2,672,128]{2,1,0:T(8,128)(2,1)S(1)}, bf16[2,672,128]{2,1,0:...) custom-call(s32[1]{0:T(128)} %bitcast.face_ref, ...), custom_call_target="tpu_custom_call" | custom-call | flops 134217728 | tf_op jit(solution)/shard_map/first/pallas_call | solution.py:324
  3.3 3.0 %collective-permute-start.1 = (bf16[2,672,128]{2,1,0:T(8,128)(2,1)S(1)}, bf16[2,672,128]{2,1,0:T(8,128)(2,1)S(1)}, u32[]{:S(2)}, u32[]{:S(2)}) collective-permute-start(bf16[2,672,128]{2,1,0:T(8,128)(2,1)S(1)} %get-tuple-element.39), channel_id=1, source_target_pairs={{1,2},{2,1},{5,6},{6,5},{9,10},{10,9},{13,14},{14,13},{17,18},{18,... | collective-permute-start | bytes 1032200 | tf_op jit(solution)/shard_map/ppermute | solution.py:351
  6.4 2.2 %fold.1 = (bf16[8,640,128]{2,1,0:T(8,128)(2,1)S(1)}, bf16[6,128,1024]{2,1,0:T(8,128)(2,1)S(1)}) custom-call(s32[1]{0:T(128)} %bitcast.face_ref, s32[2]{0:T(128)S(1)} %get-tuple-element.35.iface, s32[4,8]{1,0:T(4,128)S(1)} %get-tuple-element.36.cols, bf16[8,128,128]{2,1,0:T(8,128)(2,1)S(1)} %get-tuple-element.40.inv, ...), custom_call_target="tpu_custom_call" | custom-call | flops 2621440 | tf_op jit(solution)/shard_map/fold/pallas_call | solution.py:324
  8.5 3.4 %collective-permute-done.1.cross_in = bf16[2,672,128]{2,1,0:T(8,128)(2,1)S(1)} collective-permute-done((bf16[2,672,128]{2,1,0:T(8,128)(2,1)S(1)}, bf16[2,672,128]{2,1,0:T(8,128)(2,1)S(1)}, u32[]{:S(2)}, u32[]{:S(2)}) %collective-permute-start.1) | collective-permute-done | bytes 344096 | tf_op jit(solution)/shard_map/ppermute | solution.py:351
  11.9 1.5 %second_edges.1 = (bf16[4,512,128]{2,1,0:T(8,128)(2,1)S(1)}, bf16[2,512,128]{2,1,0:T(8,128)(2,1)S(1)}, bf16[2,512,128]{2,1,0:T(8,128)(2,1)S(1)}, bf16[12,512,128]{2,1,0:T(8,128)(2,1)S(1)}) custom-call(s32[1]{0:T(128)} %bitcast.face_ref, s32[4,8]{1,0:T(4,128)S(1)} %get-tuple-element.36.cols, bf16[8,512,128]{2,1,0:T(8,128)(2,1)S(1)} %get-tuple-element.37.field, ...), custom_call_target="tpu_custom_call" | custom-call | flops 10485760 | tf_op jit(solution)/shard_map/second_edges/pallas_call | solution.py:324
  13.5 3.0 %collective-permute-start.2 = (bf16[2,512,128]{2,1,0:T(8,128)(2,1)S(1)}, bf16[2,512,128]{2,1,0:T(8,128)(2,1)S(1)}, u32[]{:S(2)}, u32[]{:S(2)}) collective-permute-start(bf16[2,512,128]{2,1,0:T(8,128)(2,1)S(1)} %get-tuple-element.45), channel_id=1, source_target_pairs={{1,2},{2,1},{5,6},{6,5},{9,10},{10,9},{13,14},{14,13},{17,18},{18,... | collective-permute-start | bytes 786440 | tf_op jit(solution)/shard_map/ppermute | solution.py:351
  16.6 1.2 %coupling_first.1 = (bf16[8,1024,128]{2,1,0:T(8,128)(2,1)S(1)}, bf16[2,768,128]{2,1,0:T(8,128)(2,1)S(1)}, bf16[2,768,128]{2,1,0:T(8,128)(2,1)S(1)}) custom-call(s32[1]{0:T(128)} %bitcast.face_ref, s32[2]{0:T(128)S(1)} %get-tuple-element.35.iface, bf16[2,128,128]{2,1,0:T(8,128)(2,1)S(1)} %get-tuple-element.47.gfield, ...), custom_call_target="tpu_custom_call" | custom-call | flops 201326592 | tf_op jit(solution)/shard_map/coupling_first/pallas_call | solution.py:324
  17.8 2.5 %collective-permute-start.7 = (bf16[2,768,128]{2,1,0:T(8,128)(2,1)S(1)}, bf16[2,768,128]{2,1,0:T(8,128)(2,1)S(1)}, u32[]{:S(2)}, u32[]{:S(2)}) collective-permute-start(bf16[2,768,128]{2,1,0:T(8,128)(2,1)S(1)} %get-tuple-element.54), channel_id=1, source_target_pairs={{1,2},{2,1},{5,6},{6,5},{9,10},{10,9},{13,14},{14,13},{17,18},{18,... | collective-permute-start | bytes 1179656 | tf_op jit(solution)/shard_map/ppermute | solution.py:351
  20.4 1.4 %second_inner.1.inner = bf16[4,512,128]{2,1,0:T(8,128)(2,1)S(1)} custom-call(s32[1]{0:T(128)} %bitcast.face_ref, s32[4,8]{1,0:T(4,128)S(1)} %get-tuple-element.36.cols, bf16[8,512,128]{2,1,0:T(8,128)(2,1)S(1)} %get-tuple-element.37.field, bf16[12,512,128]{2,1,0:T(8,128)(2,1)S(1)} %get-tuple-element.46.ext, ...), custom_call_target="tpu_custom_call" | custom-call | tf_op jit(solution)/shard_map/second_inner/pallas_call | solution.py:324
  22.7 1.2 %collective-permute-done.4.other = bf16[2,128,128]{2,1,0:T(8,128)(2,1)S(1)} collective-permute-done((bf16[2,128,128]{2,1,0:T(8,128)(2,1)S(1)}, bf16[2,128,128]{2,1,0:T(8,128)(2,1)S(1)}, u32[]{:S(2)}, u32[]{:S(2)}) %collective-permute-start.4) | collective-permute-done | bytes 65568 | tf_op jit(solution)/shard_map/ppermute | solution.py:355
  24.0 3.7 %collective-permute-start.5 = (bf16[4,128,128]{2,1,0:T(8,128)(2,1)S(1)}, bf16[4,128,128]{2,1,0:T(8,128)(2,1)S(1)}, u32[]{:S(2)}, u32[]{:S(2)}) collective-permute-start(bf16[4,128,128]{2,1,0:T(8,128)(2,1)S(1)} %merge.1.after), channel_id=1, source_target_pairs={{0,4},{3,5},{2,6},{1,7},{4,8},{7,9},{6,10},{5,11},{8,12},{11,13},{... | collective-permute-start | bytes 393224 | tf_op jit(solution)/shard_map/ppermute | solution.py:367
  27.7 1.8 %coupling_chain.1.after.own_chain = bf16[1024,256]{1,0:T(8,128)(2,1)S(1)} custom-call(s32[1]{0:T(128)} %bitcast.face_ref, s32[2]{0:T(128)S(1)} %get-tuple-element.35.iface, s32[4,8]{1,0:T(4,128)S(1)} %get-tuple-element.36.cols, bf16[2,128,128]{2,1,0:T(8,128)(2,1)S(1)} %get-tuple-element.47.gfield, bf16[8,1024,128]{2,1,0:T(8,128)(2,1)S(1)} %get-tuple-element.50.after.gfirst, ...), custom_call_target="tpu_custom_call" | custom-call | tf_op jit(solution)/shard_map/coupling_chain/pallas_call | solution.py:324
  29.5 2.2 %third.1 = (bf16[8,512,128]{2,1,0:T(8,128)(2,1)S(1)}, bf16[2,2,128,128]{3,2,1,0:T(8,128)(2,1)S(1)}) custom-call(s32[1]{0:T(128)} %bitcast.face_ref, s32[2]{0:T(128)S(1)} %get-tuple-element.35.iface, s32[4,8]{1,0:T(4,128)S(1)} %get-tuple-element.36.cols, bf16[4,512,128]{2,1,0:T(8,128)(2,1)S(1)} %get-tuple-element.44.edges, ...), custom_call_target="tpu_custom_call" | custom-call | tf_op jit(solution)/shard_map/third/pallas_call | solution.py:324
  31.8 0.9 %collective-permute-done.5.rest_0_ = bf16[4,128,128]{2,1,0:T(8,128)(2,1)S(1)} collective-permute-done((bf16[4,128,128]{2,1,0:T(8,128)(2,1)S(1)}, bf16[4,128,128]{2,1,0:T(8,128)(2,1)S(1)}, u32[]{:S(2)}, u32[]{:S(2)}) %collective-permute-start.5) | collective-permute-done | bytes 131104 | tf_op jit(solution)/shard_map/ppermute | solution.py:367
  34.0 1.2 %collective-permute-done.9.other_faces = bf16[2,2,128,128]{3,2,1,0:T(8,128)(2,1)S(1)} collective-permute-done((bf16[2,2,128,128]{3,2,1,0:T(8,128)(2,1)S(1)}, bf16[2,2,128,128]{3,2,1,0:T(8,128)(2,1)S(1)}, u32[]{:S(2)}, u32[]{:S(2)}) %collective-permute-start.9) | collective-permute-done | bytes 131104 | tf_op jit(solution)/shard_map/ppermute | solution.py:355
  35.7 3.1 %collective-permute-start.11 = (bf16[4,128,128]{2,1,0:T(8,128)(2,1)S(1)}, bf16[4,128,128]{2,1,0:T(8,128)(2,1)S(1)}, u32[]{:S(2)}, u32[]{:S(2)}) collective-permute-start(bf16[4,128,128]{2,1,0:T(8,128)(2,1)S(1)} %chain.2), channel_id=1, source_target_pairs={{0,4},{3,5},{2,6},{1,7},{4,8},{7,9},{6,10},{5,11},{8,12},{11,13},{... | collective-permute-start | bytes 393224 | tf_op jit(solution)/shard_map/ppermute | solution.py:367
  38.8 3.8 %coupling_last.1.coupled = bf16[1024,1024]{1,0:T(8,128)(2,1)S(1)} custom-call(s32[1]{0:T(128)} %bitcast.face_ref, s32[2]{0:T(128)S(1)} %get-tuple-element.35.iface, s32[4,8]{1,0:T(4,128)S(1)} %get-tuple-element.36.cols, bf16[2,128,128]{2,1,0:T(8,128)(2,1)S(1)} %get-tuple-element.47.gfield, bf16[8,1024,128]{2,1,0:T(8,128)(2,1)S(1)} %get-tuple-element.50.after.gfirst, ...), custom_call_target="tpu_custom_call" | custom-call | flops 1342177280 | tf_op jit(solution)/shard_map/coupling_last/pallas_call | solution.py:324
  42.6 2.0 %collective-permute-done.11.rest_0_.rest_2_ = bf16[4,128,128]{2,1,0:T(8,128)(2,1)S(1)} collective-permute-done((bf16[4,128,128]{2,1,0:T(8,128)(2,1)S(1)}, bf16[4,128,128]{2,1,0:T(8,128)(2,1)S(1)}, u32[]{:S(2)}, u32[]{:S(2)}) %collective-permute-start.11) | collective-permute-done | bytes 131104 | tf_op jit(solution)/shard_map/ppermute | solution.py:367
  45.1 1.0 %collective-permute-done.12.rest_1_.rest_3_ = bf16[4,128,128]{2,1,0:T(8,128)(2,1)S(1)} collective-permute-done((bf16[4,128,128]{2,1,0:T(8,128)(2,1)S(1)}, bf16[4,128,128]{2,1,0:T(8,128)(2,1)S(1)}, u32[]{:S(2)}, u32[]{:S(2)}) %collective-permute-start.12) | collective-permute-done | bytes 131104 | tf_op jit(solution)/shard_map/ppermute | solution.py:355
  46.4 2.2 %collective-permute-start.13 = (bf16[4,128,128]{2,1,0:T(8,128)(2,1)S(1)}, bf16[4,128,128]{2,1,0:T(8,128)(2,1)S(1)}, u32[]{:S(2)}, u32[]{:S(2)}) collective-permute-start(bf16[4,128,128]{2,1,0:T(8,128)(2,1)S(1)} %chain.3), channel_id=1, source_target_pairs={{0,4},{3,5},{2,6},{1,7},{4,8},{7,9},{6,10},{5,11},{8,12},{11,13},{... | collective-permute-start | bytes 393224 | tf_op jit(solution)/shard_map/ppermute | solution.py:367
  48.6 1.7 %output.2.rest_0_ = bf16[4,128,1024]{2,1,0:T(8,128)(2,1)} custom-call(s32[1]{0:T(128)} %bitcast.face_ref, bf16[8,512,128]{2,1,0:T(8,128)(2,1)S(1)} %get-tuple-element.57.fields, bf16[1024,1024]{1,0:T(8,128)(2,1)S(1)} %coupling_last.1.coupled, bf16[4,128,128]{2,1,0:T(8,128)(2,1)S(1)} %collective-permute-done.5.rest_0_, ...), custom_call_target="tpu_custom_call" | custom-call | flops 805306368 | tf_op jit(solution)/shard_map/output/pallas_call | solution.py:324
  50.3 5.0 %collective-permute-done.13.rest_1_ = bf16[4,128,128]{2,1,0:T(8,128)(2,1)S(1)} collective-permute-done((bf16[4,128,128]{2,1,0:T(8,128)(2,1)S(1)}, bf16[4,128,128]{2,1,0:T(8,128)(2,1)S(1)}, u32[]{:S(2)}, u32[]{:S(2)}) %collective-permute-start.13) | collective-permute-done | bytes 131104 | tf_op jit(solution)/shard_map/ppermute | solution.py:367
  56.0 1.0 %collective-permute-done.14.rest_2_ = bf16[4,128,128]{2,1,0:T(8,128)(2,1)S(1)} collective-permute-done((bf16[4,128,128]{2,1,0:T(8,128)(2,1)S(1)}, bf16[4,128,128]{2,1,0:T(8,128)(2,1)S(1)}, u32[]{:S(2)}, u32[]{:S(2)}) %collective-permute-start.14) | collective-permute-done | bytes 131104 | tf_op jit(solution)/shard_map/ppermute | solution.py:355
  57.0 1.2 %output.3 = bf16[4,128,1024]{2,1,0:T(8,128)(2,1)} custom-call(s32[1]{0:T(128)} %bitcast.face_ref, bf16[8,512,128]{2,1,0:T(8,128)(2,1)S(1)} %get-tuple-element.57.fields, bf16[1024,1024]{1,0:T(8,128)(2,1)S(1)} %coupling_last.1.coupled, bf16[4,128,1024]{2,1,0:T(8,128)(2,1)} %output.2.rest_0_, ...), custom_call_target="tpu_custom_call", output_to_operand_aliasing={{}: (3, {})} | custom-call | flops 268435456 | tf_op jit(solution)/shard_map/output/pallas_call | solution.py:324
  (20 shorter events, 5.2 us)
Async XLA Ops:
  2.6 5.9 %collective-permute-start = (bf16[2,672,128]{2,1,0:T(8,128)(2,1)S(1)}, bf16[2,672,128]{2,1,0:T(8,128)(2,1)S(1)}, u32[]{:S(2)}, u32[]{:S(2)}) collective-permute-start(bf16[2,672,128]{2,1,0:T(8,128)(2,1)S(1)} %get-tuple-element.38), channel_id=1, source_target_pairs={{0,1},{1,0},{2,3},{3,2},{4,5},{5,4},{6,7},{7,6},{8,9},{9,8},{10,11... | collective-permute-start | bytes 1032200 | tf_op jit(solution)/shard_map/ppermute | solution.py:352
  3.3 8.6 %collective-permute-start.1 = (bf16[2,672,128]{2,1,0:T(8,128)(2,1)S(1)}, bf16[2,672,128]{2,1,0:T(8,128)(2,1)S(1)}, u32[]{:S(2)}, u32[]{:S(2)}) collective-permute-start(bf16[2,672,128]{2,1,0:T(8,128)(2,1)S(1)} %get-tuple-element.39), channel_id=1, source_target_pairs={{1,2},{2,1},{5,6},{6,5},{9,10},{10,9},{13,14},{14,13},{17,18},{18,... | collective-permute-start | bytes 1032200 | tf_op jit(solution)/shard_map/ppermute | solution.py:351
  13.4 3.1 %collective-permute-start.3 = (bf16[2,512,128]{2,1,0:T(8,128)(2,1)S(1)}, bf16[2,512,128]{2,1,0:T(8,128)(2,1)S(1)}, u32[]{:S(2)}, u32[]{:S(2)}) collective-permute-start(bf16[2,512,128]{2,1,0:T(8,128)(2,1)S(1)} %get-tuple-element.49), channel_id=1, source_target_pairs={{0,1},{1,0},{2,3},{3,2},{4,5},{5,4},{6,7},{7,6},{8,9},{9,8},{10,11... | collective-permute-start | bytes 786440 | tf_op jit(solution)/shard_map/ppermute | solution.py:352
  13.5 8.3 %collective-permute-start.2 = (bf16[2,512,128]{2,1,0:T(8,128)(2,1)S(1)}, bf16[2,512,128]{2,1,0:T(8,128)(2,1)S(1)}, u32[]{:S(2)}, u32[]{:S(2)}) collective-permute-start(bf16[2,512,128]{2,1,0:T(8,128)(2,1)S(1)} %get-tuple-element.45), channel_id=1, source_target_pairs={{1,2},{2,1},{5,6},{6,5},{9,10},{10,9},{13,14},{14,13},{17,18},{18,... | collective-permute-start | bytes 786440 | tf_op jit(solution)/shard_map/ppermute | solution.py:351
  17.8 10.0 %collective-permute-start.6 = (bf16[2,768,128]{2,1,0:T(8,128)(2,1)S(1)}, bf16[2,768,128]{2,1,0:T(8,128)(2,1)S(1)}, u32[]{:S(2)}, u32[]{:S(2)}) collective-permute-start(bf16[2,768,128]{2,1,0:T(8,128)(2,1)S(1)} %get-tuple-element.53), channel_id=1, source_target_pairs={{0,1},{1,0},{2,3},{3,2},{4,5},{5,4},{6,7},{7,6},{8,9},{9,8},{10,11... | collective-permute-start | bytes 1179656 | tf_op jit(solution)/shard_map/ppermute | solution.py:352
  17.8 9.9 %collective-permute-start.7 = (bf16[2,768,128]{2,1,0:T(8,128)(2,1)S(1)}, bf16[2,768,128]{2,1,0:T(8,128)(2,1)S(1)}, u32[]{:S(2)}, u32[]{:S(2)}) collective-permute-start(bf16[2,768,128]{2,1,0:T(8,128)(2,1)S(1)} %get-tuple-element.54), channel_id=1, source_target_pairs={{1,2},{2,1},{5,6},{6,5},{9,10},{10,9},{13,14},{14,13},{17,18},{18,... | collective-permute-start | bytes 1179656 | tf_op jit(solution)/shard_map/ppermute | solution.py:351
  22.6 1.3 %collective-permute-start.4 = (bf16[2,128,128]{2,1,0:T(8,128)(2,1)S(1)}, bf16[2,128,128]{2,1,0:T(8,128)(2,1)S(1)}, u32[]{:S(2)}, u32[]{:S(2)}) collective-permute-start(bf16[2,128,128]{2,1,0:T(8,128)(2,1)S(1)} %third_rows.1.own), channel_id=1, source_target_pairs={{0,1},{1,0},{2,3},{3,2},{4,5},{5,4},{6,7},{7,6},{8,9},{9,8},{10,11... | collective-permute-start | bytes 196616 | tf_op jit(solution)/shard_map/ppermute | solution.py:355
  24.0 8.7 %collective-permute-start.5 = (bf16[4,128,128]{2,1,0:T(8,128)(2,1)S(1)}, bf16[4,128,128]{2,1,0:T(8,128)(2,1)S(1)}, u32[]{:S(2)}, u32[]{:S(2)}) collective-permute-start(bf16[4,128,128]{2,1,0:T(8,128)(2,1)S(1)} %merge.1.after), channel_id=1, source_target_pairs={{0,4},{3,5},{2,6},{1,7},{4,8},{7,9},{6,10},{5,11},{8,12},{11,13},{... | collective-permute-start | bytes 393224 | tf_op jit(solution)/shard_map/ppermute | solution.py:367
  32.7 2.7 %collective-permute-start.8 = (bf16[1024,256]{1,0:T(8,128)(2,1)S(1)}, bf16[1024,256]{1,0:T(8,128)(2,1)S(1)}, u32[]{:S(2)}, u32[]{:S(2)}) collective-permute-start(bf16[1024,256]{1,0:T(8,128)(2,1)S(1)} %coupling_chain.1.after.own_chain), channel_id=1, source_target_pairs={{0,1},{1,0},{2,3},{3,2},{4,5},{5,4},{6,7},{7,6},{8,9},{9,8},{10,11... | collective-permute-start | bytes 1572872 | tf_op jit(solution)/shard_map/ppermute | solution.py:355
  33.4 1.7 %collective-permute-start.9 = (bf16[2,2,128,128]{3,2,1,0:T(8,128)(2,1)S(1)}, bf16[2,2,128,128]{3,2,1,0:T(8,128)(2,1)S(1)}, u32[]{:S(2)}, u32[]{:S(2)}) collective-permute-start(bf16[2,2,128,128]{3,2,1,0:T(8,128)(2,1)S(1)} %get-tuple-element.59.own_faces), channel_id=1, source_target_pairs={{0,1},{1,0},{2,3},{3,2},{4,5},{5,4},{6,7},{7,6},{8,9},{9,8},{10,11... | collective-permute-start | bytes 393224 | tf_op jit(solution)/shard_map/ppermute | solution.py:355
  33.4 1.9 %collective-permute-start.10 = (bf16[4,128,128]{2,1,0:T(8,128)(2,1)S(1)}, bf16[4,128,128]{2,1,0:T(8,128)(2,1)S(1)}, u32[]{:S(2)}, u32[]{:S(2)}) collective-permute-start(bf16[4,128,128]{2,1,0:T(8,128)(2,1)S(1)} %collective-permute-done.5.rest_0_), channel_id=1, source_target_pairs={{0,1},{1,0},{2,3},{3,2},{4,5},{5,4},{6,7},{7,6},{8,9},{9,8},{10,11... | collective-permute-start | bytes 393224 | tf_op jit(solution)/shard_map/ppermute | solution.py:355
  35.7 8.9 %collective-permute-start.11 = (bf16[4,128,128]{2,1,0:T(8,128)(2,1)S(1)}, bf16[4,128,128]{2,1,0:T(8,128)(2,1)S(1)}, u32[]{:S(2)}, u32[]{:S(2)}) collective-permute-start(bf16[4,128,128]{2,1,0:T(8,128)(2,1)S(1)} %chain.2), channel_id=1, source_target_pairs={{0,4},{3,5},{2,6},{1,7},{4,8},{7,9},{6,10},{5,11},{8,12},{11,13},{... | collective-permute-start | bytes 393224 | tf_op jit(solution)/shard_map/ppermute | solution.py:367
  44.5 1.6 %collective-permute-start.12 = (bf16[4,128,128]{2,1,0:T(8,128)(2,1)S(1)}, bf16[4,128,128]{2,1,0:T(8,128)(2,1)S(1)}, u32[]{:S(2)}, u32[]{:S(2)}) collective-permute-start(bf16[4,128,128]{2,1,0:T(8,128)(2,1)S(1)} %collective-permute-done.11.rest_0_.rest_2_), channel_id=1, source_target_pairs={{0,1},{1,0},{2,3},{3,2},{4,5},{5,4},{6,7},{7,6},{8,9},{9,8},{10,11... | collective-permute-start | bytes 393224 | tf_op jit(solution)/shard_map/ppermute | solution.py:355
  46.4 8.9 %collective-permute-start.13 = (bf16[4,128,128]{2,1,0:T(8,128)(2,1)S(1)}, bf16[4,128,128]{2,1,0:T(8,128)(2,1)S(1)}, u32[]{:S(2)}, u32[]{:S(2)}) collective-permute-start(bf16[4,128,128]{2,1,0:T(8,128)(2,1)S(1)} %chain.3), channel_id=1, source_target_pairs={{0,4},{3,5},{2,6},{1,7},{4,8},{7,9},{6,10},{5,11},{8,12},{11,13},{... | collective-permute-start | bytes 393224 | tf_op jit(solution)/shard_map/ppermute | solution.py:367
  55.3 1.6 %collective-permute-start.14 = (bf16[4,128,128]{2,1,0:T(8,128)(2,1)S(1)}, bf16[4,128,128]{2,1,0:T(8,128)(2,1)S(1)}, u32[]{:S(2)}, u32[]{:S(2)}) collective-permute-start(bf16[4,128,128]{2,1,0:T(8,128)(2,1)S(1)} %collective-permute-done.13.rest_1_), channel_id=1, source_target_pairs={{0,1},{1,0},{2,3},{3,2},{4,5},{5,4},{6,7},{7,6},{8,9},{9,8},{10,11... | collective-permute-start | bytes 393224 | tf_op jit(solution)/shard_map/ppermute | solution.py:355

commit v7 on v6

--- a/solution.py
+++ b/solution.py
@@ -31,6 +31,8 @@
         self.depth = (1 + neigh) * width
         self.slots = 4 if faces <= 4 else 6
         self.wide = self.slots * self.group
+        self.parts = 4 if self.slots % 4 == 0 else 3
+        self.part = self.wide // self.parts
         self.mark = 16
         self.share = -(-nq // HALO) * width
         self.first_rows = self.batch + self.share + nq * self.mark
@@ -122,19 +124,17 @@
     return dot_nn(jnp.concatenate(x, axis=1), folded[r])
 
 
-def place_halo(d, face, pair_in, cross_in, ext):
+def place_halo(d, face, pair_in, cross_in, ext, rows):
     parity = lax.rem(face, 2)
-    rows = pl.ds(0, ext.shape[1])
     ext[pl.ds(d.up * (1 - parity), HALO)] = pair_in[:, rows, :]
     ext[pl.ds(d.up * parity, HALO)] = cross_in[:, rows, :]
 
 
-def extend(d, face, edges, inner, pair_in, cross_in, ext):
-    rows = pl.ds(0, ext.shape[1])
+def extend(d, face, edges, inner, pair_in, cross_in, ext, rows):
     ext[HALO : 2 * HALO] = edges[0:HALO, rows, :]
     ext[2 * HALO : d.count] = inner[:, rows, :]
     ext[d.count : d.up] = edges[HALO : 2 * HALO, rows, :]
-    place_halo(d, face, pair_in, cross_in, ext)
+    place_halo(d, face, pair_in, cross_in, ext, rows)
 
 
 def correct(d, cols, face, base, folded, out, ext, rows, first=0):
@@ -148,7 +148,7 @@
 def second_edges_kernel(d, face_ref, cols, field, pair_in, cross_in, folded, edges, pair, cross, ext):
     face = face_ref[0]
     ext[HALO : HALO + d.count] = field[...]
-    place_halo(d, face, pair_in, cross_in, ext)
+    place_halo(d, face, pair_in, cross_in, ext, pl.ds(0, d.batch))
     correct(d, cols, face, field, folded, edges, ext, list(range(HALO)) + list(range(d.last, d.count)))
     parity = lax.rem(face, 2)
     pair[...] = edges[pl.ds(HALO * (1 - parity), HALO)]
@@ -159,22 +159,25 @@
     correct(d, cols, face_ref[0], field, folded, out, ext, range(HALO, d.last))
 
 
+def interface_rows(d, face, iface, cols, edges, inner, field, pair_in, cross_in, folded, first, outs, ext):
+    ticks = pl.ds(first * d.sources, len(outs) * d.sources)
+    extend(d, face, edges, inner, pair_in, cross_in, ext, ticks)
+    for q in range(d.nq):
+        row = iface[q]
+        value = sweep(d, cols, face, ext, pl.ds(0, len(outs) * d.sources), row, folded)
+        value = (field[row, ticks, :].astype(F32) + value).astype(BF)
+        for t, out in enumerate(outs):
+            out[q] = value[t * d.sources : (t + 1) * d.sources]
+
+
 def third_rows_kernel(d, face_ref, iface, cols, edges, inner, field, pair_in, cross_in, folded, sent, ext):
-    face = face_ref[0]
-    extend(d, face, edges, inner, pair_in, cross_in, ext)
-    span = pl.ds(0, d.sources)
-    for q in range(d.nq):
-        row = iface[q]
-        sent[q] = (field[row, span, :].astype(F32) + sweep(d, cols, face, ext, span, row, folded)).astype(BF)
-
-
-def third_kernel(d, face_ref, iface, cols, edges, inner, field, pair_in, cross_in, folded, after, out, faces_out, ext):
-    face = face_ref[0]
-    extend(d, face, edges, inner, pair_in, cross_in, ext)
+    interface_rows(d, face_ref[0], iface, cols, edges, inner, field, pair_in, cross_in, folded, 0, [sent], ext)
+
+
+def third_kernel(d, face_ref, cols, edges, inner, field, pair_in, cross_in, folded, after, out, ext):
+    face = face_ref[0]
+    extend(d, face, edges, inner, pair_in, cross_in, ext, pl.ds(0, d.batch))
     correct(d, cols, face, field, folded, out, ext, range(d.count))
-    for q in range(d.nq):
-        for t in range(1, d.ticks - 1):
-            faces_out[t - 1, q] = out[iface[q], t * d.sources : (t + 1) * d.sources, :]
 
 
 def marked(d, block, e):
@@ -225,17 +228,26 @@
             ext[pl.ds(start, HALO), pl.ds(d.start(other + shift), d.group), :] = block[:, i * d.group : (i + 1) * d.group, :]
 
 
-def coupling_chain_kernel(d, face_ref, iface, cols, gfield, gfirst, pair_in, cross_in, folded, after, chain, ext):
+def interface_kernel(d, face_ref, iface, cols, *rest):
+    edges, inner, field, pair_in, cross_in, folded, gfield, gfirst, gpair_in, gcross_in, after = rest[:11]
+    chain, (faces_out, ext, small) = rest[11 : 11 + d.parts], rest[11 + d.parts :]
     face = face_ref[0]
     w = d.width
+    interface_rows(d, face, iface, cols, edges, inner, field, pair_in, cross_in, folded, 1, [faces_out.at[t] for t in range(d.ticks - 2)], small)
+    pair_in, cross_in = gpair_in, gcross_in
     coupling_ext(d, face, gfirst, pair_in, cross_in, ext)
-    for q in range(d.nq):
-        lanes = slice(q * w, (q + 1) * w)
-        for s in range(0, d.wide, d.group):
-            span = pl.ds(s, d.group)
-            chain[span, lanes] = sweep(d, cols, face, ext, span, iface[q], folded).astype(BF)
-        span = pl.ds(pl.multiple_of(d.start(face) + q * w, w), w)
-        chain[span, lanes] = (chain[span, lanes].astype(F32) + gfield[q].astype(F32)).astype(BF)
+    for i in range(d.slots):
+        start = i * d.group % d.part
+        part = chain[i * d.group // d.part]
+        for q in range(d.nq):
+            value = sweep(d, cols, face, ext, pl.ds(i * d.group, d.group), iface[q], folded)
+            part[start : start + d.group, q * w : (q + 1) * w] = value.astype(BF)
+
+        @pl.when(lax.rem(face, d.slots) == i)
+        def _():
+            for q in range(d.nq):
+                block = (slice(start + q * w, start + (q + 1) * w), slice(q * w, (q + 1) * w))
+                part[block] = (part[block].astype(F32) + gfield[q].astype(F32)).astype(BF)
 
 
 def coupling_last_kernel(d, face_ref, iface, cols, gfield, gfirst, pair_in, cross_in, folded, after, out, ext):
@@ -269,19 +281,22 @@
             yield jnp.concatenate([block[j] for j in range(2 * d.nq)], axis=1), start
 
 
-def chain_kernel(d, tick, face_ref, own_chain, other_chain, own_faces, other_faces, *rest):
-    arrived, sent = rest[:-1], rest[-1]
+def chain_kernel(d, tick, face_ref, *rest):
+    own_chain, other_chain, rest = rest[: d.parts], rest[d.parts : 2 * d.parts], rest[2 * d.parts :]
+    own_faces, other_faces, *arrived, sent, chain = rest
     face = face_ref[0]
     parity = lax.rem(face, 2)
+    for i in range(d.parts):
+        for j, part in enumerate((own_chain[i], other_chain[i])):
+            chain[i * d.part : (i + 1) * d.part, j * d.group : (j + 1) * d.group] = part[...]
     half = len(arrived) // 2
-    blocks = list(arrived_blocks(d, face, arrived[:half], arrived[half:]))
-    for chain, base, odd in ((own_chain, own_faces, parity), (other_chain, other_faces, 1 - parity)):
-        total = jnp.zeros((d.sources, d.group), F32)
-        for x, start in blocks:
-            total += dot_nn(x, chain[pl.ds(start, 2 * d.group), :])
+    total = jnp.zeros((d.sources, 2 * d.group), F32)
+    for x, start in arrived_blocks(d, face, arrived[:half], arrived[half:]):
+        total += dot_nn(x, chain[pl.ds(start, 2 * d.group), :])
+    for j, (base, odd) in enumerate(((own_faces, parity), (other_faces, 1 - parity))):
         for q in range(d.nq):
-            value = base[tick - 1, q].astype(F32) - total[:, q * d.width : (q + 1) * d.width]
-            sent[odd * d.nq + q] = value.astype(BF)
+            at = j * d.group + q * d.width
+            sent[odd * d.nq + q] = (base[tick - 1, q].astype(F32) - total[:, at : at + d.width]).astype(BF)
 
 
 def merge_kernel(d, face_ref, own, other, sent):
@@ -326,7 +341,7 @@
         name=name,
         out_shape=outs,
         in_specs=[pl.BlockSpec(memory_space=pltpu.SMEM)] * len(smem) + specs,
-        out_specs=[pl.BlockSpec(memory_space=place if x.dtype == BF else pltpu.SMEM) for x in outs],
+        out_specs=[pl.BlockSpec(memory_space=place if x.dtype != jnp.int32 else pltpu.SMEM) for x in outs],
         scratch_shapes=[pltpu.VMEM(s, BF) for s in scratch] + ([pltpu.SemaphoreType.DMA((sems,))] if sems else []),
         input_output_aliases=aliases or {},
         compiler_params=pltpu.CompilerParams(vmem_limit_bytes=32 * 1024 * 1024),
@@ -440,30 +455,31 @@
         [(2 * nq, sources, width)],
     )
 
-    def operator_rows():
-        (chain,) = call(
-            functools.partial(coupling_chain_kernel, d),
-            "coupling_chain",
+    def beside_first():
+        rows = call(
+            functools.partial(interface_kernel, d),
+            "interface",
             [face, iface, cols],
-            [gfield, gfirst, gpair1, gcross1, folded, sent],
-            [(wide, group)],
-            [(ext, wide, width)],
-            flops=0,
-            anywhere=(5,),
+            [edges, inner, field, pair1, cross1, folded, gfield, gfirst, gpair1, gcross1, sent],
+            [(d.part, group)] * d.parts + [(ticks - 2, nq, sources, width)],
+            [(ext, wide, width), (ext, (ticks - 2) * sources, width)],
+            anywhere=(10,),
         )
-        return chain, *call(
+        other_rows = [swap(x) for x in rows[: d.parts]]
+        (twice,) = call(
             functools.partial(third_kernel, d),
             "third",
-            [face, iface, cols],
-            [edges, inner, field, pair1, cross1, folded, chain],
-            [(count, batch, width), (ticks - 2, nq, sources, width)],
+            [face, cols],
+            [edges, inner, field, pair1, cross1, folded, rows[0]],
+            [(count, batch, width)],
             [(ext, batch, width)],
-            flops=0,
             anywhere=(6,),
         )
-
-    arrived, (chain, twice, faces_out) = onward(sent, operator_rows)
-    other_chain, other_faces = swap(chain), swap(faces_out)
+        return rows, other_rows, twice
+
+    arrived, (rows, other_chain, twice) = onward(sent, beside_first)
+    *chain, faces_out = rows
+    other_faces = swap(faces_out)
     whole = (ticks, sources, count * width)
 
     def operator():
@@ -471,7 +487,7 @@
             functools.partial(coupling_last_kernel, d),
             "coupling_last",
             [face, iface, cols],
-            [gfield, gfirst, gpair1, gcross1, folded, chain],
+            [gfield, gfirst, gpair1, gcross1, folded, chain[0]],
             [(wide, count * width)],
             [(ext, wide, width)],
             flops=wide * sweep_flops,
@@ -503,8 +519,9 @@
             functools.partial(chain_kernel, d, tick),
             "chain",
             [face],
-            [chain, other_chain, faces_out, other_faces] + arrived,
+            [*chain, *other_chain, faces_out, other_faces] + arrived,
             [(2 * nq, sources, width)],
+            [(wide, 2 * group)],
             flops=4 * sources * wide * group,
         )
         if tick == 1:

time: 58.6 us -> 58.4 us (level)
  waiting for transfers between devices: 15.8 us -> 13.4 us
  starting transfers between devices: 21.1 us -> 22.5 us
  Pallas kernels: 21.1 us -> 21.8 us
    ppermute x3, waiting for transfers between devices: 7.84 us -> 5.77 us  [onward(): own.append(lax.ppermute(block, ('slab', 'face'), route))]
    ppermute x3, starting transfers between devices: 9.01 us -> 10.2 us  [onward(): own.append(lax.ppermute(block, ('slab', 'face'), route))]
    pallas_call x14, Pallas kernels: 21.1 us -> 21.8 us  [call(): pl.pallas_call(body, name=name, out_shape=outs, in_specs=[pl.BlockSpec(me...]
    ppermute x6 -> x9, waiting for transfers between devices: 4.62 us -> 4.25 us  [swap(): return lax.ppermute(block, 'face', pairing)]
    ppermute x6 -> x9, starting transfers between devices: 2.59 us -> 2.89 us  [swap(): return lax.ppermute(block, 'face', pairing)]
  transfers between devices with their start and end apart: 15 -> 18, of which waited for: 9 -> 8; matrix products, arithmetic and copies ran while one was open for 0% -> 0% of each run, Pallas kernels for 26% -> 27%
where the time goes in v7:
time: 58.4 us; the launch traced here: 58.1 us
  starting transfers between devices  22.5 us (39%)
  Pallas kernels  21.8 us (37%)
  waiting for transfers between devices  13.4 us (23%)
    pallas_call x14, Pallas kernels, call(): pl.pallas_call(body, name=name, out_shape=outs, in_specs=[pl.BlockSpec(me...  21.8 us
    ppermute x3, starting transfers between devices, onward(): own.append(lax.ppermute(block, ('slab', 'face'), route))  10.2 us
    ppermute x3, starting transfers between devices, exchange(): got = lax.ppermute(cross, 'face', crossing)  8.59 us
    ppermute x3, waiting for transfers between devices, onward(): own.append(lax.ppermute(block, ('slab', 'face'), route))  5.77 us
    ppermute x9, waiting for transfers between devices, swap(): return lax.ppermute(block, 'face', pairing)  4.25 us
    ppermute x3, waiting for transfers between devices, exchange(): got = lax.ppermute(cross, 'face', crossing)  3.35 us
    ppermute x9, starting transfers between devices, swap(): return lax.ppermute(block, 'face', pairing)  2.89 us
  transfers between devices with their start and end apart: 18, of which 8 were waited for; matrix products, arithmetic and copies ran while one was open for 0% of the time, Pallas kernels for 27%

profile of v7, /device:TPU:9, one launch (start us, length us, event | category | flops | bytes accessed | tf_op | source)
XLA Modules:
  0.0 58.1 jit_solution(11768946358836325072)
XLA Ops:
  0.0 2.6 %first.1 = (bf16[8,512,128]{2,1,0:T(8,128)(2,1)S(1)}, bf16[2,128,128]{2,1,0:T(8,128)(2,1)S(1)}, bf16[2,672,128]{2,1,0:T(8,128)(2,1)S(1)}, bf16[2,672,128]{2,1,0:...) custom-call(s32[1]{0:T(128)} %bitcast.face_ref, ...), custom_call_target="tpu_custom_call" | custom-call | flops 134217728 | tf_op jit(solution)/shard_map/first/pallas_call | solution.py:339
  3.3 3.0 %collective-permute-start.1 = (bf16[2,672,128]{2,1,0:T(8,128)(2,1)S(1)}, bf16[2,672,128]{2,1,0:T(8,128)(2,1)S(1)}, u32[]{:S(2)}, u32[]{:S(2)}) collective-permute-start(bf16[2,672,128]{2,1,0:T(8,128)(2,1)S(1)} %get-tuple-element.49), channel_id=1, source_target_pairs={{1,2},{2,1},{5,6},{6,5},{9,10},{10,9},{13,14},{14,13},{17,18},{18,... | collective-permute-start | bytes 1032200 | tf_op jit(solution)/shard_map/ppermute | solution.py:366
  6.4 2.2 %fold.1 = (bf16[8,640,128]{2,1,0:T(8,128)(2,1)S(1)}, bf16[6,128,1024]{2,1,0:T(8,128)(2,1)S(1)}) custom-call(s32[1]{0:T(128)} %bitcast.face_ref, s32[2]{0:T(128)S(1)} %get-tuple-element.45.iface, s32[4,8]{1,0:T(4,128)S(1)} %get-tuple-element.46.cols, bf16[8,128,128]{2,1,0:T(8,128)(2,1)S(1)} %get-tuple-element.50.inv, ...), custom_call_target="tpu_custom_call" | custom-call | flops 2621440 | tf_op jit(solution)/shard_map/fold/pallas_call | solution.py:339
  8.6 3.3 %collective-permute-done.1.cross_in = bf16[2,672,128]{2,1,0:T(8,128)(2,1)S(1)} collective-permute-done((bf16[2,672,128]{2,1,0:T(8,128)(2,1)S(1)}, bf16[2,672,128]{2,1,0:T(8,128)(2,1)S(1)}, u32[]{:S(2)}, u32[]{:S(2)}) %collective-permute-start.1) | collective-permute-done | bytes 344096 | tf_op jit(solution)/shard_map/ppermute | solution.py:366
  11.9 1.5 %second_edges.1 = (bf16[4,512,128]{2,1,0:T(8,128)(2,1)S(1)}, bf16[2,512,128]{2,1,0:T(8,128)(2,1)S(1)}, bf16[2,512,128]{2,1,0:T(8,128)(2,1)S(1)}, bf16[12,512,128]{2,1,0:T(8,128)(2,1)S(1)}) custom-call(s32[1]{0:T(128)} %bitcast.face_ref, s32[4,8]{1,0:T(4,128)S(1)} %get-tuple-element.46.cols, bf16[8,512,128]{2,1,0:T(8,128)(2,1)S(1)} %get-tuple-element.47.field.rest_2_, ...), custom_call_target="tpu_custom_call" | custom-call | flops 10485760 | tf_op jit(solution)/shard_map/second_edges/pallas_call | solution.py:339
  13.5 3.0 %collective-permute-start.2 = (bf16[2,512,128]{2,1,0:T(8,128)(2,1)S(1)}, bf16[2,512,128]{2,1,0:T(8,128)(2,1)S(1)}, u32[]{:S(2)}, u32[]{:S(2)}) collective-permute-start(bf16[2,512,128]{2,1,0:T(8,128)(2,1)S(1)} %get-tuple-element.55), channel_id=1, source_target_pairs={{1,2},{2,1},{5,6},{6,5},{9,10},{10,9},{13,14},{14,13},{17,18},{18,... | collective-permute-start | bytes 786440 | tf_op jit(solution)/shard_map/ppermute | solution.py:366
  16.6 1.2 %coupling_first.1 = (bf16[8,1024,128]{2,1,0:T(8,128)(2,1)S(1)}, bf16[2,768,128]{2,1,0:T(8,128)(2,1)S(1)}, bf16[2,768,128]{2,1,0:T(8,128)(2,1)S(1)}) custom-call(s32[1]{0:T(128)} %bitcast.face_ref, s32[2]{0:T(128)S(1)} %get-tuple-element.45.iface, bf16[2,128,128]{2,1,0:T(8,128)(2,1)S(1)} %get-tuple-element.57.gfield.rest_6_, ...), custom_call_target="tpu_custom_call" | custom-call | flops 201326592 | tf_op jit(solution)/shard_map/coupling_first/pallas_call | solution.py:339
  17.9 2.5 %collective-permute-start.7 = (bf16[2,768,128]{2,1,0:T(8,128)(2,1)S(1)}, bf16[2,768,128]{2,1,0:T(8,128)(2,1)S(1)}, u32[]{:S(2)}, u32[]{:S(2)}) collective-permute-start(bf16[2,768,128]{2,1,0:T(8,128)(2,1)S(1)} %get-tuple-element.64), channel_id=1, source_target_pairs={{1,2},{2,1},{5,6},{6,5},{9,10},{10,9},{13,14},{14,13},{17,18},{18,... | collective-permute-start | bytes 1179656 | tf_op jit(solution)/shard_map/ppermute | solution.py:366
  20.4 1.4 %second_inner.1.inner.rest_1_ = bf16[4,512,128]{2,1,0:T(8,128)(2,1)S(1)} custom-call(s32[1]{0:T(128)} %bitcast.face_ref, s32[4,8]{1,0:T(4,128)S(1)} %get-tuple-element.46.cols, bf16[8,512,128]{2,1,0:T(8,128)(2,1)S(1)} %get-tuple-element.47.field.rest_2_, bf16[12,512,128]{2,1,0:T(8,128)(2,1)S(1)} %get-tuple-element.56.ext, ...), custom_call_target="tpu_custom_call" | custom-call | tf_op jit(solution)/shard_map/second_inner/pallas_call | solution.py:339
  21.8 0.8 %third_rows.1.own = bf16[2,128,128]{2,1,0:T(8,128)(2,1)S(1)} custom-call(s32[1]{0:T(128)} %bitcast.face_ref, s32[2]{0:T(128)S(1)} %get-tuple-element.45.iface, s32[4,8]{1,0:T(4,128)S(1)} %get-tuple-element.46.cols, bf16[4,512,128]{2,1,0:T(8,128)(2,1)S(1)} %get-tuple-element.54.edges.rest_0_, bf16[4,512,128]{2,1,0:T(8,128)(2,1)S(1)} %second_inner.1.inner.rest_1_, ...), custom_call_target="tpu_custom_call" | custom-call | flops 1677721600 | tf_op jit(solution)/shard_map/third_rows/pallas_call | solution.py:339
  22.7 1.2 %collective-permute-done.4.other = bf16[2,128,128]{2,1,0:T(8,128)(2,1)S(1)} collective-permute-done((bf16[2,128,128]{2,1,0:T(8,128)(2,1)S(1)}, bf16[2,128,128]{2,1,0:T(8,128)(2,1)S(1)}, u32[]{:S(2)}, u32[]{:S(2)}) %collective-permute-start.4) | collective-permute-done | bytes 65568 | tf_op jit(solution)/shard_map/ppermute | solution.py:370
  24.0 3.8 %collective-permute-start.5 = (bf16[4,128,128]{2,1,0:T(8,128)(2,1)S(1)}, bf16[4,128,128]{2,1,0:T(8,128)(2,1)S(1)}, u32[]{:S(2)}, u32[]{:S(2)}) collective-permute-start(bf16[4,128,128]{2,1,0:T(8,128)(2,1)S(1)} %merge.1.rest_10_), channel_id=1, source_target_pairs={{0,4},{3,5},{2,6},{1,7},{4,8},{7,9},{6,10},{5,11},{8,12},{11,13},{... | collective-permute-start | bytes 393224 | tf_op jit(solution)/shard_map/ppermute | solution.py:382
  27.8 2.4 %interface.1 = (bf16[256,256]{1,0:T(8,128)(2,1)S(1)}, bf16[256,256]{1,0:T(8,128)(2,1)S(1)}, bf16[256,256]{1,0:T(8,128)(2,1)S(1)}, bf16[256,256]{1,0:T(8,128)(2,1)S(1)}, bf16[2,2,128,128]{3,2,1,0:T(8,128)(2,1)S(1)}) custom-call(s32[1]{0:T(128)} %bitcast.face_ref, s32[2]{0:T(128)S(1)} %get-tuple-element.45.iface, s32[4,8]{1,0:T(4,128)S(1)} %get-tuple-element.46.cols, ...), custom_call_target="tpu_custom_call" | custom-call | tf_op jit(solution)/shard_map/interface/pallas_call | solution.py:339
  31.3 2.2 %third.1.fields = bf16[8,512,128]{2,1,0:T(8,128)(2,1)S(1)} custom-call(s32[1]{0:T(128)} %bitcast.face_ref, s32[4,8]{1,0:T(4,128)S(1)} %get-tuple-element.46.cols, bf16[4,512,128]{2,1,0:T(8,128)(2,1)S(1)} %get-tuple-element.54.edges.rest_0_, bf16[4,512,128]{2,1,0:T(8,128)(2,1)S(1)} %second_inner.1.inner.rest_1_, ...), custom_call_target="tpu_custom_call" | custom-call | tf_op jit(solution)/shard_map/third/pallas_call | solution.py:339
  34.1 0.8 %collective-permute-done.12.rest_9_ = bf16[2,2,128,128]{3,2,1,0:T(8,128)(2,1)S(1)} collective-permute-done((bf16[2,2,128,128]{3,2,1,0:T(8,128)(2,1)S(1)}, bf16[2,2,128,128]{3,2,1,0:T(8,128)(2,1)S(1)}, u32[]{:S(2)}, u32[]{:S(2)}) %collective-permute-start.12) | collective-permute-done | bytes 131104 | tf_op jit(solution)/shard_map/ppermute | solution.py:370
  35.5 3.8 %collective-permute-start.14 = (bf16[4,128,128]{2,1,0:T(8,128)(2,1)S(1)}, bf16[4,128,128]{2,1,0:T(8,128)(2,1)S(1)}, u32[]{:S(2)}, u32[]{:S(2)}) collective-permute-start(bf16[4,128,128]{2,1,0:T(8,128)(2,1)S(1)} %chain.2), channel_id=1, source_target_pairs={{0,4},{3,5},{2,6},{1,7},{4,8},{7,9},{6,10},{5,11},{8,12},{11,13},{... | collective-permute-start | bytes 393224 | tf_op jit(solution)/shard_map/ppermute | solution.py:382
  39.3 3.8 %coupling_last.1.coupled = bf16[1024,1024]{1,0:T(8,128)(2,1)S(1)} custom-call(s32[1]{0:T(128)} %bitcast.face_ref, s32[2]{0:T(128)S(1)} %get-tuple-element.45.iface, s32[4,8]{1,0:T(4,128)S(1)} %get-tuple-element.46.cols, bf16[2,128,128]{2,1,0:T(8,128)(2,1)S(1)} %get-tuple-element.57.gfield.rest_6_, ...), custom_call_target="tpu_custom_call" | custom-call | flops 1342177280 | tf_op jit(solution)/shard_map/coupling_last/pallas_call | solution.py:339
  43.1 1.3 %collective-permute-done.14.rest_10_.rest_2_ = bf16[4,128,128]{2,1,0:T(8,128)(2,1)S(1)} collective-permute-done((bf16[4,128,128]{2,1,0:T(8,128)(2,1)S(1)}, bf16[4,128,128]{2,1,0:T(8,128)(2,1)S(1)}, u32[]{:S(2)}, u32[]{:S(2)}) %collective-permute-start.14) | collective-permute-done | bytes 131104 | tf_op jit(solution)/shard_map/ppermute | solution.py:382
  45.0 1.0 %collective-permute-done.15.rest_11_.rest_3_ = bf16[4,128,128]{2,1,0:T(8,128)(2,1)S(1)} collective-permute-done((bf16[4,128,128]{2,1,0:T(8,128)(2,1)S(1)}, bf16[4,128,128]{2,1,0:T(8,128)(2,1)S(1)}, u32[]{:S(2)}, u32[]{:S(2)}) %collective-permute-start.15) | collective-permute-done | bytes 131104 | tf_op jit(solution)/shard_map/ppermute | solution.py:370
  46.3 2.6 %collective-permute-start.16 = (bf16[4,128,128]{2,1,0:T(8,128)(2,1)S(1)}, bf16[4,128,128]{2,1,0:T(8,128)(2,1)S(1)}, u32[]{:S(2)}, u32[]{:S(2)}) collective-permute-start(bf16[4,128,128]{2,1,0:T(8,128)(2,1)S(1)} %chain.3), channel_id=1, source_target_pairs={{0,4},{3,5},{2,6},{1,7},{4,8},{7,9},{6,10},{5,11},{8,12},{11,13},{... | collective-permute-start | bytes 393224 | tf_op jit(solution)/shard_map/ppermute | solution.py:382
  49.0 1.7 %output.2.rest_0_ = bf16[4,128,1024]{2,1,0:T(8,128)(2,1)} custom-call(s32[1]{0:T(128)} %bitcast.face_ref, bf16[8,512,128]{2,1,0:T(8,128)(2,1)S(1)} %third.1.fields, bf16[1024,1024]{1,0:T(8,128)(2,1)S(1)} %coupling_last.1.coupled, bf16[4,128,128]{2,1,0:T(8,128)(2,1)S(1)} %collective-permute-done.5.rest_10_.rest_0_, ...), custom_call_target="tpu_custom_call" | custom-call | flops 805306368 | tf_op jit(solution)/shard_map/output/pallas_call | solution.py:339
  50.7 4.5 %collective-permute-done.16.rest_1_ = bf16[4,128,128]{2,1,0:T(8,128)(2,1)S(1)} collective-permute-done((bf16[4,128,128]{2,1,0:T(8,128)(2,1)S(1)}, bf16[4,128,128]{2,1,0:T(8,128)(2,1)S(1)}, u32[]{:S(2)}, u32[]{:S(2)}) %collective-permute-start.16) | collective-permute-done | bytes 131104 | tf_op jit(solution)/shard_map/ppermute | solution.py:382
  55.8 1.0 %collective-permute-done.17.rest_2_ = bf16[4,128,128]{2,1,0:T(8,128)(2,1)S(1)} collective-permute-done((bf16[4,128,128]{2,1,0:T(8,128)(2,1)S(1)}, bf16[4,128,128]{2,1,0:T(8,128)(2,1)S(1)}, u32[]{:S(2)}, u32[]{:S(2)}) %collective-permute-start.17) | collective-permute-done | bytes 131104 | tf_op jit(solution)/shard_map/ppermute | solution.py:370
  56.8 1.2 %output.3 = bf16[4,128,1024]{2,1,0:T(8,128)(2,1)} custom-call(s32[1]{0:T(128)} %bitcast.face_ref, bf16[8,512,128]{2,1,0:T(8,128)(2,1)S(1)} %third.1.fields, bf16[1024,1024]{1,0:T(8,128)(2,1)S(1)} %coupling_last.1.coupled, bf16[4,128,1024]{2,1,0:T(8,128)(2,1)} %output.2.rest_0_, ...), custom_call_target="tpu_custom_call", output_to_operand_aliasing={{}: (3, {})} | custom-call | flops 268435456 | tf_op jit(solution)/shard_map/output/pallas_call | solution.py:339
  (26 shorter events, 4.8 us)
Async XLA Ops:
  2.6 5.9 %collective-permute-start = (bf16[2,672,128]{2,1,0:T(8,128)(2,1)S(1)}, bf16[2,672,128]{2,1,0:T(8,128)(2,1)S(1)}, u32[]{:S(2)}, u32[]{:S(2)}) collective-permute-start(bf16[2,672,128]{2,1,0:T(8,128)(2,1)S(1)} %get-tuple-element.48), channel_id=1, source_target_pairs={{0,1},{1,0},{2,3},{3,2},{4,5},{5,4},{6,7},{7,6},{8,9},{9,8},{10,11... | collective-permute-start | bytes 1032200 | tf_op jit(solution)/shard_map/ppermute | solution.py:367
  3.3 8.6 %collective-permute-start.1 = (bf16[2,672,128]{2,1,0:T(8,128)(2,1)S(1)}, bf16[2,672,128]{2,1,0:T(8,128)(2,1)S(1)}, u32[]{:S(2)}, u32[]{:S(2)}) collective-permute-start(bf16[2,672,128]{2,1,0:T(8,128)(2,1)S(1)} %get-tuple-element.49), channel_id=1, source_target_pairs={{1,2},{2,1},{5,6},{6,5},{9,10},{10,9},{13,14},{14,13},{17,18},{18,... | collective-permute-start | bytes 1032200 | tf_op jit(solution)/shard_map/ppermute | solution.py:366
  13.4 3.1 %collective-permute-start.3 = (bf16[2,512,128]{2,1,0:T(8,128)(2,1)S(1)}, bf16[2,512,128]{2,1,0:T(8,128)(2,1)S(1)}, u32[]{:S(2)}, u32[]{:S(2)}) collective-permute-start(bf16[2,512,128]{2,1,0:T(8,128)(2,1)S(1)} %get-tuple-element.59), channel_id=1, source_target_pairs={{0,1},{1,0},{2,3},{3,2},{4,5},{5,4},{6,7},{7,6},{8,9},{9,8},{10,11... | collective-permute-start | bytes 786440 | tf_op jit(solution)/shard_map/ppermute | solution.py:367
  13.5 8.3 %collective-permute-start.2 = (bf16[2,512,128]{2,1,0:T(8,128)(2,1)S(1)}, bf16[2,512,128]{2,1,0:T(8,128)(2,1)S(1)}, u32[]{:S(2)}, u32[]{:S(2)}) collective-permute-start(bf16[2,512,128]{2,1,0:T(8,128)(2,1)S(1)} %get-tuple-element.55), channel_id=1, source_target_pairs={{1,2},{2,1},{5,6},{6,5},{9,10},{10,9},{13,14},{14,13},{17,18},{18,... | collective-permute-start | bytes 786440 | tf_op jit(solution)/shard_map/ppermute | solution.py:366
  17.8 10.0 %collective-permute-start.6 = (bf16[2,768,128]{2,1,0:T(8,128)(2,1)S(1)}, bf16[2,768,128]{2,1,0:T(8,128)(2,1)S(1)}, u32[]{:S(2)}, u32[]{:S(2)}) collective-permute-start(bf16[2,768,128]{2,1,0:T(8,128)(2,1)S(1)} %get-tuple-element.63), channel_id=1, source_target_pairs={{0,1},{1,0},{2,3},{3,2},{4,5},{5,4},{6,7},{7,6},{8,9},{9,8},{10,11... | collective-permute-start | bytes 1179656 | tf_op jit(solution)/shard_map/ppermute | solution.py:367
  17.9 9.9 %collective-permute-start.7 = (bf16[2,768,128]{2,1,0:T(8,128)(2,1)S(1)}, bf16[2,768,128]{2,1,0:T(8,128)(2,1)S(1)}, u32[]{:S(2)}, u32[]{:S(2)}) collective-permute-start(bf16[2,768,128]{2,1,0:T(8,128)(2,1)S(1)} %get-tuple-element.64), channel_id=1, source_target_pairs={{1,2},{2,1},{5,6},{6,5},{9,10},{10,9},{13,14},{14,13},{17,18},{18,... | collective-permute-start | bytes 1179656 | tf_op jit(solution)/shard_map/ppermute | solution.py:366
  22.6 1.3 %collective-permute-start.4 = (bf16[2,128,128]{2,1,0:T(8,128)(2,1)S(1)}, bf16[2,128,128]{2,1,0:T(8,128)(2,1)S(1)}, u32[]{:S(2)}, u32[]{:S(2)}) collective-permute-start(bf16[2,128,128]{2,1,0:T(8,128)(2,1)S(1)} %third_rows.1.own), channel_id=1, source_target_pairs={{0,1},{1,0},{2,3},{3,2},{4,5},{5,4},{6,7},{7,6},{8,9},{9,8},{10,11... | collective-permute-start | bytes 196616 | tf_op jit(solution)/shard_map/ppermute | solution.py:370
  24.0 9.5 %collective-permute-start.5 = (bf16[4,128,128]{2,1,0:T(8,128)(2,1)S(1)}, bf16[4,128,128]{2,1,0:T(8,128)(2,1)S(1)}, u32[]{:S(2)}, u32[]{:S(2)}) collective-permute-start(bf16[4,128,128]{2,1,0:T(8,128)(2,1)S(1)} %merge.1.rest_10_), channel_id=1, source_target_pairs={{0,4},{3,5},{2,6},{1,7},{4,8},{7,9},{6,10},{5,11},{8,12},{11,13},{... | collective-permute-start | bytes 393224 | tf_op jit(solution)/shard_map/ppermute | solution.py:382
  30.2 3.3 %collective-permute-start.9 = (bf16[256,256]{1,0:T(8,128)(2,1)S(1)}, bf16[256,256]{1,0:T(8,128)(2,1)S(1)}, u32[]{:S(2)}, u32[]{:S(2)}) collective-permute-start(bf16[256,256]{1,0:T(8,128)(2,1)S(1)} %get-tuple-element.72.rest_1_), channel_id=1, source_target_pairs={{0,1},{1,0},{2,3},{3,2},{4,5},{5,4},{6,7},{7,6},{8,9},{9,8},{10,11... | collective-permute-start | bytes 393224 | tf_op jit(solution)/shard_map/ppermute | solution.py:370
  30.2 3.2 %collective-permute-start.10 = (bf16[256,256]{1,0:T(8,128)(2,1)S(1)}, bf16[256,256]{1,0:T(8,128)(2,1)S(1)}, u32[]{:S(2)}, u32[]{:S(2)}) collective-permute-start(bf16[256,256]{1,0:T(8,128)(2,1)S(1)} %get-tuple-element.73.rest_2_), channel_id=1, source_target_pairs={{0,1},{1,0},{2,3},{3,2},{4,5},{5,4},{6,7},{7,6},{8,9},{9,8},{10,11... | collective-permute-start | bytes 393224 | tf_op jit(solution)/shard_map/ppermute | solution.py:370
  30.7 2.8 %collective-permute-start.11 = (bf16[256,256]{1,0:T(8,128)(2,1)S(1)}, bf16[256,256]{1,0:T(8,128)(2,1)S(1)}, u32[]{:S(2)}, u32[]{:S(2)}) collective-permute-start(bf16[256,256]{1,0:T(8,128)(2,1)S(1)} %get-tuple-element.74.rest_3_), channel_id=1, source_target_pairs={{0,1},{1,0},{2,3},{3,2},{4,5},{5,4},{6,7},{7,6},{8,9},{9,8},{10,11... | collective-permute-start | bytes 393224 | tf_op jit(solution)/shard_map/ppermute | solution.py:370
  30.8 2.7 %collective-permute-start.8 = (bf16[256,256]{1,0:T(8,128)(2,1)S(1)}, bf16[256,256]{1,0:T(8,128)(2,1)S(1)}, u32[]{:S(2)}, u32[]{:S(2)}) collective-permute-start(bf16[256,256]{1,0:T(8,128)(2,1)S(1)} %get-tuple-element.71.after.rest_0_), channel_id=1, source_target_pairs={{0,1},{1,0},{2,3},{3,2},{4,5},{5,4},{6,7},{7,6},{8,9},{9,8},{10,11... | collective-permute-start | bytes 393224 | tf_op jit(solution)/shard_map/ppermute | solution.py:370
  33.5 1.4 %collective-permute-start.12 = (bf16[2,2,128,128]{3,2,1,0:T(8,128)(2,1)S(1)}, bf16[2,2,128,128]{3,2,1,0:T(8,128)(2,1)S(1)}, u32[]{:S(2)}, u32[]{:S(2)}) collective-permute-start(bf16[2,2,128,128]{3,2,1,0:T(8,128)(2,1)S(1)} %get-tuple-element.79.rest_8_), channel_id=1, source_target_pairs={{0,1},{1,0},{2,3},{3,2},{4,5},{5,4},{6,7},{7,6},{8,9},{9,8},{10,11... | collective-permute-start | bytes 393224 | tf_op jit(solution)/shard_map/ppermute | solution.py:370
  33.7 1.5 %collective-permute-start.13 = (bf16[4,128,128]{2,1,0:T(8,128)(2,1)S(1)}, bf16[4,128,128]{2,1,0:T(8,128)(2,1)S(1)}, u32[]{:S(2)}, u32[]{:S(2)}) collective-permute-start(bf16[4,128,128]{2,1,0:T(8,128)(2,1)S(1)} %collective-permute-done.5.rest_10_.rest_0_), channel_id=1, source_target_pairs={{0,1},{1,0},{2,3},{3,2},{4,5},{5,4},{6,7},{7,6},{8,9},{9,8},{10,11... | collective-permute-start | bytes 393224 | tf_op jit(solution)/shard_map/ppermute | solution.py:370
  35.5 8.9 %collective-permute-start.14 = (bf16[4,128,128]{2,1,0:T(8,128)(2,1)S(1)}, bf16[4,128,128]{2,1,0:T(8,128)(2,1)S(1)}, u32[]{:S(2)}, u32[]{:S(2)}) collective-permute-start(bf16[4,128,128]{2,1,0:T(8,128)(2,1)S(1)} %chain.2), channel_id=1, source_target_pairs={{0,4},{3,5},{2,6},{1,7},{4,8},{7,9},{6,10},{5,11},{8,12},{11,13},{... | collective-permute-start | bytes 393224 | tf_op jit(solution)/shard_map/ppermute | solution.py:382
  44.4 1.6 %collective-permute-start.15 = (bf16[4,128,128]{2,1,0:T(8,128)(2,1)S(1)}, bf16[4,128,128]{2,1,0:T(8,128)(2,1)S(1)}, u32[]{:S(2)}, u32[]{:S(2)}) collective-permute-start(bf16[4,128,128]{2,1,0:T(8,128)(2,1)S(1)} %collective-permute-done.14.rest_10_.rest_2_), channel_id=1, source_target_pairs={{0,1},{1,0},{2,3},{3,2},{4,5},{5,4},{6,7},{7,6},{8,9},{9,8},{10,11... | collective-permute-start | bytes 393224 | tf_op jit(solution)/shard_map/ppermute | solution.py:370
  46.3 8.8 %collective-permute-start.16 = (bf16[4,128,128]{2,1,0:T(8,128)(2,1)S(1)}, bf16[4,128,128]{2,1,0:T(8,128)(2,1)S(1)}, u32[]{:S(2)}, u32[]{:S(2)}) collective-permute-start(bf16[4,128,128]{2,1,0:T(8,128)(2,1)S(1)} %chain.3), channel_id=1, source_target_pairs={{0,4},{3,5},{2,6},{1,7},{4,8},{7,9},{6,10},{5,11},{8,12},{11,13},{... | collective-permute-start | bytes 393224 | tf_op jit(solution)/shard_map/ppermute | solution.py:382
  55.2 1.6 %collective-permute-start.17 = (bf16[4,128,128]{2,1,0:T(8,128)(2,1)S(1)}, bf16[4,128,128]{2,1,0:T(8,128)(2,1)S(1)}, u32[]{:S(2)}, u32[]{:S(2)}) collective-permute-start(bf16[4,128,128]{2,1,0:T(8,128)(2,1)S(1)} %collective-permute-done.16.rest_1_), channel_id=1, source_target_pairs={{0,1},{1,0},{2,3},{3,2},{4,5},{5,4},{6,7},{7,6},{8,9},{9,8},{10,11... | collective-permute-start | bytes 393224 | tf_op jit(solution)/shard_map/ppermute | solution.py:370

commit v8 on v7

--- a/solution.py
+++ b/solution.py
@@ -25,7 +25,8 @@
     def __init__(self, ticks, sources, count, neigh, width, nq, faces):
         self.ticks, self.sources, self.count, self.neigh = ticks, sources, count, neigh
         self.width, self.nq, self.faces = width, nq, faces
-        self.batch = ticks * sources
+        self.split = max(ticks // 2, 1)
+        self.early, self.later = self.split * sources, (ticks - self.split) * sources
         self.group = nq * width
         self.ext = count + 2 * HALO
         self.depth = (1 + neigh) * width
@@ -35,7 +36,7 @@
         self.part = self.wide // self.parts
         self.mark = 16
         self.share = -(-nq // HALO) * width
-        self.first_rows = self.batch + self.share + nq * self.mark
+        self.first_rows = self.later + self.share + nq * self.mark
         self.last = count - HALO
         self.up = count + HALO
 
@@ -44,6 +45,11 @@
 
     def first_col(self, face):
         return face * self.count - HALO
+
+
+def spans(rows):
+    parts = -(-rows // 256)
+    return [pl.ds(i * (rows // parts), rows // parts) for i in range(parts)]
 
 
 def edge_rows(d, parity):
@@ -53,7 +59,7 @@
 def first_kernel(
     d, face_ref, iface_hbm, cols_hbm, inflow, coupling, inv, rhs, diag_hbm, off_hbm, *rest
 ):
-    field, gfield, pair, cross, tiles, diag, off, iface, cols, right, flow, couple, sems = rest
+    early, later, gfield, *buffers, tiles, diag, off, iface, cols, right, flow, couple, sems = rest
     w = d.width
     moves = [(iface_hbm, iface), (inflow, flow), (coupling, couple), (inv, tiles)]
     moves += [(rhs.at[t], right.at[t]) for t in range(d.ticks)]
@@ -72,17 +78,21 @@
         copy.wait()
     for r in range(d.count):
         x = jnp.concatenate([right[t, :, r * w : (r + 1) * w] for t in range(d.ticks)], axis=0)
-        field[r] = dot_nt(x, tiles[r]).astype(BF)
+        value = dot_nt(x, tiles[r]).astype(BF)
+        early[r] = value[: d.early]
+        later[r] = value[d.early :]
     for q in range(d.nq):
         row = iface[q]
         corrected = right[0, :, pl.ds(pl.multiple_of(row * w, w), w)].astype(F32) - coupled[q]
-        field[row, 0 : d.sources, :] = dot_nt(corrected.astype(BF), tiles[row]).astype(BF)
-    for start, buffer in zip(edge_rows(d, lax.rem(face_ref[0], 2)), (pair, cross)):
-        buffer[:, 0 : d.batch, :] = field[pl.ds(start, HALO)]
+        early[row, 0 : d.sources, :] = dot_nt(corrected.astype(BF), tiles[row]).astype(BF)
+    for i, start in enumerate(edge_rows(d, lax.rem(face_ref[0], 2))):
+        buffers[i][...] = early[pl.ds(start, HALO)]
+        buffer = buffers[2 + i]
+        buffer[:, 0 : d.later, :] = later[pl.ds(start, HALO)]
         for q in range(d.nq):
-            at = d.batch + q // HALO * w
+            at = d.later + q // HALO * w
             buffer[q % HALO, at : at + w, :] = gfield[q]
-            at = d.batch + d.share + q * d.mark
+            at = d.later + d.share + q * d.mark
             for e in range(HALO):
                 buffer[e, at : at + d.mark, :] = jnp.full((d.mark, w), iface[q] == start + e).astype(F32).astype(BF)
     for copy in copies[4 + d.ticks :]:
@@ -137,20 +147,23 @@
     place_halo(d, face, pair_in, cross_in, ext, rows)
 
 
-def correct(d, cols, face, base, folded, out, ext, rows, first=0):
+def correct(d, cols, face, base, folded, out, ext, rows):
     for i, r in enumerate(rows):
-        for s in range(0, d.batch, d.group):
-            span = pl.ds(s, d.group)
+        for span in spans(out.shape[1]):
             value = base[r, span, :].astype(F32) + sweep(d, cols, face, ext, span, r, folded)
-            out[first + i, span, :] = value.astype(BF)
+            out[i, span, :] = value.astype(BF)
+
+
+def correct_edges(d, cols, face, field, pair_in, cross_in, folded, edges, ext):
+    ext[HALO : HALO + d.count] = field[...]
+    place_halo(d, face, pair_in, cross_in, ext, pl.ds(0, field.shape[1]))
+    correct(d, cols, face, field, folded, edges, ext, list(range(HALO)) + list(range(d.last, d.count)))
 
 
 def second_edges_kernel(d, face_ref, cols, field, pair_in, cross_in, folded, edges, pair, cross, ext):
     face = face_ref[0]
-    ext[HALO : HALO + d.count] = field[...]
-    place_halo(d, face, pair_in, cross_in, ext, pl.ds(0, d.batch))
-    correct(d, cols, face, field, folded, edges, ext, list(range(HALO)) + list(range(d.last, d.count)))
     parity = lax.rem(face, 2)
+    correct_edges(d, cols, face, field, pair_in, cross_in, folded, edges, ext)
     pair[...] = edges[pl.ds(HALO * (1 - parity), HALO)]
     cross[...] = edges[pl.ds(HALO * parity, HALO)]
 
@@ -174,25 +187,33 @@
     interface_rows(d, face_ref[0], iface, cols, edges, inner, field, pair_in, cross_in, folded, 0, [sent], ext)
 
 
-def third_kernel(d, face_ref, cols, edges, inner, field, pair_in, cross_in, folded, after, out, ext):
-    face = face_ref[0]
-    extend(d, face, edges, inner, pair_in, cross_in, ext, pl.ds(0, d.batch))
-    correct(d, cols, face, field, folded, out, ext, range(d.count))
+def third_kernel(d, face_ref, cols, *rest):
+    *inputs, folded, after, early, later, early_ext, later_ext = rest
+    face = face_ref[0]
+    for i, (out, ext) in enumerate(((early, early_ext), (later, later_ext))):
+        edges, inner, field, pair_in, cross_in = inputs[5 * i : 5 * i + 5]
+        extend(d, face, edges, inner, pair_in, cross_in, ext, pl.ds(0, out.shape[1]))
+        correct(d, cols, face, field, folded, out, ext, range(d.count))
 
 
 def marked(d, block, e):
     parts = []
     for q in range(d.nq):
-        at = d.batch + q // HALO * d.width
-        mark = d.batch + d.share + q * d.mark
+        at = d.later + q // HALO * d.width
+        mark = d.later + d.share + q * d.mark
         mark = block[e, mark : mark + d.mark, :]
         parts.append(block[q % HALO, at : at + d.width, :] * jnp.concatenate([mark] * (d.width // d.mark), axis=0))
     return jnp.concatenate(parts, axis=0)
 
 
-def coupling_first_kernel(d, face_ref, iface, gfield, pair_in, cross_in, met, after, out, pair, cross):
+def behind_kernel(
+    d, face_ref, iface, cols, field, gfield, pair_in, cross_in, met, folded, after, edges, out, pair, cross, field_ext
+):
     face = face_ref[0]
     parity = lax.rem(face, 2)
+    correct_edges(d, cols, face, field, pair_in, cross_in, folded, edges, field_ext)
+    pair[:, 0 : d.later, :] = edges[pl.ds(HALO * (1 - parity), HALO)]
+    cross[:, 0 : d.later, :] = edges[pl.ds(HALO * parity, HALO)]
     w = d.width
     for shift in range(2, d.slots - 1):
         out[:, pl.ds(d.start(face + shift), d.group), :] = jnp.zeros((d.count, d.group, w), BF)
@@ -214,7 +235,8 @@
         out[row, span, :] = (out[row, span, :].astype(F32) + gfield[q].astype(F32)).astype(BF)
     for start, buffer in zip(edge_rows(d, parity), (pair, cross)):
         for i, shift in enumerate((-1, 0, 1)):
-            buffer[:, i * d.group : (i + 1) * d.group, :] = out[pl.ds(start, HALO), pl.ds(d.start(face + shift), d.group), :]
+            at = d.later + i * d.group
+            buffer[:, at : at + d.group, :] = out[pl.ds(start, HALO), pl.ds(d.start(face + shift), d.group), :]
 
 
 def coupling_ext(d, face, gfirst, pair_in, cross_in, ext):
@@ -225,16 +247,22 @@
     neighbours = ((d.up * (1 - parity), face + 1 - 2 * parity, pair_in), (d.up * parity, face - 1 + 2 * parity, cross_in))
     for start, other, block in neighbours:
         for i, shift in enumerate((-1, 0, 1)):
-            ext[pl.ds(start, HALO), pl.ds(d.start(other + shift), d.group), :] = block[:, i * d.group : (i + 1) * d.group, :]
+            at = d.later + i * d.group
+            ext[pl.ds(start, HALO), pl.ds(d.start(other + shift), d.group), :] = block[:, at : at + d.group, :]
 
 
 def interface_kernel(d, face_ref, iface, cols, *rest):
-    edges, inner, field, pair_in, cross_in, folded, gfield, gfirst, gpair_in, gcross_in, after = rest[:11]
-    chain, (faces_out, ext, small) = rest[11 : 11 + d.parts], rest[11 + d.parts :]
+    early, (edges, field, field_ext, pair_in, cross_in, folded, gfield, gfirst, after) = rest[:5], rest[5:14]
+    chain, (faces_out, inner, ext, small) = rest[14 : 14 + d.parts], rest[14 + d.parts :]
     face = face_ref[0]
     w = d.width
-    interface_rows(d, face, iface, cols, edges, inner, field, pair_in, cross_in, folded, 1, [faces_out.at[t] for t in range(d.ticks - 2)], small)
-    pair_in, cross_in = gpair_in, gcross_in
+    correct(d, cols, face, field, folded, inner, field_ext, range(HALO, d.last))
+    later = (edges, inner, field, pair_in, cross_in)
+    for group, first, last, shift in ((early, 1, d.split, 0), (later, d.split, d.ticks - 1, d.split)):
+        outs = [faces_out.at[t - 1] for t in range(first, last)]
+        if outs:
+            held = small.at[:, pl.ds(0, len(outs) * d.sources), :]
+            interface_rows(d, face, iface, cols, *group, folded, first - shift, outs, held)
     coupling_ext(d, face, gfirst, pair_in, cross_in, ext)
     for i in range(d.slots):
         start = i * d.group % d.part
@@ -306,7 +334,7 @@
         sent[(1 - parity) * d.nq + q] = other[q]
 
 
-def output_kernel(d, ticks, face_ref, fields, coupled, *rest):
+def output_kernel(d, ticks, face_ref, early, later, coupled, *rest):
     *arrived, out, held, sems = rest
     w = d.width
     face = face_ref[0]
@@ -324,7 +352,8 @@
             for x, start in blocks:
                 total += dot_nn(x, coupled[pl.ds(start, 2 * d.group), c : c + part])
             for j in range(0, part, w):
-                value = fields[(c + j) // w, t * d.sources : (t + 1) * d.sources, :].astype(F32)
+                fields, at = (early, t) if t < d.split else (later, t - d.split)
+                value = fields[(c + j) // w, at * d.sources : (at + 1) * d.sources, :].astype(F32)
                 held[i, :, c + j : c + j + w] = (value - total[:, j : j + w]).astype(BF)
             here = held.at[i, :, c : c + part]
             copies.append(pltpu.make_async_copy(here, out.at[t, :, c : c + part], sems.at[len(copies)]))
@@ -385,67 +414,68 @@
             *own, made = lax.optimization_barrier((*own, made))
         return own + [swap(x) for x in own], made
 
-    batch, group, ext, wide = d.batch, d.group, d.ext, d.wide
+    early, later, group, ext, wide = d.early, d.later, d.group, d.ext, d.wide
     sweep_flops = 2 * count * tile * (neigh + 1)
     ints = [jax.ShapeDtypeStruct(x.shape, x.dtype) for x in (iface, cols)]
     on_hbm = (iface, cols, inflow[0], couple, inv, rhs[:, 0], diag, off)
-    field, gfield, pair, cross, inv, diag, off, iface, cols = call(
+    field, field_later, gfield, pair, cross, pair_later, cross_later, inv, diag, off, iface, cols = call(
         functools.partial(first_kernel, d),
         "first",
         [face],
         [pltpu.with_memory_space_constraint(x, pltpu.HBM) for x in on_hbm],
-        [(count, batch, width), (nq, width, width)] + [(HALO, d.first_rows, width)] * 2 + [x.shape for x in (inv, diag, off)] + ints,
+        [(count, early, width), (count, later, width), (nq, width, width)]
+        + [(HALO, early, width)] * 2
+        + [(HALO, d.first_rows, width)] * 2
+        + [x.shape for x in (inv, diag, off)]
+        + ints,
         [(ticks, sources, count * width), (sources, group), (nq, width, width)],
-        flops=2 * batch * count * tile,
         anywhere=range(8),
         sems=7 + ticks,
     )
     pair0, cross0 = exchange(pair, cross)
+    pair_later0, cross_later0 = exchange(pair_later, cross_later)
     folded, met = call(
         functools.partial(fold_kernel, d),
         "fold",
         [face, iface, cols],
         [inv, diag, off],
         [(count, d.depth, width), (2 * HALO + nq, width, count * width)],
-        flops=width * sweep_flops // 64,
     )
     edges, pair, cross, ext0 = call(
         functools.partial(second_edges_kernel, d),
         "second_edges",
         [face, cols],
         [field, pair0, cross0, folded],
-        [(2 * HALO, batch, width)] + [(HALO, batch, width)] * 2 + [(ext, batch, width)],
-        flops=batch * sweep_flops // 64,
+        [(2 * HALO, early, width)] + [(HALO, early, width)] * 2 + [(ext, early, width)],
     )
     pair1, cross1 = exchange(pair, cross)
-    gfirst, gpair, gcross = call(
-        functools.partial(coupling_first_kernel, d),
-        "coupling_first",
-        [face, iface],
-        [gfield, pair0, cross0, met, pair1],
-        [(count, wide, width)] + [(HALO, 3 * group, width)] * 2,
-        flops=2 * (2 * HALO + nq) * width * count * tile,
-        anywhere=(4,),
-    )
-    gpair1, gcross1 = exchange(gpair, gcross)
+    edges_later, gfirst, pair, cross, ext_later0 = call(
+        functools.partial(behind_kernel, d),
+        "behind",
+        [face, iface, cols],
+        [field_later, gfield, pair_later0, cross_later0, met, folded, pair1],
+        [(2 * HALO, later, width), (count, wide, width)] + [(HALO, later + 3 * group, width)] * 2 + [(ext, later, width)],
+        anywhere=(6,),
+    )
+    pair_later1, cross_later1 = exchange(pair, cross)
     (inner,) = call(
         functools.partial(second_inner_kernel, d),
         "second_inner",
         [face, cols],
         [field, ext0, folded, gfirst],
-        [(count - 2 * HALO, batch, width)],
-        flops=0,
+        [(count - 2 * HALO, early, width)],
         anywhere=(3,),
     )
     cross1, inner = lax.optimization_barrier((cross1, inner))
+    early_parts = (edges, inner, field, pair1, cross1)
     (own_first,) = call(
         functools.partial(third_rows_kernel, d),
         "third_rows",
         [face, iface, cols],
-        [edges, inner, field, pair1, cross1, folded],
+        [*early_parts, folded],
         [(nq, sources, width)],
         [(ext, sources, width)],
-        flops=batch * sweep_flops * 5 // 2,
+        flops=12 * early * sweep_flops,
     )
     (sent,) = call(
         functools.partial(merge_kernel, d),
@@ -456,30 +486,31 @@
     )
 
     def beside_first():
-        rows = call(
+        *rows, faces_out, inner_later = call(
             functools.partial(interface_kernel, d),
             "interface",
             [face, iface, cols],
-            [edges, inner, field, pair1, cross1, folded, gfield, gfirst, gpair1, gcross1, sent],
-            [(d.part, group)] * d.parts + [(ticks - 2, nq, sources, width)],
-            [(ext, wide, width), (ext, (ticks - 2) * sources, width)],
-            anywhere=(10,),
+            [*early_parts, edges_later, field_later, ext_later0, pair_later1, cross_later1, folded, gfield, gfirst, sent],
+            [(d.part, group)] * d.parts + [(ticks - 2, nq, sources, width), (count - 2 * HALO, later, width)],
+            [(ext, wide, width), (ext, max(early, later), width)],
+            anywhere=(13,),
         )
-        other_rows = [swap(x) for x in rows[: d.parts]]
-        (twice,) = call(
+        return rows, [swap(x) for x in rows], faces_out, inner_later
+
+    arrived, (chain, other_chain, faces_out, inner_later) = onward(sent, beside_first)
+    other_faces = swap(faces_out)
+
+    def fields(after):
+        return call(
             functools.partial(third_kernel, d),
             "third",
             [face, cols],
-            [edges, inner, field, pair1, cross1, folded, rows[0]],
-            [(count, batch, width)],
-            [(ext, batch, width)],
-            anywhere=(6,),
+            [*early_parts, edges_later, inner_later, field_later, pair_later1, cross_later1, folded, after],
+            [(count, early, width), (count, later, width)],
+            [(ext, early, width), (ext, later, width)],
+            anywhere=(11,),
         )
-        return rows, other_rows, twice
-
-    arrived, (rows, other_chain, twice) = onward(sent, beside_first)
-    *chain, faces_out = rows
-    other_faces = swap(faces_out)
+
     whole = (ticks, sources, count * width)
 
     def operator():
@@ -487,7 +518,7 @@
             functools.partial(coupling_last_kernel, d),
             "coupling_last",
             [face, iface, cols],
-            [gfield, gfirst, gpair1, gcross1, folded, chain[0]],
+            [gfield, gfirst, pair_later1, cross_later1, folded, chain[0]],
             [(wide, count * width)],
             [(ext, wide, width)],
             flops=wide * sweep_flops,
@@ -499,14 +530,14 @@
             functools.partial(output_kernel, d, which),
             "output",
             [face],
-            [twice, coupled] + earlier + blocks,
+            [*twice, coupled] + earlier + blocks,
             [whole],
             [(len(which), sources, count * width)],
             flops=2 * len(which) * sources * wide * count * width,
-            anywhere=(2,) if earlier else (),
+            anywhere=(3,) if earlier else (),
             sems=len(which) * count,
             place=pl.ANY,
-            aliases={3: 0} if earlier else None,
+            aliases={4: 0} if earlier else None,
         )[0]
 
     everything = []
@@ -527,6 +558,7 @@
         if tick == 1:
             arrived, coupled = onward(sent, operator)
         else:
+            twice = fields(sent)
             arrived, most = onward(sent, lambda: output(tuple(range(ticks - 1)), everything, []))
     out = output((ticks - 1,), arrived, [most])
     return out[:, None]

time: 58.4 us -> 57.4 us (0.983)
  waiting for transfers between devices: 13.4 us -> 10.5 us
  starting transfers between devices: 22.5 us -> 24.3 us
    ppermute x3 -> x4, starting transfers between devices: 8.59 us -> 11.1 us  [exchange(): got = lax.ppermute(cross, 'face', crossing)]
    ppermute x3 -> x4, waiting for transfers between devices: 3.35 us -> 0.99 us  [exchange(): got = lax.ppermute(cross, 'face', crossing)]
    ppermute x3, waiting for transfers between devices: 5.77 us -> 3.96 us  [onward(): own.append(lax.ppermute(block, ('slab', 'face'), route))]
    ppermute x9, waiting for transfers between devices: 4.25 us -> 5.5 us  [swap(): return lax.ppermute(block, 'face', pairing)]
  transfers between devices with their start and end apart: 18 -> 20, of which waited for: 8 -> 13; matrix products, arithmetic and copies ran while one was open for 0% -> 0% of each run, Pallas kernels for 27% -> 30%
where the time goes in v8:
time: 57.4 us; the launch traced here: 57.1 us
  starting transfers between devices  24.3 us (42%)
  Pallas kernels  21.9 us (38%)
  waiting for transfers between devices  10.5 us (18%)
    pallas_call x14, Pallas kernels, call(): pl.pallas_call(body, name=name, out_shape=outs, in_specs=[pl.BlockSpec(me...  21.9 us
    ppermute x4, starting transfers between devices, exchange(): got = lax.ppermute(cross, 'face', crossing)  11.1 us
    ppermute x3, starting transfers between devices, onward(): own.append(lax.ppermute(block, ('slab', 'face'), route))  9.79 us
    ppermute x9, waiting for transfers between devices, swap(): return lax.ppermute(block, 'face', pairing)  5.5 us
    ppermute x3, waiting for transfers between devices, onward(): own.append(lax.ppermute(block, ('slab', 'face'), route))  3.96 us
    ppermute x9, starting transfers between devices, swap(): return lax.ppermute(block, 'face', pairing)  2.46 us
  transfers between devices with their start and end apart: 20, of which 13 were waited for; matrix products, arithmetic and copies ran while one was open for 0% of the time, Pallas kernels for 30%

profile of v8, /device:TPU:9, one launch (start us, length us, event | category | flops | bytes accessed | tf_op | source)
XLA Modules:
  0.0 57.1 jit_solution(565415746571111357)
XLA Ops:
  0.0 2.6 %first.1 = (bf16[8,256,128]{2,1,0:T(8,128)(2,1)S(1)}, bf16[8,256,128]{2,1,0:T(8,128)(2,1)S(1)}, bf16[2,128,128]{2,1,0:T(8,128)(2,1)S(1)}, bf16[2,256,128]{2,1,0:...) custom-call(s32[1]{0:T(128)} %bitcast.face_ref, ...), custom_call_target="tpu_custom_call" | custom-call | tf_op jit(solution)/shard_map/first/pallas_call | solution.py:368
  3.4 3.0 %collective-permute-start.1 = (bf16[2,256,128]{2,1,0:T(8,128)(2,1)S(1)}, bf16[2,256,128]{2,1,0:T(8,128)(2,1)S(1)}, u32[]{:S(2)}, u32[]{:S(2)}) collective-permute-start(bf16[2,256,128]{2,1,0:T(8,128)(2,1)S(1)} %get-tuple-element.56), channel_id=1, source_target_pairs={{1,2},{2,1},{5,6},{6,5},{9,10},{10,9},{13,14},{14,13},{17,18},{18,... | collective-permute-start | bytes 393224 | tf_op jit(solution)/shard_map/ppermute | solution.py:395
  6.5 2.5 %collective-permute-start.4 = (bf16[2,416,128]{2,1,0:T(8,128)(2,1)S(1)}, bf16[2,416,128]{2,1,0:T(8,128)(2,1)S(1)}, u32[]{:S(2)}, u32[]{:S(2)}) collective-permute-start(bf16[2,416,128]{2,1,0:T(8,128)(2,1)S(1)} %get-tuple-element.68), channel_id=1, source_target_pairs={{1,2},{2,1},{5,6},{6,5},{9,10},{10,9},{13,14},{14,13},{17,18},{18,... | collective-permute-start | bytes 638984 | tf_op jit(solution)/shard_map/ppermute | solution.py:395
  9.0 2.2 %fold.1 = (bf16[8,640,128]{2,1,0:T(8,128)(2,1)S(1)}, bf16[6,128,1024]{2,1,0:T(8,128)(2,1)S(1)}) custom-call(s32[1]{0:T(128)} %bitcast.face_ref, s32[2]{0:T(128)S(1)} %get-tuple-element.57.iface, s32[4,8]{1,0:T(4,128)S(1)} %get-tuple-element.53.cols, bf16[8,128,128]{2,1,0:T(8,128)(2,1)S(1)} %get-tuple-element.58.inv, ...), custom_call_target="tpu_custom_call" | custom-call | tf_op jit(solution)/shard_map/fold/pallas_call | solution.py:368
  11.2 1.1 %second_edges.1 = (bf16[4,256,128]{2,1,0:T(8,128)(2,1)S(1)}, bf16[2,256,128]{2,1,0:T(8,128)(2,1)S(1)}, bf16[2,256,128]{2,1,0:T(8,128)(2,1)S(1)}, bf16[12,256,128]{2,1,0:T(8,128)(2,1)S(1)}) custom-call(s32[1]{0:T(128)} %bitcast.face_ref, s32[4,8]{1,0:T(4,128)S(1)} %get-tuple-element.53.cols, bf16[8,256,128]{2,1,0:T(8,128)(2,1)S(1)} %get-tuple-element.54.field.rest_2_, ...), custom_call_target="tpu_custom_call" | custom-call | tf_op jit(solution)/shard_map/second_edges/pallas_call | solution.py:368
  12.4 3.0 %collective-permute-start.2 = (bf16[2,256,128]{2,1,0:T(8,128)(2,1)S(1)}, bf16[2,256,128]{2,1,0:T(8,128)(2,1)S(1)}, u32[]{:S(2)}, u32[]{:S(2)}) collective-permute-start(bf16[2,256,128]{2,1,0:T(8,128)(2,1)S(1)} %get-tuple-element.63), channel_id=1, source_target_pairs={{1,2},{2,1},{5,6},{6,5},{9,10},{10,9},{13,14},{14,13},{17,18},{18,... | collective-permute-start | bytes 393224 | tf_op jit(solution)/shard_map/ppermute | solution.py:395
  15.5 1.7 %behind.1 = (bf16[4,256,128]{2,1,0:T(8,128)(2,1)S(1)}, bf16[8,1024,128]{2,1,0:T(8,128)(2,1)S(1)}, bf16[2,1024,128]{2,1,0:T(8,128)(2,1)S(1)}, bf16[2,1024,128]{2,1,0:T(8,128)(2,1)S(1)}, bf16[12,256,128]{2,1,0:T(8,128)(2,1)S(1)}) custom-call(s32[1]{0:T(128)} %bitcast.face_ref, s32[2]{0:T(128)S(1)} %get-tuple-element.57.iface, ...), custom_call_target="tpu_custom_call" | custom-call | tf_op jit(solution)/shard_map/behind/pallas_call | solution.py:368
  17.3 2.5 %collective-permute-start.9 = (bf16[2,1024,128]{2,1,0:T(8,128)(2,1)S(1)}, bf16[2,1024,128]{2,1,0:T(8,128)(2,1)S(1)}, u32[]{:S(2)}, u32[]{:S(2)}) collective-permute-start(bf16[2,1024,128]{2,1,0:T(8,128)(2,1)S(1)} %get-tuple-element.77), channel_id=1, source_target_pairs={{1,2},{2,1},{5,6},{6,5},{9,10},{10,9},{13,14},{14,13},{17,18},{18,... | collective-permute-start | bytes 1572872 | tf_op jit(solution)/shard_map/ppermute | solution.py:395
  19.8 1.1 %second_inner.1.inner.rest_1_ = bf16[4,256,128]{2,1,0:T(8,128)(2,1)S(1)} custom-call(s32[1]{0:T(128)} %bitcast.face_ref, s32[4,8]{1,0:T(4,128)S(1)} %get-tuple-element.53.cols, bf16[8,256,128]{2,1,0:T(8,128)(2,1)S(1)} %get-tuple-element.54.field.rest_2_, bf16[12,256,128]{2,1,0:T(8,128)(2,1)S(1)} %get-tuple-element.64.ext, ...), custom_call_target="tpu_custom_call" | custom-call | tf_op jit(solution)/shard_map/second_inner/pallas_call | solution.py:368
  21.8 1.2 %collective-permute-done.6.other = bf16[2,128,128]{2,1,0:T(8,128)(2,1)S(1)} collective-permute-done((bf16[2,128,128]{2,1,0:T(8,128)(2,1)S(1)}, bf16[2,128,128]{2,1,0:T(8,128)(2,1)S(1)}, u32[]{:S(2)}, u32[]{:S(2)}) %collective-permute-start.6) | collective-permute-done | bytes 65568 | tf_op jit(solution)/shard_map/ppermute | solution.py:399
  23.1 3.7 %collective-permute-start.7 = (bf16[4,128,128]{2,1,0:T(8,128)(2,1)S(1)}, bf16[4,128,128]{2,1,0:T(8,128)(2,1)S(1)}, u32[]{:S(2)}, u32[]{:S(2)}) collective-permute-start(bf16[4,128,128]{2,1,0:T(8,128)(2,1)S(1)} %merge.1.rest_13_), channel_id=1, source_target_pairs={{0,4},{3,5},{2,6},{1,7},{4,8},{7,9},{6,10},{5,11},{8,12},{11,13},{... | collective-permute-start | bytes 393224 | tf_op jit(solution)/shard_map/ppermute | solution.py:411
  26.8 1.0 %collective-permute-done.9.rest_9_.cross_in = bf16[2,1024,128]{2,1,0:T(8,128)(2,1)S(1)} collective-permute-done((bf16[2,1024,128]{2,1,0:T(8,128)(2,1)S(1)}, bf16[2,1024,128]{2,1,0:T(8,128)(2,1)S(1)}, u32[]{:S(2)}, u32[]{:S(2)}) %collective-permute-start.9) | collective-permute-done | bytes 524320 | tf_op jit(solution)/shard_map/ppermute | solution.py:395
  27.8 2.8 %interface.1 = (bf16[256,256]{1,0:T(8,128)(2,1)S(1)}, bf16[256,256]{1,0:T(8,128)(2,1)S(1)}, bf16[256,256]{1,0:T(8,128)(2,1)S(1)}, bf16[256,256]{1,0:T(8,128)(2,1...) custom-call(s32[1]{0:T(128)} %bitcast.face_ref, s32[2]{0:T(128)S(1)} %get-tuple-element.57.iface, ...), custom_call_target="tpu_custom_call" | custom-call | tf_op jit(solution)/shard_map/interface/pallas_call | solution.py:368
  33.2 0.8 %collective-permute-done.14.rest_9_ = bf16[2,2,128,128]{3,2,1,0:T(8,128)(2,1)S(1)} collective-permute-done((bf16[2,2,128,128]{3,2,1,0:T(8,128)(2,1)S(1)}, bf16[2,2,128,128]{3,2,1,0:T(8,128)(2,1)S(1)}, u32[]{:S(2)}, u32[]{:S(2)}) %collective-permute-start.14) | collective-permute-done | bytes 131104 | tf_op jit(solution)/shard_map/ppermute | solution.py:399
  34.8 3.3 %collective-permute-start.16 = (bf16[4,128,128]{2,1,0:T(8,128)(2,1)S(1)}, bf16[4,128,128]{2,1,0:T(8,128)(2,1)S(1)}, u32[]{:S(2)}, u32[]{:S(2)}) collective-permute-start(bf16[4,128,128]{2,1,0:T(8,128)(2,1)S(1)} %chain.2), channel_id=1, source_target_pairs={{0,4},{3,5},{2,6},{1,7},{4,8},{7,9},{6,10},{5,11},{8,12},{11,13},{... | collective-permute-start | bytes 393224 | tf_op jit(solution)/shard_map/ppermute | solution.py:411
  38.0 3.8 %coupling_last.1.coupled = bf16[1024,1024]{1,0:T(8,128)(2,1)S(1)} custom-call(s32[1]{0:T(128)} %bitcast.face_ref, s32[2]{0:T(128)S(1)} %get-tuple-element.57.iface, s32[4,8]{1,0:T(4,128)S(1)} %get-tuple-element.53.cols, bf16[2,128,128]{2,1,0:T(8,128)(2,1)S(1)} %get-tuple-element.66.gfield.rest_11_, ...), custom_call_target="tpu_custom_call" | custom-call | flops 1342177280 | tf_op jit(solution)/shard_map/coupling_last/pallas_call | solution.py:368
  41.9 1.8 %collective-permute-done.16.rest_10_.rest_2_ = bf16[4,128,128]{2,1,0:T(8,128)(2,1)S(1)} collective-permute-done((bf16[4,128,128]{2,1,0:T(8,128)(2,1)S(1)}, bf16[4,128,128]{2,1,0:T(8,128)(2,1)S(1)}, u32[]{:S(2)}, u32[]{:S(2)}) %collective-permute-start.16) | collective-permute-done | bytes 131104 | tf_op jit(solution)/shard_map/ppermute | solution.py:411
  43.8 1.2 %collective-permute-done.17.rest_11_.rest_3_ = bf16[4,128,128]{2,1,0:T(8,128)(2,1)S(1)} collective-permute-done((bf16[4,128,128]{2,1,0:T(8,128)(2,1)S(1)}, bf16[4,128,128]{2,1,0:T(8,128)(2,1)S(1)}, u32[]{:S(2)}, u32[]{:S(2)}) %collective-permute-start.17) | collective-permute-done | bytes 131104 | tf_op jit(solution)/shard_map/ppermute | solution.py:399
  45.4 2.8 %collective-permute-start.18 = (bf16[4,128,128]{2,1,0:T(8,128)(2,1)S(1)}, bf16[4,128,128]{2,1,0:T(8,128)(2,1)S(1)}, u32[]{:S(2)}, u32[]{:S(2)}) collective-permute-start(bf16[4,128,128]{2,1,0:T(8,128)(2,1)S(1)} %chain.3.rest_11_), channel_id=1, source_target_pairs={{0,4},{3,5},{2,6},{1,7},{4,8},{7,9},{6,10},{5,11},{8,12},{11,13},{... | collective-permute-start | bytes 393224 | tf_op jit(solution)/shard_map/ppermute | solution.py:411
  48.2 2.2 %third.1 = (bf16[8,256,128]{2,1,0:T(8,128)(2,1)S(1)}, bf16[8,256,128]{2,1,0:T(8,128)(2,1)S(1)}) custom-call(s32[1]{0:T(128)} %bitcast.face_ref, s32[4,8]{1,0:T(4,128)S(1)} %get-tuple-element.53.cols, bf16[4,256,128]{2,1,0:T(8,128)(2,1)S(1)} %get-tuple-element.62.edges.rest_0_, bf16[4,256,128]{2,1,0:T(8,128)(2,1)S(1)} %second_inner.1.inner.rest_1_, ...), custom_call_target="tpu_custom_call" | custom-call | tf_op jit(solution)/shard_map/third/pallas_call | solution.py:368
  50.4 1.7 %output.2.rest_0_ = bf16[4,128,1024]{2,1,0:T(8,128)(2,1)} custom-call(s32[1]{0:T(128)} %bitcast.face_ref, bf16[8,256,128]{2,1,0:T(8,128)(2,1)S(1)} %get-tuple-element.96.early, bf16[8,256,128]{2,1,0:T(8,128)(2,1)S(1)} %get-tuple-element.97.later, bf16[1024,1024]{1,0:T(8,128)(2,1)S(1)} %coupling_last.1.coupled, ...), custom_call_target="tpu_custom_call" | custom-call | flops 805306368 | tf_op jit(solution)/shard_map/output/pallas_call | solution.py:368
  52.1 2.1 %collective-permute-done.18.rest_1_ = bf16[4,128,128]{2,1,0:T(8,128)(2,1)S(1)} collective-permute-done((bf16[4,128,128]{2,1,0:T(8,128)(2,1)S(1)}, bf16[4,128,128]{2,1,0:T(8,128)(2,1)S(1)}, u32[]{:S(2)}, u32[]{:S(2)}) %collective-permute-start.18) | collective-permute-done | bytes 131104 | tf_op jit(solution)/shard_map/ppermute | solution.py:411
  54.8 1.0 %collective-permute-done.19.rest_2_ = bf16[4,128,128]{2,1,0:T(8,128)(2,1)S(1)} collective-permute-done((bf16[4,128,128]{2,1,0:T(8,128)(2,1)S(1)}, bf16[4,128,128]{2,1,0:T(8,128)(2,1)S(1)}, u32[]{:S(2)}, u32[]{:S(2)}) %collective-permute-start.19) | collective-permute-done | bytes 131104 | tf_op jit(solution)/shard_map/ppermute | solution.py:399
  55.8 1.2 %output.3 = bf16[4,128,1024]{2,1,0:T(8,128)(2,1)} custom-call(s32[1]{0:T(128)} %bitcast.face_ref, bf16[8,256,128]{2,1,0:T(8,128)(2,1)S(1)} %get-tuple-element.96.early, bf16[8,256,128]{2,1,0:T(8,128)(2,1)S(1)} %get-tuple-element.97.later, bf16[1024,1024]{1,0:T(8,128)(2,1)S(1)} %coupling_last.1.coupled, ...), custom_call_target="tpu_custom_call", output_to_operand_aliasing={{}: (4, {})} | custom-call | flops 268435456 | tf_op jit(solution)/shard_map/output/pallas_call | solution.py:368
  (30 shorter events, 6.4 us)
Async XLA Ops:
  2.6 8.6 %collective-permute-start = (bf16[2,256,128]{2,1,0:T(8,128)(2,1)S(1)}, bf16[2,256,128]{2,1,0:T(8,128)(2,1)S(1)}, u32[]{:S(2)}, u32[]{:S(2)}) collective-permute-start(bf16[2,256,128]{2,1,0:T(8,128)(2,1)S(1)} %get-tuple-element.55), channel_id=1, source_target_pairs={{0,1},{1,0},{2,3},{3,2},{4,5},{5,4},{6,7},{7,6},{8,9},{9,8},{10,11... | collective-permute-start | bytes 393224 | tf_op jit(solution)/shard_map/ppermute | solution.py:396
  3.4 7.8 %collective-permute-start.1 = (bf16[2,256,128]{2,1,0:T(8,128)(2,1)S(1)}, bf16[2,256,128]{2,1,0:T(8,128)(2,1)S(1)}, u32[]{:S(2)}, u32[]{:S(2)}) collective-permute-start(bf16[2,256,128]{2,1,0:T(8,128)(2,1)S(1)} %get-tuple-element.56), channel_id=1, source_target_pairs={{1,2},{2,1},{5,6},{6,5},{9,10},{10,9},{13,14},{14,13},{17,18},{18,... | collective-permute-start | bytes 393224 | tf_op jit(solution)/shard_map/ppermute | solution.py:395
  6.4 9.1 %collective-permute-start.3 = (bf16[2,416,128]{2,1,0:T(8,128)(2,1)S(1)}, bf16[2,416,128]{2,1,0:T(8,128)(2,1)S(1)}, u32[]{:S(2)}, u32[]{:S(2)}) collective-permute-start(bf16[2,416,128]{2,1,0:T(8,128)(2,1)S(1)} %get-tuple-element.67), channel_id=1, source_target_pairs={{0,1},{1,0},{2,3},{3,2},{4,5},{5,4},{6,7},{7,6},{8,9},{9,8},{10,11... | collective-permute-start | bytes 638984 | tf_op jit(solution)/shard_map/ppermute | solution.py:396
  6.5 9.0 %collective-permute-start.4 = (bf16[2,416,128]{2,1,0:T(8,128)(2,1)S(1)}, bf16[2,416,128]{2,1,0:T(8,128)(2,1)S(1)}, u32[]{:S(2)}, u32[]{:S(2)}) collective-permute-start(bf16[2,416,128]{2,1,0:T(8,128)(2,1)S(1)} %get-tuple-element.68), channel_id=1, source_target_pairs={{1,2},{2,1},{5,6},{6,5},{9,10},{10,9},{13,14},{14,13},{17,18},{18,... | collective-permute-start | bytes 638984 | tf_op jit(solution)/shard_map/ppermute | solution.py:395
  12.3 3.2 %collective-permute-start.5 = (bf16[2,256,128]{2,1,0:T(8,128)(2,1)S(1)}, bf16[2,256,128]{2,1,0:T(8,128)(2,1)S(1)}, u32[]{:S(2)}, u32[]{:S(2)}) collective-permute-start(bf16[2,256,128]{2,1,0:T(8,128)(2,1)S(1)} %get-tuple-element.70), channel_id=1, source_target_pairs={{0,1},{1,0},{2,3},{3,2},{4,5},{5,4},{6,7},{7,6},{8,9},{9,8},{10,11... | collective-permute-start | bytes 393224 | tf_op jit(solution)/shard_map/ppermute | solution.py:396
  12.4 8.5 %collective-permute-start.2 = (bf16[2,256,128]{2,1,0:T(8,128)(2,1)S(1)}, bf16[2,256,128]{2,1,0:T(8,128)(2,1)S(1)}, u32[]{:S(2)}, u32[]{:S(2)}) collective-permute-start(bf16[2,256,128]{2,1,0:T(8,128)(2,1)S(1)} %get-tuple-element.63), channel_id=1, source_target_pairs={{1,2},{2,1},{5,6},{6,5},{9,10},{10,9},{13,14},{14,13},{17,18},{18,... | collective-permute-start | bytes 393224 | tf_op jit(solution)/shard_map/ppermute | solution.py:395
  17.2 9.6 %collective-permute-start.8 = (bf16[2,1024,128]{2,1,0:T(8,128)(2,1)S(1)}, bf16[2,1024,128]{2,1,0:T(8,128)(2,1)S(1)}, u32[]{:S(2)}, u32[]{:S(2)}) collective-permute-start(bf16[2,1024,128]{2,1,0:T(8,128)(2,1)S(1)} %get-tuple-element.76), channel_id=1, source_target_pairs={{0,1},{1,0},{2,3},{3,2},{4,5},{5,4},{6,7},{7,6},{8,9},{9,8},{10,11... | collective-permute-start | bytes 1572872 | tf_op jit(solution)/shard_map/ppermute | solution.py:396
  17.3 10.5 %collective-permute-start.9 = (bf16[2,1024,128]{2,1,0:T(8,128)(2,1)S(1)}, bf16[2,1024,128]{2,1,0:T(8,128)(2,1)S(1)}, u32[]{:S(2)}, u32[]{:S(2)}) collective-permute-start(bf16[2,1024,128]{2,1,0:T(8,128)(2,1)S(1)} %get-tuple-element.77), channel_id=1, source_target_pairs={{1,2},{2,1},{5,6},{6,5},{9,10},{10,9},{13,14},{14,13},{17,18},{18,... | collective-permute-start | bytes 1572872 | tf_op jit(solution)/shard_map/ppermute | solution.py:395
  21.7 1.3 %collective-permute-start.6 = (bf16[2,128,128]{2,1,0:T(8,128)(2,1)S(1)}, bf16[2,128,128]{2,1,0:T(8,128)(2,1)S(1)}, u32[]{:S(2)}, u32[]{:S(2)}) collective-permute-start(bf16[2,128,128]{2,1,0:T(8,128)(2,1)S(1)} %third_rows.1.own), channel_id=1, source_target_pairs={{0,1},{1,0},{2,3},{3,2},{4,5},{5,4},{6,7},{7,6},{8,9},{9,8},{10,11... | collective-permute-start | bytes 196616 | tf_op jit(solution)/shard_map/ppermute | solution.py:399
  23.1 8.7 %collective-permute-start.7 = (bf16[4,128,128]{2,1,0:T(8,128)(2,1)S(1)}, bf16[4,128,128]{2,1,0:T(8,128)(2,1)S(1)}, u32[]{:S(2)}, u32[]{:S(2)}) collective-permute-start(bf16[4,128,128]{2,1,0:T(8,128)(2,1)S(1)} %merge.1.rest_13_), channel_id=1, source_target_pairs={{0,4},{3,5},{2,6},{1,7},{4,8},{7,9},{6,10},{5,11},{8,12},{11,13},{... | collective-permute-start | bytes 393224 | tf_op jit(solution)/shard_map/ppermute | solution.py:411
  30.6 1.4 %collective-permute-start.10 = (bf16[256,256]{1,0:T(8,128)(2,1)S(1)}, bf16[256,256]{1,0:T(8,128)(2,1)S(1)}, u32[]{:S(2)}, u32[]{:S(2)}) collective-permute-start(bf16[256,256]{1,0:T(8,128)(2,1)S(1)} %get-tuple-element.85.rest_0_.after), channel_id=1, source_target_pairs={{0,1},{1,0},{2,3},{3,2},{4,5},{5,4},{6,7},{7,6},{8,9},{9,8},{10,11... | collective-permute-start | bytes 393224 | tf_op jit(solution)/shard_map/ppermute | solution.py:399
  30.7 1.5 %collective-permute-start.11 = (bf16[256,256]{1,0:T(8,128)(2,1)S(1)}, bf16[256,256]{1,0:T(8,128)(2,1)S(1)}, u32[]{:S(2)}, u32[]{:S(2)}) collective-permute-start(bf16[256,256]{1,0:T(8,128)(2,1)S(1)} %get-tuple-element.86.rest_1_), channel_id=1, source_target_pairs={{0,1},{1,0},{2,3},{3,2},{4,5},{5,4},{6,7},{7,6},{8,9},{9,8},{10,11... | collective-permute-start | bytes 393224 | tf_op jit(solution)/shard_map/ppermute | solution.py:399
  31.1 1.3 %collective-permute-start.12 = (bf16[256,256]{1,0:T(8,128)(2,1)S(1)}, bf16[256,256]{1,0:T(8,128)(2,1)S(1)}, u32[]{:S(2)}, u32[]{:S(2)}) collective-permute-start(bf16[256,256]{1,0:T(8,128)(2,1)S(1)} %get-tuple-element.87.rest_2_), channel_id=1, source_target_pairs={{0,1},{1,0},{2,3},{3,2},{4,5},{5,4},{6,7},{7,6},{8,9},{9,8},{10,11... | collective-permute-start | bytes 393224 | tf_op jit(solution)/shard_map/ppermute | solution.py:399
  31.2 1.5 %collective-permute-start.13 = (bf16[256,256]{1,0:T(8,128)(2,1)S(1)}, bf16[256,256]{1,0:T(8,128)(2,1)S(1)}, u32[]{:S(2)}, u32[]{:S(2)}) collective-permute-start(bf16[256,256]{1,0:T(8,128)(2,1)S(1)} %get-tuple-element.88.rest_3_), channel_id=1, source_target_pairs={{0,1},{1,0},{2,3},{3,2},{4,5},{5,4},{6,7},{7,6},{8,9},{9,8},{10,11... | collective-permute-start | bytes 393224 | tf_op jit(solution)/shard_map/ppermute | solution.py:399
  32.7 1.3 %collective-permute-start.14 = (bf16[2,2,128,128]{3,2,1,0:T(8,128)(2,1)S(1)}, bf16[2,2,128,128]{3,2,1,0:T(8,128)(2,1)S(1)}, u32[]{:S(2)}, u32[]{:S(2)}) collective-permute-start(bf16[2,2,128,128]{3,2,1,0:T(8,128)(2,1)S(1)} %get-tuple-element.93.rest_8_), channel_id=1, source_target_pairs={{0,1},{1,0},{2,3},{3,2},{4,5},{5,4},{6,7},{7,6},{8,9},{9,8},{10,11... | collective-permute-start | bytes 393224 | tf_op jit(solution)/shard_map/ppermute | solution.py:399
  33.0 1.3 %collective-permute-start.15 = (bf16[4,128,128]{2,1,0:T(8,128)(2,1)S(1)}, bf16[4,128,128]{2,1,0:T(8,128)(2,1)S(1)}, u32[]{:S(2)}, u32[]{:S(2)}) collective-permute-start(bf16[4,128,128]{2,1,0:T(8,128)(2,1)S(1)} %collective-permute-done.7.rest_10_.rest_0_), channel_id=1, source_target_pairs={{0,1},{1,0},{2,3},{3,2},{4,5},{5,4},{6,7},{7,6},{8,9},{9,8},{10,11... | collective-permute-start | bytes 393224 | tf_op jit(solution)/shard_map/ppermute | solution.py:399
  34.8 8.9 %collective-permute-start.16 = (bf16[4,128,128]{2,1,0:T(8,128)(2,1)S(1)}, bf16[4,128,128]{2,1,0:T(8,128)(2,1)S(1)}, u32[]{:S(2)}, u32[]{:S(2)}) collective-permute-start(bf16[4,128,128]{2,1,0:T(8,128)(2,1)S(1)} %chain.2), channel_id=1, source_target_pairs={{0,4},{3,5},{2,6},{1,7},{4,8},{7,9},{6,10},{5,11},{8,12},{11,13},{... | collective-permute-start | bytes 393224 | tf_op jit(solution)/shard_map/ppermute | solution.py:411
  43.6 1.3 %collective-permute-start.17 = (bf16[4,128,128]{2,1,0:T(8,128)(2,1)S(1)}, bf16[4,128,128]{2,1,0:T(8,128)(2,1)S(1)}, u32[]{:S(2)}, u32[]{:S(2)}) collective-permute-start(bf16[4,128,128]{2,1,0:T(8,128)(2,1)S(1)} %collective-permute-done.16.rest_10_.rest_2_), channel_id=1, source_target_pairs={{0,1},{1,0},{2,3},{3,2},{4,5},{5,4},{6,7},{7,6},{8,9},{9,8},{10,11... | collective-permute-start | bytes 393224 | tf_op jit(solution)/shard_map/ppermute | solution.py:399
  45.4 8.8 %collective-permute-start.18 = (bf16[4,128,128]{2,1,0:T(8,128)(2,1)S(1)}, bf16[4,128,128]{2,1,0:T(8,128)(2,1)S(1)}, u32[]{:S(2)}, u32[]{:S(2)}) collective-permute-start(bf16[4,128,128]{2,1,0:T(8,128)(2,1)S(1)} %chain.3.rest_11_), channel_id=1, source_target_pairs={{0,4},{3,5},{2,6},{1,7},{4,8},{7,9},{6,10},{5,11},{8,12},{11,13},{... | collective-permute-start | bytes 393224 | tf_op jit(solution)/shard_map/ppermute | solution.py:411
  54.2 1.6 %collective-permute-start.19 = (bf16[4,128,128]{2,1,0:T(8,128)(2,1)S(1)}, bf16[4,128,128]{2,1,0:T(8,128)(2,1)S(1)}, u32[]{:S(2)}, u32[]{:S(2)}) collective-permute-start(bf16[4,128,128]{2,1,0:T(8,128)(2,1)S(1)} %collective-permute-done.18.rest_1_), channel_id=1, source_target_pairs={{0,1},{1,0},{2,3},{3,2},{4,5},{5,4},{6,7},{7,6},{8,9},{9,8},{10,11... | collective-permute-start | bytes 393224 | tf_op jit(solution)/shard_map/ppermute | solution.py:399

commit v9 on v8

--- a/solution.py
+++ b/solution.py
@@ -334,30 +334,58 @@
         sent[(1 - parity) * d.nq + q] = other[q]
 
 
-def output_kernel(d, ticks, face_ref, early, later, coupled, *rest):
+def tick_rows(d, early, later, tick, row):
+    fields, at = (early, tick) if tick < d.split else (later, tick - d.split)
+    return fields[row, at * d.sources : (at + 1) * d.sources, :].astype(F32)
+
+
+def output_kernel(d, face_ref, early, later, coupled, *rest):
     *arrived, out, held, sems = rest
     w = d.width
-    face = face_ref[0]
     each = 2 * len(chip_hops(d.faces))
     copies = []
-    arrived = arrived[len(arrived) % each :]
     part = 2 * w
-    for i, t in enumerate(ticks):
+    for t in range(d.ticks - 1):
         blocks = []
         if t:
             mine, arrived = arrived[:each], arrived[each:]
-            blocks = list(arrived_blocks(d, face, mine[: each // 2], mine[each // 2 :]))
+            blocks = list(arrived_blocks(d, face_ref[0], mine[: each // 2], mine[each // 2 :]))
         for c in range(0, d.count * w, part):
             total = jnp.zeros((d.sources, part), F32)
             for x, start in blocks:
                 total += dot_nn(x, coupled[pl.ds(start, 2 * d.group), c : c + part])
             for j in range(0, part, w):
-                fields, at = (early, t) if t < d.split else (later, t - d.split)
-                value = fields[(c + j) // w, at * d.sources : (at + 1) * d.sources, :].astype(F32)
-                held[i, :, c + j : c + j + w] = (value - total[:, j : j + w]).astype(BF)
-            here = held.at[i, :, c : c + part]
-            copies.append(pltpu.make_async_copy(here, out.at[t, :, c : c + part], sems.at[len(copies)]))
-            copies[-1].start()
+                value = tick_rows(d, early, later, t, (c + j) // w) - total[:, j : j + w]
+                held[t, :, c + j : c + j + w] = value.astype(BF)
+        copies.append(pltpu.make_async_copy(held.at[t], out.at[t], sems.at[t]))
+        copies[-1].start()
+    for copy in copies:
+        copy.wait()
+
+
+def last_own_kernel(d, face_ref, early, later, coupled, *rest):
+    own, out = rest[:-1], rest[-1]
+    w = d.width
+    total = jnp.zeros((d.sources, d.count * w), F32)
+    for x, start in list(arrived_blocks(d, face_ref[0], own, own))[0::2]:
+        total += dot_nn(x, coupled[pl.ds(start, 2 * d.group), :])
+    for r in range(d.count):
+        out[:, r * w : (r + 1) * w] = tick_rows(d, early, later, d.ticks - 1, r) - total[:, r * w : (r + 1) * w]
+
+
+def last_other_kernel(d, face_ref, own_part, coupled, earlier, *rest):
+    other, (out, held, sems) = rest[:-3], rest[-3:]
+    blocks = list(arrived_blocks(d, face_ref[0], other, other))[1::2]
+    part = 2 * d.width
+    copies = []
+    for i, c in enumerate(range(0, d.count * d.width, part)):
+        total = own_part[:, c : c + part]
+        for x, start in blocks:
+            total -= dot_nn(x, coupled[pl.ds(start, 2 * d.group), c : c + part])
+        held[:, c : c + part] = total.astype(BF)
+        here = held.at[:, c : c + part]
+        copies.append(pltpu.make_async_copy(here, out.at[d.ticks - 1, :, c : c + part], sems.at[i]))
+        copies[-1].start()
     for copy in copies:
         copy.wait()
 
@@ -433,7 +461,6 @@
         sems=7 + ticks,
     )
     pair0, cross0 = exchange(pair, cross)
-    pair_later0, cross_later0 = exchange(pair_later, cross_later)
     folded, met = call(
         functools.partial(fold_kernel, d),
         "fold",
@@ -441,12 +468,15 @@
         [inv, diag, off],
         [(count, d.depth, width), (2 * HALO + nq, width, count * width)],
     )
+    pair_later, cross_later, folded = lax.optimization_barrier((pair_later, cross_later, folded))
+    pair_later0, cross_later0 = exchange(pair_later, cross_later)
     edges, pair, cross, ext0 = call(
         functools.partial(second_edges_kernel, d),
         "second_edges",
         [face, cols],
         [field, pair0, cross0, folded],
         [(2 * HALO, early, width)] + [(HALO, early, width)] * 2 + [(ext, early, width)],
+        flops=12 * early * sweep_flops,
     )
     pair1, cross1 = exchange(pair, cross)
     edges_later, gfirst, pair, cross, ext_later0 = call(
@@ -457,7 +487,6 @@
         [(2 * HALO, later, width), (count, wide, width)] + [(HALO, later + 3 * group, width)] * 2 + [(ext, later, width)],
         anywhere=(6,),
     )
-    pair_later1, cross_later1 = exchange(pair, cross)
     (inner,) = call(
         functools.partial(second_inner_kernel, d),
         "second_inner",
@@ -466,7 +495,8 @@
         [(count - 2 * HALO, early, width)],
         anywhere=(3,),
     )
-    cross1, inner = lax.optimization_barrier((cross1, inner))
+    pair, cross, inner = lax.optimization_barrier((pair, cross, inner))
+    pair_later1, cross_later1 = exchange(pair, cross)
     early_parts = (edges, inner, field, pair1, cross1)
     (own_first,) = call(
         functools.partial(third_rows_kernel, d),
@@ -525,19 +555,16 @@
             anywhere=(5,),
         )[0]
 
-    def output(which, blocks, earlier):
+    def output(blocks):
         return call(
-            functools.partial(output_kernel, d, which),
+            functools.partial(output_kernel, d),
             "output",
             [face],
-            [*twice, coupled] + earlier + blocks,
+            [*twice, coupled] + blocks,
             [whole],
-            [(len(which), sources, count * width)],
-            flops=2 * len(which) * sources * wide * count * width,
-            anywhere=(3,) if earlier else (),
-            sems=len(which) * count,
+            [(ticks - 1, sources, count * width)],
+            sems=ticks - 1,
             place=pl.ANY,
-            aliases={4: 0} if earlier else None,
         )[0]
 
     everything = []
@@ -559,8 +586,27 @@
             arrived, coupled = onward(sent, operator)
         else:
             twice = fields(sent)
-            arrived, most = onward(sent, lambda: output(tuple(range(ticks - 1)), everything, []))
-    out = output((ticks - 1,), arrived, [most])
+            arrived, most = onward(sent, lambda: output(everything))
+    half = len(arrived) // 2
+    (own_part,) = call(
+        functools.partial(last_own_kernel, d),
+        "last_own",
+        [face],
+        [*twice, coupled] + arrived[:half],
+        [jax.ShapeDtypeStruct((sources, count * width), F32)],
+    )
+    (out,) = call(
+        functools.partial(last_other_kernel, d),
+        "last_other",
+        [face],
+        [own_part, coupled, most] + arrived[half:],
+        [whole],
+        [(sources, count * width)],
+        anywhere=(2,),
+        sems=count,
+        place=pl.ANY,
+        aliases={3: 0},
+    )
     return out[:, None]
 
 

time: 57.4 us -> 59 us (1.028)
  waiting for transfers between devices: 10.5 us -> 13.4 us
  starting transfers between devices: 24.3 us -> 23 us
    ppermute x4, waiting for transfers between devices: 0.99 us -> 3.02 us  [exchange(): got = lax.ppermute(cross, 'face', crossing)]
    ppermute x3, starting transfers between devices: 9.79 us -> 8.89 us  [onward(): own.append(lax.ppermute(block, ('slab', 'face'), route))]
    ppermute x3, waiting for transfers between devices: 3.96 us -> 4.8 us  [onward(): own.append(lax.ppermute(block, ('slab', 'face'), route))]
    pallas_call x14 -> x15, Pallas kernels: 21.9 us -> 21.9 us  [call(): pl.pallas_call(body, name=name, out_shape=outs, in_specs=[pl.BlockSpec(me...]
where the time goes in v9:
time: 59 us; the launch traced here: 58.6 us
  starting transfers between devices  23 us (39%)
  Pallas kernels  21.9 us (37%)
  waiting for transfers between devices  13.4 us (23%)
    pallas_call x15, Pallas kernels, call(): pl.pallas_call(body, name=name, out_shape=outs, in_specs=[pl.BlockSpec(me...  21.9 us
    ppermute x4, starting transfers between devices, exchange(): got = lax.ppermute(cross, 'face', crossing)  11.2 us
    ppermute x3, starting transfers between devices, onward(): own.append(lax.ppermute(block, ('slab', 'face'), route))  8.89 us
    ppermute x9, waiting for transfers between devices, swap(): return lax.ppermute(block, 'face', pairing)  5.53 us
    ppermute x3, waiting for transfers between devices, onward(): own.append(lax.ppermute(block, ('slab', 'face'), route))  4.8 us
    ppermute x4, waiting for transfers between devices, exchange(): got = lax.ppermute(cross, 'face', crossing)  3.02 us
    ppermute x9, starting transfers between devices, swap(): return lax.ppermute(block, 'face', pairing)  1.92 us
  transfers between devices with their start and end apart: 20, of which 13 were waited for; matrix products, arithmetic and copies ran while one was open for 0% of the time, Pallas kernels for 30%

profile of v9, /device:TPU:9, one launch (start us, length us, event | category | flops | bytes accessed | tf_op | source)
XLA Modules:
  0.0 58.6 jit_solution(9688500005052279476)
XLA Ops:
  0.0 2.6 %first.1 = (bf16[8,256,128]{2,1,0:T(8,128)(2,1)S(1)}, bf16[8,256,128]{2,1,0:T(8,128)(2,1)S(1)}, bf16[2,128,128]{2,1,0:T(8,128)(2,1)S(1)}, bf16[2,256,128]{2,1,0:...) custom-call(s32[1]{0:T(128)} %bitcast.face_ref, ...), custom_call_target="tpu_custom_call" | custom-call | tf_op jit(solution)/shard_map/first/pallas_call | solution.py:396
  3.4 3.0 %collective-permute-start.1 = (bf16[2,256,128]{2,1,0:T(8,128)(2,1)S(1)}, bf16[2,256,128]{2,1,0:T(8,128)(2,1)S(1)}, u32[]{:S(2)}, u32[]{:S(2)}) collective-permute-start(bf16[2,256,128]{2,1,0:T(8,128)(2,1)S(1)} %get-tuple-element.60), channel_id=1, source_target_pairs={{1,2},{2,1},{5,6},{6,5},{9,10},{10,9},{13,14},{14,13},{17,18},{18,... | collective-permute-start | bytes 393224 | tf_op jit(solution)/shard_map/ppermute | solution.py:423
  6.4 2.1 %fold.1 = (bf16[8,640,128]{2,1,0:T(8,128)(2,1)S(1)}, bf16[6,128,1024]{2,1,0:T(8,128)(2,1)S(1)}) custom-call(s32[1]{0:T(128)} %bitcast.face_ref, s32[2]{0:T(128)S(1)} %get-tuple-element.63.iface, s32[4,8]{1,0:T(4,128)S(1)} %get-tuple-element.57.cols, bf16[8,128,128]{2,1,0:T(8,128)(2,1)S(1)} %get-tuple-element.64.inv, ...), custom_call_target="tpu_custom_call" | custom-call | tf_op jit(solution)/shard_map/fold/pallas_call | solution.py:396
  8.6 2.6 %collective-permute-start.3 = (bf16[2,416,128]{2,1,0:T(8,128)(2,1)S(1)}, bf16[2,416,128]{2,1,0:T(8,128)(2,1)S(1)}, u32[]{:S(2)}, u32[]{:S(2)}) collective-permute-start(bf16[2,416,128]{2,1,0:T(8,128)(2,1)S(1)} %get-tuple-element.73), channel_id=1, source_target_pairs={{1,2},{2,1},{5,6},{6,5},{9,10},{10,9},{13,14},{14,13},{17,18},{18,... | collective-permute-start | bytes 638984 | tf_op jit(solution)/shard_map/ppermute | solution.py:423
  11.2 1.1 %second_edges.1 = (bf16[4,256,128]{2,1,0:T(8,128)(2,1)S(1)}, bf16[2,256,128]{2,1,0:T(8,128)(2,1)S(1)}, bf16[2,256,128]{2,1,0:T(8,128)(2,1)S(1)}, bf16[12,256,128]{2,1,0:T(8,128)(2,1)S(1)}) custom-call(s32[1]{0:T(128)} %bitcast.face_ref, s32[4,8]{1,0:T(4,128)S(1)} %get-tuple-element.57.cols, bf16[8,256,128]{2,1,0:T(8,128)(2,1)S(1)} %get-tuple-element.58.field.rest_2_, ...), custom_call_target="tpu_custom_call" | custom-call | flops 4026531840 | tf_op jit(solution)/shard_map/second_edges/pallas_call | solution.py:396
  12.4 3.0 %collective-permute-start.5 = (bf16[2,256,128]{2,1,0:T(8,128)(2,1)S(1)}, bf16[2,256,128]{2,1,0:T(8,128)(2,1)S(1)}, u32[]{:S(2)}, u32[]{:S(2)}) collective-permute-start(bf16[2,256,128]{2,1,0:T(8,128)(2,1)S(1)} %get-tuple-element.81), channel_id=1, source_target_pairs={{1,2},{2,1},{5,6},{6,5},{9,10},{10,9},{13,14},{14,13},{17,18},{18,... | collective-permute-start | bytes 393224 | tf_op jit(solution)/shard_map/ppermute | solution.py:423
  15.8 1.7 %behind.1 = (bf16[4,256,128]{2,1,0:T(8,128)(2,1)S(1)}, bf16[8,1024,128]{2,1,0:T(8,128)(2,1)S(1)}, bf16[2,1024,128]{2,1,0:T(8,128)(2,1)S(1)}, bf16[2,1024,128]{2,1,0:T(8,128)(2,1)S(1)}, bf16[12,256,128]{2,1,0:T(8,128)(2,1)S(1)}) custom-call(s32[1]{0:T(128)} %bitcast.face_ref, s32[2]{0:T(128)S(1)} %get-tuple-element.63.iface, ...), custom_call_target="tpu_custom_call" | custom-call | tf_op jit(solution)/shard_map/behind/pallas_call | solution.py:396
  17.5 1.1 %second_inner.1.inner.rest_1_ = bf16[4,256,128]{2,1,0:T(8,128)(2,1)S(1)} custom-call(s32[1]{0:T(128)} %bitcast.face_ref, s32[4,8]{1,0:T(4,128)S(1)} %get-tuple-element.57.cols, bf16[8,256,128]{2,1,0:T(8,128)(2,1)S(1)} %get-tuple-element.58.field.rest_2_, bf16[12,256,128]{2,1,0:T(8,128)(2,1)S(1)} %get-tuple-element.78.ext, ...), custom_call_target="tpu_custom_call" | custom-call | tf_op jit(solution)/shard_map/second_inner/pallas_call | solution.py:396
  18.6 2.6 %collective-permute-start.9 = (bf16[2,1024,128]{2,1,0:T(8,128)(2,1)S(1)}, bf16[2,1024,128]{2,1,0:T(8,128)(2,1)S(1)}, u32[]{:S(2)}, u32[]{:S(2)}) collective-permute-start(bf16[2,1024,128]{2,1,0:T(8,128)(2,1)S(1)} %get-tuple-element.85), channel_id=1, source_target_pairs={{1,2},{2,1},{5,6},{6,5},{9,10},{10,9},{13,14},{14,13},{17,18},{18,... | collective-permute-start | bytes 1572872 | tf_op jit(solution)/shard_map/ppermute | solution.py:423
  22.1 1.2 %collective-permute-done.6.other = bf16[2,128,128]{2,1,0:T(8,128)(2,1)S(1)} collective-permute-done((bf16[2,128,128]{2,1,0:T(8,128)(2,1)S(1)}, bf16[2,128,128]{2,1,0:T(8,128)(2,1)S(1)}, u32[]{:S(2)}, u32[]{:S(2)}) %collective-permute-start.6) | collective-permute-done | bytes 65568 | tf_op jit(solution)/shard_map/ppermute | solution.py:427
  23.4 3.7 %collective-permute-start.7 = (bf16[4,128,128]{2,1,0:T(8,128)(2,1)S(1)}, bf16[4,128,128]{2,1,0:T(8,128)(2,1)S(1)}, u32[]{:S(2)}, u32[]{:S(2)}) collective-permute-start(bf16[4,128,128]{2,1,0:T(8,128)(2,1)S(1)} %merge.1.rest_13_), channel_id=1, source_target_pairs={{0,4},{3,5},{2,6},{1,7},{4,8},{7,9},{6,10},{5,11},{8,12},{11,13},{... | collective-permute-start | bytes 393224 | tf_op jit(solution)/shard_map/ppermute | solution.py:439
  27.1 2.7 %collective-permute-done.9.rest_9_.cross_in = bf16[2,1024,128]{2,1,0:T(8,128)(2,1)S(1)} collective-permute-done((bf16[2,1024,128]{2,1,0:T(8,128)(2,1)S(1)}, bf16[2,1024,128]{2,1,0:T(8,128)(2,1)S(1)}, u32[]{:S(2)}, u32[]{:S(2)}) %collective-permute-start.9) | collective-permute-done | bytes 524320 | tf_op jit(solution)/shard_map/ppermute | solution.py:423
  29.8 2.8 %interface.1 = (bf16[256,256]{1,0:T(8,128)(2,1)S(1)}, bf16[256,256]{1,0:T(8,128)(2,1)S(1)}, bf16[256,256]{1,0:T(8,128)(2,1)S(1)}, bf16[256,256]{1,0:T(8,128)(2,1...) custom-call(s32[1]{0:T(128)} %bitcast.face_ref, s32[2]{0:T(128)S(1)} %get-tuple-element.63.iface, ...), custom_call_target="tpu_custom_call" | custom-call | tf_op jit(solution)/shard_map/interface/pallas_call | solution.py:396
  35.2 0.8 %collective-permute-done.14.rest_9_ = bf16[2,2,128,128]{3,2,1,0:T(8,128)(2,1)S(1)} collective-permute-done((bf16[2,2,128,128]{3,2,1,0:T(8,128)(2,1)S(1)}, bf16[2,2,128,128]{3,2,1,0:T(8,128)(2,1)S(1)}, u32[]{:S(2)}, u32[]{:S(2)}) %collective-permute-start.14) | collective-permute-done | bytes 131104 | tf_op jit(solution)/shard_map/ppermute | solution.py:427
  36.7 2.7 %collective-permute-start.16 = (bf16[4,128,128]{2,1,0:T(8,128)(2,1)S(1)}, bf16[4,128,128]{2,1,0:T(8,128)(2,1)S(1)}, u32[]{:S(2)}, u32[]{:S(2)}) collective-permute-start(bf16[4,128,128]{2,1,0:T(8,128)(2,1)S(1)} %chain.2), channel_id=1, source_target_pairs={{0,4},{3,5},{2,6},{1,7},{4,8},{7,9},{6,10},{5,11},{8,12},{11,13},{... | collective-permute-start | bytes 393224 | tf_op jit(solution)/shard_map/ppermute | solution.py:439
  39.4 3.8 %coupling_last.1.coupled = bf16[1024,1024]{1,0:T(8,128)(2,1)S(1)} custom-call(s32[1]{0:T(128)} %bitcast.face_ref, s32[2]{0:T(128)S(1)} %get-tuple-element.63.iface, s32[4,8]{1,0:T(4,128)S(1)} %get-tuple-element.57.cols, bf16[2,128,128]{2,1,0:T(8,128)(2,1)S(1)} %get-tuple-element.71.gfield.rest_11_, ...), custom_call_target="tpu_custom_call" | custom-call | flops 1342177280 | tf_op jit(solution)/shard_map/coupling_last/pallas_call | solution.py:396
  43.3 2.3 %collective-permute-done.16.rest_10_.rest_2_ = bf16[4,128,128]{2,1,0:T(8,128)(2,1)S(1)} collective-permute-done((bf16[4,128,128]{2,1,0:T(8,128)(2,1)S(1)}, bf16[4,128,128]{2,1,0:T(8,128)(2,1)S(1)}, u32[]{:S(2)}, u32[]{:S(2)}) %collective-permute-start.16) | collective-permute-done | bytes 131104 | tf_op jit(solution)/shard_map/ppermute | solution.py:439
  45.6 1.3 %collective-permute-done.17.rest_11_.rest_3_ = bf16[4,128,128]{2,1,0:T(8,128)(2,1)S(1)} collective-permute-done((bf16[4,128,128]{2,1,0:T(8,128)(2,1)S(1)}, bf16[4,128,128]{2,1,0:T(8,128)(2,1)S(1)}, u32[]{:S(2)}, u32[]{:S(2)}) %collective-permute-start.17) | collective-permute-done | bytes 131104 | tf_op jit(solution)/shard_map/ppermute | solution.py:427
  47.3 2.5 %collective-permute-start.18 = (bf16[4,128,128]{2,1,0:T(8,128)(2,1)S(1)}, bf16[4,128,128]{2,1,0:T(8,128)(2,1)S(1)}, u32[]{:S(2)}, u32[]{:S(2)}) collective-permute-start(bf16[4,128,128]{2,1,0:T(8,128)(2,1)S(1)} %chain.3.rest_11_), channel_id=1, source_target_pairs={{0,4},{3,5},{2,6},{1,7},{4,8},{7,9},{6,10},{5,11},{8,12},{11,13},{... | collective-permute-start | bytes 393224 | tf_op jit(solution)/shard_map/ppermute | solution.py:439
  49.8 2.2 %third.1 = (bf16[8,256,128]{2,1,0:T(8,128)(2,1)S(1)}, bf16[8,256,128]{2,1,0:T(8,128)(2,1)S(1)}) custom-call(s32[1]{0:T(128)} %bitcast.face_ref, s32[4,8]{1,0:T(4,128)S(1)} %get-tuple-element.57.cols, bf16[4,256,128]{2,1,0:T(8,128)(2,1)S(1)} %get-tuple-element.69.edges.rest_0_, bf16[4,256,128]{2,1,0:T(8,128)(2,1)S(1)} %second_inner.1.inner.rest_1_, ...), custom_call_target="tpu_custom_call" | custom-call | tf_op jit(solution)/shard_map/third/pallas_call | solution.py:396
  52.0 1.5 %output.1.earlier = bf16[4,128,1024]{2,1,0:T(8,128)(2,1)} custom-call(s32[1]{0:T(128)} %bitcast.face_ref, bf16[8,256,128]{2,1,0:T(8,128)(2,1)S(1)} %get-tuple-element.104.early, bf16[8,256,128]{2,1,0:T(8,128)(2,1)S(1)} %get-tuple-element.105.later, bf16[1024,1024]{1,0:T(8,128)(2,1)S(1)} %coupling_last.1.coupled, ...), custom_call_target="tpu_custom_call" | custom-call | tf_op jit(solution)/shard_map/output/pallas_call | solution.py:396
  53.5 2.5 %collective-permute-done.18.rest_0_ = bf16[4,128,128]{2,1,0:T(8,128)(2,1)S(1)} collective-permute-done((bf16[4,128,128]{2,1,0:T(8,128)(2,1)S(1)}, bf16[4,128,128]{2,1,0:T(8,128)(2,1)S(1)}, u32[]{:S(2)}, u32[]{:S(2)}) %collective-permute-start.18) | collective-permute-done | bytes 131104 | tf_op jit(solution)/shard_map/ppermute | solution.py:439
  56.5 0.8 %collective-permute-done.19.rest_0_ = bf16[4,128,128]{2,1,0:T(8,128)(2,1)S(1)} collective-permute-done((bf16[4,128,128]{2,1,0:T(8,128)(2,1)S(1)}, bf16[4,128,128]{2,1,0:T(8,128)(2,1)S(1)}, u32[]{:S(2)}, u32[]{:S(2)}) %collective-permute-start.19) | collective-permute-done | bytes 131104 | tf_op jit(solution)/shard_map/ppermute | solution.py:427
  57.4 1.0 %last_other.1 = bf16[4,128,1024]{2,1,0:T(8,128)(2,1)} custom-call(s32[1]{0:T(128)} %bitcast.face_ref, f32[128,1024]{1,0:T(8,128)S(1)} %last_own.1.own_part, bf16[1024,1024]{1,0:T(8,128)(2,1)S(1)} %coupling_last.1.coupled, bf16[4,128,1024]{2,1,0:T(8,128)(2,1)} %output.1.earlier, ...), custom_call_target="tpu_custom_call", output_to_operand_aliasing={{}: (3, {})} | custom-call | tf_op jit(solution)/shard_map/last_other/pallas_call | solution.py:396
  (31 shorter events, 6.5 us)
Async XLA Ops:
  2.6 8.6 %collective-permute-start = (bf16[2,256,128]{2,1,0:T(8,128)(2,1)S(1)}, bf16[2,256,128]{2,1,0:T(8,128)(2,1)S(1)}, u32[]{:S(2)}, u32[]{:S(2)}) collective-permute-start(bf16[2,256,128]{2,1,0:T(8,128)(2,1)S(1)} %get-tuple-element.59), channel_id=1, source_target_pairs={{0,1},{1,0},{2,3},{3,2},{4,5},{5,4},{6,7},{7,6},{8,9},{9,8},{10,11... | collective-permute-start | bytes 393224 | tf_op jit(solution)/shard_map/ppermute | solution.py:424
  3.4 7.9 %collective-permute-start.1 = (bf16[2,256,128]{2,1,0:T(8,128)(2,1)S(1)}, bf16[2,256,128]{2,1,0:T(8,128)(2,1)S(1)}, u32[]{:S(2)}, u32[]{:S(2)}) collective-permute-start(bf16[2,256,128]{2,1,0:T(8,128)(2,1)S(1)} %get-tuple-element.60), channel_id=1, source_target_pairs={{1,2},{2,1},{5,6},{6,5},{9,10},{10,9},{13,14},{14,13},{17,18},{18,... | collective-permute-start | bytes 393224 | tf_op jit(solution)/shard_map/ppermute | solution.py:423
  8.5 6.9 %collective-permute-start.2 = (bf16[2,416,128]{2,1,0:T(8,128)(2,1)S(1)}, bf16[2,416,128]{2,1,0:T(8,128)(2,1)S(1)}, u32[]{:S(2)}, u32[]{:S(2)}) collective-permute-start(bf16[2,416,128]{2,1,0:T(8,128)(2,1)S(1)} %get-tuple-element.72), channel_id=1, source_target_pairs={{0,1},{1,0},{2,3},{3,2},{4,5},{5,4},{6,7},{7,6},{8,9},{9,8},{10,11... | collective-permute-start | bytes 638984 | tf_op jit(solution)/shard_map/ppermute | solution.py:424
  8.6 7.2 %collective-permute-start.3 = (bf16[2,416,128]{2,1,0:T(8,128)(2,1)S(1)}, bf16[2,416,128]{2,1,0:T(8,128)(2,1)S(1)}, u32[]{:S(2)}, u32[]{:S(2)}) collective-permute-start(bf16[2,416,128]{2,1,0:T(8,128)(2,1)S(1)} %get-tuple-element.73), channel_id=1, source_target_pairs={{1,2},{2,1},{5,6},{6,5},{9,10},{10,9},{13,14},{14,13},{17,18},{18,... | collective-permute-start | bytes 638984 | tf_op jit(solution)/shard_map/ppermute | solution.py:423
  12.4 3.4 %collective-permute-start.4 = (bf16[2,256,128]{2,1,0:T(8,128)(2,1)S(1)}, bf16[2,256,128]{2,1,0:T(8,128)(2,1)S(1)}, u32[]{:S(2)}, u32[]{:S(2)}) collective-permute-start(bf16[2,256,128]{2,1,0:T(8,128)(2,1)S(1)} %get-tuple-element.75), channel_id=1, source_target_pairs={{0,1},{1,0},{2,3},{3,2},{4,5},{5,4},{6,7},{7,6},{8,9},{9,8},{10,11... | collective-permute-start | bytes 393224 | tf_op jit(solution)/shard_map/ppermute | solution.py:424
  12.4 8.8 %collective-permute-start.5 = (bf16[2,256,128]{2,1,0:T(8,128)(2,1)S(1)}, bf16[2,256,128]{2,1,0:T(8,128)(2,1)S(1)}, u32[]{:S(2)}, u32[]{:S(2)}) collective-permute-start(bf16[2,256,128]{2,1,0:T(8,128)(2,1)S(1)} %get-tuple-element.81), channel_id=1, source_target_pairs={{1,2},{2,1},{5,6},{6,5},{9,10},{10,9},{13,14},{14,13},{17,18},{18,... | collective-permute-start | bytes 393224 | tf_op jit(solution)/shard_map/ppermute | solution.py:423
  18.5 8.6 %collective-permute-start.8 = (bf16[2,1024,128]{2,1,0:T(8,128)(2,1)S(1)}, bf16[2,1024,128]{2,1,0:T(8,128)(2,1)S(1)}, u32[]{:S(2)}, u32[]{:S(2)}) collective-permute-start(bf16[2,1024,128]{2,1,0:T(8,128)(2,1)S(1)} %get-tuple-element.84), channel_id=1, source_target_pairs={{0,1},{1,0},{2,3},{3,2},{4,5},{5,4},{6,7},{7,6},{8,9},{9,8},{10,11... | collective-permute-start | bytes 1572872 | tf_op jit(solution)/shard_map/ppermute | solution.py:424
  18.6 11.2 %collective-permute-start.9 = (bf16[2,1024,128]{2,1,0:T(8,128)(2,1)S(1)}, bf16[2,1024,128]{2,1,0:T(8,128)(2,1)S(1)}, u32[]{:S(2)}, u32[]{:S(2)}) collective-permute-start(bf16[2,1024,128]{2,1,0:T(8,128)(2,1)S(1)} %get-tuple-element.85), channel_id=1, source_target_pairs={{1,2},{2,1},{5,6},{6,5},{9,10},{10,9},{13,14},{14,13},{17,18},{18,... | collective-permute-start | bytes 1572872 | tf_op jit(solution)/shard_map/ppermute | solution.py:423
  22.1 1.3 %collective-permute-start.6 = (bf16[2,128,128]{2,1,0:T(8,128)(2,1)S(1)}, bf16[2,128,128]{2,1,0:T(8,128)(2,1)S(1)}, u32[]{:S(2)}, u32[]{:S(2)}) collective-permute-start(bf16[2,128,128]{2,1,0:T(8,128)(2,1)S(1)} %third_rows.1.own), channel_id=1, source_target_pairs={{0,1},{1,0},{2,3},{3,2},{4,5},{5,4},{6,7},{7,6},{8,9},{9,8},{10,11... | collective-permute-start | bytes 196616 | tf_op jit(solution)/shard_map/ppermute | solution.py:427
  23.4 10.2 %collective-permute-start.7 = (bf16[4,128,128]{2,1,0:T(8,128)(2,1)S(1)}, bf16[4,128,128]{2,1,0:T(8,128)(2,1)S(1)}, u32[]{:S(2)}, u32[]{:S(2)}) collective-permute-start(bf16[4,128,128]{2,1,0:T(8,128)(2,1)S(1)} %merge.1.rest_13_), channel_id=1, source_target_pairs={{0,4},{3,5},{2,6},{1,7},{4,8},{7,9},{6,10},{5,11},{8,12},{11,13},{... | collective-permute-start | bytes 393224 | tf_op jit(solution)/shard_map/ppermute | solution.py:439
  32.6 1.4 %collective-permute-start.10 = (bf16[256,256]{1,0:T(8,128)(2,1)S(1)}, bf16[256,256]{1,0:T(8,128)(2,1)S(1)}, u32[]{:S(2)}, u32[]{:S(2)}) collective-permute-start(bf16[256,256]{1,0:T(8,128)(2,1)S(1)} %get-tuple-element.93.rest_0_.after), channel_id=1, source_target_pairs={{0,1},{1,0},{2,3},{3,2},{4,5},{5,4},{6,7},{7,6},{8,9},{9,8},{10,11... | collective-permute-start | bytes 393224 | tf_op jit(solution)/shard_map/ppermute | solution.py:427
  32.6 1.5 %collective-permute-start.11 = (bf16[256,256]{1,0:T(8,128)(2,1)S(1)}, bf16[256,256]{1,0:T(8,128)(2,1)S(1)}, u32[]{:S(2)}, u32[]{:S(2)}) collective-permute-start(bf16[256,256]{1,0:T(8,128)(2,1)S(1)} %get-tuple-element.94.rest_1_), channel_id=1, source_target_pairs={{0,1},{1,0},{2,3},{3,2},{4,5},{5,4},{6,7},{7,6},{8,9},{9,8},{10,11... | collective-permute-start | bytes 393224 | tf_op jit(solution)/shard_map/ppermute | solution.py:427
  33.1 1.3 %collective-permute-start.12 = (bf16[256,256]{1,0:T(8,128)(2,1)S(1)}, bf16[256,256]{1,0:T(8,128)(2,1)S(1)}, u32[]{:S(2)}, u32[]{:S(2)}) collective-permute-start(bf16[256,256]{1,0:T(8,128)(2,1)S(1)} %get-tuple-element.95.rest_2_), channel_id=1, source_target_pairs={{0,1},{1,0},{2,3},{3,2},{4,5},{5,4},{6,7},{7,6},{8,9},{9,8},{10,11... | collective-permute-start | bytes 393224 | tf_op jit(solution)/shard_map/ppermute | solution.py:427
  33.2 1.5 %collective-permute-start.13 = (bf16[256,256]{1,0:T(8,128)(2,1)S(1)}, bf16[256,256]{1,0:T(8,128)(2,1)S(1)}, u32[]{:S(2)}, u32[]{:S(2)}) collective-permute-start(bf16[256,256]{1,0:T(8,128)(2,1)S(1)} %get-tuple-element.96.rest_3_), channel_id=1, source_target_pairs={{0,1},{1,0},{2,3},{3,2},{4,5},{5,4},{6,7},{7,6},{8,9},{9,8},{10,11... | collective-permute-start | bytes 393224 | tf_op jit(solution)/shard_map/ppermute | solution.py:427
  34.7 1.3 %collective-permute-start.14 = (bf16[2,2,128,128]{3,2,1,0:T(8,128)(2,1)S(1)}, bf16[2,2,128,128]{3,2,1,0:T(8,128)(2,1)S(1)}, u32[]{:S(2)}, u32[]{:S(2)}) collective-permute-start(bf16[2,2,128,128]{3,2,1,0:T(8,128)(2,1)S(1)} %get-tuple-element.101.rest_8_), channel_id=1, source_target_pairs={{0,1},{1,0},{2,3},{3,2},{4,5},{5,4},{6,7},{7,6},{8,9},{9,8},{10,11... | collective-permute-start | bytes 393224 | tf_op jit(solution)/shard_map/ppermute | solution.py:427
  35.0 1.3 %collective-permute-start.15 = (bf16[4,128,128]{2,1,0:T(8,128)(2,1)S(1)}, bf16[4,128,128]{2,1,0:T(8,128)(2,1)S(1)}, u32[]{:S(2)}, u32[]{:S(2)}) collective-permute-start(bf16[4,128,128]{2,1,0:T(8,128)(2,1)S(1)} %collective-permute-done.7.rest_10_.rest_0_), channel_id=1, source_target_pairs={{0,1},{1,0},{2,3},{3,2},{4,5},{5,4},{6,7},{7,6},{8,9},{9,8},{10,11... | collective-permute-start | bytes 393224 | tf_op jit(solution)/shard_map/ppermute | solution.py:427
  36.7 8.8 %collective-permute-start.16 = (bf16[4,128,128]{2,1,0:T(8,128)(2,1)S(1)}, bf16[4,128,128]{2,1,0:T(8,128)(2,1)S(1)}, u32[]{:S(2)}, u32[]{:S(2)}) collective-permute-start(bf16[4,128,128]{2,1,0:T(8,128)(2,1)S(1)} %chain.2), channel_id=1, source_target_pairs={{0,4},{3,5},{2,6},{1,7},{4,8},{7,9},{6,10},{5,11},{8,12},{11,13},{... | collective-permute-start | bytes 393224 | tf_op jit(solution)/shard_map/ppermute | solution.py:439
  45.5 1.3 %collective-permute-start.17 = (bf16[4,128,128]{2,1,0:T(8,128)(2,1)S(1)}, bf16[4,128,128]{2,1,0:T(8,128)(2,1)S(1)}, u32[]{:S(2)}, u32[]{:S(2)}) collective-permute-start(bf16[4,128,128]{2,1,0:T(8,128)(2,1)S(1)} %collective-permute-done.16.rest_10_.rest_2_), channel_id=1, source_target_pairs={{0,1},{1,0},{2,3},{3,2},{4,5},{5,4},{6,7},{7,6},{8,9},{9,8},{10,11... | collective-permute-start | bytes 393224 | tf_op jit(solution)/shard_map/ppermute | solution.py:427
  47.3 8.8 %collective-permute-start.18 = (bf16[4,128,128]{2,1,0:T(8,128)(2,1)S(1)}, bf16[4,128,128]{2,1,0:T(8,128)(2,1)S(1)}, u32[]{:S(2)}, u32[]{:S(2)}) collective-permute-start(bf16[4,128,128]{2,1,0:T(8,128)(2,1)S(1)} %chain.3.rest_11_), channel_id=1, source_target_pairs={{0,4},{3,5},{2,6},{1,7},{4,8},{7,9},{6,10},{5,11},{8,12},{11,13},{... | collective-permute-start | bytes 393224 | tf_op jit(solution)/shard_map/ppermute | solution.py:439
  56.0 1.3 %collective-permute-start.19 = (bf16[4,128,128]{2,1,0:T(8,128)(2,1)S(1)}, bf16[4,128,128]{2,1,0:T(8,128)(2,1)S(1)}, u32[]{:S(2)}, u32[]{:S(2)}) collective-permute-start(bf16[4,128,128]{2,1,0:T(8,128)(2,1)S(1)} %collective-permute-done.18.rest_0_), channel_id=1, source_target_pairs={{0,1},{1,0},{2,3},{3,2},{4,5},{5,4},{6,7},{7,6},{8,9},{9,8},{10,11... | collective-permute-start | bytes 393224 | tf_op jit(solution)/shard_map/ppermute | solution.py:427

commit v10 on v9

--- a/solution.py
+++ b/solution.py
@@ -251,18 +251,25 @@
             ext[pl.ds(start, HALO), pl.ds(d.start(other + shift), d.group), :] = block[:, at : at + d.group, :]
 
 
+def second_rest_kernel(d, face_ref, iface, cols, edges, field, ext0, pair_in, cross_in, later, later_ext0, folded, after, *rest):
+    inner, inner_later, *faces_out, ext = rest
+    face = face_ref[0]
+    correct(d, cols, face, field, folded, inner, ext0, range(HALO, d.last))
+    correct(d, cols, face, later, folded, inner_later, later_ext0, range(HALO, d.last))
+    for out in faces_out:
+        outs = [out.at[t] for t in range(d.split - 1)]
+        held = ext.at[:, pl.ds(0, len(outs) * d.sources), :]
+        interface_rows(d, face, iface, cols, edges, inner, field, pair_in, cross_in, folded, 1, outs, held)
+
+
 def interface_kernel(d, face_ref, iface, cols, *rest):
-    early, (edges, field, field_ext, pair_in, cross_in, folded, gfield, gfirst, after) = rest[:5], rest[5:14]
-    chain, (faces_out, inner, ext, small) = rest[14 : 14 + d.parts], rest[14 + d.parts :]
+    later, (folded, gfield, gfirst) = rest[:5], rest[5:8]
+    chain, (faces_out, ext, small) = rest[8 : 8 + d.parts], rest[8 + d.parts :]
     face = face_ref[0]
     w = d.width
-    correct(d, cols, face, field, folded, inner, field_ext, range(HALO, d.last))
-    later = (edges, inner, field, pair_in, cross_in)
-    for group, first, last, shift in ((early, 1, d.split, 0), (later, d.split, d.ticks - 1, d.split)):
-        outs = [faces_out.at[t - 1] for t in range(first, last)]
-        if outs:
-            held = small.at[:, pl.ds(0, len(outs) * d.sources), :]
-            interface_rows(d, face, iface, cols, *group, folded, first - shift, outs, held)
+    pair_in, cross_in = later[3:]
+    outs = [faces_out.at[t] for t in range(d.ticks - 1 - d.split)]
+    interface_rows(d, face, iface, cols, *later, folded, 0, outs, small.at[:, pl.ds(0, len(outs) * d.sources), :])
     coupling_ext(d, face, gfirst, pair_in, cross_in, ext)
     for i in range(d.slots):
         start = i * d.group % d.part
@@ -324,7 +331,7 @@
     for j, (base, odd) in enumerate(((own_faces, parity), (other_faces, 1 - parity))):
         for q in range(d.nq):
             at = j * d.group + q * d.width
-            sent[odd * d.nq + q] = (base[tick - 1, q].astype(F32) - total[:, at : at + d.width]).astype(BF)
+            sent[odd * d.nq + q] = (base[tick, q].astype(F32) - total[:, at : at + d.width]).astype(BF)
 
 
 def merge_kernel(d, face_ref, own, other, sent):
@@ -442,7 +449,7 @@
             *own, made = lax.optimization_barrier((*own, made))
         return own + [swap(x) for x in own], made
 
-    early, later, group, ext, wide = d.early, d.later, d.group, d.ext, d.wide
+    split, early, later, group, ext, wide = d.split, d.early, d.later, d.group, d.ext, d.wide
     sweep_flops = 2 * count * tile * (neigh + 1)
     ints = [jax.ShapeDtypeStruct(x.shape, x.dtype) for x in (iface, cols)]
     on_hbm = (iface, cols, inflow[0], couple, inv, rhs[:, 0], diag, off)
@@ -461,6 +468,7 @@
         sems=7 + ticks,
     )
     pair0, cross0 = exchange(pair, cross)
+    pair_later0, cross_later0 = exchange(pair_later, cross_later)
     folded, met = call(
         functools.partial(fold_kernel, d),
         "fold",
@@ -468,15 +476,12 @@
         [inv, diag, off],
         [(count, d.depth, width), (2 * HALO + nq, width, count * width)],
     )
-    pair_later, cross_later, folded = lax.optimization_barrier((pair_later, cross_later, folded))
-    pair_later0, cross_later0 = exchange(pair_later, cross_later)
     edges, pair, cross, ext0 = call(
         functools.partial(second_edges_kernel, d),
         "second_edges",
         [face, cols],
         [field, pair0, cross0, folded],
         [(2 * HALO, early, width)] + [(HALO, early, width)] * 2 + [(ext, early, width)],
-        flops=12 * early * sweep_flops,
     )
     pair1, cross1 = exchange(pair, cross)
     edges_later, gfirst, pair, cross, ext_later0 = call(
@@ -487,22 +492,21 @@
         [(2 * HALO, later, width), (count, wide, width)] + [(HALO, later + 3 * group, width)] * 2 + [(ext, later, width)],
         anywhere=(6,),
     )
-    (inner,) = call(
+    pair_later1, cross_later1 = exchange(pair, cross)
+    (inner_first,) = call(
         functools.partial(second_inner_kernel, d),
         "second_inner",
         [face, cols],
         [field, ext0, folded, gfirst],
-        [(count - 2 * HALO, early, width)],
+        [(count - 2 * HALO, sources, width)],
         anywhere=(3,),
     )
-    pair, cross, inner = lax.optimization_barrier((pair, cross, inner))
-    pair_later1, cross_later1 = exchange(pair, cross)
-    early_parts = (edges, inner, field, pair1, cross1)
+    cross1, inner_first = lax.optimization_barrier((cross1, inner_first))
     (own_first,) = call(
         functools.partial(third_rows_kernel, d),
         "third_rows",
         [face, iface, cols],
-        [*early_parts, folded],
+        [edges, inner_first, field, pair1, cross1, folded],
         [(nq, sources, width)],
         [(ext, sources, width)],
         flops=12 * early * sweep_flops,
@@ -515,27 +519,39 @@
         [(2 * nq, sources, width)],
     )
 
+    inner, inner_later, *faces_early = call(
+        functools.partial(second_rest_kernel, d),
+        "second_rest",
+        [face, iface, cols],
+        [edges, field, ext0, pair1, cross1, field_later, ext_later0, folded, sent],
+        [(count - 2 * HALO, early, width), (count - 2 * HALO, later, width)]
+        + [(split - 1, nq, sources, width)] * (split > 1),
+        [(ext, early, width)],
+        anywhere=(8,),
+    )
+    other_early = [swap(x) for x in faces_early]
+    early_parts = (edges, inner, field, pair1, cross1)
+    later_parts = (edges_later, inner_later, field_later, pair_later1, cross_later1)
+
     def beside_first():
-        *rows, faces_out, inner_later = call(
+        *rows, faces_later = call(
             functools.partial(interface_kernel, d),
             "interface",
             [face, iface, cols],
-            [*early_parts, edges_later, field_later, ext_later0, pair_later1, cross_later1, folded, gfield, gfirst, sent],
-            [(d.part, group)] * d.parts + [(ticks - 2, nq, sources, width), (count - 2 * HALO, later, width)],
-            [(ext, wide, width), (ext, max(early, later), width)],
-            anywhere=(13,),
+            [*later_parts, folded, gfield, gfirst],
+            [(d.part, group)] * d.parts + [(ticks - 1 - split, nq, sources, width)],
+            [(ext, wide, width), (ext, later, width)],
         )
-        return rows, [swap(x) for x in rows], faces_out, inner_later
-
-    arrived, (chain, other_chain, faces_out, inner_later) = onward(sent, beside_first)
-    other_faces = swap(faces_out)
+        return rows, [swap(x) for x in rows], faces_later
+
+    arrived, (chain, other_chain, faces_later) = onward(sent, beside_first)
 
     def fields(after):
         return call(
             functools.partial(third_kernel, d),
             "third",
             [face, cols],
-            [*early_parts, edges_later, inner_later, field_later, pair_later1, cross_later1, folded, after],
+            [*early_parts, *later_parts, folded, after],
             [(count, early, width), (count, later, width)],
             [(ext, early, width), (ext, later, width)],
             anywhere=(11,),
@@ -573,17 +589,19 @@
         everything += arrived
         if tick == ticks - 1:
             break
+        early_tick = tick < split
+        bases = (faces_early[0], other_early[0]) if early_tick else (faces_later, other_later)
         (sent,) = call(
-            functools.partial(chain_kernel, d, tick),
+            functools.partial(chain_kernel, d, tick - 1 if early_tick else tick - split),
             "chain",
             [face],
-            [*chain, *other_chain, faces_out, other_faces] + arrived,
+            [*chain, *other_chain, *bases] + arrived,
             [(2 * nq, sources, width)],
             [(wide, 2 * group)],
             flops=4 * sources * wide * group,
         )
         if tick == 1:
-            arrived, coupled = onward(sent, operator)
+            arrived, (coupled, other_later) = onward(sent, lambda: (operator(), swap(faces_later)))
         else:
             twice = fields(sent)
             arrived, most = onward(sent, lambda: output(everything))

time: 59 us -> 57.3 us (0.971)
  waiting for transfers between devices: 13.4 us -> 8.34 us
  starting transfers between devices: 23 us -> 25.4 us
  Pallas kernels: 21.9 us -> 22.8 us
    ppermute x4, waiting for transfers between devices: 3.02 us -> 0.01 us  [exchange(): got = lax.ppermute(cross, 'face', crossing)]
    ppermute x3, waiting for transfers between devices: 4.8 us -> 3.38 us  [onward(): own.append(lax.ppermute(block, ('slab', 'face'), route))]
    ppermute x3, starting transfers between devices: 8.89 us -> 10.1 us  [onward(): own.append(lax.ppermute(block, ('slab', 'face'), route))]
    ppermute x9 -> x10, starting transfers between devices: 1.92 us -> 3.17 us  [swap(): return lax.ppermute(block, 'face', pairing)]
    pallas_call x15 -> x16, Pallas kernels: 21.9 us -> 22.8 us  [call(): pl.pallas_call(body, name=name, out_shape=outs, in_specs=[pl.BlockSpec(me...]
    ppermute x9 -> x10, waiting for transfers between devices: 5.53 us -> 4.94 us  [swap(): return lax.ppermute(block, 'face', pairing)]
  transfers between devices with their start and end apart: 20 -> 21, of which waited for: 13 -> 10; matrix products, arithmetic and copies ran while one was open for 0% -> 0% of each run, Pallas kernels for 30% -> 32%
where the time goes in v10:
time: 57.3 us; the launch traced here: 57 us
  starting transfers between devices  25.4 us (44%)
  Pallas kernels  22.8 us (40%)
  waiting for transfers between devices  8.34 us (15%)
    pallas_call x16, Pallas kernels, call(): pl.pallas_call(body, name=name, out_shape=outs, in_specs=[pl.BlockSpec(me...  22.8 us
    ppermute x4, starting transfers between devices, exchange(): got = lax.ppermute(cross, 'face', crossing)  11.1 us
    ppermute x3, starting transfers between devices, onward(): own.append(lax.ppermute(block, ('slab', 'face'), route))  10.1 us
    ppermute x10, waiting for transfers between devices, swap(): return lax.ppermute(block, 'face', pairing)  4.94 us
    ppermute x3, waiting for transfers between devices, onward(): own.append(lax.ppermute(block, ('slab', 'face'), route))  3.38 us
    ppermute x10, starting transfers between devices, swap(): return lax.ppermute(block, 'face', pairing)  3.17 us
  transfers between devices with their start and end apart: 21, of which 10 were waited for; matrix products, arithmetic and copies ran while one was open for 0% of the time, Pallas kernels for 32%

profile of v10, /device:TPU:9, one launch (start us, length us, event | category | flops | bytes accessed | tf_op | source)
XLA Modules:
  0.0 57.0 jit_solution(2836636954990440257)
XLA Ops:
  0.0 2.6 %first.1 = (bf16[8,256,128]{2,1,0:T(8,128)(2,1)S(1)}, bf16[8,256,128]{2,1,0:T(8,128)(2,1)S(1)}, bf16[2,128,128]{2,1,0:T(8,128)(2,1)S(1)}, bf16[2,256,128]{2,1,0:...) custom-call(s32[1]{0:T(128)} %bitcast.face_ref, ...), custom_call_target="tpu_custom_call" | custom-call | tf_op jit(solution)/shard_map/first/pallas_call | solution.py:403
  3.4 3.0 %collective-permute-start.1 = (bf16[2,256,128]{2,1,0:T(8,128)(2,1)S(1)}, bf16[2,256,128]{2,1,0:T(8,128)(2,1)S(1)}, u32[]{:S(2)}, u32[]{:S(2)}) collective-permute-start(bf16[2,256,128]{2,1,0:T(8,128)(2,1)S(1)} %get-tuple-element.58), channel_id=1, source_target_pairs={{1,2},{2,1},{5,6},{6,5},{9,10},{10,9},{13,14},{14,13},{17,18},{18,... | collective-permute-start | bytes 393224 | tf_op jit(solution)/shard_map/ppermute | solution.py:430
  6.5 2.5 %collective-permute-start.5 = (bf16[2,416,128]{2,1,0:T(8,128)(2,1)S(1)}, bf16[2,416,128]{2,1,0:T(8,128)(2,1)S(1)}, u32[]{:S(2)}, u32[]{:S(2)}) collective-permute-start(bf16[2,416,128]{2,1,0:T(8,128)(2,1)S(1)} %get-tuple-element.71), channel_id=1, source_target_pairs={{1,2},{2,1},{5,6},{6,5},{9,10},{10,9},{13,14},{14,13},{17,18},{18,... | collective-permute-start | bytes 638984 | tf_op jit(solution)/shard_map/ppermute | solution.py:430
  9.0 2.2 %fold.1 = (bf16[8,640,128]{2,1,0:T(8,128)(2,1)S(1)}, bf16[6,128,1024]{2,1,0:T(8,128)(2,1)S(1)}) custom-call(s32[1]{0:T(128)} %bitcast.face_ref, s32[2]{0:T(128)S(1)} %get-tuple-element.59.iface, s32[4,8]{1,0:T(4,128)S(1)} %get-tuple-element.55.cols, bf16[8,128,128]{2,1,0:T(8,128)(2,1)S(1)} %get-tuple-element.60.inv, ...), custom_call_target="tpu_custom_call" | custom-call | tf_op jit(solution)/shard_map/fold/pallas_call | solution.py:403
  11.2 1.1 %second_edges.1 = (bf16[4,256,128]{2,1,0:T(8,128)(2,1)S(1)}, bf16[2,256,128]{2,1,0:T(8,128)(2,1)S(1)}, bf16[2,256,128]{2,1,0:T(8,128)(2,1)S(1)}, bf16[12,256,128]{2,1,0:T(8,128)(2,1)S(1)}) custom-call(s32[1]{0:T(128)} %bitcast.face_ref, s32[4,8]{1,0:T(4,128)S(1)} %get-tuple-element.55.cols, bf16[8,256,128]{2,1,0:T(8,128)(2,1)S(1)} %get-tuple-element.56.field.rest_2_, ...), custom_call_target="tpu_custom_call" | custom-call | tf_op jit(solution)/shard_map/second_edges/pallas_call | solution.py:403
  12.4 3.0 %collective-permute-start.3 = (bf16[2,256,128]{2,1,0:T(8,128)(2,1)S(1)}, bf16[2,256,128]{2,1,0:T(8,128)(2,1)S(1)}, u32[]{:S(2)}, u32[]{:S(2)}) collective-permute-start(bf16[2,256,128]{2,1,0:T(8,128)(2,1)S(1)} %get-tuple-element.67), channel_id=1, source_target_pairs={{1,2},{2,1},{5,6},{6,5},{9,10},{10,9},{13,14},{14,13},{17,18},{18,... | collective-permute-start | bytes 393224 | tf_op jit(solution)/shard_map/ppermute | solution.py:430
  15.5 1.7 %behind.1 = (bf16[4,256,128]{2,1,0:T(8,128)(2,1)S(1)}, bf16[8,1024,128]{2,1,0:T(8,128)(2,1)S(1)}, bf16[2,1024,128]{2,1,0:T(8,128)(2,1)S(1)}, bf16[2,1024,128]{2,1,0:T(8,128)(2,1)S(1)}, bf16[12,256,128]{2,1,0:T(8,128)(2,1)S(1)}) custom-call(s32[1]{0:T(128)} %bitcast.face_ref, s32[2]{0:T(128)S(1)} %get-tuple-element.59.iface, ...), custom_call_target="tpu_custom_call" | custom-call | tf_op jit(solution)/shard_map/behind/pallas_call | solution.py:403
  17.2 2.6 %collective-permute-start.8 = (bf16[2,1024,128]{2,1,0:T(8,128)(2,1)S(1)}, bf16[2,1024,128]{2,1,0:T(8,128)(2,1)S(1)}, u32[]{:S(2)}, u32[]{:S(2)}) collective-permute-start(bf16[2,1024,128]{2,1,0:T(8,128)(2,1)S(1)} %get-tuple-element.81), channel_id=1, source_target_pairs={{1,2},{2,1},{5,6},{6,5},{9,10},{10,9},{13,14},{14,13},{17,18},{18,... | collective-permute-start | bytes 1572872 | tf_op jit(solution)/shard_map/ppermute | solution.py:430
  19.8 0.9 %second_inner.1.inner = bf16[4,128,128]{2,1,0:T(8,128)(2,1)S(1)} custom-call(s32[1]{0:T(128)} %bitcast.face_ref, s32[4,8]{1,0:T(4,128)S(1)} %get-tuple-element.55.cols, bf16[8,256,128]{2,1,0:T(8,128)(2,1)S(1)} %get-tuple-element.56.field.rest_2_, bf16[12,256,128]{2,1,0:T(8,128)(2,1)S(1)} %get-tuple-element.65.ext.ext0, ...), custom_call_target="tpu_custom_call" | custom-call | tf_op jit(solution)/shard_map/second_inner/pallas_call | solution.py:403
  20.7 0.8 %third_rows.1.own = bf16[2,128,128]{2,1,0:T(8,128)(2,1)S(1)} custom-call(s32[1]{0:T(128)} %bitcast.face_ref, s32[2]{0:T(128)S(1)} %get-tuple-element.59.iface, s32[4,8]{1,0:T(4,128)S(1)} %get-tuple-element.55.cols, bf16[4,256,128]{2,1,0:T(8,128)(2,1)S(1)} %get-tuple-element.64.edges.rest_0_, bf16[4,128,128]{2,1,0:T(8,128)(2,1)S(1)} %second_inner.1.inner, ...), custom_call_target="tpu_custom_call" | custom-call | flops 4026531840 | tf_op jit(solution)/shard_map/third_rows/pallas_call | solution.py:403
  21.6 1.2 %collective-permute-done.6.other = bf16[2,128,128]{2,1,0:T(8,128)(2,1)S(1)} collective-permute-done((bf16[2,128,128]{2,1,0:T(8,128)(2,1)S(1)}, bf16[2,128,128]{2,1,0:T(8,128)(2,1)S(1)}, u32[]{:S(2)}, u32[]{:S(2)}) %collective-permute-start.6) | collective-permute-done | bytes 65568 | tf_op jit(solution)/shard_map/ppermute | solution.py:434
  22.9 3.7 %collective-permute-start.9 = (bf16[4,128,128]{2,1,0:T(8,128)(2,1)S(1)}, bf16[4,128,128]{2,1,0:T(8,128)(2,1)S(1)}, u32[]{:S(2)}, u32[]{:S(2)}) collective-permute-start(bf16[4,128,128]{2,1,0:T(8,128)(2,1)S(1)} %merge.1.after), channel_id=1, source_target_pairs={{0,4},{3,5},{2,6},{1,7},{4,8},{7,9},{6,10},{5,11},{8,12},{11,13},{... | collective-permute-start | bytes 393224 | tf_op jit(solution)/shard_map/ppermute | solution.py:446
  26.6 1.5 %second_rest.1 = (bf16[4,256,128]{2,1,0:T(8,128)(2,1)S(1)}, bf16[4,256,128]{2,1,0:T(8,128)(2,1)S(1)}, bf16[1,2,128,128]{3,2,1,0:T(8,128)(2,1)S(1)}) custom-call(s32[1]{0:T(128)} %bitcast.face_ref, s32[2]{0:T(128)S(1)} %get-tuple-element.59.iface, s32[4,8]{1,0:T(4,128)S(1)} %get-tuple-element.55.cols, ...), custom_call_target="tpu_custom_call" | custom-call | tf_op jit(solution)/shard_map/second_rest/pallas_call | solution.py:403
  28.2 2.3 %interface.1 = (bf16[256,256]{1,0:T(8,128)(2,1)S(1)}, bf16[256,256]{1,0:T(8,128)(2,1)S(1)}, bf16[256,256]{1,0:T(8,128)(2,1)S(1)}, bf16[256,256]{1,0:T(8,128)(2,1)S(1)}, bf16[1,2,128,128]{3,2,1,0:T(8,128)(2,1)S(1)}) custom-call(s32[1]{0:T(128)} %bitcast.face_ref, s32[2]{0:T(128)S(1)} %get-tuple-element.59.iface, s32[4,8]{1,0:T(4,128)S(1)} %get-tuple-element.55.cols, ...), custom_call_target="tpu_custom_call" | custom-call | tf_op jit(solution)/shard_map/interface/pallas_call | solution.py:403
  33.1 1.1 %collective-permute-done.14.rest_9_ = bf16[1,2,128,128]{3,2,1,0:T(8,128)(2,1)S(1)} collective-permute-done((bf16[1,2,128,128]{3,2,1,0:T(8,128)(2,1)S(1)}, bf16[1,2,128,128]{3,2,1,0:T(8,128)(2,1)S(1)}, u32[]{:S(2)}, u32[]{:S(2)}) %collective-permute-start.14) | collective-permute-done | bytes 65568 | tf_op jit(solution)/shard_map/ppermute | solution.py:434
  34.6 3.6 %collective-permute-start.16 = (bf16[4,128,128]{2,1,0:T(8,128)(2,1)S(1)}, bf16[4,128,128]{2,1,0:T(8,128)(2,1)S(1)}, u32[]{:S(2)}, u32[]{:S(2)}) collective-permute-start(bf16[4,128,128]{2,1,0:T(8,128)(2,1)S(1)} %chain.2), channel_id=1, source_target_pairs={{0,4},{3,5},{2,6},{1,7},{4,8},{7,9},{6,10},{5,11},{8,12},{11,13},{... | collective-permute-start | bytes 393224 | tf_op jit(solution)/shard_map/ppermute | solution.py:446
  38.5 3.8 %coupling_last.1.coupled = bf16[1024,1024]{1,0:T(8,128)(2,1)S(1)} custom-call(s32[1]{0:T(128)} %bitcast.face_ref, s32[2]{0:T(128)S(1)} %get-tuple-element.59.iface, s32[4,8]{1,0:T(4,128)S(1)} %get-tuple-element.55.cols, bf16[2,128,128]{2,1,0:T(8,128)(2,1)S(1)} %get-tuple-element.69.gfield.rest_6_, ...), custom_call_target="tpu_custom_call" | custom-call | flops 1342177280 | tf_op jit(solution)/shard_map/coupling_last/pallas_call | solution.py:403
  42.3 1.1 %collective-permute-done.16.rest_10_.rest_2_ = bf16[4,128,128]{2,1,0:T(8,128)(2,1)S(1)} collective-permute-done((bf16[4,128,128]{2,1,0:T(8,128)(2,1)S(1)}, bf16[4,128,128]{2,1,0:T(8,128)(2,1)S(1)}, u32[]{:S(2)}, u32[]{:S(2)}) %collective-permute-start.16) | collective-permute-done | bytes 131104 | tf_op jit(solution)/shard_map/ppermute | solution.py:446
  43.9 1.0 %collective-permute-done.18.rest_11_.rest_3_ = bf16[4,128,128]{2,1,0:T(8,128)(2,1)S(1)} collective-permute-done((bf16[4,128,128]{2,1,0:T(8,128)(2,1)S(1)}, bf16[4,128,128]{2,1,0:T(8,128)(2,1)S(1)}, u32[]{:S(2)}, u32[]{:S(2)}) %collective-permute-start.18) | collective-permute-done | bytes 131104 | tf_op jit(solution)/shard_map/ppermute | solution.py:434
  45.3 2.8 %collective-permute-start.19 = (bf16[4,128,128]{2,1,0:T(8,128)(2,1)S(1)}, bf16[4,128,128]{2,1,0:T(8,128)(2,1)S(1)}, u32[]{:S(2)}, u32[]{:S(2)}) collective-permute-start(bf16[4,128,128]{2,1,0:T(8,128)(2,1)S(1)} %chain.3.rest_11_), channel_id=1, source_target_pairs={{0,4},{3,5},{2,6},{1,7},{4,8},{7,9},{6,10},{5,11},{8,12},{11,13},{... | collective-permute-start | bytes 393224 | tf_op jit(solution)/shard_map/ppermute | solution.py:446
  48.0 2.2 %third.1 = (bf16[8,256,128]{2,1,0:T(8,128)(2,1)S(1)}, bf16[8,256,128]{2,1,0:T(8,128)(2,1)S(1)}) custom-call(s32[1]{0:T(128)} %bitcast.face_ref, s32[4,8]{1,0:T(4,128)S(1)} %get-tuple-element.55.cols, bf16[4,256,128]{2,1,0:T(8,128)(2,1)S(1)} %get-tuple-element.64.edges.rest_0_, bf16[4,256,128]{2,1,0:T(8,128)(2,1)S(1)} %get-tuple-element.77.rest_1_, ...), custom_call_target="tpu_custom_call" | custom-call | tf_op jit(solution)/shard_map/third/pallas_call | solution.py:403
  50.2 1.5 %output.1.earlier = bf16[4,128,1024]{2,1,0:T(8,128)(2,1)} custom-call(s32[1]{0:T(128)} %bitcast.face_ref, bf16[8,256,128]{2,1,0:T(8,128)(2,1)S(1)} %get-tuple-element.100.early, bf16[8,256,128]{2,1,0:T(8,128)(2,1)S(1)} %get-tuple-element.101.later, bf16[1024,1024]{1,0:T(8,128)(2,1)S(1)} %coupling_last.1.coupled, ...), custom_call_target="tpu_custom_call" | custom-call | tf_op jit(solution)/shard_map/output/pallas_call | solution.py:403
  51.8 2.2 %collective-permute-done.19.rest_0_ = bf16[4,128,128]{2,1,0:T(8,128)(2,1)S(1)} collective-permute-done((bf16[4,128,128]{2,1,0:T(8,128)(2,1)S(1)}, bf16[4,128,128]{2,1,0:T(8,128)(2,1)S(1)}, u32[]{:S(2)}, u32[]{:S(2)}) %collective-permute-start.19) | collective-permute-done | bytes 131104 | tf_op jit(solution)/shard_map/ppermute | solution.py:446
  55.8 1.0 %last_other.1 = bf16[4,128,1024]{2,1,0:T(8,128)(2,1)} custom-call(s32[1]{0:T(128)} %bitcast.face_ref, f32[128,1024]{1,0:T(8,128)S(1)} %last_own.1.own_part, bf16[1024,1024]{1,0:T(8,128)(2,1)S(1)} %coupling_last.1.coupled, bf16[4,128,1024]{2,1,0:T(8,128)(2,1)} %output.1.earlier, ...), custom_call_target="tpu_custom_call", output_to_operand_aliasing={{}: (3, {})} | custom-call | tf_op jit(solution)/shard_map/last_other/pallas_call | solution.py:403
  (34 shorter events, 7.0 us)
Async XLA Ops:
  2.6 8.6 %collective-permute-start = (bf16[2,256,128]{2,1,0:T(8,128)(2,1)S(1)}, bf16[2,256,128]{2,1,0:T(8,128)(2,1)S(1)}, u32[]{:S(2)}, u32[]{:S(2)}) collective-permute-start(bf16[2,256,128]{2,1,0:T(8,128)(2,1)S(1)} %get-tuple-element.57), channel_id=1, source_target_pairs={{0,1},{1,0},{2,3},{3,2},{4,5},{5,4},{6,7},{7,6},{8,9},{9,8},{10,11... | collective-permute-start | bytes 393224 | tf_op jit(solution)/shard_map/ppermute | solution.py:431
  3.4 7.8 %collective-permute-start.1 = (bf16[2,256,128]{2,1,0:T(8,128)(2,1)S(1)}, bf16[2,256,128]{2,1,0:T(8,128)(2,1)S(1)}, u32[]{:S(2)}, u32[]{:S(2)}) collective-permute-start(bf16[2,256,128]{2,1,0:T(8,128)(2,1)S(1)} %get-tuple-element.58), channel_id=1, source_target_pairs={{1,2},{2,1},{5,6},{6,5},{9,10},{10,9},{13,14},{14,13},{17,18},{18,... | collective-permute-start | bytes 393224 | tf_op jit(solution)/shard_map/ppermute | solution.py:430
  6.4 9.1 %collective-permute-start.4 = (bf16[2,416,128]{2,1,0:T(8,128)(2,1)S(1)}, bf16[2,416,128]{2,1,0:T(8,128)(2,1)S(1)}, u32[]{:S(2)}, u32[]{:S(2)}) collective-permute-start(bf16[2,416,128]{2,1,0:T(8,128)(2,1)S(1)} %get-tuple-element.70), channel_id=1, source_target_pairs={{0,1},{1,0},{2,3},{3,2},{4,5},{5,4},{6,7},{7,6},{8,9},{9,8},{10,11... | collective-permute-start | bytes 638984 | tf_op jit(solution)/shard_map/ppermute | solution.py:431
  6.5 9.0 %collective-permute-start.5 = (bf16[2,416,128]{2,1,0:T(8,128)(2,1)S(1)}, bf16[2,416,128]{2,1,0:T(8,128)(2,1)S(1)}, u32[]{:S(2)}, u32[]{:S(2)}) collective-permute-start(bf16[2,416,128]{2,1,0:T(8,128)(2,1)S(1)} %get-tuple-element.71), channel_id=1, source_target_pairs={{1,2},{2,1},{5,6},{6,5},{9,10},{10,9},{13,14},{14,13},{17,18},{18,... | collective-permute-start | bytes 638984 | tf_op jit(solution)/shard_map/ppermute | solution.py:430
  12.3 3.1 %collective-permute-start.2 = (bf16[2,256,128]{2,1,0:T(8,128)(2,1)S(1)}, bf16[2,256,128]{2,1,0:T(8,128)(2,1)S(1)}, u32[]{:S(2)}, u32[]{:S(2)}) collective-permute-start(bf16[2,256,128]{2,1,0:T(8,128)(2,1)S(1)} %get-tuple-element.66), channel_id=1, source_target_pairs={{0,1},{1,0},{2,3},{3,2},{4,5},{5,4},{6,7},{7,6},{8,9},{9,8},{10,11... | collective-permute-start | bytes 393224 | tf_op jit(solution)/shard_map/ppermute | solution.py:431
  12.4 8.3 %collective-permute-start.3 = (bf16[2,256,128]{2,1,0:T(8,128)(2,1)S(1)}, bf16[2,256,128]{2,1,0:T(8,128)(2,1)S(1)}, u32[]{:S(2)}, u32[]{:S(2)}) collective-permute-start(bf16[2,256,128]{2,1,0:T(8,128)(2,1)S(1)} %get-tuple-element.67), channel_id=1, source_target_pairs={{1,2},{2,1},{5,6},{6,5},{9,10},{10,9},{13,14},{14,13},{17,18},{18,... | collective-permute-start | bytes 393224 | tf_op jit(solution)/shard_map/ppermute | solution.py:430
  17.2 11.0 %collective-permute-start.7 = (bf16[2,1024,128]{2,1,0:T(8,128)(2,1)S(1)}, bf16[2,1024,128]{2,1,0:T(8,128)(2,1)S(1)}, u32[]{:S(2)}, u32[]{:S(2)}) collective-permute-start(bf16[2,1024,128]{2,1,0:T(8,128)(2,1)S(1)} %get-tuple-element.80), channel_id=1, source_target_pairs={{0,1},{1,0},{2,3},{3,2},{4,5},{5,4},{6,7},{7,6},{8,9},{9,8},{10,11... | collective-permute-start | bytes 1572872 | tf_op jit(solution)/shard_map/ppermute | solution.py:431
  17.2 10.9 %collective-permute-start.8 = (bf16[2,1024,128]{2,1,0:T(8,128)(2,1)S(1)}, bf16[2,1024,128]{2,1,0:T(8,128)(2,1)S(1)}, u32[]{:S(2)}, u32[]{:S(2)}) collective-permute-start(bf16[2,1024,128]{2,1,0:T(8,128)(2,1)S(1)} %get-tuple-element.81), channel_id=1, source_target_pairs={{1,2},{2,1},{5,6},{6,5},{9,10},{10,9},{13,14},{14,13},{17,18},{18,... | collective-permute-start | bytes 1572872 | tf_op jit(solution)/shard_map/ppermute | solution.py:430
  21.6 1.3 %collective-permute-start.6 = (bf16[2,128,128]{2,1,0:T(8,128)(2,1)S(1)}, bf16[2,128,128]{2,1,0:T(8,128)(2,1)S(1)}, u32[]{:S(2)}, u32[]{:S(2)}) collective-permute-start(bf16[2,128,128]{2,1,0:T(8,128)(2,1)S(1)} %third_rows.1.own), channel_id=1, source_target_pairs={{0,1},{1,0},{2,3},{3,2},{4,5},{5,4},{6,7},{7,6},{8,9},{9,8},{10,11... | collective-permute-start | bytes 196616 | tf_op jit(solution)/shard_map/ppermute | solution.py:434
  22.9 8.7 %collective-permute-start.9 = (bf16[4,128,128]{2,1,0:T(8,128)(2,1)S(1)}, bf16[4,128,128]{2,1,0:T(8,128)(2,1)S(1)}, u32[]{:S(2)}, u32[]{:S(2)}) collective-permute-start(bf16[4,128,128]{2,1,0:T(8,128)(2,1)S(1)} %merge.1.after), channel_id=1, source_target_pairs={{0,4},{3,5},{2,6},{1,7},{4,8},{7,9},{6,10},{5,11},{8,12},{11,13},{... | collective-permute-start | bytes 393224 | tf_op jit(solution)/shard_map/ppermute | solution.py:446
  30.5 1.4 %collective-permute-start.10 = (bf16[256,256]{1,0:T(8,128)(2,1)S(1)}, bf16[256,256]{1,0:T(8,128)(2,1)S(1)}, u32[]{:S(2)}, u32[]{:S(2)}) collective-permute-start(bf16[256,256]{1,0:T(8,128)(2,1)S(1)} %get-tuple-element.87.rest_0_.after), channel_id=1, source_target_pairs={{0,1},{1,0},{2,3},{3,2},{4,5},{5,4},{6,7},{7,6},{8,9},{9,8},{10,11... | collective-permute-start | bytes 393224 | tf_op jit(solution)/shard_map/ppermute | solution.py:434
  30.6 1.5 %collective-permute-start.11 = (bf16[256,256]{1,0:T(8,128)(2,1)S(1)}, bf16[256,256]{1,0:T(8,128)(2,1)S(1)}, u32[]{:S(2)}, u32[]{:S(2)}) collective-permute-start(bf16[256,256]{1,0:T(8,128)(2,1)S(1)} %get-tuple-element.88.rest_1_), channel_id=1, source_target_pairs={{0,1},{1,0},{2,3},{3,2},{4,5},{5,4},{6,7},{7,6},{8,9},{9,8},{10,11... | collective-permute-start | bytes 393224 | tf_op jit(solution)/shard_map/ppermute | solution.py:434
  31.1 1.3 %collective-permute-start.12 = (bf16[256,256]{1,0:T(8,128)(2,1)S(1)}, bf16[256,256]{1,0:T(8,128)(2,1)S(1)}, u32[]{:S(2)}, u32[]{:S(2)}) collective-permute-start(bf16[256,256]{1,0:T(8,128)(2,1)S(1)} %get-tuple-element.89.rest_2_), channel_id=1, source_target_pairs={{0,1},{1,0},{2,3},{3,2},{4,5},{5,4},{6,7},{7,6},{8,9},{9,8},{10,11... | collective-permute-start | bytes 393224 | tf_op jit(solution)/shard_map/ppermute | solution.py:434
  31.1 1.5 %collective-permute-start.13 = (bf16[256,256]{1,0:T(8,128)(2,1)S(1)}, bf16[256,256]{1,0:T(8,128)(2,1)S(1)}, u32[]{:S(2)}, u32[]{:S(2)}) collective-permute-start(bf16[256,256]{1,0:T(8,128)(2,1)S(1)} %get-tuple-element.90.rest_3_), channel_id=1, source_target_pairs={{0,1},{1,0},{2,3},{3,2},{4,5},{5,4},{6,7},{7,6},{8,9},{9,8},{10,11... | collective-permute-start | bytes 393224 | tf_op jit(solution)/shard_map/ppermute | solution.py:434
  32.6 1.6 %collective-permute-start.15 = (bf16[4,128,128]{2,1,0:T(8,128)(2,1)S(1)}, bf16[4,128,128]{2,1,0:T(8,128)(2,1)S(1)}, u32[]{:S(2)}, u32[]{:S(2)}) collective-permute-start(bf16[4,128,128]{2,1,0:T(8,128)(2,1)S(1)} %collective-permute-done.9.rest_10_.rest_0_), channel_id=1, source_target_pairs={{0,1},{1,0},{2,3},{3,2},{4,5},{5,4},{6,7},{7,6},{8,9},{9,8},{10,11... | collective-permute-start | bytes 393224 | tf_op jit(solution)/shard_map/ppermute | solution.py:434
  32.9 1.3 %collective-permute-start.14 = (bf16[1,2,128,128]{3,2,1,0:T(8,128)(2,1)S(1)}, bf16[1,2,128,128]{3,2,1,0:T(8,128)(2,1)S(1)}, u32[]{:S(2)}, u32[]{:S(2)}) collective-permute-start(bf16[1,2,128,128]{3,2,1,0:T(8,128)(2,1)S(1)} %get-tuple-element.96.rest_8_), channel_id=1, source_target_pairs={{0,1},{1,0},{2,3},{3,2},{4,5},{5,4},{6,7},{7,6},{8,9},{9,8},{10,11... | collective-permute-start | bytes 196616 | tf_op jit(solution)/shard_map/ppermute | solution.py:434
  34.6 8.8 %collective-permute-start.16 = (bf16[4,128,128]{2,1,0:T(8,128)(2,1)S(1)}, bf16[4,128,128]{2,1,0:T(8,128)(2,1)S(1)}, u32[]{:S(2)}, u32[]{:S(2)}) collective-permute-start(bf16[4,128,128]{2,1,0:T(8,128)(2,1)S(1)} %chain.2), channel_id=1, source_target_pairs={{0,4},{3,5},{2,6},{1,7},{4,8},{7,9},{6,10},{5,11},{8,12},{11,13},{... | collective-permute-start | bytes 393224 | tf_op jit(solution)/shard_map/ppermute | solution.py:446
  38.2 4.0 %collective-permute-start.17 = (bf16[1,2,128,128]{3,2,1,0:T(8,128)(2,1)S(1)}, bf16[1,2,128,128]{3,2,1,0:T(8,128)(2,1)S(1)}, u32[]{:S(2)}, u32[]{:S(2)}) collective-permute-start(bf16[1,2,128,128]{3,2,1,0:T(8,128)(2,1)S(1)} %get-tuple-element.95.rest_8_), channel_id=1, source_target_pairs={{0,1},{1,0},{2,3},{3,2},{4,5},{5,4},{6,7},{7,6},{8,9},{9,8},{10,11... | collective-permute-start | bytes 196616 | tf_op jit(solution)/shard_map/ppermute | solution.py:434
  43.4 1.5 %collective-permute-start.18 = (bf16[4,128,128]{2,1,0:T(8,128)(2,1)S(1)}, bf16[4,128,128]{2,1,0:T(8,128)(2,1)S(1)}, u32[]{:S(2)}, u32[]{:S(2)}) collective-permute-start(bf16[4,128,128]{2,1,0:T(8,128)(2,1)S(1)} %collective-permute-done.16.rest_10_.rest_2_), channel_id=1, source_target_pairs={{0,1},{1,0},{2,3},{3,2},{4,5},{5,4},{6,7},{7,6},{8,9},{9,8},{10,11... | collective-permute-start | bytes 393224 | tf_op jit(solution)/shard_map/ppermute | solution.py:434
  45.3 8.8 %collective-permute-start.19 = (bf16[4,128,128]{2,1,0:T(8,128)(2,1)S(1)}, bf16[4,128,128]{2,1,0:T(8,128)(2,1)S(1)}, u32[]{:S(2)}, u32[]{:S(2)}) collective-permute-start(bf16[4,128,128]{2,1,0:T(8,128)(2,1)S(1)} %chain.3.rest_11_), channel_id=1, source_target_pairs={{0,4},{3,5},{2,6},{1,7},{4,8},{7,9},{6,10},{5,11},{8,12},{11,13},{... | collective-permute-start | bytes 393224 | tf_op jit(solution)/shard_map/ppermute | solution.py:446
  54.0 1.8 %collective-permute-start.20 = (bf16[4,128,128]{2,1,0:T(8,128)(2,1)S(1)}, bf16[4,128,128]{2,1,0:T(8,128)(2,1)S(1)}, u32[]{:S(2)}, u32[]{:S(2)}) collective-permute-start(bf16[4,128,128]{2,1,0:T(8,128)(2,1)S(1)} %collective-permute-done.19.rest_0_), channel_id=1, source_target_pairs={{0,1},{1,0},{2,3},{3,2},{4,5},{5,4},{6,7},{7,6},{8,9},{9,8},{10,11... | collective-permute-start | bytes 393224 | tf_op jit(solution)/shard_map/ppermute | solution.py:434

commit v11 on v10

--- a/solution.py
+++ b/solution.py
@@ -251,25 +251,24 @@
             ext[pl.ds(start, HALO), pl.ds(d.start(other + shift), d.group), :] = block[:, at : at + d.group, :]
 
 
-def second_rest_kernel(d, face_ref, iface, cols, edges, field, ext0, pair_in, cross_in, later, later_ext0, folded, after, *rest):
-    inner, inner_later, *faces_out, ext = rest
+def second_rest_kernel(d, face_ref, iface, cols, *rest):
+    edges, field, ext0, pair_in, cross_in = rest[:5]
+    later_edges, later, later_ext0, later_pair_in, later_cross_in, folded, after = rest[5:12]
+    inner, inner_later, faces_later, *faces_early, ext = rest[12:]
     face = face_ref[0]
     correct(d, cols, face, field, folded, inner, ext0, range(HALO, d.last))
     correct(d, cols, face, later, folded, inner_later, later_ext0, range(HALO, d.last))
-    for out in faces_out:
-        outs = [out.at[t] for t in range(d.split - 1)]
-        held = ext.at[:, pl.ds(0, len(outs) * d.sources), :]
-        interface_rows(d, face, iface, cols, edges, inner, field, pair_in, cross_in, folded, 1, outs, held)
-
-
-def interface_kernel(d, face_ref, iface, cols, *rest):
-    later, (folded, gfield, gfirst) = rest[:5], rest[5:8]
-    chain, (faces_out, ext, small) = rest[8 : 8 + d.parts], rest[8 + d.parts :]
+    groups = [((later_edges, inner_later, later, later_pair_in, later_cross_in), 0, faces_later, d.ticks - 1 - d.split)]
+    groups += [((edges, inner, field, pair_in, cross_in), 1, out, d.split - 1) for out in faces_early]
+    for group, first, out, ticks in groups:
+        outs = [out.at[t] for t in range(ticks)]
+        interface_rows(d, face, iface, cols, *group, folded, first, outs, ext.at[:, pl.ds(0, ticks * d.sources), :])
+
+
+def interface_kernel(d, face_ref, iface, cols, gfield, gfirst, pair_in, cross_in, folded, after, *rest):
+    *chain, ext = rest
     face = face_ref[0]
     w = d.width
-    pair_in, cross_in = later[3:]
-    outs = [faces_out.at[t] for t in range(d.ticks - 1 - d.split)]
-    interface_rows(d, face, iface, cols, *later, folded, 0, outs, small.at[:, pl.ds(0, len(outs) * d.sources), :])
     coupling_ext(d, face, gfirst, pair_in, cross_in, ext)
     for i in range(d.slots):
         start = i * d.group % d.part
@@ -519,32 +518,32 @@
         [(2 * nq, sources, width)],
     )
 
-    inner, inner_later, *faces_early = call(
-        functools.partial(second_rest_kernel, d),
-        "second_rest",
-        [face, iface, cols],
-        [edges, field, ext0, pair1, cross1, field_later, ext_later0, folded, sent],
-        [(count - 2 * HALO, early, width), (count - 2 * HALO, later, width)]
-        + [(split - 1, nq, sources, width)] * (split > 1),
-        [(ext, early, width)],
-        anywhere=(8,),
-    )
+    def beside_first():
+        rows = call(
+            functools.partial(interface_kernel, d),
+            "interface",
+            [face, iface, cols],
+            [gfield, gfirst, pair_later1, cross_later1, folded, sent],
+            [(d.part, group)] * d.parts,
+            [(ext, wide, width)],
+            anywhere=(5,),
+        )
+        rest = call(
+            functools.partial(second_rest_kernel, d),
+            "second_rest",
+            [face, iface, cols],
+            [edges, field, ext0, pair1, cross1, edges_later, field_later, ext_later0, pair_later1, cross_later1, folded, rows[0]],
+            [(count - 2 * HALO, early, width), (count - 2 * HALO, later, width), (ticks - 1 - split, nq, sources, width)]
+            + [(split - 1, nq, sources, width)] * (split > 1),
+            [(ext, max(early, later), width)],
+            anywhere=(11,),
+        )
+        return rows, [swap(x) for x in rows], rest
+
+    arrived, (chain, other_chain, (inner, inner_later, faces_later, *faces_early)) = onward(sent, beside_first)
     other_early = [swap(x) for x in faces_early]
     early_parts = (edges, inner, field, pair1, cross1)
     later_parts = (edges_later, inner_later, field_later, pair_later1, cross_later1)
-
-    def beside_first():
-        *rows, faces_later = call(
-            functools.partial(interface_kernel, d),
-            "interface",
-            [face, iface, cols],
-            [*later_parts, folded, gfield, gfirst],
-            [(d.part, group)] * d.parts + [(ticks - 1 - split, nq, sources, width)],
-            [(ext, wide, width), (ext, later, width)],
-        )
-        return rows, [swap(x) for x in rows], faces_later
-
-    arrived, (chain, other_chain, faces_later) = onward(sent, beside_first)
 
     def fields(after):
         return call(

time: 57.3 us -> 57.4 us (level)
    ppermute x4, waiting for transfers between devices: 0.01 us -> 1.12 us  [exchange(): got = lax.ppermute(cross, 'face', crossing)]
    ppermute x10, waiting for transfers between devices: 4.94 us -> 3.87 us  [swap(): return lax.ppermute(block, 'face', pairing)]
  transfers between devices with their start and end apart: 21 -> 21, of which waited for: 10 -> 7; matrix products, arithmetic and copies ran while one was open for 0% -> 0% of each run, Pallas kernels for 32% -> 32%
where the time goes in v11:
time: 57.4 us; the launch traced here: 57.1 us
  starting transfers between devices  25.2 us (44%)
  Pallas kernels  23 us (40%)
  waiting for transfers between devices  8.52 us (15%)
    pallas_call x16, Pallas kernels, call(): pl.pallas_call(body, name=name, out_shape=outs, in_specs=[pl.BlockSpec(me...  23 us
    ppermute x4, starting transfers between devices, exchange(): got = lax.ppermute(cross, 'face', crossing)  11.1 us
    ppermute x3, starting transfers between devices, onward(): own.append(lax.ppermute(block, ('slab', 'face'), route))  10 us
    ppermute x10, waiting for transfers between devices, swap(): return lax.ppermute(block, 'face', pairing)  3.87 us
    ppermute x3, waiting for transfers between devices, onward(): own.append(lax.ppermute(block, ('slab', 'face'), route))  3.51 us
    ppermute x10, starting transfers between devices, swap(): return lax.ppermute(block, 'face', pairing)  3.09 us
  transfers between devices with their start and end apart: 21, of which 7 were waited for; matrix products, arithmetic and copies ran while one was open for 0% of the time, Pallas kernels for 32%

profile of v11, /device:TPU:9, one launch (start us, length us, event | category | flops | bytes accessed | tf_op | source)
XLA Modules:
  0.0 57.1 jit_solution(16158841351525995171)
XLA Ops:
  0.0 2.6 %first.1 = (bf16[8,256,128]{2,1,0:T(8,128)(2,1)S(1)}, bf16[8,256,128]{2,1,0:T(8,128)(2,1)S(1)}, bf16[2,128,128]{2,1,0:T(8,128)(2,1)S(1)}, bf16[2,256,128]{2,1,0:...) custom-call(s32[1]{0:T(128)} %bitcast.face_ref, ...), custom_call_target="tpu_custom_call" | custom-call | tf_op jit(solution)/shard_map/first/pallas_call | solution.py:402
  3.4 3.0 %collective-permute-start.1 = (bf16[2,256,128]{2,1,0:T(8,128)(2,1)S(1)}, bf16[2,256,128]{2,1,0:T(8,128)(2,1)S(1)}, u32[]{:S(2)}, u32[]{:S(2)}) collective-permute-start(bf16[2,256,128]{2,1,0:T(8,128)(2,1)S(1)} %get-tuple-element.61), channel_id=1, source_target_pairs={{1,2},{2,1},{5,6},{6,5},{9,10},{10,9},{13,14},{14,13},{17,18},{18,... | collective-permute-start | bytes 393224 | tf_op jit(solution)/shard_map/ppermute | solution.py:429
  6.5 2.5 %collective-permute-start.4 = (bf16[2,416,128]{2,1,0:T(8,128)(2,1)S(1)}, bf16[2,416,128]{2,1,0:T(8,128)(2,1)S(1)}, u32[]{:S(2)}, u32[]{:S(2)}) collective-permute-start(bf16[2,416,128]{2,1,0:T(8,128)(2,1)S(1)} %get-tuple-element.73), channel_id=1, source_target_pairs={{1,2},{2,1},{5,6},{6,5},{9,10},{10,9},{13,14},{14,13},{17,18},{18,... | collective-permute-start | bytes 638984 | tf_op jit(solution)/shard_map/ppermute | solution.py:429
  9.0 2.2 %fold.1 = (bf16[8,640,128]{2,1,0:T(8,128)(2,1)S(1)}, bf16[6,128,1024]{2,1,0:T(8,128)(2,1)S(1)}) custom-call(s32[1]{0:T(128)} %bitcast.face_ref, s32[2]{0:T(128)S(1)} %get-tuple-element.62.iface, s32[4,8]{1,0:T(4,128)S(1)} %get-tuple-element.58.cols, bf16[8,128,128]{2,1,0:T(8,128)(2,1)S(1)} %get-tuple-element.63.inv, ...), custom_call_target="tpu_custom_call" | custom-call | tf_op jit(solution)/shard_map/fold/pallas_call | solution.py:402
  11.2 1.1 %second_edges.1 = (bf16[4,256,128]{2,1,0:T(8,128)(2,1)S(1)}, bf16[2,256,128]{2,1,0:T(8,128)(2,1)S(1)}, bf16[2,256,128]{2,1,0:T(8,128)(2,1)S(1)}, bf16[12,256,128]{2,1,0:T(8,128)(2,1)S(1)}) custom-call(s32[1]{0:T(128)} %bitcast.face_ref, s32[4,8]{1,0:T(4,128)S(1)} %get-tuple-element.58.cols, bf16[8,256,128]{2,1,0:T(8,128)(2,1)S(1)} %get-tuple-element.59.field.rest_1_.rest_2_, ...), custom_call_target="tpu_custom_call" | custom-call | tf_op jit(solution)/shard_map/second_edges/pallas_call | solution.py:402
  12.4 3.0 %collective-permute-start.2 = (bf16[2,256,128]{2,1,0:T(8,128)(2,1)S(1)}, bf16[2,256,128]{2,1,0:T(8,128)(2,1)S(1)}, u32[]{:S(2)}, u32[]{:S(2)}) collective-permute-start(bf16[2,256,128]{2,1,0:T(8,128)(2,1)S(1)} %get-tuple-element.68), channel_id=1, source_target_pairs={{1,2},{2,1},{5,6},{6,5},{9,10},{10,9},{13,14},{14,13},{17,18},{18,... | collective-permute-start | bytes 393224 | tf_op jit(solution)/shard_map/ppermute | solution.py:429
  15.5 1.7 %behind.1 = (bf16[4,256,128]{2,1,0:T(8,128)(2,1)S(1)}, bf16[8,1024,128]{2,1,0:T(8,128)(2,1)S(1)}, bf16[2,1024,128]{2,1,0:T(8,128)(2,1)S(1)}, bf16[2,1024,128]{2,1,0:T(8,128)(2,1)S(1)}, bf16[12,256,128]{2,1,0:T(8,128)(2,1)S(1)}) custom-call(s32[1]{0:T(128)} %bitcast.face_ref, s32[2]{0:T(128)S(1)} %get-tuple-element.62.iface, ...), custom_call_target="tpu_custom_call" | custom-call | tf_op jit(solution)/shard_map/behind/pallas_call | solution.py:402
  17.2 2.5 %collective-permute-start.9 = (bf16[2,1024,128]{2,1,0:T(8,128)(2,1)S(1)}, bf16[2,1024,128]{2,1,0:T(8,128)(2,1)S(1)}, u32[]{:S(2)}, u32[]{:S(2)}) collective-permute-start(bf16[2,1024,128]{2,1,0:T(8,128)(2,1)S(1)} %get-tuple-element.80), channel_id=1, source_target_pairs={{1,2},{2,1},{5,6},{6,5},{9,10},{10,9},{13,14},{14,13},{17,18},{18,... | collective-permute-start | bytes 1572872 | tf_op jit(solution)/shard_map/ppermute | solution.py:429
  19.8 0.9 %second_inner.1.inner = bf16[4,128,128]{2,1,0:T(8,128)(2,1)S(1)} custom-call(s32[1]{0:T(128)} %bitcast.face_ref, s32[4,8]{1,0:T(4,128)S(1)} %get-tuple-element.58.cols, bf16[8,256,128]{2,1,0:T(8,128)(2,1)S(1)} %get-tuple-element.59.field.rest_1_.rest_2_, bf16[12,256,128]{2,1,0:T(8,128)(2,1)S(1)} %get-tuple-element.69.ext.rest_2_, ...), custom_call_target="tpu_custom_call" | custom-call | tf_op jit(solution)/shard_map/second_inner/pallas_call | solution.py:402
  21.6 1.2 %collective-permute-done.6.other = bf16[2,128,128]{2,1,0:T(8,128)(2,1)S(1)} collective-permute-done((bf16[2,128,128]{2,1,0:T(8,128)(2,1)S(1)}, bf16[2,128,128]{2,1,0:T(8,128)(2,1)S(1)}, u32[]{:S(2)}, u32[]{:S(2)}) %collective-permute-start.6) | collective-permute-done | bytes 65568 | tf_op jit(solution)/shard_map/ppermute | solution.py:433
  22.9 3.7 %collective-permute-start.7 = (bf16[4,128,128]{2,1,0:T(8,128)(2,1)S(1)}, bf16[4,128,128]{2,1,0:T(8,128)(2,1)S(1)}, u32[]{:S(2)}, u32[]{:S(2)}) collective-permute-start(bf16[4,128,128]{2,1,0:T(8,128)(2,1)S(1)} %merge.1.after), channel_id=1, source_target_pairs={{0,4},{3,5},{2,6},{1,7},{4,8},{7,9},{6,10},{5,11},{8,12},{11,13},{... | collective-permute-start | bytes 393224 | tf_op jit(solution)/shard_map/ppermute | solution.py:445
  26.6 1.1 %collective-permute-done.9.cross_in.rest_9_ = bf16[2,1024,128]{2,1,0:T(8,128)(2,1)S(1)} collective-permute-done((bf16[2,1024,128]{2,1,0:T(8,128)(2,1)S(1)}, bf16[2,1024,128]{2,1,0:T(8,128)(2,1)S(1)}, u32[]{:S(2)}, u32[]{:S(2)}) %collective-permute-start.9) | collective-permute-done | bytes 524320 | tf_op jit(solution)/shard_map/ppermute | solution.py:429
  27.7 2.2 %interface.1 = (bf16[256,256]{1,0:T(8,128)(2,1)S(1)}, bf16[256,256]{1,0:T(8,128)(2,1)S(1)}, bf16[256,256]{1,0:T(8,128)(2,1)S(1)}, bf16[256,256]{1,0:T(8,128)(2,1)S(1)}) custom-call(s32[1]{0:T(128)} %bitcast.face_ref, s32[2]{0:T(128)S(1)} %get-tuple-element.62.iface, s32[4,8]{1,0:T(4,128)S(1)} %get-tuple-element.58.cols, ...), custom_call_target="tpu_custom_call" | custom-call | tf_op jit(solution)/shard_map/interface/pallas_call | solution.py:402
  31.0 1.7 %second_rest.1 = (bf16[4,256,128]{2,1,0:T(8,128)(2,1)S(1)}, bf16[4,256,128]{2,1,0:T(8,128)(2,1)S(1)}, bf16[1,2,128,128]{3,2,1,0:T(8,128)(2,1)S(1)}, bf16[1,2,128,128]{3,2,1,0:T(8,128)(2,1)S(1)}) custom-call(s32[1]{0:T(128)} %bitcast.face_ref, s32[2]{0:T(128)S(1)} %get-tuple-element.62.iface, s32[4,8]{1,0:T(4,128)S(1)} %get-tuple-element.58.cols, ...), custom_call_target="tpu_custom_call" | custom-call | tf_op jit(solution)/shard_map/second_rest/pallas_call | solution.py:402
  33.4 0.9 %collective-permute-done.14.rest_9_ = bf16[1,2,128,128]{3,2,1,0:T(8,128)(2,1)S(1)} collective-permute-done((bf16[1,2,128,128]{3,2,1,0:T(8,128)(2,1)S(1)}, bf16[1,2,128,128]{3,2,1,0:T(8,128)(2,1)S(1)}, u32[]{:S(2)}, u32[]{:S(2)}) %collective-permute-start.14) | collective-permute-done | bytes 65568 | tf_op jit(solution)/shard_map/ppermute | solution.py:433
  34.8 3.6 %collective-permute-start.16 = (bf16[4,128,128]{2,1,0:T(8,128)(2,1)S(1)}, bf16[4,128,128]{2,1,0:T(8,128)(2,1)S(1)}, u32[]{:S(2)}, u32[]{:S(2)}) collective-permute-start(bf16[4,128,128]{2,1,0:T(8,128)(2,1)S(1)} %chain.2), channel_id=1, source_target_pairs={{0,4},{3,5},{2,6},{1,7},{4,8},{7,9},{6,10},{5,11},{8,12},{11,13},{... | collective-permute-start | bytes 393224 | tf_op jit(solution)/shard_map/ppermute | solution.py:445
  38.8 3.8 %coupling_last.1.coupled = bf16[1024,1024]{1,0:T(8,128)(2,1)S(1)} custom-call(s32[1]{0:T(128)} %bitcast.face_ref, s32[2]{0:T(128)S(1)} %get-tuple-element.62.iface, s32[4,8]{1,0:T(4,128)S(1)} %get-tuple-element.58.cols, bf16[2,128,128]{2,1,0:T(8,128)(2,1)S(1)} %get-tuple-element.71.gfield, bf16[8,1024,128]{2,1,0:T(8,128)(2,1)S(1)} %get-tuple-element.76.after.gfirst, ...), custom_call_target="tpu_custom_call" | custom-call | flops 1342177280 | tf_op jit(solution)/shard_map/coupling_last/pallas_call | solution.py:402
  42.6 1.1 %collective-permute-done.16.rest_10_.rest_2_ = bf16[4,128,128]{2,1,0:T(8,128)(2,1)S(1)} collective-permute-done((bf16[4,128,128]{2,1,0:T(8,128)(2,1)S(1)}, bf16[4,128,128]{2,1,0:T(8,128)(2,1)S(1)}, u32[]{:S(2)}, u32[]{:S(2)}) %collective-permute-start.16) | collective-permute-done | bytes 131104 | tf_op jit(solution)/shard_map/ppermute | solution.py:445
  44.0 1.0 %collective-permute-done.18.rest_11_.rest_3_ = bf16[4,128,128]{2,1,0:T(8,128)(2,1)S(1)} collective-permute-done((bf16[4,128,128]{2,1,0:T(8,128)(2,1)S(1)}, bf16[4,128,128]{2,1,0:T(8,128)(2,1)S(1)}, u32[]{:S(2)}, u32[]{:S(2)}) %collective-permute-start.18) | collective-permute-done | bytes 131104 | tf_op jit(solution)/shard_map/ppermute | solution.py:433
  45.4 2.7 %collective-permute-start.19 = (bf16[4,128,128]{2,1,0:T(8,128)(2,1)S(1)}, bf16[4,128,128]{2,1,0:T(8,128)(2,1)S(1)}, u32[]{:S(2)}, u32[]{:S(2)}) collective-permute-start(bf16[4,128,128]{2,1,0:T(8,128)(2,1)S(1)} %chain.3.rest_11_), channel_id=1, source_target_pairs={{0,4},{3,5},{2,6},{1,7},{4,8},{7,9},{6,10},{5,11},{8,12},{11,13},{... | collective-permute-start | bytes 393224 | tf_op jit(solution)/shard_map/ppermute | solution.py:445
  48.1 2.2 %third.1 = (bf16[8,256,128]{2,1,0:T(8,128)(2,1)S(1)}, bf16[8,256,128]{2,1,0:T(8,128)(2,1)S(1)}) custom-call(s32[1]{0:T(128)} %bitcast.face_ref, s32[4,8]{1,0:T(4,128)S(1)} %get-tuple-element.58.cols, bf16[4,256,128]{2,1,0:T(8,128)(2,1)S(1)} %get-tuple-element.67.edges.rest_0_, bf16[4,256,128]{2,1,0:T(8,128)(2,1)S(1)} %get-tuple-element.91.rest_1_, ...), custom_call_target="tpu_custom_call" | custom-call | tf_op jit(solution)/shard_map/third/pallas_call | solution.py:402
  50.3 1.5 %output.1.earlier = bf16[4,128,1024]{2,1,0:T(8,128)(2,1)} custom-call(s32[1]{0:T(128)} %bitcast.face_ref, bf16[8,256,128]{2,1,0:T(8,128)(2,1)S(1)} %get-tuple-element.106.early, bf16[8,256,128]{2,1,0:T(8,128)(2,1)S(1)} %get-tuple-element.107.later, bf16[1024,1024]{1,0:T(8,128)(2,1)S(1)} %coupling_last.1.coupled, ...), custom_call_target="tpu_custom_call" | custom-call | tf_op jit(solution)/shard_map/output/pallas_call | solution.py:402
  51.8 2.5 %collective-permute-done.19.rest_0_ = bf16[4,128,128]{2,1,0:T(8,128)(2,1)S(1)} collective-permute-done((bf16[4,128,128]{2,1,0:T(8,128)(2,1)S(1)}, bf16[4,128,128]{2,1,0:T(8,128)(2,1)S(1)}, u32[]{:S(2)}, u32[]{:S(2)}) %collective-permute-start.19) | collective-permute-done | bytes 131104 | tf_op jit(solution)/shard_map/ppermute | solution.py:445
  55.9 1.0 %last_other.1 = bf16[4,128,1024]{2,1,0:T(8,128)(2,1)} custom-call(s32[1]{0:T(128)} %bitcast.face_ref, f32[128,1024]{1,0:T(8,128)S(1)} %last_own.1.own_part, bf16[1024,1024]{1,0:T(8,128)(2,1)S(1)} %coupling_last.1.coupled, bf16[4,128,1024]{2,1,0:T(8,128)(2,1)} %output.1.earlier, ...), custom_call_target="tpu_custom_call", output_to_operand_aliasing={{}: (3, {})} | custom-call | tf_op jit(solution)/shard_map/last_other/pallas_call | solution.py:402
  (34 shorter events, 6.7 us)
Async XLA Ops:
  2.6 8.6 %collective-permute-start = (bf16[2,256,128]{2,1,0:T(8,128)(2,1)S(1)}, bf16[2,256,128]{2,1,0:T(8,128)(2,1)S(1)}, u32[]{:S(2)}, u32[]{:S(2)}) collective-permute-start(bf16[2,256,128]{2,1,0:T(8,128)(2,1)S(1)} %get-tuple-element.60), channel_id=1, source_target_pairs={{0,1},{1,0},{2,3},{3,2},{4,5},{5,4},{6,7},{7,6},{8,9},{9,8},{10,11... | collective-permute-start | bytes 393224 | tf_op jit(solution)/shard_map/ppermute | solution.py:430
  3.4 7.8 %collective-permute-start.1 = (bf16[2,256,128]{2,1,0:T(8,128)(2,1)S(1)}, bf16[2,256,128]{2,1,0:T(8,128)(2,1)S(1)}, u32[]{:S(2)}, u32[]{:S(2)}) collective-permute-start(bf16[2,256,128]{2,1,0:T(8,128)(2,1)S(1)} %get-tuple-element.61), channel_id=1, source_target_pairs={{1,2},{2,1},{5,6},{6,5},{9,10},{10,9},{13,14},{14,13},{17,18},{18,... | collective-permute-start | bytes 393224 | tf_op jit(solution)/shard_map/ppermute | solution.py:429
  6.4 9.1 %collective-permute-start.3 = (bf16[2,416,128]{2,1,0:T(8,128)(2,1)S(1)}, bf16[2,416,128]{2,1,0:T(8,128)(2,1)S(1)}, u32[]{:S(2)}, u32[]{:S(2)}) collective-permute-start(bf16[2,416,128]{2,1,0:T(8,128)(2,1)S(1)} %get-tuple-element.72), channel_id=1, source_target_pairs={{0,1},{1,0},{2,3},{3,2},{4,5},{5,4},{6,7},{7,6},{8,9},{9,8},{10,11... | collective-permute-start | bytes 638984 | tf_op jit(solution)/shard_map/ppermute | solution.py:430
  6.5 9.0 %collective-permute-start.4 = (bf16[2,416,128]{2,1,0:T(8,128)(2,1)S(1)}, bf16[2,416,128]{2,1,0:T(8,128)(2,1)S(1)}, u32[]{:S(2)}, u32[]{:S(2)}) collective-permute-start(bf16[2,416,128]{2,1,0:T(8,128)(2,1)S(1)} %get-tuple-element.73), channel_id=1, source_target_pairs={{1,2},{2,1},{5,6},{6,5},{9,10},{10,9},{13,14},{14,13},{17,18},{18,... | collective-permute-start | bytes 638984 | tf_op jit(solution)/shard_map/ppermute | solution.py:429
  12.3 3.1 %collective-permute-start.5 = (bf16[2,256,128]{2,1,0:T(8,128)(2,1)S(1)}, bf16[2,256,128]{2,1,0:T(8,128)(2,1)S(1)}, u32[]{:S(2)}, u32[]{:S(2)}) collective-permute-start(bf16[2,256,128]{2,1,0:T(8,128)(2,1)S(1)} %get-tuple-element.75), channel_id=1, source_target_pairs={{0,1},{1,0},{2,3},{3,2},{4,5},{5,4},{6,7},{7,6},{8,9},{9,8},{10,11... | collective-permute-start | bytes 393224 | tf_op jit(solution)/shard_map/ppermute | solution.py:430
  12.4 8.3 %collective-permute-start.2 = (bf16[2,256,128]{2,1,0:T(8,128)(2,1)S(1)}, bf16[2,256,128]{2,1,0:T(8,128)(2,1)S(1)}, u32[]{:S(2)}, u32[]{:S(2)}) collective-permute-start(bf16[2,256,128]{2,1,0:T(8,128)(2,1)S(1)} %get-tuple-element.68), channel_id=1, source_target_pairs={{1,2},{2,1},{5,6},{6,5},{9,10},{10,9},{13,14},{14,13},{17,18},{18,... | collective-permute-start | bytes 393224 | tf_op jit(solution)/shard_map/ppermute | solution.py:429
  17.2 9.5 %collective-permute-start.8 = (bf16[2,1024,128]{2,1,0:T(8,128)(2,1)S(1)}, bf16[2,1024,128]{2,1,0:T(8,128)(2,1)S(1)}, u32[]{:S(2)}, u32[]{:S(2)}) collective-permute-start(bf16[2,1024,128]{2,1,0:T(8,128)(2,1)S(1)} %get-tuple-element.79), channel_id=1, source_target_pairs={{0,1},{1,0},{2,3},{3,2},{4,5},{5,4},{6,7},{7,6},{8,9},{9,8},{10,11... | collective-permute-start | bytes 1572872 | tf_op jit(solution)/shard_map/ppermute | solution.py:430
  17.2 10.5 %collective-permute-start.9 = (bf16[2,1024,128]{2,1,0:T(8,128)(2,1)S(1)}, bf16[2,1024,128]{2,1,0:T(8,128)(2,1)S(1)}, u32[]{:S(2)}, u32[]{:S(2)}) collective-permute-start(bf16[2,1024,128]{2,1,0:T(8,128)(2,1)S(1)} %get-tuple-element.80), channel_id=1, source_target_pairs={{1,2},{2,1},{5,6},{6,5},{9,10},{10,9},{13,14},{14,13},{17,18},{18,... | collective-permute-start | bytes 1572872 | tf_op jit(solution)/shard_map/ppermute | solution.py:429
  21.5 1.3 %collective-permute-start.6 = (bf16[2,128,128]{2,1,0:T(8,128)(2,1)S(1)}, bf16[2,128,128]{2,1,0:T(8,128)(2,1)S(1)}, u32[]{:S(2)}, u32[]{:S(2)}) collective-permute-start(bf16[2,128,128]{2,1,0:T(8,128)(2,1)S(1)} %third_rows.1.own), channel_id=1, source_target_pairs={{0,1},{1,0},{2,3},{3,2},{4,5},{5,4},{6,7},{7,6},{8,9},{9,8},{10,11... | collective-permute-start | bytes 196616 | tf_op jit(solution)/shard_map/ppermute | solution.py:433
  22.9 9.9 %collective-permute-start.7 = (bf16[4,128,128]{2,1,0:T(8,128)(2,1)S(1)}, bf16[4,128,128]{2,1,0:T(8,128)(2,1)S(1)}, u32[]{:S(2)}, u32[]{:S(2)}) collective-permute-start(bf16[4,128,128]{2,1,0:T(8,128)(2,1)S(1)} %merge.1.after), channel_id=1, source_target_pairs={{0,4},{3,5},{2,6},{1,7},{4,8},{7,9},{6,10},{5,11},{8,12},{11,13},{... | collective-permute-start | bytes 393224 | tf_op jit(solution)/shard_map/ppermute | solution.py:445
  30.0 2.8 %collective-permute-start.11 = (bf16[256,256]{1,0:T(8,128)(2,1)S(1)}, bf16[256,256]{1,0:T(8,128)(2,1)S(1)}, u32[]{:S(2)}, u32[]{:S(2)}) collective-permute-start(bf16[256,256]{1,0:T(8,128)(2,1)S(1)} %get-tuple-element.94.rest_1_), channel_id=1, source_target_pairs={{0,1},{1,0},{2,3},{3,2},{4,5},{5,4},{6,7},{7,6},{8,9},{9,8},{10,11... | collective-permute-start | bytes 393224 | tf_op jit(solution)/shard_map/ppermute | solution.py:433
  30.0 2.8 %collective-permute-start.12 = (bf16[256,256]{1,0:T(8,128)(2,1)S(1)}, bf16[256,256]{1,0:T(8,128)(2,1)S(1)}, u32[]{:S(2)}, u32[]{:S(2)}) collective-permute-start(bf16[256,256]{1,0:T(8,128)(2,1)S(1)} %get-tuple-element.95.rest_2_), channel_id=1, source_target_pairs={{0,1},{1,0},{2,3},{3,2},{4,5},{5,4},{6,7},{7,6},{8,9},{9,8},{10,11... | collective-permute-start | bytes 393224 | tf_op jit(solution)/shard_map/ppermute | solution.py:433
  30.5 2.3 %collective-permute-start.13 = (bf16[256,256]{1,0:T(8,128)(2,1)S(1)}, bf16[256,256]{1,0:T(8,128)(2,1)S(1)}, u32[]{:S(2)}, u32[]{:S(2)}) collective-permute-start(bf16[256,256]{1,0:T(8,128)(2,1)S(1)} %get-tuple-element.96.rest_3_), channel_id=1, source_target_pairs={{0,1},{1,0},{2,3},{3,2},{4,5},{5,4},{6,7},{7,6},{8,9},{9,8},{10,11... | collective-permute-start | bytes 393224 | tf_op jit(solution)/shard_map/ppermute | solution.py:433
  30.6 2.2 %collective-permute-start.10 = (bf16[256,256]{1,0:T(8,128)(2,1)S(1)}, bf16[256,256]{1,0:T(8,128)(2,1)S(1)}, u32[]{:S(2)}, u32[]{:S(2)}) collective-permute-start(bf16[256,256]{1,0:T(8,128)(2,1)S(1)} %get-tuple-element.93.rest_11_.rest_0_.after), channel_id=1, source_target_pairs={{0,1},{1,0},{2,3},{3,2},{4,5},{5,4},{6,7},{7,6},{8,9},{9,8},{10,11... | collective-permute-start | bytes 393224 | tf_op jit(solution)/shard_map/ppermute | solution.py:433
  32.8 1.5 %collective-permute-start.15 = (bf16[4,128,128]{2,1,0:T(8,128)(2,1)S(1)}, bf16[4,128,128]{2,1,0:T(8,128)(2,1)S(1)}, u32[]{:S(2)}, u32[]{:S(2)}) collective-permute-start(bf16[4,128,128]{2,1,0:T(8,128)(2,1)S(1)} %collective-permute-done.7.rest_10_.rest_0_), channel_id=1, source_target_pairs={{0,1},{1,0},{2,3},{3,2},{4,5},{5,4},{6,7},{7,6},{8,9},{9,8},{10,11... | collective-permute-start | bytes 393224 | tf_op jit(solution)/shard_map/ppermute | solution.py:433
  33.0 1.4 %collective-permute-start.14 = (bf16[1,2,128,128]{3,2,1,0:T(8,128)(2,1)S(1)}, bf16[1,2,128,128]{3,2,1,0:T(8,128)(2,1)S(1)}, u32[]{:S(2)}, u32[]{:S(2)}) collective-permute-start(bf16[1,2,128,128]{3,2,1,0:T(8,128)(2,1)S(1)} %get-tuple-element.102.rest_8_), channel_id=1, source_target_pairs={{0,1},{1,0},{2,3},{3,2},{4,5},{5,4},{6,7},{7,6},{8,9},{9,8},{10,11... | collective-permute-start | bytes 196616 | tf_op jit(solution)/shard_map/ppermute | solution.py:433
  34.8 8.9 %collective-permute-start.16 = (bf16[4,128,128]{2,1,0:T(8,128)(2,1)S(1)}, bf16[4,128,128]{2,1,0:T(8,128)(2,1)S(1)}, u32[]{:S(2)}, u32[]{:S(2)}) collective-permute-start(bf16[4,128,128]{2,1,0:T(8,128)(2,1)S(1)} %chain.2), channel_id=1, source_target_pairs={{0,4},{3,5},{2,6},{1,7},{4,8},{7,9},{6,10},{5,11},{8,12},{11,13},{... | collective-permute-start | bytes 393224 | tf_op jit(solution)/shard_map/ppermute | solution.py:445
  38.4 4.2 %collective-permute-start.17 = (bf16[1,2,128,128]{3,2,1,0:T(8,128)(2,1)S(1)}, bf16[1,2,128,128]{3,2,1,0:T(8,128)(2,1)S(1)}, u32[]{:S(2)}, u32[]{:S(2)}) collective-permute-start(bf16[1,2,128,128]{3,2,1,0:T(8,128)(2,1)S(1)} %get-tuple-element.101.rest_8_), channel_id=1, source_target_pairs={{0,1},{1,0},{2,3},{3,2},{4,5},{5,4},{6,7},{7,6},{8,9},{9,8},{10,11... | collective-permute-start | bytes 196616 | tf_op jit(solution)/shard_map/ppermute | solution.py:433
  43.6 1.3 %collective-permute-start.18 = (bf16[4,128,128]{2,1,0:T(8,128)(2,1)S(1)}, bf16[4,128,128]{2,1,0:T(8,128)(2,1)S(1)}, u32[]{:S(2)}, u32[]{:S(2)}) collective-permute-start(bf16[4,128,128]{2,1,0:T(8,128)(2,1)S(1)} %collective-permute-done.16.rest_10_.rest_2_), channel_id=1, source_target_pairs={{0,1},{1,0},{2,3},{3,2},{4,5},{5,4},{6,7},{7,6},{8,9},{9,8},{10,11... | collective-permute-start | bytes 393224 | tf_op jit(solution)/shard_map/ppermute | solution.py:433
  45.4 8.9 %collective-permute-start.19 = (bf16[4,128,128]{2,1,0:T(8,128)(2,1)S(1)}, bf16[4,128,128]{2,1,0:T(8,128)(2,1)S(1)}, u32[]{:S(2)}, u32[]{:S(2)}) collective-permute-start(bf16[4,128,128]{2,1,0:T(8,128)(2,1)S(1)} %chain.3.rest_11_), channel_id=1, source_target_pairs={{0,4},{3,5},{2,6},{1,7},{4,8},{7,9},{6,10},{5,11},{8,12},{11,13},{... | collective-permute-start | bytes 393224 | tf_op jit(solution)/shard_map/ppermute | solution.py:445
  54.3 1.7 %collective-permute-start.20 = (bf16[4,128,128]{2,1,0:T(8,128)(2,1)S(1)}, bf16[4,128,128]{2,1,0:T(8,128)(2,1)S(1)}, u32[]{:S(2)}, u32[]{:S(2)}) collective-permute-start(bf16[4,128,128]{2,1,0:T(8,128)(2,1)S(1)} %collective-permute-done.19.rest_0_), channel_id=1, source_target_pairs={{0,1},{1,0},{2,3},{3,2},{4,5},{5,4},{6,7},{7,6},{8,9},{9,8},{10,11... | collective-permute-start | bytes 393224 | tf_op jit(solution)/shard_map/ppermute | solution.py:433

commit v12 on v11

--- a/solution.py
+++ b/solution.py
@@ -251,18 +251,11 @@
             ext[pl.ds(start, HALO), pl.ds(d.start(other + shift), d.group), :] = block[:, at : at + d.group, :]
 
 
-def second_rest_kernel(d, face_ref, iface, cols, *rest):
-    edges, field, ext0, pair_in, cross_in = rest[:5]
-    later_edges, later, later_ext0, later_pair_in, later_cross_in, folded, after = rest[5:12]
-    inner, inner_later, faces_later, *faces_early, ext = rest[12:]
+def rest_kernel(d, first, face_ref, iface, cols, edges, field, ext0, pair_in, cross_in, folded, after, inner, faces_out, ext):
     face = face_ref[0]
     correct(d, cols, face, field, folded, inner, ext0, range(HALO, d.last))
-    correct(d, cols, face, later, folded, inner_later, later_ext0, range(HALO, d.last))
-    groups = [((later_edges, inner_later, later, later_pair_in, later_cross_in), 0, faces_later, d.ticks - 1 - d.split)]
-    groups += [((edges, inner, field, pair_in, cross_in), 1, out, d.split - 1) for out in faces_early]
-    for group, first, out, ticks in groups:
-        outs = [out.at[t] for t in range(ticks)]
-        interface_rows(d, face, iface, cols, *group, folded, first, outs, ext.at[:, pl.ds(0, ticks * d.sources), :])
+    outs = [faces_out.at[t] for t in range(faces_out.shape[0])]
+    interface_rows(d, face, iface, cols, edges, inner, field, pair_in, cross_in, folded, first, outs, ext)
 
 
 def interface_kernel(d, face_ref, iface, cols, gfield, gfirst, pair_in, cross_in, folded, after, *rest):
@@ -518,32 +511,38 @@
         [(2 * nq, sources, width)],
     )
 
+    def rest(first, ticks, rows, edges, field, ext0, pair, cross, after):
+        return call(
+            functools.partial(rest_kernel, d, first),
+            "rest",
+            [face, iface, cols],
+            [edges, field, ext0, pair, cross, folded, after],
+            [(count - 2 * HALO, rows, width), (ticks, nq, sources, width)],
+            [(ext, ticks * sources, width)],
+            anywhere=(6,),
+        )
+
+    inner, faces_early = rest(1, split - 1, early, edges, field, ext0, pair1, cross1, sent)
+    early_parts = (edges, inner, field, pair1, cross1)
+
     def beside_first():
         rows = call(
             functools.partial(interface_kernel, d),
             "interface",
             [face, iface, cols],
-            [gfield, gfirst, pair_later1, cross_later1, folded, sent],
+            [gfield, gfirst, pair_later1, cross_later1, folded, inner],
             [(d.part, group)] * d.parts,
             [(ext, wide, width)],
             anywhere=(5,),
         )
-        rest = call(
-            functools.partial(second_rest_kernel, d),
-            "second_rest",
-            [face, iface, cols],
-            [edges, field, ext0, pair1, cross1, edges_later, field_later, ext_later0, pair_later1, cross_later1, folded, rows[0]],
-            [(count - 2 * HALO, early, width), (count - 2 * HALO, later, width), (ticks - 1 - split, nq, sources, width)]
-            + [(split - 1, nq, sources, width)] * (split > 1),
-            [(ext, max(early, later), width)],
-            anywhere=(11,),
-        )
-        return rows, [swap(x) for x in rows], rest
-
-    arrived, (chain, other_chain, (inner, inner_later, faces_later, *faces_early)) = onward(sent, beside_first)
-    other_early = [swap(x) for x in faces_early]
-    early_parts = (edges, inner, field, pair1, cross1)
-    later_parts = (edges_later, inner_later, field_later, pair_later1, cross_later1)
+        return rows, [swap(x) for x in rows]
+
+    arrived, (chain, other_chain) = onward(sent, beside_first)
+    other_early = swap(faces_early)
+
+    def beside_second(sent):
+        made = rest(0, ticks - 1 - split, later, edges_later, field_later, ext_later0, pair_later1, cross_later1, sent)
+        return operator(), *made, swap(made[1])
 
     def fields(after):
         return call(
@@ -589,7 +588,7 @@
         if tick == ticks - 1:
             break
         early_tick = tick < split
-        bases = (faces_early[0], other_early[0]) if early_tick else (faces_later, other_later)
+        bases = (faces_early, other_early) if early_tick else (faces_later, other_later)
         (sent,) = call(
             functools.partial(chain_kernel, d, tick - 1 if early_tick else tick - split),
             "chain",
@@ -600,7 +599,8 @@
             flops=4 * sources * wide * group,
         )
         if tick == 1:
-            arrived, (coupled, other_later) = onward(sent, lambda: (operator(), swap(faces_later)))
+            arrived, (coupled, inner_later, faces_later, other_later) = onward(sent, functools.partial(beside_second, sent))
+            later_parts = (edges_later, inner_later, field_later, pair_later1, cross_later1)
         else:
             twice = fields(sent)
             arrived, most = onward(sent, lambda: output(everything))

time: 57.4 us -> 57.2 us (level)
  waiting for transfers between devices: 8.52 us -> 6.33 us
  starting transfers between devices: 25.2 us -> 26.3 us
  Pallas kernels: 23 us -> 23.8 us
    ppermute x3, waiting for transfers between devices: 3.51 us -> 1.6 us  [onward(): own.append(lax.ppermute(block, ('slab', 'face'), route))]
    ppermute x4, waiting for transfers between devices: 1.12 us -> 0.01 us  [exchange(): got = lax.ppermute(cross, 'face', crossing)]
    ppermute x3, starting transfers between devices: 10 us -> 11.1 us  [onward(): own.append(lax.ppermute(block, ('slab', 'face'), route))]
    pallas_call x16 -> x17, Pallas kernels: 23 us -> 23.8 us  [call(): pl.pallas_call(body, name=name, out_shape=outs, in_specs=[pl.BlockSpec(me...]
    ppermute x10, waiting for transfers between devices: 3.87 us -> 4.7 us  [swap(): return lax.ppermute(block, 'face', pairing)]
  transfers between devices with their start and end apart: 21 -> 21, of which waited for: 7 -> 9; matrix products, arithmetic and copies ran while one was open for 0% -> 0% of each run, Pallas kernels for 32% -> 34%
where the time goes in v12:
time: 57.2 us; the launch traced here: 56.9 us
  starting transfers between devices  26.3 us (46%)
  Pallas kernels  23.8 us (42%)
  waiting for transfers between devices  6.33 us (11%)
    pallas_call x17, Pallas kernels, call(): pl.pallas_call(body, name=name, out_shape=outs, in_specs=[pl.BlockSpec(me...  23.8 us
    ppermute x4, starting transfers between devices, exchange(): got = lax.ppermute(cross, 'face', crossing)  11.1 us
    ppermute x3, starting transfers between devices, onward(): own.append(lax.ppermute(block, ('slab', 'face'), route))  11.1 us
    ppermute x10, waiting for transfers between devices, swap(): return lax.ppermute(block, 'face', pairing)  4.7 us
    ppermute x10, starting transfers between devices, swap(): return lax.ppermute(block, 'face', pairing)  3.11 us
    ppermute x3, waiting for transfers between devices, onward(): own.append(lax.ppermute(block, ('slab', 'face'), route))  1.6 us
  transfers between devices with their start and end apart: 21, of which 9 were waited for; matrix products, arithmetic and copies ran while one was open for 0% of the time, Pallas kernels for 34%

profile of v12, /device:TPU:9, one launch (start us, length us, event | category | flops | bytes accessed | tf_op | source)
XLA Modules:
  0.0 56.9 jit_solution(9501735030794242208)
XLA Ops:
  0.0 2.6 %first.1 = (bf16[8,256,128]{2,1,0:T(8,128)(2,1)S(1)}, bf16[8,256,128]{2,1,0:T(8,128)(2,1)S(1)}, bf16[2,128,128]{2,1,0:T(8,128)(2,1)S(1)}, bf16[2,256,128]{2,1,0:...) custom-call(s32[1]{0:T(128)} %bitcast.face_ref, ...), custom_call_target="tpu_custom_call" | custom-call | tf_op jit(solution)/shard_map/first/pallas_call | solution.py:395
  3.4 3.0 %collective-permute-start.1 = (bf16[2,256,128]{2,1,0:T(8,128)(2,1)S(1)}, bf16[2,256,128]{2,1,0:T(8,128)(2,1)S(1)}, u32[]{:S(2)}, u32[]{:S(2)}) collective-permute-start(bf16[2,256,128]{2,1,0:T(8,128)(2,1)S(1)} %get-tuple-element.59), channel_id=1, source_target_pairs={{1,2},{2,1},{5,6},{6,5},{9,10},{10,9},{13,14},{14,13},{17,18},{18,... | collective-permute-start | bytes 393224 | tf_op jit(solution)/shard_map/ppermute | solution.py:422
  6.5 2.5 %collective-permute-start.5 = (bf16[2,416,128]{2,1,0:T(8,128)(2,1)S(1)}, bf16[2,416,128]{2,1,0:T(8,128)(2,1)S(1)}, u32[]{:S(2)}, u32[]{:S(2)}) collective-permute-start(bf16[2,416,128]{2,1,0:T(8,128)(2,1)S(1)} %get-tuple-element.72), channel_id=1, source_target_pairs={{1,2},{2,1},{5,6},{6,5},{9,10},{10,9},{13,14},{14,13},{17,18},{18,... | collective-permute-start | bytes 638984 | tf_op jit(solution)/shard_map/ppermute | solution.py:422
  9.0 2.2 %fold.1 = (bf16[8,640,128]{2,1,0:T(8,128)(2,1)S(1)}, bf16[6,128,1024]{2,1,0:T(8,128)(2,1)S(1)}) custom-call(s32[1]{0:T(128)} %bitcast.face_ref, s32[2]{0:T(128)S(1)} %get-tuple-element.60.iface, s32[4,8]{1,0:T(4,128)S(1)} %get-tuple-element.56.cols, bf16[8,128,128]{2,1,0:T(8,128)(2,1)S(1)} %get-tuple-element.61.inv, ...), custom_call_target="tpu_custom_call" | custom-call | tf_op jit(solution)/shard_map/fold/pallas_call | solution.py:395
  11.2 1.1 %second_edges.1 = (bf16[4,256,128]{2,1,0:T(8,128)(2,1)S(1)}, bf16[2,256,128]{2,1,0:T(8,128)(2,1)S(1)}, bf16[2,256,128]{2,1,0:T(8,128)(2,1)S(1)}, bf16[12,256,128]{2,1,0:T(8,128)(2,1)S(1)}) custom-call(s32[1]{0:T(128)} %bitcast.face_ref, s32[4,8]{1,0:T(4,128)S(1)} %get-tuple-element.56.cols, bf16[8,256,128]{2,1,0:T(8,128)(2,1)S(1)} %get-tuple-element.57.field.rest_2_, ...), custom_call_target="tpu_custom_call" | custom-call | tf_op jit(solution)/shard_map/second_edges/pallas_call | solution.py:395
  12.4 3.0 %collective-permute-start.3 = (bf16[2,256,128]{2,1,0:T(8,128)(2,1)S(1)}, bf16[2,256,128]{2,1,0:T(8,128)(2,1)S(1)}, u32[]{:S(2)}, u32[]{:S(2)}) collective-permute-start(bf16[2,256,128]{2,1,0:T(8,128)(2,1)S(1)} %get-tuple-element.68), channel_id=1, source_target_pairs={{1,2},{2,1},{5,6},{6,5},{9,10},{10,9},{13,14},{14,13},{17,18},{18,... | collective-permute-start | bytes 393224 | tf_op jit(solution)/shard_map/ppermute | solution.py:422
  15.4 1.7 %behind.1 = (bf16[4,256,128]{2,1,0:T(8,128)(2,1)S(1)}, bf16[8,1024,128]{2,1,0:T(8,128)(2,1)S(1)}, bf16[2,1024,128]{2,1,0:T(8,128)(2,1)S(1)}, bf16[2,1024,128]{2,1,0:T(8,128)(2,1)S(1)}, bf16[12,256,128]{2,1,0:T(8,128)(2,1)S(1)}) custom-call(s32[1]{0:T(128)} %bitcast.face_ref, s32[2]{0:T(128)S(1)} %get-tuple-element.60.iface, ...), custom_call_target="tpu_custom_call" | custom-call | tf_op jit(solution)/shard_map/behind/pallas_call | solution.py:395
  17.2 2.6 %collective-permute-start.9 = (bf16[2,1024,128]{2,1,0:T(8,128)(2,1)S(1)}, bf16[2,1024,128]{2,1,0:T(8,128)(2,1)S(1)}, u32[]{:S(2)}, u32[]{:S(2)}) collective-permute-start(bf16[2,1024,128]{2,1,0:T(8,128)(2,1)S(1)} %get-tuple-element.80), channel_id=1, source_target_pairs={{1,2},{2,1},{5,6},{6,5},{9,10},{10,9},{13,14},{14,13},{17,18},{18,... | collective-permute-start | bytes 1572872 | tf_op jit(solution)/shard_map/ppermute | solution.py:422
  19.8 0.9 %second_inner.1.inner = bf16[4,128,128]{2,1,0:T(8,128)(2,1)S(1)} custom-call(s32[1]{0:T(128)} %bitcast.face_ref, s32[4,8]{1,0:T(4,128)S(1)} %get-tuple-element.56.cols, bf16[8,256,128]{2,1,0:T(8,128)(2,1)S(1)} %get-tuple-element.57.field.rest_2_, bf16[12,256,128]{2,1,0:T(8,128)(2,1)S(1)} %get-tuple-element.66.ext.ext0, ...), custom_call_target="tpu_custom_call" | custom-call | tf_op jit(solution)/shard_map/second_inner/pallas_call | solution.py:395
  20.7 0.8 %third_rows.1.own = bf16[2,128,128]{2,1,0:T(8,128)(2,1)S(1)} custom-call(s32[1]{0:T(128)} %bitcast.face_ref, s32[2]{0:T(128)S(1)} %get-tuple-element.60.iface, s32[4,8]{1,0:T(4,128)S(1)} %get-tuple-element.56.cols, bf16[4,256,128]{2,1,0:T(8,128)(2,1)S(1)} %get-tuple-element.65.edges.rest_0_, bf16[4,128,128]{2,1,0:T(8,128)(2,1)S(1)} %second_inner.1.inner, ...), custom_call_target="tpu_custom_call" | custom-call | flops 4026531840 | tf_op jit(solution)/shard_map/third_rows/pallas_call | solution.py:395
  21.6 1.2 %collective-permute-done.6.other = bf16[2,128,128]{2,1,0:T(8,128)(2,1)S(1)} collective-permute-done((bf16[2,128,128]{2,1,0:T(8,128)(2,1)S(1)}, bf16[2,128,128]{2,1,0:T(8,128)(2,1)S(1)}, u32[]{:S(2)}, u32[]{:S(2)}) %collective-permute-start.6) | collective-permute-done | bytes 65568 | tf_op jit(solution)/shard_map/ppermute | solution.py:426
  22.9 3.8 %collective-permute-start.7 = (bf16[4,128,128]{2,1,0:T(8,128)(2,1)S(1)}, bf16[4,128,128]{2,1,0:T(8,128)(2,1)S(1)}, u32[]{:S(2)}, u32[]{:S(2)}) collective-permute-start(bf16[4,128,128]{2,1,0:T(8,128)(2,1)S(1)} %merge.1.after), channel_id=1, source_target_pairs={{0,4},{3,5},{2,6},{1,7},{4,8},{7,9},{6,10},{5,11},{8,12},{11,13},{... | collective-permute-start | bytes 393224 | tf_op jit(solution)/shard_map/ppermute | solution.py:438
  26.6 1.3 %rest.2 = (bf16[4,256,128]{2,1,0:T(8,128)(2,1)S(1)}, bf16[1,2,128,128]{3,2,1,0:T(8,128)(2,1)S(1)}) custom-call(s32[1]{0:T(128)} %bitcast.face_ref, s32[2]{0:T(128)S(1)} %get-tuple-element.60.iface, s32[4,8]{1,0:T(4,128)S(1)} %get-tuple-element.56.cols, bf16[4,256,128]{2,1,0:T(8,128)(2,1)S(1)} %get-tuple-element.65.edges.rest_0_, ...), custom_call_target="tpu_custom_call" | custom-call | tf_op jit(solution)/shard_map/rest/pallas_call | solution.py:395
  28.0 2.2 %interface.1 = (bf16[256,256]{1,0:T(8,128)(2,1)S(1)}, bf16[256,256]{1,0:T(8,128)(2,1)S(1)}, bf16[256,256]{1,0:T(8,128)(2,1)S(1)}, bf16[256,256]{1,0:T(8,128)(2,1)S(1)}) custom-call(s32[1]{0:T(128)} %bitcast.face_ref, s32[2]{0:T(128)S(1)} %get-tuple-element.60.iface, s32[4,8]{1,0:T(4,128)S(1)} %get-tuple-element.56.cols, ...), custom_call_target="tpu_custom_call" | custom-call | tf_op jit(solution)/shard_map/interface/pallas_call | solution.py:395
  32.8 1.1 %collective-permute-done.14.rest_9_ = bf16[1,2,128,128]{3,2,1,0:T(8,128)(2,1)S(1)} collective-permute-done((bf16[1,2,128,128]{3,2,1,0:T(8,128)(2,1)S(1)}, bf16[1,2,128,128]{3,2,1,0:T(8,128)(2,1)S(1)}, u32[]{:S(2)}, u32[]{:S(2)}) %collective-permute-start.14) | collective-permute-done | bytes 65568 | tf_op jit(solution)/shard_map/ppermute | solution.py:426
  34.3 3.6 %collective-permute-start.16 = (bf16[4,128,128]{2,1,0:T(8,128)(2,1)S(1)}, bf16[4,128,128]{2,1,0:T(8,128)(2,1)S(1)}, u32[]{:S(2)}, u32[]{:S(2)}) collective-permute-start(bf16[4,128,128]{2,1,0:T(8,128)(2,1)S(1)} %chain.2.after), channel_id=1, source_target_pairs={{0,4},{3,5},{2,6},{1,7},{4,8},{7,9},{6,10},{5,11},{8,12},{11,13},{... | collective-permute-start | bytes 393224 | tf_op jit(solution)/shard_map/ppermute | solution.py:438
  37.9 1.3 %rest.3 = (bf16[4,256,128]{2,1,0:T(8,128)(2,1)S(1)}, bf16[1,2,128,128]{3,2,1,0:T(8,128)(2,1)S(1)}) custom-call(s32[1]{0:T(128)} %bitcast.face_ref, s32[2]{0:T(128)S(1)} %get-tuple-element.60.iface, s32[4,8]{1,0:T(4,128)S(1)} %get-tuple-element.56.cols, bf16[4,256,128]{2,1,0:T(8,128)(2,1)S(1)} %get-tuple-element.78.edges.rest_5_, ...), custom_call_target="tpu_custom_call" | custom-call | tf_op jit(solution)/shard_map/rest/pallas_call | solution.py:395
  39.5 3.8 %coupling_last.1.coupled = bf16[1024,1024]{1,0:T(8,128)(2,1)S(1)} custom-call(s32[1]{0:T(128)} %bitcast.face_ref, s32[2]{0:T(128)S(1)} %get-tuple-element.60.iface, s32[4,8]{1,0:T(4,128)S(1)} %get-tuple-element.56.cols, bf16[2,128,128]{2,1,0:T(8,128)(2,1)S(1)} %get-tuple-element.70.gfield, bf16[8,1024,128]{2,1,0:T(8,128)(2,1)S(1)} %get-tuple-element.74.after.gfirst, ...), custom_call_target="tpu_custom_call" | custom-call | flops 1342177280 | tf_op jit(solution)/shard_map/coupling_last/pallas_call | solution.py:395
  43.7 1.0 %collective-permute-done.18.rest_11_.rest_3_ = bf16[4,128,128]{2,1,0:T(8,128)(2,1)S(1)} collective-permute-done((bf16[4,128,128]{2,1,0:T(8,128)(2,1)S(1)}, bf16[4,128,128]{2,1,0:T(8,128)(2,1)S(1)}, u32[]{:S(2)}, u32[]{:S(2)}) %collective-permute-start.18) | collective-permute-done | bytes 131104 | tf_op jit(solution)/shard_map/ppermute | solution.py:426
  45.1 3.7 %collective-permute-start.19 = (bf16[4,128,128]{2,1,0:T(8,128)(2,1)S(1)}, bf16[4,128,128]{2,1,0:T(8,128)(2,1)S(1)}, u32[]{:S(2)}, u32[]{:S(2)}) collective-permute-start(bf16[4,128,128]{2,1,0:T(8,128)(2,1)S(1)} %chain.3.rest_11_), channel_id=1, source_target_pairs={{0,4},{3,5},{2,6},{1,7},{4,8},{7,9},{6,10},{5,11},{8,12},{11,13},{... | collective-permute-start | bytes 393224 | tf_op jit(solution)/shard_map/ppermute | solution.py:438
  48.8 2.2 %third.1 = (bf16[8,256,128]{2,1,0:T(8,128)(2,1)S(1)}, bf16[8,256,128]{2,1,0:T(8,128)(2,1)S(1)}) custom-call(s32[1]{0:T(128)} %bitcast.face_ref, s32[4,8]{1,0:T(4,128)S(1)} %get-tuple-element.56.cols, bf16[4,256,128]{2,1,0:T(8,128)(2,1)S(1)} %get-tuple-element.65.edges.rest_0_, bf16[4,256,128]{2,1,0:T(8,128)(2,1)S(1)} %get-tuple-element.77.after.rest_1_, ...), custom_call_target="tpu_custom_call" | custom-call | tf_op jit(solution)/shard_map/third/pallas_call | solution.py:395
  51.0 1.5 %output.1.earlier = bf16[4,128,1024]{2,1,0:T(8,128)(2,1)} custom-call(s32[1]{0:T(128)} %bitcast.face_ref, bf16[8,256,128]{2,1,0:T(8,128)(2,1)S(1)} %get-tuple-element.102.early, bf16[8,256,128]{2,1,0:T(8,128)(2,1)S(1)} %get-tuple-element.103.later, bf16[1024,1024]{1,0:T(8,128)(2,1)S(1)} %coupling_last.1.coupled, ...), custom_call_target="tpu_custom_call" | custom-call | tf_op jit(solution)/shard_map/output/pallas_call | solution.py:395
  52.6 1.3 %collective-permute-done.19.rest_0_ = bf16[4,128,128]{2,1,0:T(8,128)(2,1)S(1)} collective-permute-done((bf16[4,128,128]{2,1,0:T(8,128)(2,1)S(1)}, bf16[4,128,128]{2,1,0:T(8,128)(2,1)S(1)}, u32[]{:S(2)}, u32[]{:S(2)}) %collective-permute-start.19) | collective-permute-done | bytes 131104 | tf_op jit(solution)/shard_map/ppermute | solution.py:438
  55.7 1.0 %last_other.1 = bf16[4,128,1024]{2,1,0:T(8,128)(2,1)} custom-call(s32[1]{0:T(128)} %bitcast.face_ref, f32[128,1024]{1,0:T(8,128)S(1)} %last_own.1.own_part, bf16[1024,1024]{1,0:T(8,128)(2,1)S(1)} %coupling_last.1.coupled, bf16[4,128,1024]{2,1,0:T(8,128)(2,1)} %output.1.earlier, ...), custom_call_target="tpu_custom_call", output_to_operand_aliasing={{}: (3, {})} | custom-call | tf_op jit(solution)/shard_map/last_other/pallas_call | solution.py:395
  (35 shorter events, 6.9 us)
Async XLA Ops:
  2.6 8.6 %collective-permute-start = (bf16[2,256,128]{2,1,0:T(8,128)(2,1)S(1)}, bf16[2,256,128]{2,1,0:T(8,128)(2,1)S(1)}, u32[]{:S(2)}, u32[]{:S(2)}) collective-permute-start(bf16[2,256,128]{2,1,0:T(8,128)(2,1)S(1)} %get-tuple-element.58), channel_id=1, source_target_pairs={{0,1},{1,0},{2,3},{3,2},{4,5},{5,4},{6,7},{7,6},{8,9},{9,8},{10,11... | collective-permute-start | bytes 393224 | tf_op jit(solution)/shard_map/ppermute | solution.py:423
  3.4 7.8 %collective-permute-start.1 = (bf16[2,256,128]{2,1,0:T(8,128)(2,1)S(1)}, bf16[2,256,128]{2,1,0:T(8,128)(2,1)S(1)}, u32[]{:S(2)}, u32[]{:S(2)}) collective-permute-start(bf16[2,256,128]{2,1,0:T(8,128)(2,1)S(1)} %get-tuple-element.59), channel_id=1, source_target_pairs={{1,2},{2,1},{5,6},{6,5},{9,10},{10,9},{13,14},{14,13},{17,18},{18,... | collective-permute-start | bytes 393224 | tf_op jit(solution)/shard_map/ppermute | solution.py:422
  6.4 9.0 %collective-permute-start.4 = (bf16[2,416,128]{2,1,0:T(8,128)(2,1)S(1)}, bf16[2,416,128]{2,1,0:T(8,128)(2,1)S(1)}, u32[]{:S(2)}, u32[]{:S(2)}) collective-permute-start(bf16[2,416,128]{2,1,0:T(8,128)(2,1)S(1)} %get-tuple-element.71), channel_id=1, source_target_pairs={{0,1},{1,0},{2,3},{3,2},{4,5},{5,4},{6,7},{7,6},{8,9},{9,8},{10,11... | collective-permute-start | bytes 638984 | tf_op jit(solution)/shard_map/ppermute | solution.py:423
  6.5 9.0 %collective-permute-start.5 = (bf16[2,416,128]{2,1,0:T(8,128)(2,1)S(1)}, bf16[2,416,128]{2,1,0:T(8,128)(2,1)S(1)}, u32[]{:S(2)}, u32[]{:S(2)}) collective-permute-start(bf16[2,416,128]{2,1,0:T(8,128)(2,1)S(1)} %get-tuple-element.72), channel_id=1, source_target_pairs={{1,2},{2,1},{5,6},{6,5},{9,10},{10,9},{13,14},{14,13},{17,18},{18,... | collective-permute-start | bytes 638984 | tf_op jit(solution)/shard_map/ppermute | solution.py:422
  12.3 3.1 %collective-permute-start.2 = (bf16[2,256,128]{2,1,0:T(8,128)(2,1)S(1)}, bf16[2,256,128]{2,1,0:T(8,128)(2,1)S(1)}, u32[]{:S(2)}, u32[]{:S(2)}) collective-permute-start(bf16[2,256,128]{2,1,0:T(8,128)(2,1)S(1)} %get-tuple-element.67), channel_id=1, source_target_pairs={{0,1},{1,0},{2,3},{3,2},{4,5},{5,4},{6,7},{7,6},{8,9},{9,8},{10,11... | collective-permute-start | bytes 393224 | tf_op jit(solution)/shard_map/ppermute | solution.py:423
  12.4 8.3 %collective-permute-start.3 = (bf16[2,256,128]{2,1,0:T(8,128)(2,1)S(1)}, bf16[2,256,128]{2,1,0:T(8,128)(2,1)S(1)}, u32[]{:S(2)}, u32[]{:S(2)}) collective-permute-start(bf16[2,256,128]{2,1,0:T(8,128)(2,1)S(1)} %get-tuple-element.68), channel_id=1, source_target_pairs={{1,2},{2,1},{5,6},{6,5},{9,10},{10,9},{13,14},{14,13},{17,18},{18,... | collective-permute-start | bytes 393224 | tf_op jit(solution)/shard_map/ppermute | solution.py:422
  17.1 10.8 %collective-permute-start.8 = (bf16[2,1024,128]{2,1,0:T(8,128)(2,1)S(1)}, bf16[2,1024,128]{2,1,0:T(8,128)(2,1)S(1)}, u32[]{:S(2)}, u32[]{:S(2)}) collective-permute-start(bf16[2,1024,128]{2,1,0:T(8,128)(2,1)S(1)} %get-tuple-element.79), channel_id=1, source_target_pairs={{0,1},{1,0},{2,3},{3,2},{4,5},{5,4},{6,7},{7,6},{8,9},{9,8},{10,11... | collective-permute-start | bytes 1572872 | tf_op jit(solution)/shard_map/ppermute | solution.py:423
  17.2 10.8 %collective-permute-start.9 = (bf16[2,1024,128]{2,1,0:T(8,128)(2,1)S(1)}, bf16[2,1024,128]{2,1,0:T(8,128)(2,1)S(1)}, u32[]{:S(2)}, u32[]{:S(2)}) collective-permute-start(bf16[2,1024,128]{2,1,0:T(8,128)(2,1)S(1)} %get-tuple-element.80), channel_id=1, source_target_pairs={{1,2},{2,1},{5,6},{6,5},{9,10},{10,9},{13,14},{14,13},{17,18},{18,... | collective-permute-start | bytes 1572872 | tf_op jit(solution)/shard_map/ppermute | solution.py:422
  21.5 1.3 %collective-permute-start.6 = (bf16[2,128,128]{2,1,0:T(8,128)(2,1)S(1)}, bf16[2,128,128]{2,1,0:T(8,128)(2,1)S(1)}, u32[]{:S(2)}, u32[]{:S(2)}) collective-permute-start(bf16[2,128,128]{2,1,0:T(8,128)(2,1)S(1)} %third_rows.1.own), channel_id=1, source_target_pairs={{0,1},{1,0},{2,3},{3,2},{4,5},{5,4},{6,7},{7,6},{8,9},{9,8},{10,11... | collective-permute-start | bytes 196616 | tf_op jit(solution)/shard_map/ppermute | solution.py:426
  22.9 8.7 %collective-permute-start.7 = (bf16[4,128,128]{2,1,0:T(8,128)(2,1)S(1)}, bf16[4,128,128]{2,1,0:T(8,128)(2,1)S(1)}, u32[]{:S(2)}, u32[]{:S(2)}) collective-permute-start(bf16[4,128,128]{2,1,0:T(8,128)(2,1)S(1)} %merge.1.after), channel_id=1, source_target_pairs={{0,4},{3,5},{2,6},{1,7},{4,8},{7,9},{6,10},{5,11},{8,12},{11,13},{... | collective-permute-start | bytes 393224 | tf_op jit(solution)/shard_map/ppermute | solution.py:438
  30.2 1.4 %collective-permute-start.10 = (bf16[256,256]{1,0:T(8,128)(2,1)S(1)}, bf16[256,256]{1,0:T(8,128)(2,1)S(1)}, u32[]{:S(2)}, u32[]{:S(2)}) collective-permute-start(bf16[256,256]{1,0:T(8,128)(2,1)S(1)} %get-tuple-element.85.rest_0_.after), channel_id=1, source_target_pairs={{0,1},{1,0},{2,3},{3,2},{4,5},{5,4},{6,7},{7,6},{8,9},{9,8},{10,11... | collective-permute-start | bytes 393224 | tf_op jit(solution)/shard_map/ppermute | solution.py:426
  30.3 1.5 %collective-permute-start.11 = (bf16[256,256]{1,0:T(8,128)(2,1)S(1)}, bf16[256,256]{1,0:T(8,128)(2,1)S(1)}, u32[]{:S(2)}, u32[]{:S(2)}) collective-permute-start(bf16[256,256]{1,0:T(8,128)(2,1)S(1)} %get-tuple-element.86.rest_1_), channel_id=1, source_target_pairs={{0,1},{1,0},{2,3},{3,2},{4,5},{5,4},{6,7},{7,6},{8,9},{9,8},{10,11... | collective-permute-start | bytes 393224 | tf_op jit(solution)/shard_map/ppermute | solution.py:426
  30.8 1.3 %collective-permute-start.12 = (bf16[256,256]{1,0:T(8,128)(2,1)S(1)}, bf16[256,256]{1,0:T(8,128)(2,1)S(1)}, u32[]{:S(2)}, u32[]{:S(2)}) collective-permute-start(bf16[256,256]{1,0:T(8,128)(2,1)S(1)} %get-tuple-element.87.rest_2_), channel_id=1, source_target_pairs={{0,1},{1,0},{2,3},{3,2},{4,5},{5,4},{6,7},{7,6},{8,9},{9,8},{10,11... | collective-permute-start | bytes 393224 | tf_op jit(solution)/shard_map/ppermute | solution.py:426
  30.9 1.5 %collective-permute-start.13 = (bf16[256,256]{1,0:T(8,128)(2,1)S(1)}, bf16[256,256]{1,0:T(8,128)(2,1)S(1)}, u32[]{:S(2)}, u32[]{:S(2)}) collective-permute-start(bf16[256,256]{1,0:T(8,128)(2,1)S(1)} %get-tuple-element.88.rest_3_), channel_id=1, source_target_pairs={{0,1},{1,0},{2,3},{3,2},{4,5},{5,4},{6,7},{7,6},{8,9},{9,8},{10,11... | collective-permute-start | bytes 393224 | tf_op jit(solution)/shard_map/ppermute | solution.py:426
  32.3 1.6 %collective-permute-start.15 = (bf16[4,128,128]{2,1,0:T(8,128)(2,1)S(1)}, bf16[4,128,128]{2,1,0:T(8,128)(2,1)S(1)}, u32[]{:S(2)}, u32[]{:S(2)}) collective-permute-start(bf16[4,128,128]{2,1,0:T(8,128)(2,1)S(1)} %collective-permute-done.7.rest_10_.rest_0_), channel_id=1, source_target_pairs={{0,1},{1,0},{2,3},{3,2},{4,5},{5,4},{6,7},{7,6},{8,9},{9,8},{10,11... | collective-permute-start | bytes 393224 | tf_op jit(solution)/shard_map/ppermute | solution.py:426
  32.6 1.3 %collective-permute-start.14 = (bf16[1,2,128,128]{3,2,1,0:T(8,128)(2,1)S(1)}, bf16[1,2,128,128]{3,2,1,0:T(8,128)(2,1)S(1)}, u32[]{:S(2)}, u32[]{:S(2)}) collective-permute-start(bf16[1,2,128,128]{3,2,1,0:T(8,128)(2,1)S(1)} %get-tuple-element.93.rest_8_), channel_id=1, source_target_pairs={{0,1},{1,0},{2,3},{3,2},{4,5},{5,4},{6,7},{7,6},{8,9},{9,8},{10,11... | collective-permute-start | bytes 196616 | tf_op jit(solution)/shard_map/ppermute | solution.py:426
  34.3 9.0 %collective-permute-start.16 = (bf16[4,128,128]{2,1,0:T(8,128)(2,1)S(1)}, bf16[4,128,128]{2,1,0:T(8,128)(2,1)S(1)}, u32[]{:S(2)}, u32[]{:S(2)}) collective-permute-start(bf16[4,128,128]{2,1,0:T(8,128)(2,1)S(1)} %chain.2.after), channel_id=1, source_target_pairs={{0,4},{3,5},{2,6},{1,7},{4,8},{7,9},{6,10},{5,11},{8,12},{11,13},{... | collective-permute-start | bytes 393224 | tf_op jit(solution)/shard_map/ppermute | solution.py:438
  39.2 4.0 %collective-permute-start.17 = (bf16[1,2,128,128]{3,2,1,0:T(8,128)(2,1)S(1)}, bf16[1,2,128,128]{3,2,1,0:T(8,128)(2,1)S(1)}, u32[]{:S(2)}, u32[]{:S(2)}) collective-permute-start(bf16[1,2,128,128]{3,2,1,0:T(8,128)(2,1)S(1)} %get-tuple-element.99.rest_8_), channel_id=1, source_target_pairs={{0,1},{1,0},{2,3},{3,2},{4,5},{5,4},{6,7},{7,6},{8,9},{9,8},{10,11... | collective-permute-start | bytes 196616 | tf_op jit(solution)/shard_map/ppermute | solution.py:426
  43.3 1.4 %collective-permute-start.18 = (bf16[4,128,128]{2,1,0:T(8,128)(2,1)S(1)}, bf16[4,128,128]{2,1,0:T(8,128)(2,1)S(1)}, u32[]{:S(2)}, u32[]{:S(2)}) collective-permute-start(bf16[4,128,128]{2,1,0:T(8,128)(2,1)S(1)} %collective-permute-done.16.rest_10_.rest_2_), channel_id=1, source_target_pairs={{0,1},{1,0},{2,3},{3,2},{4,5},{5,4},{6,7},{7,6},{8,9},{9,8},{10,11... | collective-permute-start | bytes 393224 | tf_op jit(solution)/shard_map/ppermute | solution.py:426
  45.1 8.8 %collective-permute-start.19 = (bf16[4,128,128]{2,1,0:T(8,128)(2,1)S(1)}, bf16[4,128,128]{2,1,0:T(8,128)(2,1)S(1)}, u32[]{:S(2)}, u32[]{:S(2)}) collective-permute-start(bf16[4,128,128]{2,1,0:T(8,128)(2,1)S(1)} %chain.3.rest_11_), channel_id=1, source_target_pairs={{0,4},{3,5},{2,6},{1,7},{4,8},{7,9},{6,10},{5,11},{8,12},{11,13},{... | collective-permute-start | bytes 393224 | tf_op jit(solution)/shard_map/ppermute | solution.py:438
  53.9 1.8 %collective-permute-start.20 = (bf16[4,128,128]{2,1,0:T(8,128)(2,1)S(1)}, bf16[4,128,128]{2,1,0:T(8,128)(2,1)S(1)}, u32[]{:S(2)}, u32[]{:S(2)}) collective-permute-start(bf16[4,128,128]{2,1,0:T(8,128)(2,1)S(1)} %collective-permute-done.19.rest_0_), channel_id=1, source_target_pairs={{0,1},{1,0},{2,3},{3,2},{4,5},{5,4},{6,7},{7,6},{8,9},{9,8},{10,11... | collective-permute-start | bytes 393224 | tf_op jit(solution)/shard_map/ppermute | solution.py:426

commit v13 on v12

--- a/solution.py
+++ b/solution.py
@@ -277,18 +277,34 @@
                 part[block] = (part[block].astype(F32) + gfield[q].astype(F32)).astype(BF)
 
 
-def coupling_last_kernel(d, face_ref, iface, cols, gfield, gfirst, pair_in, cross_in, folded, after, out, ext):
-    face = face_ref[0]
+def operator_rows(d, face, iface, cols, gfield, folded, ext, rows, out):
     w = d.width
-    coupling_ext(d, face, gfirst, pair_in, cross_in, ext)
-    for r in range(d.count):
+    for i, r in enumerate(rows):
         for s in range(0, d.wide, d.group):
             span = pl.ds(s, d.group)
-            out[span, r * w : (r + 1) * w] = sweep(d, cols, face, ext, span, r, folded).astype(BF)
+            out[span, i * w : (i + 1) * w] = sweep(d, cols, face, ext, span, r, folded).astype(BF)
     for q in range(d.nq):
-        lane = pl.ds(pl.multiple_of(iface[q] * w, w), w)
-        span = pl.ds(pl.multiple_of(d.start(face) + q * w, w), w)
-        out[span, lane] = (out[span, lane].astype(F32) + gfield[q].astype(F32)).astype(BF)
+
+        @pl.when(jnp.logical_and(iface[q] >= rows[0], iface[q] <= rows[-1]))
+        def _():
+            lane = pl.ds(pl.multiple_of((iface[q] - rows[0]) * w, w), w)
+            span = pl.ds(pl.multiple_of(d.start(face) + q * w, w), w)
+            out[span, lane] = (out[span, lane].astype(F32) + gfield[q].astype(F32)).astype(BF)
+
+
+def operator_kernel(d, face_ref, iface, cols, gfield, gfirst, pair_in, cross_in, folded, after, out, ext):
+    coupling_ext(d, face_ref[0], gfirst, pair_in, cross_in, ext)
+    operator_rows(d, face_ref[0], iface, cols, gfield, folded, ext, range(d.count // 2), out)
+
+
+def operator_rest_kernel(d, face_ref, iface, cols, gfield, folded, ext, after, out):
+    operator_rows(d, face_ref[0], iface, cols, gfield, folded, ext, range(d.count // 2, d.count), out)
+
+
+def operator_part(d, halves, row, depth, lane, lanes):
+    width = halves[0].shape[1]
+    half = halves[lane // width]
+    return half[pl.ds(row, depth), lane % width : lane % width + lanes]
 
 
 def chip_hops(faces):
@@ -338,7 +354,7 @@
     return fields[row, at * d.sources : (at + 1) * d.sources, :].astype(F32)
 
 
-def output_kernel(d, face_ref, early, later, coupled, *rest):
+def output_kernel(d, face_ref, early, later, first_half, second_half, *rest):
     *arrived, out, held, sems = rest
     w = d.width
     each = 2 * len(chip_hops(d.faces))
@@ -352,7 +368,7 @@
         for c in range(0, d.count * w, part):
             total = jnp.zeros((d.sources, part), F32)
             for x, start in blocks:
-                total += dot_nn(x, coupled[pl.ds(start, 2 * d.group), c : c + part])
+                total += dot_nn(x, operator_part(d, (first_half, second_half), start, 2 * d.group, c, part))
             for j in range(0, part, w):
                 value = tick_rows(d, early, later, t, (c + j) // w) - total[:, j : j + w]
                 held[t, :, c + j : c + j + w] = value.astype(BF)
@@ -362,17 +378,19 @@
         copy.wait()
 
 
-def last_own_kernel(d, face_ref, early, later, coupled, *rest):
+def last_own_kernel(d, face_ref, early, later, first_half, second_half, *rest):
     own, out = rest[:-1], rest[-1]
     w = d.width
-    total = jnp.zeros((d.sources, d.count * w), F32)
-    for x, start in list(arrived_blocks(d, face_ref[0], own, own))[0::2]:
-        total += dot_nn(x, coupled[pl.ds(start, 2 * d.group), :])
-    for r in range(d.count):
-        out[:, r * w : (r + 1) * w] = tick_rows(d, early, later, d.ticks - 1, r) - total[:, r * w : (r + 1) * w]
-
-
-def last_other_kernel(d, face_ref, own_part, coupled, earlier, *rest):
+    blocks = list(arrived_blocks(d, face_ref[0], own, own))[0::2]
+    for c in range(0, d.count * w, 2 * w):
+        total = jnp.zeros((d.sources, 2 * w), F32)
+        for x, start in blocks:
+            total += dot_nn(x, operator_part(d, (first_half, second_half), start, 2 * d.group, c, 2 * w))
+        for j in range(0, 2 * w, w):
+            out[:, c + j : c + j + w] = tick_rows(d, early, later, d.ticks - 1, (c + j) // w) - total[:, j : j + w]
+
+
+def last_other_kernel(d, face_ref, own_part, first_half, second_half, earlier, *rest):
     other, (out, held, sems) = rest[:-3], rest[-3:]
     blocks = list(arrived_blocks(d, face_ref[0], other, other))[1::2]
     part = 2 * d.width
@@ -380,7 +398,7 @@
     for i, c in enumerate(range(0, d.count * d.width, part)):
         total = own_part[:, c : c + part]
         for x, start in blocks:
-            total -= dot_nn(x, coupled[pl.ds(start, 2 * d.group), c : c + part])
+            total -= dot_nn(x, operator_part(d, (first_half, second_half), start, 2 * d.group, c, part))
         held[:, c : c + part] = total.astype(BF)
         here = held.at[:, c : c + part]
         copies.append(pltpu.make_async_copy(here, out.at[d.ticks - 1, :, c : c + part], sems.at[i]))
@@ -542,7 +560,7 @@
 
     def beside_second(sent):
         made = rest(0, ticks - 1 - split, later, edges_later, field_later, ext_later0, pair_later1, cross_later1, sent)
-        return operator(), *made, swap(made[1])
+        return *operator(), *made, swap(made[1])
 
     def fields(after):
         return call(
@@ -559,14 +577,23 @@
 
     def operator():
         return call(
-            functools.partial(coupling_last_kernel, d),
-            "coupling_last",
+            functools.partial(operator_kernel, d),
+            "operator",
             [face, iface, cols],
             [gfield, gfirst, pair_later1, cross_later1, folded, chain[0]],
-            [(wide, count * width)],
-            [(ext, wide, width)],
-            flops=wide * sweep_flops,
+            [(wide, count // 2 * width), (ext, wide, width)],
+            flops=wide * sweep_flops // 2,
             anywhere=(5,),
+        )
+
+    def operator_rest(after):
+        return call(
+            functools.partial(operator_rest_kernel, d),
+            "operator_rest",
+            [face, iface, cols],
+            [gfield, folded, read, after],
+            [(wide, (count - count // 2) * width)],
+            anywhere=(3,),
         )[0]
 
     def output(blocks):
@@ -574,7 +601,7 @@
             functools.partial(output_kernel, d),
             "output",
             [face],
-            [*twice, coupled] + blocks,
+            [*twice, first_half, second_half] + blocks,
             [whole],
             [(ticks - 1, sources, count * width)],
             sems=ticks - 1,
@@ -582,7 +609,7 @@
         )[0]
 
     everything = []
-    coupled = most = None
+    most = None
     for tick in range(1, ticks):
         everything += arrived
         if tick == ticks - 1:
@@ -599,30 +626,31 @@
             flops=4 * sources * wide * group,
         )
         if tick == 1:
-            arrived, (coupled, inner_later, faces_later, other_later) = onward(sent, functools.partial(beside_second, sent))
+            arrived, (first_half, read, inner_later, faces_later, other_later) = onward(sent, functools.partial(beside_second, sent))
             later_parts = (edges_later, inner_later, field_later, pair_later1, cross_later1)
         else:
             twice = fields(sent)
+            second_half = operator_rest(sent)
             arrived, most = onward(sent, lambda: output(everything))
     half = len(arrived) // 2
     (own_part,) = call(
         functools.partial(last_own_kernel, d),
         "last_own",
         [face],
-        [*twice, coupled] + arrived[:half],
+        [*twice, first_half, second_half] + arrived[:half],
         [jax.ShapeDtypeStruct((sources, count * width), F32)],
     )
     (out,) = call(
         functools.partial(last_other_kernel, d),
         "last_other",
         [face],
-        [own_part, coupled, most] + arrived[half:],
+        [own_part, first_half, second_half, most] + arrived[half:],
         [whole],
         [(sources, count * width)],
-        anywhere=(2,),
+        anywhere=(3,),
         sems=count,
         place=pl.ANY,
-        aliases={3: 0},
+        aliases={4: 0},
     )
     return out[:, None]
 

time: 57.2 us -> 57.6 us (level)
  starting transfers between devices: 26.3 us -> 25.3 us
  Pallas kernels: 23.8 us -> 24.5 us
    ppermute x3, starting transfers between devices: 11.1 us -> 10.1 us  [onward(): own.append(lax.ppermute(block, ('slab', 'face'), route))]
    pallas_call x17 -> x18, Pallas kernels: 23.8 us -> 24.5 us  [call(): pl.pallas_call(body, name=name, out_shape=outs, in_specs=[pl.BlockSpec(me...]
  transfers between devices with their start and end apart: 21 -> 21, of which waited for: 9 -> 11; matrix products, arithmetic and copies ran while one was open for 0% -> 0% of each run, Pallas kernels for 34% -> 35%
where the time goes in v13:
time: 57.6 us; the launch traced here: 56.7 us
  starting transfers between devices  25.3 us (44%)
  Pallas kernels  24.5 us (43%)
  waiting for transfers between devices  6.49 us (11%)
    pallas_call x18, Pallas kernels, call(): pl.pallas_call(body, name=name, out_shape=outs, in_specs=[pl.BlockSpec(me...  24.5 us
    ppermute x4, starting transfers between devices, exchange(): got = lax.ppermute(cross, 'face', crossing)  11.1 us
    ppermute x3, starting transfers between devices, onward(): own.append(lax.ppermute(block, ('slab', 'face'), route))  10.1 us
    ppermute x10, waiting for transfers between devices, swap(): return lax.ppermute(block, 'face', pairing)  4.75 us
    ppermute x10, starting transfers between devices, swap(): return lax.ppermute(block, 'face', pairing)  3.18 us
    ppermute x3, waiting for transfers between devices, onward(): own.append(lax.ppermute(block, ('slab', 'face'), route))  1.72 us
  transfers between devices with their start and end apart: 21, of which 11 were waited for; matrix products, arithmetic and copies ran while one was open for 0% of the time, Pallas kernels for 35%

profile of v13, /device:TPU:9, one launch (start us, length us, event | category | flops | bytes accessed | tf_op | source)
XLA Modules:
  0.0 56.7 jit_solution(7876962341127268692)
XLA Ops:
  0.0 2.6 %first.1 = (bf16[8,256,128]{2,1,0:T(8,128)(2,1)S(1)}, bf16[8,256,128]{2,1,0:T(8,128)(2,1)S(1)}, bf16[2,128,128]{2,1,0:T(8,128)(2,1)S(1)}, bf16[2,256,128]{2,1,0:...) custom-call(s32[1]{0:T(128)} %bitcast.face_ref, ...), custom_call_target="tpu_custom_call" | custom-call | tf_op jit(solution)/shard_map/first/pallas_call | solution.py:413
  3.4 3.0 %collective-permute-start.1 = (bf16[2,256,128]{2,1,0:T(8,128)(2,1)S(1)}, bf16[2,256,128]{2,1,0:T(8,128)(2,1)S(1)}, u32[]{:S(2)}, u32[]{:S(2)}) collective-permute-start(bf16[2,256,128]{2,1,0:T(8,128)(2,1)S(1)} %get-tuple-element.62), channel_id=1, source_target_pairs={{1,2},{2,1},{5,6},{6,5},{9,10},{10,9},{13,14},{14,13},{17,18},{18,... | collective-permute-start | bytes 393224 | tf_op jit(solution)/shard_map/ppermute | solution.py:440
  6.5 2.5 %collective-permute-start.5 = (bf16[2,416,128]{2,1,0:T(8,128)(2,1)S(1)}, bf16[2,416,128]{2,1,0:T(8,128)(2,1)S(1)}, u32[]{:S(2)}, u32[]{:S(2)}) collective-permute-start(bf16[2,416,128]{2,1,0:T(8,128)(2,1)S(1)} %get-tuple-element.75), channel_id=1, source_target_pairs={{1,2},{2,1},{5,6},{6,5},{9,10},{10,9},{13,14},{14,13},{17,18},{18,... | collective-permute-start | bytes 638984 | tf_op jit(solution)/shard_map/ppermute | solution.py:440
  9.0 2.2 %fold.1 = (bf16[8,640,128]{2,1,0:T(8,128)(2,1)S(1)}, bf16[6,128,1024]{2,1,0:T(8,128)(2,1)S(1)}) custom-call(s32[1]{0:T(128)} %bitcast.face_ref, s32[2]{0:T(128)S(1)} %get-tuple-element.63.iface, s32[4,8]{1,0:T(4,128)S(1)} %get-tuple-element.59.cols, bf16[8,128,128]{2,1,0:T(8,128)(2,1)S(1)} %get-tuple-element.64.inv, ...), custom_call_target="tpu_custom_call" | custom-call | tf_op jit(solution)/shard_map/fold/pallas_call | solution.py:413
  11.2 1.1 %second_edges.1 = (bf16[4,256,128]{2,1,0:T(8,128)(2,1)S(1)}, bf16[2,256,128]{2,1,0:T(8,128)(2,1)S(1)}, bf16[2,256,128]{2,1,0:T(8,128)(2,1)S(1)}, bf16[12,256,128]{2,1,0:T(8,128)(2,1)S(1)}) custom-call(s32[1]{0:T(128)} %bitcast.face_ref, s32[4,8]{1,0:T(4,128)S(1)} %get-tuple-element.59.cols, bf16[8,256,128]{2,1,0:T(8,128)(2,1)S(1)} %get-tuple-element.60.field.rest_2_, ...), custom_call_target="tpu_custom_call" | custom-call | tf_op jit(solution)/shard_map/second_edges/pallas_call | solution.py:413
  12.4 3.0 %collective-permute-start.3 = (bf16[2,256,128]{2,1,0:T(8,128)(2,1)S(1)}, bf16[2,256,128]{2,1,0:T(8,128)(2,1)S(1)}, u32[]{:S(2)}, u32[]{:S(2)}) collective-permute-start(bf16[2,256,128]{2,1,0:T(8,128)(2,1)S(1)} %get-tuple-element.71), channel_id=1, source_target_pairs={{1,2},{2,1},{5,6},{6,5},{9,10},{10,9},{13,14},{14,13},{17,18},{18,... | collective-permute-start | bytes 393224 | tf_op jit(solution)/shard_map/ppermute | solution.py:440
  15.4 1.7 %behind.1 = (bf16[4,256,128]{2,1,0:T(8,128)(2,1)S(1)}, bf16[8,1024,128]{2,1,0:T(8,128)(2,1)S(1)}, bf16[2,1024,128]{2,1,0:T(8,128)(2,1)S(1)}, bf16[2,1024,128]{2,1,0:T(8,128)(2,1)S(1)}, bf16[12,256,128]{2,1,0:T(8,128)(2,1)S(1)}) custom-call(s32[1]{0:T(128)} %bitcast.face_ref, s32[2]{0:T(128)S(1)} %get-tuple-element.63.iface, ...), custom_call_target="tpu_custom_call" | custom-call | tf_op jit(solution)/shard_map/behind/pallas_call | solution.py:413
  17.2 2.5 %collective-permute-start.9 = (bf16[2,1024,128]{2,1,0:T(8,128)(2,1)S(1)}, bf16[2,1024,128]{2,1,0:T(8,128)(2,1)S(1)}, u32[]{:S(2)}, u32[]{:S(2)}) collective-permute-start(bf16[2,1024,128]{2,1,0:T(8,128)(2,1)S(1)} %get-tuple-element.83), channel_id=1, source_target_pairs={{1,2},{2,1},{5,6},{6,5},{9,10},{10,9},{13,14},{14,13},{17,18},{18,... | collective-permute-start | bytes 1572872 | tf_op jit(solution)/shard_map/ppermute | solution.py:440
  19.8 0.9 %second_inner.1.inner = bf16[4,128,128]{2,1,0:T(8,128)(2,1)S(1)} custom-call(s32[1]{0:T(128)} %bitcast.face_ref, s32[4,8]{1,0:T(4,128)S(1)} %get-tuple-element.59.cols, bf16[8,256,128]{2,1,0:T(8,128)(2,1)S(1)} %get-tuple-element.60.field.rest_2_, bf16[12,256,128]{2,1,0:T(8,128)(2,1)S(1)} %get-tuple-element.69.ext.ext0, ...), custom_call_target="tpu_custom_call" | custom-call | tf_op jit(solution)/shard_map/second_inner/pallas_call | solution.py:413
  21.6 1.2 %collective-permute-done.6.other = bf16[2,128,128]{2,1,0:T(8,128)(2,1)S(1)} collective-permute-done((bf16[2,128,128]{2,1,0:T(8,128)(2,1)S(1)}, bf16[2,128,128]{2,1,0:T(8,128)(2,1)S(1)}, u32[]{:S(2)}, u32[]{:S(2)}) %collective-permute-start.6) | collective-permute-done | bytes 65568 | tf_op jit(solution)/shard_map/ppermute | solution.py:444
  22.9 3.8 %collective-permute-start.7 = (bf16[4,128,128]{2,1,0:T(8,128)(2,1)S(1)}, bf16[4,128,128]{2,1,0:T(8,128)(2,1)S(1)}, u32[]{:S(2)}, u32[]{:S(2)}) collective-permute-start(bf16[4,128,128]{2,1,0:T(8,128)(2,1)S(1)} %merge.1.after), channel_id=1, source_target_pairs={{0,4},{3,5},{2,6},{1,7},{4,8},{7,9},{6,10},{5,11},{8,12},{11,13},{... | collective-permute-start | bytes 393224 | tf_op jit(solution)/shard_map/ppermute | solution.py:456
  26.7 1.3 %rest.2 = (bf16[4,256,128]{2,1,0:T(8,128)(2,1)S(1)}, bf16[1,2,128,128]{3,2,1,0:T(8,128)(2,1)S(1)}) custom-call(s32[1]{0:T(128)} %bitcast.face_ref, s32[2]{0:T(128)S(1)} %get-tuple-element.63.iface, s32[4,8]{1,0:T(4,128)S(1)} %get-tuple-element.59.cols, bf16[4,256,128]{2,1,0:T(8,128)(2,1)S(1)} %get-tuple-element.68.edges.rest_0_, ...), custom_call_target="tpu_custom_call" | custom-call | tf_op jit(solution)/shard_map/rest/pallas_call | solution.py:413
  28.0 2.2 %interface.1 = (bf16[256,256]{1,0:T(8,128)(2,1)S(1)}, bf16[256,256]{1,0:T(8,128)(2,1)S(1)}, bf16[256,256]{1,0:T(8,128)(2,1)S(1)}, bf16[256,256]{1,0:T(8,128)(2,1)S(1)}) custom-call(s32[1]{0:T(128)} %bitcast.face_ref, s32[2]{0:T(128)S(1)} %get-tuple-element.63.iface, s32[4,8]{1,0:T(4,128)S(1)} %get-tuple-element.59.cols, ...), custom_call_target="tpu_custom_call" | custom-call | tf_op jit(solution)/shard_map/interface/pallas_call | solution.py:413
  32.8 1.1 %collective-permute-done.14.rest_9_ = bf16[1,2,128,128]{3,2,1,0:T(8,128)(2,1)S(1)} collective-permute-done((bf16[1,2,128,128]{3,2,1,0:T(8,128)(2,1)S(1)}, bf16[1,2,128,128]{3,2,1,0:T(8,128)(2,1)S(1)}, u32[]{:S(2)}, u32[]{:S(2)}) %collective-permute-start.14) | collective-permute-done | bytes 65568 | tf_op jit(solution)/shard_map/ppermute | solution.py:444
  34.3 3.4 %collective-permute-start.16 = (bf16[4,128,128]{2,1,0:T(8,128)(2,1)S(1)}, bf16[4,128,128]{2,1,0:T(8,128)(2,1)S(1)}, u32[]{:S(2)}, u32[]{:S(2)}) collective-permute-start(bf16[4,128,128]{2,1,0:T(8,128)(2,1)S(1)} %chain.2.after), channel_id=1, source_target_pairs={{0,4},{3,5},{2,6},{1,7},{4,8},{7,9},{6,10},{5,11},{8,12},{11,13},{... | collective-permute-start | bytes 393224 | tf_op jit(solution)/shard_map/ppermute | solution.py:456
  37.7 1.3 %rest.3 = (bf16[4,256,128]{2,1,0:T(8,128)(2,1)S(1)}, bf16[1,2,128,128]{3,2,1,0:T(8,128)(2,1)S(1)}) custom-call(s32[1]{0:T(128)} %bitcast.face_ref, s32[2]{0:T(128)S(1)} %get-tuple-element.63.iface, s32[4,8]{1,0:T(4,128)S(1)} %get-tuple-element.59.cols, bf16[4,256,128]{2,1,0:T(8,128)(2,1)S(1)} %get-tuple-element.81.edges.rest_5_, ...), custom_call_target="tpu_custom_call" | custom-call | tf_op jit(solution)/shard_map/rest/pallas_call | solution.py:413
  39.3 2.4 %operator.1 = (bf16[1024,512]{1,0:T(8,128)(2,1)S(1)}, bf16[12,1024,128]{2,1,0:T(8,128)(2,1)S(1)}) custom-call(s32[1]{0:T(128)} %bitcast.face_ref, s32[2]{0:T(128)S(1)} %get-tuple-element.63.iface, s32[4,8]{1,0:T(4,128)S(1)} %get-tuple-element.59.cols, bf16[2,128,128]{2,1,0:T(8,128)(2,1)S(1)} %get-tuple-element.73.gfield, ...), custom_call_target="tpu_custom_call" | custom-call | flops 671088640 | tf_op jit(solution)/shard_map/operator/pallas_call | solution.py:413
  41.7 1.4 %collective-permute-done.16.rest_10_.rest_2_ = bf16[4,128,128]{2,1,0:T(8,128)(2,1)S(1)} collective-permute-done((bf16[4,128,128]{2,1,0:T(8,128)(2,1)S(1)}, bf16[4,128,128]{2,1,0:T(8,128)(2,1)S(1)}, u32[]{:S(2)}, u32[]{:S(2)}) %collective-permute-start.16) | collective-permute-done | bytes 131104 | tf_op jit(solution)/shard_map/ppermute | solution.py:456
  43.6 1.0 %collective-permute-done.18.rest_11_.rest_3_ = bf16[4,128,128]{2,1,0:T(8,128)(2,1)S(1)} collective-permute-done((bf16[4,128,128]{2,1,0:T(8,128)(2,1)S(1)}, bf16[4,128,128]{2,1,0:T(8,128)(2,1)S(1)}, u32[]{:S(2)}, u32[]{:S(2)}) %collective-permute-start.18) | collective-permute-done | bytes 131104 | tf_op jit(solution)/shard_map/ppermute | solution.py:444
  45.0 2.9 %collective-permute-start.19 = (bf16[4,128,128]{2,1,0:T(8,128)(2,1)S(1)}, bf16[4,128,128]{2,1,0:T(8,128)(2,1)S(1)}, u32[]{:S(2)}, u32[]{:S(2)}) collective-permute-start(bf16[4,128,128]{2,1,0:T(8,128)(2,1)S(1)} %chain.3.rest_11_.after), channel_id=1, source_target_pairs={{0,4},{3,5},{2,6},{1,7},{4,8},{7,9},{6,10},{5,11},{8,12},{11,13},{... | collective-permute-start | bytes 393224 | tf_op jit(solution)/shard_map/ppermute | solution.py:456
  47.9 2.1 %operator_rest.1.second_half = bf16[1024,512]{1,0:T(8,128)(2,1)S(1)} custom-call(s32[1]{0:T(128)} %bitcast.face_ref, s32[2]{0:T(128)S(1)} %get-tuple-element.63.iface, s32[4,8]{1,0:T(4,128)S(1)} %get-tuple-element.59.cols, bf16[2,128,128]{2,1,0:T(8,128)(2,1)S(1)} %get-tuple-element.73.gfield, bf16[8,640,128]{2,1,0:T(8,128)(2,1)S(1)} %get-tuple-element.67.folded.rest_10_, ...), custom_call_target="tpu_custom_call" | custom-call | tf_op jit(solution)/shard_map/operator_rest/pallas_call | solution.py:413
  50.0 2.2 %third.1 = (bf16[8,256,128]{2,1,0:T(8,128)(2,1)S(1)}, bf16[8,256,128]{2,1,0:T(8,128)(2,1)S(1)}) custom-call(s32[1]{0:T(128)} %bitcast.face_ref, s32[4,8]{1,0:T(4,128)S(1)} %get-tuple-element.59.cols, bf16[4,256,128]{2,1,0:T(8,128)(2,1)S(1)} %get-tuple-element.68.edges.rest_0_, bf16[4,256,128]{2,1,0:T(8,128)(2,1)S(1)} %get-tuple-element.80.after.rest_1_, ...), custom_call_target="tpu_custom_call" | custom-call | tf_op jit(solution)/shard_map/third/pallas_call | solution.py:413
  52.2 1.5 %output.1.earlier = bf16[4,128,1024]{2,1,0:T(8,128)(2,1)} custom-call(s32[1]{0:T(128)} %bitcast.face_ref, bf16[8,256,128]{2,1,0:T(8,128)(2,1)S(1)} %get-tuple-element.107.early, bf16[8,256,128]{2,1,0:T(8,128)(2,1)S(1)} %get-tuple-element.108.later, bf16[1024,512]{1,0:T(8,128)(2,1)S(1)} %get-tuple-element.109.first_half, ...), custom_call_target="tpu_custom_call" | custom-call | tf_op jit(solution)/shard_map/output/pallas_call | solution.py:413
  55.5 1.0 %last_other.1 = bf16[4,128,1024]{2,1,0:T(8,128)(2,1)} custom-call(s32[1]{0:T(128)} %bitcast.face_ref, f32[128,1024]{1,0:T(8,128)S(1)} %last_own.1.own_part, bf16[1024,512]{1,0:T(8,128)(2,1)S(1)} %get-tuple-element.109.first_half, bf16[1024,512]{1,0:T(8,128)(2,1)S(1)} %operator_rest.1.second_half, ...), custom_call_target="tpu_custom_call", output_to_operand_aliasing={{}: (4, {})} | custom-call | tf_op jit(solution)/shard_map/last_other/pallas_call | solution.py:413
  (36 shorter events, 7.8 us)
Async XLA Ops:
  2.6 8.6 %collective-permute-start = (bf16[2,256,128]{2,1,0:T(8,128)(2,1)S(1)}, bf16[2,256,128]{2,1,0:T(8,128)(2,1)S(1)}, u32[]{:S(2)}, u32[]{:S(2)}) collective-permute-start(bf16[2,256,128]{2,1,0:T(8,128)(2,1)S(1)} %get-tuple-element.61), channel_id=1, source_target_pairs={{0,1},{1,0},{2,3},{3,2},{4,5},{5,4},{6,7},{7,6},{8,9},{9,8},{10,11... | collective-permute-start | bytes 393224 | tf_op jit(solution)/shard_map/ppermute | solution.py:441
  3.4 7.8 %collective-permute-start.1 = (bf16[2,256,128]{2,1,0:T(8,128)(2,1)S(1)}, bf16[2,256,128]{2,1,0:T(8,128)(2,1)S(1)}, u32[]{:S(2)}, u32[]{:S(2)}) collective-permute-start(bf16[2,256,128]{2,1,0:T(8,128)(2,1)S(1)} %get-tuple-element.62), channel_id=1, source_target_pairs={{1,2},{2,1},{5,6},{6,5},{9,10},{10,9},{13,14},{14,13},{17,18},{18,... | collective-permute-start | bytes 393224 | tf_op jit(solution)/shard_map/ppermute | solution.py:440
  6.4 9.0 %collective-permute-start.4 = (bf16[2,416,128]{2,1,0:T(8,128)(2,1)S(1)}, bf16[2,416,128]{2,1,0:T(8,128)(2,1)S(1)}, u32[]{:S(2)}, u32[]{:S(2)}) collective-permute-start(bf16[2,416,128]{2,1,0:T(8,128)(2,1)S(1)} %get-tuple-element.74), channel_id=1, source_target_pairs={{0,1},{1,0},{2,3},{3,2},{4,5},{5,4},{6,7},{7,6},{8,9},{9,8},{10,11... | collective-permute-start | bytes 638984 | tf_op jit(solution)/shard_map/ppermute | solution.py:441
  6.5 9.0 %collective-permute-start.5 = (bf16[2,416,128]{2,1,0:T(8,128)(2,1)S(1)}, bf16[2,416,128]{2,1,0:T(8,128)(2,1)S(1)}, u32[]{:S(2)}, u32[]{:S(2)}) collective-permute-start(bf16[2,416,128]{2,1,0:T(8,128)(2,1)S(1)} %get-tuple-element.75), channel_id=1, source_target_pairs={{1,2},{2,1},{5,6},{6,5},{9,10},{10,9},{13,14},{14,13},{17,18},{18,... | collective-permute-start | bytes 638984 | tf_op jit(solution)/shard_map/ppermute | solution.py:440
  12.3 3.1 %collective-permute-start.2 = (bf16[2,256,128]{2,1,0:T(8,128)(2,1)S(1)}, bf16[2,256,128]{2,1,0:T(8,128)(2,1)S(1)}, u32[]{:S(2)}, u32[]{:S(2)}) collective-permute-start(bf16[2,256,128]{2,1,0:T(8,128)(2,1)S(1)} %get-tuple-element.70), channel_id=1, source_target_pairs={{0,1},{1,0},{2,3},{3,2},{4,5},{5,4},{6,7},{7,6},{8,9},{9,8},{10,11... | collective-permute-start | bytes 393224 | tf_op jit(solution)/shard_map/ppermute | solution.py:441
  12.4 8.3 %collective-permute-start.3 = (bf16[2,256,128]{2,1,0:T(8,128)(2,1)S(1)}, bf16[2,256,128]{2,1,0:T(8,128)(2,1)S(1)}, u32[]{:S(2)}, u32[]{:S(2)}) collective-permute-start(bf16[2,256,128]{2,1,0:T(8,128)(2,1)S(1)} %get-tuple-element.71), channel_id=1, source_target_pairs={{1,2},{2,1},{5,6},{6,5},{9,10},{10,9},{13,14},{14,13},{17,18},{18,... | collective-permute-start | bytes 393224 | tf_op jit(solution)/shard_map/ppermute | solution.py:440
  17.1 10.8 %collective-permute-start.8 = (bf16[2,1024,128]{2,1,0:T(8,128)(2,1)S(1)}, bf16[2,1024,128]{2,1,0:T(8,128)(2,1)S(1)}, u32[]{:S(2)}, u32[]{:S(2)}) collective-permute-start(bf16[2,1024,128]{2,1,0:T(8,128)(2,1)S(1)} %get-tuple-element.82), channel_id=1, source_target_pairs={{0,1},{1,0},{2,3},{3,2},{4,5},{5,4},{6,7},{7,6},{8,9},{9,8},{10,11... | collective-permute-start | bytes 1572872 | tf_op jit(solution)/shard_map/ppermute | solution.py:441
  17.2 10.8 %collective-permute-start.9 = (bf16[2,1024,128]{2,1,0:T(8,128)(2,1)S(1)}, bf16[2,1024,128]{2,1,0:T(8,128)(2,1)S(1)}, u32[]{:S(2)}, u32[]{:S(2)}) collective-permute-start(bf16[2,1024,128]{2,1,0:T(8,128)(2,1)S(1)} %get-tuple-element.83), channel_id=1, source_target_pairs={{1,2},{2,1},{5,6},{6,5},{9,10},{10,9},{13,14},{14,13},{17,18},{18,... | collective-permute-start | bytes 1572872 | tf_op jit(solution)/shard_map/ppermute | solution.py:440
  21.5 1.3 %collective-permute-start.6 = (bf16[2,128,128]{2,1,0:T(8,128)(2,1)S(1)}, bf16[2,128,128]{2,1,0:T(8,128)(2,1)S(1)}, u32[]{:S(2)}, u32[]{:S(2)}) collective-permute-start(bf16[2,128,128]{2,1,0:T(8,128)(2,1)S(1)} %third_rows.1.own), channel_id=1, source_target_pairs={{0,1},{1,0},{2,3},{3,2},{4,5},{5,4},{6,7},{7,6},{8,9},{9,8},{10,11... | collective-permute-start | bytes 196616 | tf_op jit(solution)/shard_map/ppermute | solution.py:444
  22.9 8.7 %collective-permute-start.7 = (bf16[4,128,128]{2,1,0:T(8,128)(2,1)S(1)}, bf16[4,128,128]{2,1,0:T(8,128)(2,1)S(1)}, u32[]{:S(2)}, u32[]{:S(2)}) collective-permute-start(bf16[4,128,128]{2,1,0:T(8,128)(2,1)S(1)} %merge.1.after), channel_id=1, source_target_pairs={{0,4},{3,5},{2,6},{1,7},{4,8},{7,9},{6,10},{5,11},{8,12},{11,13},{... | collective-permute-start | bytes 393224 | tf_op jit(solution)/shard_map/ppermute | solution.py:456
  30.2 1.4 %collective-permute-start.10 = (bf16[256,256]{1,0:T(8,128)(2,1)S(1)}, bf16[256,256]{1,0:T(8,128)(2,1)S(1)}, u32[]{:S(2)}, u32[]{:S(2)}) collective-permute-start(bf16[256,256]{1,0:T(8,128)(2,1)S(1)} %get-tuple-element.88.rest_0_.after), channel_id=1, source_target_pairs={{0,1},{1,0},{2,3},{3,2},{4,5},{5,4},{6,7},{7,6},{8,9},{9,8},{10,11... | collective-permute-start | bytes 393224 | tf_op jit(solution)/shard_map/ppermute | solution.py:444
  30.3 1.5 %collective-permute-start.11 = (bf16[256,256]{1,0:T(8,128)(2,1)S(1)}, bf16[256,256]{1,0:T(8,128)(2,1)S(1)}, u32[]{:S(2)}, u32[]{:S(2)}) collective-permute-start(bf16[256,256]{1,0:T(8,128)(2,1)S(1)} %get-tuple-element.89.rest_1_), channel_id=1, source_target_pairs={{0,1},{1,0},{2,3},{3,2},{4,5},{5,4},{6,7},{7,6},{8,9},{9,8},{10,11... | collective-permute-start | bytes 393224 | tf_op jit(solution)/shard_map/ppermute | solution.py:444
  30.8 1.3 %collective-permute-start.12 = (bf16[256,256]{1,0:T(8,128)(2,1)S(1)}, bf16[256,256]{1,0:T(8,128)(2,1)S(1)}, u32[]{:S(2)}, u32[]{:S(2)}) collective-permute-start(bf16[256,256]{1,0:T(8,128)(2,1)S(1)} %get-tuple-element.90.rest_2_), channel_id=1, source_target_pairs={{0,1},{1,0},{2,3},{3,2},{4,5},{5,4},{6,7},{7,6},{8,9},{9,8},{10,11... | collective-permute-start | bytes 393224 | tf_op jit(solution)/shard_map/ppermute | solution.py:444
  30.9 1.5 %collective-permute-start.13 = (bf16[256,256]{1,0:T(8,128)(2,1)S(1)}, bf16[256,256]{1,0:T(8,128)(2,1)S(1)}, u32[]{:S(2)}, u32[]{:S(2)}) collective-permute-start(bf16[256,256]{1,0:T(8,128)(2,1)S(1)} %get-tuple-element.91.rest_3_), channel_id=1, source_target_pairs={{0,1},{1,0},{2,3},{3,2},{4,5},{5,4},{6,7},{7,6},{8,9},{9,8},{10,11... | collective-permute-start | bytes 393224 | tf_op jit(solution)/shard_map/ppermute | solution.py:444
  32.3 1.6 %collective-permute-start.15 = (bf16[4,128,128]{2,1,0:T(8,128)(2,1)S(1)}, bf16[4,128,128]{2,1,0:T(8,128)(2,1)S(1)}, u32[]{:S(2)}, u32[]{:S(2)}) collective-permute-start(bf16[4,128,128]{2,1,0:T(8,128)(2,1)S(1)} %collective-permute-done.7.rest_10_.rest_0_), channel_id=1, source_target_pairs={{0,1},{1,0},{2,3},{3,2},{4,5},{5,4},{6,7},{7,6},{8,9},{9,8},{10,11... | collective-permute-start | bytes 393224 | tf_op jit(solution)/shard_map/ppermute | solution.py:444
  32.7 1.3 %collective-permute-start.14 = (bf16[1,2,128,128]{3,2,1,0:T(8,128)(2,1)S(1)}, bf16[1,2,128,128]{3,2,1,0:T(8,128)(2,1)S(1)}, u32[]{:S(2)}, u32[]{:S(2)}) collective-permute-start(bf16[1,2,128,128]{3,2,1,0:T(8,128)(2,1)S(1)} %get-tuple-element.96.rest_8_), channel_id=1, source_target_pairs={{0,1},{1,0},{2,3},{3,2},{4,5},{5,4},{6,7},{7,6},{8,9},{9,8},{10,11... | collective-permute-start | bytes 196616 | tf_op jit(solution)/shard_map/ppermute | solution.py:444
  34.3 8.8 %collective-permute-start.16 = (bf16[4,128,128]{2,1,0:T(8,128)(2,1)S(1)}, bf16[4,128,128]{2,1,0:T(8,128)(2,1)S(1)}, u32[]{:S(2)}, u32[]{:S(2)}) collective-permute-start(bf16[4,128,128]{2,1,0:T(8,128)(2,1)S(1)} %chain.2.after), channel_id=1, source_target_pairs={{0,4},{3,5},{2,6},{1,7},{4,8},{7,9},{6,10},{5,11},{8,12},{11,13},{... | collective-permute-start | bytes 393224 | tf_op jit(solution)/shard_map/ppermute | solution.py:456
  39.0 2.6 %collective-permute-start.17 = (bf16[1,2,128,128]{3,2,1,0:T(8,128)(2,1)S(1)}, bf16[1,2,128,128]{3,2,1,0:T(8,128)(2,1)S(1)}, u32[]{:S(2)}, u32[]{:S(2)}) collective-permute-start(bf16[1,2,128,128]{3,2,1,0:T(8,128)(2,1)S(1)} %get-tuple-element.104.rest_8_), channel_id=1, source_target_pairs={{0,1},{1,0},{2,3},{3,2},{4,5},{5,4},{6,7},{7,6},{8,9},{9,8},{10,11... | collective-permute-start | bytes 196616 | tf_op jit(solution)/shard_map/ppermute | solution.py:444
  43.1 1.5 %collective-permute-start.18 = (bf16[4,128,128]{2,1,0:T(8,128)(2,1)S(1)}, bf16[4,128,128]{2,1,0:T(8,128)(2,1)S(1)}, u32[]{:S(2)}, u32[]{:S(2)}) collective-permute-start(bf16[4,128,128]{2,1,0:T(8,128)(2,1)S(1)} %collective-permute-done.16.rest_10_.rest_2_), channel_id=1, source_target_pairs={{0,1},{1,0},{2,3},{3,2},{4,5},{5,4},{6,7},{7,6},{8,9},{9,8},{10,11... | collective-permute-start | bytes 393224 | tf_op jit(solution)/shard_map/ppermute | solution.py:444
  45.0 8.8 %collective-permute-start.19 = (bf16[4,128,128]{2,1,0:T(8,128)(2,1)S(1)}, bf16[4,128,128]{2,1,0:T(8,128)(2,1)S(1)}, u32[]{:S(2)}, u32[]{:S(2)}) collective-permute-start(bf16[4,128,128]{2,1,0:T(8,128)(2,1)S(1)} %chain.3.rest_11_.after), channel_id=1, source_target_pairs={{0,4},{3,5},{2,6},{1,7},{4,8},{7,9},{6,10},{5,11},{8,12},{11,13},{... | collective-permute-start | bytes 393224 | tf_op jit(solution)/shard_map/ppermute | solution.py:456
  53.7 1.8 %collective-permute-start.20 = (bf16[4,128,128]{2,1,0:T(8,128)(2,1)S(1)}, bf16[4,128,128]{2,1,0:T(8,128)(2,1)S(1)}, u32[]{:S(2)}, u32[]{:S(2)}) collective-permute-start(bf16[4,128,128]{2,1,0:T(8,128)(2,1)S(1)} %collective-permute-done.19.rest_0_), channel_id=1, source_target_pairs={{0,1},{1,0},{2,3},{3,2},{4,5},{5,4},{6,7},{7,6},{8,9},{9,8},{10,11... | collective-permute-start | bytes 393224 | tf_op jit(solution)/shard_map/ppermute | solution.py:444

commit v14 on v12

--- a/solution.py
+++ b/solution.py
@@ -109,24 +109,18 @@
         for k in range(1 + d.neigh):
             part = product[:, k * w : (k + 1) * w].T
             folded[r, k * w : (k + 1) * w, :] = ((unit if k == 0 else 0.0) - part).astype(BF)
-    met[...] = jnp.zeros_like(met)
+    spare = 2 * HALO + d.nq
+    met[0 : 2 * HALO] = jnp.zeros((2 * HALO, w, d.count * w), BF)
     for r in range(d.count):
         lanes = slice(r * w, (r + 1) * w)
         for q in range(d.nq):
             met[2 * HALO + q, :, lanes] = jnp.where(iface[q] == r, folded[r, 0:w, :], jnp.zeros((w, w), BF))
         for k in range(d.neigh):
             c = cols[k, r] - d.first_col(face_ref[0])
-            inside = jnp.logical_and(c >= HALO, c < d.up)
-            at = jnp.where(c < HALO, c, c - d.count)
-            hit = jnp.logical_not(inside)
+            at = jnp.where(c < HALO, c, jnp.where(c >= d.up, c - d.count, spare))
             for q in range(d.nq):
-                here = c == iface[q] + HALO
-                at = jnp.where(here, 2 * HALO + q, at)
-                hit = jnp.logical_or(hit, here)
-
-            @pl.when(hit)
-            def _():
-                met[at, :, lanes] += folded[r, (1 + k) * w : (2 + k) * w, :]
+                at = jnp.where(c == iface[q] + HALO, 2 * HALO + q, at)
+            met[at, :, lanes] += folded[r, (1 + k) * w : (2 + k) * w, :]
 
 
 def sweep(d, cols, face, ext, span, r, folded):
@@ -166,10 +160,6 @@
     correct_edges(d, cols, face, field, pair_in, cross_in, folded, edges, ext)
     pair[...] = edges[pl.ds(HALO * (1 - parity), HALO)]
     cross[...] = edges[pl.ds(HALO * parity, HALO)]
-
-
-def second_inner_kernel(d, face_ref, cols, field, ext, folded, after, out):
-    correct(d, cols, face_ref[0], field, folded, out, ext, range(HALO, d.last))
 
 
 def interface_rows(d, face, iface, cols, edges, inner, field, pair_in, cross_in, folded, first, outs, ext):
@@ -183,8 +173,10 @@
             out[q] = value[t * d.sources : (t + 1) * d.sources]
 
 
-def third_rows_kernel(d, face_ref, iface, cols, edges, inner, field, pair_in, cross_in, folded, sent, ext):
-    interface_rows(d, face_ref[0], iface, cols, edges, inner, field, pair_in, cross_in, folded, 0, [sent], ext)
+def third_rows_kernel(d, face_ref, iface, cols, edges, field, ext0, pair_in, cross_in, folded, after, sent, inner, ext):
+    face = face_ref[0]
+    correct(d, cols, face, field, folded, inner, ext0, range(HALO, d.last))
+    interface_rows(d, face, iface, cols, edges, inner, field, pair_in, cross_in, folded, 0, [sent], ext)
 
 
 def third_kernel(d, face_ref, cols, *rest):
@@ -466,7 +458,7 @@
         "fold",
         [face, iface, cols],
         [inv, diag, off],
-        [(count, d.depth, width), (2 * HALO + nq, width, count * width)],
+        [(count, d.depth, width), (2 * HALO + nq + 1, width, count * width)],
     )
     edges, pair, cross, ext0 = call(
         functools.partial(second_edges_kernel, d),
@@ -485,23 +477,16 @@
         anywhere=(6,),
     )
     pair_later1, cross_later1 = exchange(pair, cross)
-    (inner_first,) = call(
-        functools.partial(second_inner_kernel, d),
-        "second_inner",
-        [face, cols],
-        [field, ext0, folded, gfirst],
-        [(count - 2 * HALO, sources, width)],
-        anywhere=(3,),
-    )
-    cross1, inner_first = lax.optimization_barrier((cross1, inner_first))
+    cross1, gfirst = lax.optimization_barrier((cross1, gfirst))
     (own_first,) = call(
         functools.partial(third_rows_kernel, d),
         "third_rows",
         [face, iface, cols],
-        [edges, inner_first, field, pair1, cross1, folded],
+        [edges, field, ext0, pair1, cross1, folded, gfirst],
         [(nq, sources, width)],
-        [(ext, sources, width)],
+        [(count - 2 * HALO, sources, width), (ext, sources, width)],
         flops=12 * early * sweep_flops,
+        anywhere=(6,),
     )
     (sent,) = call(
         functools.partial(merge_kernel, d),

time: 57.2 us -> 57.4 us (level)
  waiting for transfers between devices: 6.33 us -> 7.79 us
  Pallas kernels: 23.8 us -> 22.9 us
    ppermute x3, starting transfers between devices: 11.1 us -> 9.93 us  [onward(): own.append(lax.ppermute(block, ('slab', 'face'), route))]
    pallas_call x17 -> x16, Pallas kernels: 23.8 us -> 22.9 us  [call(): pl.pallas_call(body, name=name, out_shape=outs, in_specs=[pl.BlockSpec(me...]
    ppermute x10, starting transfers between devices: 3.11 us -> 3.93 us  [swap(): return lax.ppermute(block, 'face', pairing)]
    ppermute x10, waiting for transfers between devices: 4.7 us -> 5.33 us  [swap(): return lax.ppermute(block, 'face', pairing)]
  transfers between devices with their start and end apart: 21 -> 21, of which waited for: 9 -> 10; matrix products, arithmetic and copies ran while one was open for 0% -> 0% of each run, Pallas kernels for 34% -> 32%
where the time goes in v14:
time: 57.4 us; the launch traced here: 57.1 us
  starting transfers between devices  25.9 us (45%)
  Pallas kernels  22.9 us (40%)
  waiting for transfers between devices  7.79 us (14%)
    pallas_call x16, Pallas kernels, call(): pl.pallas_call(body, name=name, out_shape=outs, in_specs=[pl.BlockSpec(me...  22.9 us
    ppermute x4, starting transfers between devices, exchange(): got = lax.ppermute(cross, 'face', crossing)  11.1 us
    ppermute x3, starting transfers between devices, onward(): own.append(lax.ppermute(block, ('slab', 'face'), route))  9.93 us
    ppermute x10, waiting for transfers between devices, swap(): return lax.ppermute(block, 'face', pairing)  5.33 us
    ppermute x10, starting transfers between devices, swap(): return lax.ppermute(block, 'face', pairing)  3.93 us
    ppermute x3, waiting for transfers between devices, onward(): own.append(lax.ppermute(block, ('slab', 'face'), route))  1.98 us
  transfers between devices with their start and end apart: 21, of which 10 were waited for; matrix products, arithmetic and copies ran while one was open for 0% of the time, Pallas kernels for 32%

profile of v14, /device:TPU:9, one launch (start us, length us, event | category | flops | bytes accessed | tf_op | source)
XLA Modules:
  0.0 57.1 jit_solution(8295228877398880888)
XLA Ops:
  0.0 2.6 %first.1 = (bf16[8,256,128]{2,1,0:T(8,128)(2,1)S(1)}, bf16[8,256,128]{2,1,0:T(8,128)(2,1)S(1)}, bf16[2,128,128]{2,1,0:T(8,128)(2,1)S(1)}, bf16[2,256,128]{2,1,0:...) custom-call(s32[1]{0:T(128)} %bitcast.face_ref, ...), custom_call_target="tpu_custom_call" | custom-call | tf_op jit(solution)/shard_map/first/pallas_call | solution.py:387
  3.4 3.0 %collective-permute-start.1 = (bf16[2,256,128]{2,1,0:T(8,128)(2,1)S(1)}, bf16[2,256,128]{2,1,0:T(8,128)(2,1)S(1)}, u32[]{:S(2)}, u32[]{:S(2)}) collective-permute-start(bf16[2,256,128]{2,1,0:T(8,128)(2,1)S(1)} %get-tuple-element.59), channel_id=1, source_target_pairs={{1,2},{2,1},{5,6},{6,5},{9,10},{10,9},{13,14},{14,13},{17,18},{18,... | collective-permute-start | bytes 393224 | tf_op jit(solution)/shard_map/ppermute | solution.py:414
  6.5 2.5 %collective-permute-start.5 = (bf16[2,416,128]{2,1,0:T(8,128)(2,1)S(1)}, bf16[2,416,128]{2,1,0:T(8,128)(2,1)S(1)}, u32[]{:S(2)}, u32[]{:S(2)}) collective-permute-start(bf16[2,416,128]{2,1,0:T(8,128)(2,1)S(1)} %get-tuple-element.72), channel_id=1, source_target_pairs={{1,2},{2,1},{5,6},{6,5},{9,10},{10,9},{13,14},{14,13},{17,18},{18,... | collective-permute-start | bytes 638984 | tf_op jit(solution)/shard_map/ppermute | solution.py:414
  9.0 1.8 %fold.1 = (bf16[8,640,128]{2,1,0:T(8,128)(2,1)S(1)}, bf16[7,128,1024]{2,1,0:T(8,128)(2,1)S(1)}) custom-call(s32[1]{0:T(128)} %bitcast.face_ref, s32[2]{0:T(128)S(1)} %get-tuple-element.60.iface, s32[4,8]{1,0:T(4,128)S(1)} %get-tuple-element.56.cols, bf16[8,128,128]{2,1,0:T(8,128)(2,1)S(1)} %get-tuple-element.61.inv, ...), custom_call_target="tpu_custom_call" | custom-call | tf_op jit(solution)/shard_map/fold/pallas_call | solution.py:387
  10.9 1.1 %second_edges.1 = (bf16[4,256,128]{2,1,0:T(8,128)(2,1)S(1)}, bf16[2,256,128]{2,1,0:T(8,128)(2,1)S(1)}, bf16[2,256,128]{2,1,0:T(8,128)(2,1)S(1)}, bf16[12,256,128]{2,1,0:T(8,128)(2,1)S(1)}) custom-call(s32[1]{0:T(128)} %bitcast.face_ref, s32[4,8]{1,0:T(4,128)S(1)} %get-tuple-element.56.cols, bf16[8,256,128]{2,1,0:T(8,128)(2,1)S(1)} %get-tuple-element.57.field.rest_2_, ...), custom_call_target="tpu_custom_call" | custom-call | tf_op jit(solution)/shard_map/second_edges/pallas_call | solution.py:387
  12.1 3.0 %collective-permute-start.3 = (bf16[2,256,128]{2,1,0:T(8,128)(2,1)S(1)}, bf16[2,256,128]{2,1,0:T(8,128)(2,1)S(1)}, u32[]{:S(2)}, u32[]{:S(2)}) collective-permute-start(bf16[2,256,128]{2,1,0:T(8,128)(2,1)S(1)} %get-tuple-element.68), channel_id=1, source_target_pairs={{1,2},{2,1},{5,6},{6,5},{9,10},{10,9},{13,14},{14,13},{17,18},{18,... | collective-permute-start | bytes 393224 | tf_op jit(solution)/shard_map/ppermute | solution.py:414
  15.2 1.7 %behind.1 = (bf16[4,256,128]{2,1,0:T(8,128)(2,1)S(1)}, bf16[8,1024,128]{2,1,0:T(8,128)(2,1)S(1)}, bf16[2,1024,128]{2,1,0:T(8,128)(2,1)S(1)}, bf16[2,1024,128]{2,1,0:T(8,128)(2,1)S(1)}, bf16[12,256,128]{2,1,0:T(8,128)(2,1)S(1)}) custom-call(s32[1]{0:T(128)} %bitcast.face_ref, s32[2]{0:T(128)S(1)} %get-tuple-element.60.iface, ...), custom_call_target="tpu_custom_call" | custom-call | tf_op jit(solution)/shard_map/behind/pallas_call | solution.py:387
  16.9 2.5 %collective-permute-start.9 = (bf16[2,1024,128]{2,1,0:T(8,128)(2,1)S(1)}, bf16[2,1024,128]{2,1,0:T(8,128)(2,1)S(1)}, u32[]{:S(2)}, u32[]{:S(2)}) collective-permute-start(bf16[2,1024,128]{2,1,0:T(8,128)(2,1)S(1)} %get-tuple-element.80), channel_id=1, source_target_pairs={{1,2},{2,1},{5,6},{6,5},{9,10},{10,9},{13,14},{14,13},{17,18},{18,... | collective-permute-start | bytes 1572872 | tf_op jit(solution)/shard_map/ppermute | solution.py:414
  19.5 1.2 %third_rows.1.own = bf16[2,128,128]{2,1,0:T(8,128)(2,1)S(1)} custom-call(s32[1]{0:T(128)} %bitcast.face_ref, s32[2]{0:T(128)S(1)} %get-tuple-element.60.iface, s32[4,8]{1,0:T(4,128)S(1)} %get-tuple-element.56.cols, bf16[4,256,128]{2,1,0:T(8,128)(2,1)S(1)} %get-tuple-element.65.edges.rest_0_, bf16[8,256,128]{2,1,0:T(8,128)(2,1)S(1)} %get-tuple-element.57.field.rest_2_, ...), custom_call_target="tpu_custom_call" | custom-call | flops 4026531840 | tf_op jit(solution)/shard_map/third_rows/pallas_call | solution.py:387
  20.7 1.2 %collective-permute-done.6.other = bf16[2,128,128]{2,1,0:T(8,128)(2,1)S(1)} collective-permute-done((bf16[2,128,128]{2,1,0:T(8,128)(2,1)S(1)}, bf16[2,128,128]{2,1,0:T(8,128)(2,1)S(1)}, u32[]{:S(2)}, u32[]{:S(2)}) %collective-permute-start.6) | collective-permute-done | bytes 65568 | tf_op jit(solution)/shard_map/ppermute | solution.py:418
  22.0 3.7 %collective-permute-start.7 = (bf16[4,128,128]{2,1,0:T(8,128)(2,1)S(1)}, bf16[4,128,128]{2,1,0:T(8,128)(2,1)S(1)}, u32[]{:S(2)}, u32[]{:S(2)}) collective-permute-start(bf16[4,128,128]{2,1,0:T(8,128)(2,1)S(1)} %merge.1.after), channel_id=1, source_target_pairs={{0,4},{3,5},{2,6},{1,7},{4,8},{7,9},{6,10},{5,11},{8,12},{11,13},{... | collective-permute-start | bytes 393224 | tf_op jit(solution)/shard_map/ppermute | solution.py:430
  25.7 1.3 %rest.2 = (bf16[4,256,128]{2,1,0:T(8,128)(2,1)S(1)}, bf16[1,2,128,128]{3,2,1,0:T(8,128)(2,1)S(1)}) custom-call(s32[1]{0:T(128)} %bitcast.face_ref, s32[2]{0:T(128)S(1)} %get-tuple-element.60.iface, s32[4,8]{1,0:T(4,128)S(1)} %get-tuple-element.56.cols, bf16[4,256,128]{2,1,0:T(8,128)(2,1)S(1)} %get-tuple-element.65.edges.rest_0_, ...), custom_call_target="tpu_custom_call" | custom-call | tf_op jit(solution)/shard_map/rest/pallas_call | solution.py:387
  27.5 2.2 %interface.1 = (bf16[256,256]{1,0:T(8,128)(2,1)S(1)}, bf16[256,256]{1,0:T(8,128)(2,1)S(1)}, bf16[256,256]{1,0:T(8,128)(2,1)S(1)}, bf16[256,256]{1,0:T(8,128)(2,1)S(1)}) custom-call(s32[1]{0:T(128)} %bitcast.face_ref, s32[2]{0:T(128)S(1)} %get-tuple-element.60.iface, s32[4,8]{1,0:T(4,128)S(1)} %get-tuple-element.56.cols, ...), custom_call_target="tpu_custom_call" | custom-call | tf_op jit(solution)/shard_map/interface/pallas_call | solution.py:387
  32.4 1.1 %collective-permute-done.14.rest_9_ = bf16[1,2,128,128]{3,2,1,0:T(8,128)(2,1)S(1)} collective-permute-done((bf16[1,2,128,128]{3,2,1,0:T(8,128)(2,1)S(1)}, bf16[1,2,128,128]{3,2,1,0:T(8,128)(2,1)S(1)}, u32[]{:S(2)}, u32[]{:S(2)}) %collective-permute-start.14) | collective-permute-done | bytes 65568 | tf_op jit(solution)/shard_map/ppermute | solution.py:418
  33.8 3.2 %collective-permute-start.16 = (bf16[4,128,128]{2,1,0:T(8,128)(2,1)S(1)}, bf16[4,128,128]{2,1,0:T(8,128)(2,1)S(1)}, u32[]{:S(2)}, u32[]{:S(2)}) collective-permute-start(bf16[4,128,128]{2,1,0:T(8,128)(2,1)S(1)} %chain.2.after), channel_id=1, source_target_pairs={{0,4},{3,5},{2,6},{1,7},{4,8},{7,9},{6,10},{5,11},{8,12},{11,13},{... | collective-permute-start | bytes 393224 | tf_op jit(solution)/shard_map/ppermute | solution.py:430
  37.0 1.3 %rest.3 = (bf16[4,256,128]{2,1,0:T(8,128)(2,1)S(1)}, bf16[1,2,128,128]{3,2,1,0:T(8,128)(2,1)S(1)}) custom-call(s32[1]{0:T(128)} %bitcast.face_ref, s32[2]{0:T(128)S(1)} %get-tuple-element.60.iface, s32[4,8]{1,0:T(4,128)S(1)} %get-tuple-element.56.cols, bf16[4,256,128]{2,1,0:T(8,128)(2,1)S(1)} %get-tuple-element.78.edges.rest_5_, ...), custom_call_target="tpu_custom_call" | custom-call | tf_op jit(solution)/shard_map/rest/pallas_call | solution.py:387
  38.3 1.4 %collective-permute-start.17 = (bf16[1,2,128,128]{3,2,1,0:T(8,128)(2,1)S(1)}, bf16[1,2,128,128]{3,2,1,0:T(8,128)(2,1)S(1)}, u32[]{:S(2)}, u32[]{:S(2)}) collective-permute-start(bf16[1,2,128,128]{3,2,1,0:T(8,128)(2,1)S(1)} %get-tuple-element.99.rest_8_), channel_id=1, source_target_pairs={{0,1},{1,0},{2,3},{3,2},{4,5},{5,4},{6,7},{7,6},{8,9},{9,8},{10,11... | collective-permute-start | bytes 196616 | tf_op jit(solution)/shard_map/ppermute | solution.py:418
  39.8 3.8 %coupling_last.1.coupled = bf16[1024,1024]{1,0:T(8,128)(2,1)S(1)} custom-call(s32[1]{0:T(128)} %bitcast.face_ref, s32[2]{0:T(128)S(1)} %get-tuple-element.60.iface, s32[4,8]{1,0:T(4,128)S(1)} %get-tuple-element.56.cols, bf16[2,128,128]{2,1,0:T(8,128)(2,1)S(1)} %get-tuple-element.70.gfield, bf16[8,1024,128]{2,1,0:T(8,128)(2,1)S(1)} %get-tuple-element.76.after.gfirst, ...), custom_call_target="tpu_custom_call" | custom-call | flops 1342177280 | tf_op jit(solution)/shard_map/coupling_last/pallas_call | solution.py:387
  43.7 1.3 %collective-permute-done.18.rest_11_.rest_3_ = bf16[4,128,128]{2,1,0:T(8,128)(2,1)S(1)} collective-permute-done((bf16[4,128,128]{2,1,0:T(8,128)(2,1)S(1)}, bf16[4,128,128]{2,1,0:T(8,128)(2,1)S(1)}, u32[]{:S(2)}, u32[]{:S(2)}) %collective-permute-start.18) | collective-permute-done | bytes 131104 | tf_op jit(solution)/shard_map/ppermute | solution.py:418
  45.4 3.0 %collective-permute-start.19 = (bf16[4,128,128]{2,1,0:T(8,128)(2,1)S(1)}, bf16[4,128,128]{2,1,0:T(8,128)(2,1)S(1)}, u32[]{:S(2)}, u32[]{:S(2)}) collective-permute-start(bf16[4,128,128]{2,1,0:T(8,128)(2,1)S(1)} %chain.3.rest_11_), channel_id=1, source_target_pairs={{0,4},{3,5},{2,6},{1,7},{4,8},{7,9},{6,10},{5,11},{8,12},{11,13},{... | collective-permute-start | bytes 393224 | tf_op jit(solution)/shard_map/ppermute | solution.py:430
  48.4 2.2 %third.1 = (bf16[8,256,128]{2,1,0:T(8,128)(2,1)S(1)}, bf16[8,256,128]{2,1,0:T(8,128)(2,1)S(1)}) custom-call(s32[1]{0:T(128)} %bitcast.face_ref, s32[4,8]{1,0:T(4,128)S(1)} %get-tuple-element.56.cols, bf16[4,256,128]{2,1,0:T(8,128)(2,1)S(1)} %get-tuple-element.65.edges.rest_0_, bf16[4,256,128]{2,1,0:T(8,128)(2,1)S(1)} %get-tuple-element.77.after.rest_1_, ...), custom_call_target="tpu_custom_call" | custom-call | tf_op jit(solution)/shard_map/third/pallas_call | solution.py:387
  50.6 1.5 %output.1.earlier = bf16[4,128,1024]{2,1,0:T(8,128)(2,1)} custom-call(s32[1]{0:T(128)} %bitcast.face_ref, bf16[8,256,128]{2,1,0:T(8,128)(2,1)S(1)} %get-tuple-element.102.early, bf16[8,256,128]{2,1,0:T(8,128)(2,1)S(1)} %get-tuple-element.103.later, bf16[1024,1024]{1,0:T(8,128)(2,1)S(1)} %coupling_last.1.coupled, ...), custom_call_target="tpu_custom_call" | custom-call | tf_op jit(solution)/shard_map/output/pallas_call | solution.py:387
  52.1 2.0 %collective-permute-done.19.rest_0_ = bf16[4,128,128]{2,1,0:T(8,128)(2,1)S(1)} collective-permute-done((bf16[4,128,128]{2,1,0:T(8,128)(2,1)S(1)}, bf16[4,128,128]{2,1,0:T(8,128)(2,1)S(1)}, u32[]{:S(2)}, u32[]{:S(2)}) %collective-permute-start.19) | collective-permute-done | bytes 131104 | tf_op jit(solution)/shard_map/ppermute | solution.py:430
  55.9 1.0 %last_other.1 = bf16[4,128,1024]{2,1,0:T(8,128)(2,1)} custom-call(s32[1]{0:T(128)} %bitcast.face_ref, f32[128,1024]{1,0:T(8,128)S(1)} %last_own.1.own_part, bf16[1024,1024]{1,0:T(8,128)(2,1)S(1)} %coupling_last.1.coupled, bf16[4,128,1024]{2,1,0:T(8,128)(2,1)} %output.1.earlier, ...), custom_call_target="tpu_custom_call", output_to_operand_aliasing={{}: (3, {})} | custom-call | tf_op jit(solution)/shard_map/last_other/pallas_call | solution.py:387
  (34 shorter events, 6.7 us)
Async XLA Ops:
  2.6 8.2 %collective-permute-start = (bf16[2,256,128]{2,1,0:T(8,128)(2,1)S(1)}, bf16[2,256,128]{2,1,0:T(8,128)(2,1)S(1)}, u32[]{:S(2)}, u32[]{:S(2)}) collective-permute-start(bf16[2,256,128]{2,1,0:T(8,128)(2,1)S(1)} %get-tuple-element.58), channel_id=1, source_target_pairs={{0,1},{1,0},{2,3},{3,2},{4,5},{5,4},{6,7},{7,6},{8,9},{9,8},{10,11... | collective-permute-start | bytes 393224 | tf_op jit(solution)/shard_map/ppermute | solution.py:415
  3.4 7.5 %collective-permute-start.1 = (bf16[2,256,128]{2,1,0:T(8,128)(2,1)S(1)}, bf16[2,256,128]{2,1,0:T(8,128)(2,1)S(1)}, u32[]{:S(2)}, u32[]{:S(2)}) collective-permute-start(bf16[2,256,128]{2,1,0:T(8,128)(2,1)S(1)} %get-tuple-element.59), channel_id=1, source_target_pairs={{1,2},{2,1},{5,6},{6,5},{9,10},{10,9},{13,14},{14,13},{17,18},{18,... | collective-permute-start | bytes 393224 | tf_op jit(solution)/shard_map/ppermute | solution.py:414
  6.4 8.7 %collective-permute-start.4 = (bf16[2,416,128]{2,1,0:T(8,128)(2,1)S(1)}, bf16[2,416,128]{2,1,0:T(8,128)(2,1)S(1)}, u32[]{:S(2)}, u32[]{:S(2)}) collective-permute-start(bf16[2,416,128]{2,1,0:T(8,128)(2,1)S(1)} %get-tuple-element.71), channel_id=1, source_target_pairs={{0,1},{1,0},{2,3},{3,2},{4,5},{5,4},{6,7},{7,6},{8,9},{9,8},{10,11... | collective-permute-start | bytes 638984 | tf_op jit(solution)/shard_map/ppermute | solution.py:415
  6.5 8.7 %collective-permute-start.5 = (bf16[2,416,128]{2,1,0:T(8,128)(2,1)S(1)}, bf16[2,416,128]{2,1,0:T(8,128)(2,1)S(1)}, u32[]{:S(2)}, u32[]{:S(2)}) collective-permute-start(bf16[2,416,128]{2,1,0:T(8,128)(2,1)S(1)} %get-tuple-element.72), channel_id=1, source_target_pairs={{1,2},{2,1},{5,6},{6,5},{9,10},{10,9},{13,14},{14,13},{17,18},{18,... | collective-permute-start | bytes 638984 | tf_op jit(solution)/shard_map/ppermute | solution.py:414
  12.0 3.1 %collective-permute-start.2 = (bf16[2,256,128]{2,1,0:T(8,128)(2,1)S(1)}, bf16[2,256,128]{2,1,0:T(8,128)(2,1)S(1)}, u32[]{:S(2)}, u32[]{:S(2)}) collective-permute-start(bf16[2,256,128]{2,1,0:T(8,128)(2,1)S(1)} %get-tuple-element.67), channel_id=1, source_target_pairs={{0,1},{1,0},{2,3},{3,2},{4,5},{5,4},{6,7},{7,6},{8,9},{9,8},{10,11... | collective-permute-start | bytes 393224 | tf_op jit(solution)/shard_map/ppermute | solution.py:415
  12.1 7.4 %collective-permute-start.3 = (bf16[2,256,128]{2,1,0:T(8,128)(2,1)S(1)}, bf16[2,256,128]{2,1,0:T(8,128)(2,1)S(1)}, u32[]{:S(2)}, u32[]{:S(2)}) collective-permute-start(bf16[2,256,128]{2,1,0:T(8,128)(2,1)S(1)} %get-tuple-element.68), channel_id=1, source_target_pairs={{1,2},{2,1},{5,6},{6,5},{9,10},{10,9},{13,14},{14,13},{17,18},{18,... | collective-permute-start | bytes 393224 | tf_op jit(solution)/shard_map/ppermute | solution.py:414
  16.8 10.2 %collective-permute-start.8 = (bf16[2,1024,128]{2,1,0:T(8,128)(2,1)S(1)}, bf16[2,1024,128]{2,1,0:T(8,128)(2,1)S(1)}, u32[]{:S(2)}, u32[]{:S(2)}) collective-permute-start(bf16[2,1024,128]{2,1,0:T(8,128)(2,1)S(1)} %get-tuple-element.79), channel_id=1, source_target_pairs={{0,1},{1,0},{2,3},{3,2},{4,5},{5,4},{6,7},{7,6},{8,9},{9,8},{10,11... | collective-permute-start | bytes 1572872 | tf_op jit(solution)/shard_map/ppermute | solution.py:415
  16.9 10.6 %collective-permute-start.9 = (bf16[2,1024,128]{2,1,0:T(8,128)(2,1)S(1)}, bf16[2,1024,128]{2,1,0:T(8,128)(2,1)S(1)}, u32[]{:S(2)}, u32[]{:S(2)}) collective-permute-start(bf16[2,1024,128]{2,1,0:T(8,128)(2,1)S(1)} %get-tuple-element.80), channel_id=1, source_target_pairs={{1,2},{2,1},{5,6},{6,5},{9,10},{10,9},{13,14},{14,13},{17,18},{18,... | collective-permute-start | bytes 1572872 | tf_op jit(solution)/shard_map/ppermute | solution.py:414
  20.6 1.3 %collective-permute-start.6 = (bf16[2,128,128]{2,1,0:T(8,128)(2,1)S(1)}, bf16[2,128,128]{2,1,0:T(8,128)(2,1)S(1)}, u32[]{:S(2)}, u32[]{:S(2)}) collective-permute-start(bf16[2,128,128]{2,1,0:T(8,128)(2,1)S(1)} %third_rows.1.own), channel_id=1, source_target_pairs={{0,1},{1,0},{2,3},{3,2},{4,5},{5,4},{6,7},{7,6},{8,9},{9,8},{10,11... | collective-permute-start | bytes 196616 | tf_op jit(solution)/shard_map/ppermute | solution.py:418
  22.0 8.9 %collective-permute-start.7 = (bf16[4,128,128]{2,1,0:T(8,128)(2,1)S(1)}, bf16[4,128,128]{2,1,0:T(8,128)(2,1)S(1)}, u32[]{:S(2)}, u32[]{:S(2)}) collective-permute-start(bf16[4,128,128]{2,1,0:T(8,128)(2,1)S(1)} %merge.1.after), channel_id=1, source_target_pairs={{0,4},{3,5},{2,6},{1,7},{4,8},{7,9},{6,10},{5,11},{8,12},{11,13},{... | collective-permute-start | bytes 393224 | tf_op jit(solution)/shard_map/ppermute | solution.py:430
  29.8 1.4 %collective-permute-start.10 = (bf16[256,256]{1,0:T(8,128)(2,1)S(1)}, bf16[256,256]{1,0:T(8,128)(2,1)S(1)}, u32[]{:S(2)}, u32[]{:S(2)}) collective-permute-start(bf16[256,256]{1,0:T(8,128)(2,1)S(1)} %get-tuple-element.85.rest_0_.after), channel_id=1, source_target_pairs={{0,1},{1,0},{2,3},{3,2},{4,5},{5,4},{6,7},{7,6},{8,9},{9,8},{10,11... | collective-permute-start | bytes 393224 | tf_op jit(solution)/shard_map/ppermute | solution.py:418
  29.8 1.5 %collective-permute-start.11 = (bf16[256,256]{1,0:T(8,128)(2,1)S(1)}, bf16[256,256]{1,0:T(8,128)(2,1)S(1)}, u32[]{:S(2)}, u32[]{:S(2)}) collective-permute-start(bf16[256,256]{1,0:T(8,128)(2,1)S(1)} %get-tuple-element.86.rest_1_), channel_id=1, source_target_pairs={{0,1},{1,0},{2,3},{3,2},{4,5},{5,4},{6,7},{7,6},{8,9},{9,8},{10,11... | collective-permute-start | bytes 393224 | tf_op jit(solution)/shard_map/ppermute | solution.py:418
  30.3 1.3 %collective-permute-start.12 = (bf16[256,256]{1,0:T(8,128)(2,1)S(1)}, bf16[256,256]{1,0:T(8,128)(2,1)S(1)}, u32[]{:S(2)}, u32[]{:S(2)}) collective-permute-start(bf16[256,256]{1,0:T(8,128)(2,1)S(1)} %get-tuple-element.87.rest_2_), channel_id=1, source_target_pairs={{0,1},{1,0},{2,3},{3,2},{4,5},{5,4},{6,7},{7,6},{8,9},{9,8},{10,11... | collective-permute-start | bytes 393224 | tf_op jit(solution)/shard_map/ppermute | solution.py:418
  30.4 1.5 %collective-permute-start.13 = (bf16[256,256]{1,0:T(8,128)(2,1)S(1)}, bf16[256,256]{1,0:T(8,128)(2,1)S(1)}, u32[]{:S(2)}, u32[]{:S(2)}) collective-permute-start(bf16[256,256]{1,0:T(8,128)(2,1)S(1)} %get-tuple-element.88.rest_3_), channel_id=1, source_target_pairs={{0,1},{1,0},{2,3},{3,2},{4,5},{5,4},{6,7},{7,6},{8,9},{9,8},{10,11... | collective-permute-start | bytes 393224 | tf_op jit(solution)/shard_map/ppermute | solution.py:418
  31.9 1.6 %collective-permute-start.15 = (bf16[4,128,128]{2,1,0:T(8,128)(2,1)S(1)}, bf16[4,128,128]{2,1,0:T(8,128)(2,1)S(1)}, u32[]{:S(2)}, u32[]{:S(2)}) collective-permute-start(bf16[4,128,128]{2,1,0:T(8,128)(2,1)S(1)} %collective-permute-done.7.rest_10_.rest_0_), channel_id=1, source_target_pairs={{0,1},{1,0},{2,3},{3,2},{4,5},{5,4},{6,7},{7,6},{8,9},{9,8},{10,11... | collective-permute-start | bytes 393224 | tf_op jit(solution)/shard_map/ppermute | solution.py:418
  32.2 1.3 %collective-permute-start.14 = (bf16[1,2,128,128]{3,2,1,0:T(8,128)(2,1)S(1)}, bf16[1,2,128,128]{3,2,1,0:T(8,128)(2,1)S(1)}, u32[]{:S(2)}, u32[]{:S(2)}) collective-permute-start(bf16[1,2,128,128]{3,2,1,0:T(8,128)(2,1)S(1)} %get-tuple-element.93.rest_8_), channel_id=1, source_target_pairs={{0,1},{1,0},{2,3},{3,2},{4,5},{5,4},{6,7},{7,6},{8,9},{9,8},{10,11... | collective-permute-start | bytes 196616 | tf_op jit(solution)/shard_map/ppermute | solution.py:418
  33.8 9.8 %collective-permute-start.16 = (bf16[4,128,128]{2,1,0:T(8,128)(2,1)S(1)}, bf16[4,128,128]{2,1,0:T(8,128)(2,1)S(1)}, u32[]{:S(2)}, u32[]{:S(2)}) collective-permute-start(bf16[4,128,128]{2,1,0:T(8,128)(2,1)S(1)} %chain.2.after), channel_id=1, source_target_pairs={{0,4},{3,5},{2,6},{1,7},{4,8},{7,9},{6,10},{5,11},{8,12},{11,13},{... | collective-permute-start | bytes 393224 | tf_op jit(solution)/shard_map/ppermute | solution.py:430
  38.3 5.2 %collective-permute-start.17 = (bf16[1,2,128,128]{3,2,1,0:T(8,128)(2,1)S(1)}, bf16[1,2,128,128]{3,2,1,0:T(8,128)(2,1)S(1)}, u32[]{:S(2)}, u32[]{:S(2)}) collective-permute-start(bf16[1,2,128,128]{3,2,1,0:T(8,128)(2,1)S(1)} %get-tuple-element.99.rest_8_), channel_id=1, source_target_pairs={{0,1},{1,0},{2,3},{3,2},{4,5},{5,4},{6,7},{7,6},{8,9},{9,8},{10,11... | collective-permute-start | bytes 196616 | tf_op jit(solution)/shard_map/ppermute | solution.py:418
  43.6 1.4 %collective-permute-start.18 = (bf16[4,128,128]{2,1,0:T(8,128)(2,1)S(1)}, bf16[4,128,128]{2,1,0:T(8,128)(2,1)S(1)}, u32[]{:S(2)}, u32[]{:S(2)}) collective-permute-start(bf16[4,128,128]{2,1,0:T(8,128)(2,1)S(1)} %collective-permute-done.16.rest_10_.rest_2_), channel_id=1, source_target_pairs={{0,1},{1,0},{2,3},{3,2},{4,5},{5,4},{6,7},{7,6},{8,9},{9,8},{10,11... | collective-permute-start | bytes 393224 | tf_op jit(solution)/shard_map/ppermute | solution.py:418
  45.4 8.7 %collective-permute-start.19 = (bf16[4,128,128]{2,1,0:T(8,128)(2,1)S(1)}, bf16[4,128,128]{2,1,0:T(8,128)(2,1)S(1)}, u32[]{:S(2)}, u32[]{:S(2)}) collective-permute-start(bf16[4,128,128]{2,1,0:T(8,128)(2,1)S(1)} %chain.3.rest_11_), channel_id=1, source_target_pairs={{0,4},{3,5},{2,6},{1,7},{4,8},{7,9},{6,10},{5,11},{8,12},{11,13},{... | collective-permute-start | bytes 393224 | tf_op jit(solution)/shard_map/ppermute | solution.py:430
  54.1 1.7 %collective-permute-start.20 = (bf16[4,128,128]{2,1,0:T(8,128)(2,1)S(1)}, bf16[4,128,128]{2,1,0:T(8,128)(2,1)S(1)}, u32[]{:S(2)}, u32[]{:S(2)}) collective-permute-start(bf16[4,128,128]{2,1,0:T(8,128)(2,1)S(1)} %collective-permute-done.19.rest_0_), channel_id=1, source_target_pairs={{0,1},{1,0},{2,3},{3,2},{4,5},{5,4},{6,7},{7,6},{8,9},{9,8},{10,11... | collective-permute-start | bytes 393224 | tf_op jit(solution)/shard_map/ppermute | solution.py:418

commit v15 on v13

--- a/solution.py
+++ b/solution.py
@@ -37,6 +37,7 @@
         self.mark = 16
         self.share = -(-nq // HALO) * width
         self.first_rows = self.later + self.share + nq * self.mark
+        self.ahead = max(count * 3 // 4 // 2 * 2, 2)
         self.last = count - HALO
         self.up = count + HALO
 
@@ -109,24 +110,18 @@
         for k in range(1 + d.neigh):
             part = product[:, k * w : (k + 1) * w].T
             folded[r, k * w : (k + 1) * w, :] = ((unit if k == 0 else 0.0) - part).astype(BF)
-    met[...] = jnp.zeros_like(met)
+    spare = 2 * HALO + d.nq
+    met[0 : 2 * HALO] = jnp.zeros((2 * HALO, w, d.count * w), BF)
     for r in range(d.count):
         lanes = slice(r * w, (r + 1) * w)
         for q in range(d.nq):
             met[2 * HALO + q, :, lanes] = jnp.where(iface[q] == r, folded[r, 0:w, :], jnp.zeros((w, w), BF))
         for k in range(d.neigh):
             c = cols[k, r] - d.first_col(face_ref[0])
-            inside = jnp.logical_and(c >= HALO, c < d.up)
-            at = jnp.where(c < HALO, c, c - d.count)
-            hit = jnp.logical_not(inside)
+            at = jnp.where(c < HALO, c, jnp.where(c >= d.up, c - d.count, spare))
             for q in range(d.nq):
-                here = c == iface[q] + HALO
-                at = jnp.where(here, 2 * HALO + q, at)
-                hit = jnp.logical_or(hit, here)
-
-            @pl.when(hit)
-            def _():
-                met[at, :, lanes] += folded[r, (1 + k) * w : (2 + k) * w, :]
+                at = jnp.where(c == iface[q] + HALO, 2 * HALO + q, at)
+            met[at, :, lanes] += folded[r, (1 + k) * w : (2 + k) * w, :]
 
 
 def sweep(d, cols, face, ext, span, r, folded):
@@ -166,10 +161,6 @@
     correct_edges(d, cols, face, field, pair_in, cross_in, folded, edges, ext)
     pair[...] = edges[pl.ds(HALO * (1 - parity), HALO)]
     cross[...] = edges[pl.ds(HALO * parity, HALO)]
-
-
-def second_inner_kernel(d, face_ref, cols, field, ext, folded, after, out):
-    correct(d, cols, face_ref[0], field, folded, out, ext, range(HALO, d.last))
 
 
 def interface_rows(d, face, iface, cols, edges, inner, field, pair_in, cross_in, folded, first, outs, ext):
@@ -183,8 +174,10 @@
             out[q] = value[t * d.sources : (t + 1) * d.sources]
 
 
-def third_rows_kernel(d, face_ref, iface, cols, edges, inner, field, pair_in, cross_in, folded, sent, ext):
-    interface_rows(d, face_ref[0], iface, cols, edges, inner, field, pair_in, cross_in, folded, 0, [sent], ext)
+def third_rows_kernel(d, face_ref, iface, cols, edges, field, ext0, pair_in, cross_in, folded, after, sent, inner, ext):
+    face = face_ref[0]
+    correct(d, cols, face, field, folded, inner, ext0, range(HALO, d.last))
+    interface_rows(d, face, iface, cols, edges, inner, field, pair_in, cross_in, folded, 0, [sent], ext)
 
 
 def third_kernel(d, face_ref, cols, *rest):
@@ -294,11 +287,11 @@
 
 def operator_kernel(d, face_ref, iface, cols, gfield, gfirst, pair_in, cross_in, folded, after, out, ext):
     coupling_ext(d, face_ref[0], gfirst, pair_in, cross_in, ext)
-    operator_rows(d, face_ref[0], iface, cols, gfield, folded, ext, range(d.count // 2), out)
+    operator_rows(d, face_ref[0], iface, cols, gfield, folded, ext, range(d.ahead), out)
 
 
 def operator_rest_kernel(d, face_ref, iface, cols, gfield, folded, ext, after, out):
-    operator_rows(d, face_ref[0], iface, cols, gfield, folded, ext, range(d.count // 2, d.count), out)
+    operator_rows(d, face_ref[0], iface, cols, gfield, folded, ext, range(d.ahead, d.count), out)
 
 
 def operator_part(d, halves, row, depth, lane, lanes):
@@ -484,7 +477,7 @@
         "fold",
         [face, iface, cols],
         [inv, diag, off],
-        [(count, d.depth, width), (2 * HALO + nq, width, count * width)],
+        [(count, d.depth, width), (2 * HALO + nq + 1, width, count * width)],
     )
     edges, pair, cross, ext0 = call(
         functools.partial(second_edges_kernel, d),
@@ -503,23 +496,16 @@
         anywhere=(6,),
     )
     pair_later1, cross_later1 = exchange(pair, cross)
-    (inner_first,) = call(
-        functools.partial(second_inner_kernel, d),
-        "second_inner",
-        [face, cols],
-        [field, ext0, folded, gfirst],
-        [(count - 2 * HALO, sources, width)],
-        anywhere=(3,),
-    )
-    cross1, inner_first = lax.optimization_barrier((cross1, inner_first))
+    cross1, gfirst = lax.optimization_barrier((cross1, gfirst))
     (own_first,) = call(
         functools.partial(third_rows_kernel, d),
         "third_rows",
         [face, iface, cols],
-        [edges, inner_first, field, pair1, cross1, folded],
+        [edges, field, ext0, pair1, cross1, folded, gfirst],
         [(nq, sources, width)],
-        [(ext, sources, width)],
+        [(count - 2 * HALO, sources, width), (ext, sources, width)],
         flops=12 * early * sweep_flops,
+        anywhere=(6,),
     )
     (sent,) = call(
         functools.partial(merge_kernel, d),
@@ -559,8 +545,9 @@
     other_early = swap(faces_early)
 
     def beside_second(sent):
-        made = rest(0, ticks - 1 - split, later, edges_later, field_later, ext_later0, pair_later1, cross_later1, sent)
-        return *operator(), *made, swap(made[1])
+        first_half, read = operator(sent)
+        made = rest(0, ticks - 1 - split, later, edges_later, field_later, ext_later0, pair_later1, cross_later1, first_half)
+        return first_half, read, *made, swap(made[1])
 
     def fields(after):
         return call(
@@ -575,13 +562,13 @@
 
     whole = (ticks, sources, count * width)
 
-    def operator():
+    def operator(after):
         return call(
             functools.partial(operator_kernel, d),
             "operator",
             [face, iface, cols],
-            [gfield, gfirst, pair_later1, cross_later1, folded, chain[0]],
-            [(wide, count // 2 * width), (ext, wide, width)],
+            [gfield, gfirst, pair_later1, cross_later1, folded, after],
+            [(wide, d.ahead * width), (ext, wide, width)],
             flops=wide * sweep_flops // 2,
             anywhere=(5,),
         )
@@ -592,7 +579,7 @@
             "operator_rest",
             [face, iface, cols],
             [gfield, folded, read, after],
-            [(wide, (count - count // 2) * width)],
+            [(wide, (count - d.ahead) * width)],
             anywhere=(3,),
         )[0]
 

time: 57.6 us -> 57.7 us (level)
  starting transfers between devices: 25.3 us -> 26.5 us
  Pallas kernels: 24.5 us -> 23.6 us
    ppermute x3, waiting for transfers between devices: 1.72 us -> 0.36 us  [onward(): own.append(lax.ppermute(block, ('slab', 'face'), route))]
    ppermute x10, waiting for transfers between devices: 4.75 us -> 5.89 us  [swap(): return lax.ppermute(block, 'face', pairing)]
    ppermute x10, starting transfers between devices: 3.18 us -> 4.28 us  [swap(): return lax.ppermute(block, 'face', pairing)]
    pallas_call x18 -> x17, Pallas kernels: 24.5 us -> 23.6 us  [call(): pl.pallas_call(body, name=name, out_shape=outs, in_specs=[pl.BlockSpec(me...]
  transfers between devices with their start and end apart: 21 -> 21, of which waited for: 11 -> 11; matrix products, arithmetic and copies ran while one was open for 0% -> 0% of each run, Pallas kernels for 35% -> 34%
where the time goes in v15:
time: 57.7 us; the launch traced here: 57.3 us
  starting transfers between devices  26.5 us (46%)
  Pallas kernels  23.6 us (41%)
  waiting for transfers between devices  6.74 us (12%)
    pallas_call x17, Pallas kernels, call(): pl.pallas_call(body, name=name, out_shape=outs, in_specs=[pl.BlockSpec(me...  23.6 us
    ppermute x4, starting transfers between devices, exchange(): got = lax.ppermute(cross, 'face', crossing)  11.1 us
    ppermute x3, starting transfers between devices, onward(): own.append(lax.ppermute(block, ('slab', 'face'), route))  10.1 us
    ppermute x10, waiting for transfers between devices, swap(): return lax.ppermute(block, 'face', pairing)  5.89 us
    ppermute x10, starting transfers between devices, swap(): return lax.ppermute(block, 'face', pairing)  4.28 us
  transfers between devices with their start and end apart: 21, of which 11 were waited for; matrix products, arithmetic and copies ran while one was open for 0% of the time, Pallas kernels for 34%

profile of v15, /device:TPU:9, one launch (start us, length us, event | category | flops | bytes accessed | tf_op | source)
XLA Modules:
  0.0 57.3 jit_solution(18041340940494219563)
XLA Ops:
  0.0 2.6 %first.1 = (bf16[8,256,128]{2,1,0:T(8,128)(2,1)S(1)}, bf16[8,256,128]{2,1,0:T(8,128)(2,1)S(1)}, bf16[2,128,128]{2,1,0:T(8,128)(2,1)S(1)}, bf16[2,256,128]{2,1,0:...) custom-call(s32[1]{0:T(128)} %bitcast.face_ref, ...), custom_call_target="tpu_custom_call" | custom-call | tf_op jit(solution)/shard_map/first/pallas_call | solution.py:406
  3.4 3.0 %collective-permute-start.1 = (bf16[2,256,128]{2,1,0:T(8,128)(2,1)S(1)}, bf16[2,256,128]{2,1,0:T(8,128)(2,1)S(1)}, u32[]{:S(2)}, u32[]{:S(2)}) collective-permute-start(bf16[2,256,128]{2,1,0:T(8,128)(2,1)S(1)} %get-tuple-element.62), channel_id=1, source_target_pairs={{1,2},{2,1},{5,6},{6,5},{9,10},{10,9},{13,14},{14,13},{17,18},{18,... | collective-permute-start | bytes 393224 | tf_op jit(solution)/shard_map/ppermute | solution.py:433
  6.5 2.5 %collective-permute-start.5 = (bf16[2,416,128]{2,1,0:T(8,128)(2,1)S(1)}, bf16[2,416,128]{2,1,0:T(8,128)(2,1)S(1)}, u32[]{:S(2)}, u32[]{:S(2)}) collective-permute-start(bf16[2,416,128]{2,1,0:T(8,128)(2,1)S(1)} %get-tuple-element.75), channel_id=1, source_target_pairs={{1,2},{2,1},{5,6},{6,5},{9,10},{10,9},{13,14},{14,13},{17,18},{18,... | collective-permute-start | bytes 638984 | tf_op jit(solution)/shard_map/ppermute | solution.py:433
  9.0 1.8 %fold.1 = (bf16[8,640,128]{2,1,0:T(8,128)(2,1)S(1)}, bf16[7,128,1024]{2,1,0:T(8,128)(2,1)S(1)}) custom-call(s32[1]{0:T(128)} %bitcast.face_ref, s32[2]{0:T(128)S(1)} %get-tuple-element.63.iface, s32[4,8]{1,0:T(4,128)S(1)} %get-tuple-element.59.cols, bf16[8,128,128]{2,1,0:T(8,128)(2,1)S(1)} %get-tuple-element.64.inv, ...), custom_call_target="tpu_custom_call" | custom-call | tf_op jit(solution)/shard_map/fold/pallas_call | solution.py:406
  10.9 1.1 %second_edges.1 = (bf16[4,256,128]{2,1,0:T(8,128)(2,1)S(1)}, bf16[2,256,128]{2,1,0:T(8,128)(2,1)S(1)}, bf16[2,256,128]{2,1,0:T(8,128)(2,1)S(1)}, bf16[12,256,128]{2,1,0:T(8,128)(2,1)S(1)}) custom-call(s32[1]{0:T(128)} %bitcast.face_ref, s32[4,8]{1,0:T(4,128)S(1)} %get-tuple-element.59.cols, bf16[8,256,128]{2,1,0:T(8,128)(2,1)S(1)} %get-tuple-element.60.field.rest_2_, ...), custom_call_target="tpu_custom_call" | custom-call | tf_op jit(solution)/shard_map/second_edges/pallas_call | solution.py:406
  12.1 3.0 %collective-permute-start.3 = (bf16[2,256,128]{2,1,0:T(8,128)(2,1)S(1)}, bf16[2,256,128]{2,1,0:T(8,128)(2,1)S(1)}, u32[]{:S(2)}, u32[]{:S(2)}) collective-permute-start(bf16[2,256,128]{2,1,0:T(8,128)(2,1)S(1)} %get-tuple-element.71), channel_id=1, source_target_pairs={{1,2},{2,1},{5,6},{6,5},{9,10},{10,9},{13,14},{14,13},{17,18},{18,... | collective-permute-start | bytes 393224 | tf_op jit(solution)/shard_map/ppermute | solution.py:433
  15.1 1.7 %behind.1 = (bf16[4,256,128]{2,1,0:T(8,128)(2,1)S(1)}, bf16[8,1024,128]{2,1,0:T(8,128)(2,1)S(1)}, bf16[2,1024,128]{2,1,0:T(8,128)(2,1)S(1)}, bf16[2,1024,128]{2,1,0:T(8,128)(2,1)S(1)}, bf16[12,256,128]{2,1,0:T(8,128)(2,1)S(1)}) custom-call(s32[1]{0:T(128)} %bitcast.face_ref, s32[2]{0:T(128)S(1)} %get-tuple-element.63.iface, ...), custom_call_target="tpu_custom_call" | custom-call | tf_op jit(solution)/shard_map/behind/pallas_call | solution.py:406
  16.9 2.5 %collective-permute-start.9 = (bf16[2,1024,128]{2,1,0:T(8,128)(2,1)S(1)}, bf16[2,1024,128]{2,1,0:T(8,128)(2,1)S(1)}, u32[]{:S(2)}, u32[]{:S(2)}) collective-permute-start(bf16[2,1024,128]{2,1,0:T(8,128)(2,1)S(1)} %get-tuple-element.83), channel_id=1, source_target_pairs={{1,2},{2,1},{5,6},{6,5},{9,10},{10,9},{13,14},{14,13},{17,18},{18,... | collective-permute-start | bytes 1572872 | tf_op jit(solution)/shard_map/ppermute | solution.py:433
  19.5 1.2 %third_rows.1.own = bf16[2,128,128]{2,1,0:T(8,128)(2,1)S(1)} custom-call(s32[1]{0:T(128)} %bitcast.face_ref, s32[2]{0:T(128)S(1)} %get-tuple-element.63.iface, s32[4,8]{1,0:T(4,128)S(1)} %get-tuple-element.59.cols, bf16[4,256,128]{2,1,0:T(8,128)(2,1)S(1)} %get-tuple-element.68.edges.rest_0_, bf16[8,256,128]{2,1,0:T(8,128)(2,1)S(1)} %get-tuple-element.60.field.rest_2_, ...), custom_call_target="tpu_custom_call" | custom-call | flops 4026531840 | tf_op jit(solution)/shard_map/third_rows/pallas_call | solution.py:406
  20.7 1.2 %collective-permute-done.6.other = bf16[2,128,128]{2,1,0:T(8,128)(2,1)S(1)} collective-permute-done((bf16[2,128,128]{2,1,0:T(8,128)(2,1)S(1)}, bf16[2,128,128]{2,1,0:T(8,128)(2,1)S(1)}, u32[]{:S(2)}, u32[]{:S(2)}) %collective-permute-start.6) | collective-permute-done | bytes 65568 | tf_op jit(solution)/shard_map/ppermute | solution.py:437
  22.0 3.7 %collective-permute-start.7 = (bf16[4,128,128]{2,1,0:T(8,128)(2,1)S(1)}, bf16[4,128,128]{2,1,0:T(8,128)(2,1)S(1)}, u32[]{:S(2)}, u32[]{:S(2)}) collective-permute-start(bf16[4,128,128]{2,1,0:T(8,128)(2,1)S(1)} %merge.1.after), channel_id=1, source_target_pairs={{0,4},{3,5},{2,6},{1,7},{4,8},{7,9},{6,10},{5,11},{8,12},{11,13},{... | collective-permute-start | bytes 393224 | tf_op jit(solution)/shard_map/ppermute | solution.py:449
  25.7 1.3 %rest.2 = (bf16[4,256,128]{2,1,0:T(8,128)(2,1)S(1)}, bf16[1,2,128,128]{3,2,1,0:T(8,128)(2,1)S(1)}) custom-call(s32[1]{0:T(128)} %bitcast.face_ref, s32[2]{0:T(128)S(1)} %get-tuple-element.63.iface, s32[4,8]{1,0:T(4,128)S(1)} %get-tuple-element.59.cols, bf16[4,256,128]{2,1,0:T(8,128)(2,1)S(1)} %get-tuple-element.68.edges.rest_0_, ...), custom_call_target="tpu_custom_call" | custom-call | tf_op jit(solution)/shard_map/rest/pallas_call | solution.py:406
  27.5 2.2 %interface.1 = (bf16[256,256]{1,0:T(8,128)(2,1)S(1)}, bf16[256,256]{1,0:T(8,128)(2,1)S(1)}, bf16[256,256]{1,0:T(8,128)(2,1)S(1)}, bf16[256,256]{1,0:T(8,128)(2,1)S(1)}) custom-call(s32[1]{0:T(128)} %bitcast.face_ref, s32[2]{0:T(128)S(1)} %get-tuple-element.63.iface, s32[4,8]{1,0:T(4,128)S(1)} %get-tuple-element.59.cols, ...), custom_call_target="tpu_custom_call" | custom-call | tf_op jit(solution)/shard_map/interface/pallas_call | solution.py:406
  32.4 1.1 %collective-permute-done.14.rest_9_ = bf16[1,2,128,128]{3,2,1,0:T(8,128)(2,1)S(1)} collective-permute-done((bf16[1,2,128,128]{3,2,1,0:T(8,128)(2,1)S(1)}, bf16[1,2,128,128]{3,2,1,0:T(8,128)(2,1)S(1)}, u32[]{:S(2)}, u32[]{:S(2)}) %collective-permute-start.14) | collective-permute-done | bytes 65568 | tf_op jit(solution)/shard_map/ppermute | solution.py:437
  33.8 3.2 %collective-permute-start.16 = (bf16[4,128,128]{2,1,0:T(8,128)(2,1)S(1)}, bf16[4,128,128]{2,1,0:T(8,128)(2,1)S(1)}, u32[]{:S(2)}, u32[]{:S(2)}) collective-permute-start(bf16[4,128,128]{2,1,0:T(8,128)(2,1)S(1)} %chain.2.after), channel_id=1, source_target_pairs={{0,4},{3,5},{2,6},{1,7},{4,8},{7,9},{6,10},{5,11},{8,12},{11,13},{... | collective-permute-start | bytes 393224 | tf_op jit(solution)/shard_map/ppermute | solution.py:449
  37.0 3.1 %operator.1 = (bf16[1024,768]{1,0:T(8,128)(2,1)S(1)}, bf16[12,1024,128]{2,1,0:T(8,128)(2,1)S(1)}) custom-call(s32[1]{0:T(128)} %bitcast.face_ref, s32[2]{0:T(128)S(1)} %get-tuple-element.63.iface, s32[4,8]{1,0:T(4,128)S(1)} %get-tuple-element.59.cols, bf16[2,128,128]{2,1,0:T(8,128)(2,1)S(1)} %get-tuple-element.73.gfield, ...), custom_call_target="tpu_custom_call" | custom-call | flops 671088640 | tf_op jit(solution)/shard_map/operator/pallas_call | solution.py:406
  40.1 1.3 %rest.3 = (bf16[4,256,128]{2,1,0:T(8,128)(2,1)S(1)}, bf16[1,2,128,128]{3,2,1,0:T(8,128)(2,1)S(1)}) custom-call(s32[1]{0:T(128)} %bitcast.face_ref, s32[2]{0:T(128)S(1)} %get-tuple-element.63.iface, s32[4,8]{1,0:T(4,128)S(1)} %get-tuple-element.59.cols, bf16[4,256,128]{2,1,0:T(8,128)(2,1)S(1)} %get-tuple-element.81.edges.rest_5_, ...), custom_call_target="tpu_custom_call" | custom-call | tf_op jit(solution)/shard_map/rest/pallas_call | solution.py:406
  41.5 1.4 %collective-permute-start.17 = (bf16[1,2,128,128]{3,2,1,0:T(8,128)(2,1)S(1)}, bf16[1,2,128,128]{3,2,1,0:T(8,128)(2,1)S(1)}, u32[]{:S(2)}, u32[]{:S(2)}) collective-permute-start(bf16[1,2,128,128]{3,2,1,0:T(8,128)(2,1)S(1)} %get-tuple-element.104.rest_8_), channel_id=1, source_target_pairs={{0,1},{1,0},{2,3},{3,2},{4,5},{5,4},{6,7},{7,6},{8,9},{9,8},{10,11... | collective-permute-start | bytes 196616 | tf_op jit(solution)/shard_map/ppermute | solution.py:437
  44.1 1.0 %collective-permute-done.18.rest_11_.rest_3_ = bf16[4,128,128]{2,1,0:T(8,128)(2,1)S(1)} collective-permute-done((bf16[4,128,128]{2,1,0:T(8,128)(2,1)S(1)}, bf16[4,128,128]{2,1,0:T(8,128)(2,1)S(1)}, u32[]{:S(2)}, u32[]{:S(2)}) %collective-permute-start.18) | collective-permute-done | bytes 131104 | tf_op jit(solution)/shard_map/ppermute | solution.py:437
  45.5 3.2 %collective-permute-start.19 = (bf16[4,128,128]{2,1,0:T(8,128)(2,1)S(1)}, bf16[4,128,128]{2,1,0:T(8,128)(2,1)S(1)}, u32[]{:S(2)}, u32[]{:S(2)}) collective-permute-start(bf16[4,128,128]{2,1,0:T(8,128)(2,1)S(1)} %chain.3.rest_11_.after), channel_id=1, source_target_pairs={{0,4},{3,5},{2,6},{1,7},{4,8},{7,9},{6,10},{5,11},{8,12},{11,13},{... | collective-permute-start | bytes 393224 | tf_op jit(solution)/shard_map/ppermute | solution.py:449
  48.7 1.4 %operator_rest.1.second_half = bf16[1024,256]{1,0:T(8,128)(2,1)S(1)} custom-call(s32[1]{0:T(128)} %bitcast.face_ref, s32[2]{0:T(128)S(1)} %get-tuple-element.63.iface, s32[4,8]{1,0:T(4,128)S(1)} %get-tuple-element.59.cols, bf16[2,128,128]{2,1,0:T(8,128)(2,1)S(1)} %get-tuple-element.73.gfield, bf16[8,640,128]{2,1,0:T(8,128)(2,1)S(1)} %get-tuple-element.67.folded.rest_10_, ...), custom_call_target="tpu_custom_call" | custom-call | tf_op jit(solution)/shard_map/operator_rest/pallas_call | solution.py:406
  50.2 2.2 %third.1 = (bf16[8,256,128]{2,1,0:T(8,128)(2,1)S(1)}, bf16[8,256,128]{2,1,0:T(8,128)(2,1)S(1)}) custom-call(s32[1]{0:T(128)} %bitcast.face_ref, s32[4,8]{1,0:T(4,128)S(1)} %get-tuple-element.59.cols, bf16[4,256,128]{2,1,0:T(8,128)(2,1)S(1)} %get-tuple-element.68.edges.rest_0_, bf16[4,256,128]{2,1,0:T(8,128)(2,1)S(1)} %get-tuple-element.80.after.rest_1_, ...), custom_call_target="tpu_custom_call" | custom-call | tf_op jit(solution)/shard_map/third/pallas_call | solution.py:406
  52.4 1.5 %output.1.earlier = bf16[4,128,1024]{2,1,0:T(8,128)(2,1)} custom-call(s32[1]{0:T(128)} %bitcast.face_ref, bf16[8,256,128]{2,1,0:T(8,128)(2,1)S(1)} %get-tuple-element.107.early, bf16[8,256,128]{2,1,0:T(8,128)(2,1)S(1)} %get-tuple-element.108.later, bf16[1024,768]{1,0:T(8,128)(2,1)S(1)} %get-tuple-element.109.after.first_half, ...), custom_call_target="tpu_custom_call" | custom-call | tf_op jit(solution)/shard_map/output/pallas_call | solution.py:406
  56.1 1.0 %last_other.1 = bf16[4,128,1024]{2,1,0:T(8,128)(2,1)} custom-call(s32[1]{0:T(128)} %bitcast.face_ref, f32[128,1024]{1,0:T(8,128)S(1)} %last_own.1.own_part, bf16[1024,768]{1,0:T(8,128)(2,1)S(1)} %get-tuple-element.109.after.first_half, bf16[1024,256]{1,0:T(8,128)(2,1)S(1)} %operator_rest.1.second_half, ...), custom_call_target="tpu_custom_call", output_to_operand_aliasing={{}: (4, {})} | custom-call | tf_op jit(solution)/shard_map/last_other/pallas_call | solution.py:406
  (35 shorter events, 8.4 us)
Async XLA Ops:
  2.6 8.2 %collective-permute-start = (bf16[2,256,128]{2,1,0:T(8,128)(2,1)S(1)}, bf16[2,256,128]{2,1,0:T(8,128)(2,1)S(1)}, u32[]{:S(2)}, u32[]{:S(2)}) collective-permute-start(bf16[2,256,128]{2,1,0:T(8,128)(2,1)S(1)} %get-tuple-element.61), channel_id=1, source_target_pairs={{0,1},{1,0},{2,3},{3,2},{4,5},{5,4},{6,7},{7,6},{8,9},{9,8},{10,11... | collective-permute-start | bytes 393224 | tf_op jit(solution)/shard_map/ppermute | solution.py:434
  3.4 7.5 %collective-permute-start.1 = (bf16[2,256,128]{2,1,0:T(8,128)(2,1)S(1)}, bf16[2,256,128]{2,1,0:T(8,128)(2,1)S(1)}, u32[]{:S(2)}, u32[]{:S(2)}) collective-permute-start(bf16[2,256,128]{2,1,0:T(8,128)(2,1)S(1)} %get-tuple-element.62), channel_id=1, source_target_pairs={{1,2},{2,1},{5,6},{6,5},{9,10},{10,9},{13,14},{14,13},{17,18},{18,... | collective-permute-start | bytes 393224 | tf_op jit(solution)/shard_map/ppermute | solution.py:433
  6.4 8.7 %collective-permute-start.4 = (bf16[2,416,128]{2,1,0:T(8,128)(2,1)S(1)}, bf16[2,416,128]{2,1,0:T(8,128)(2,1)S(1)}, u32[]{:S(2)}, u32[]{:S(2)}) collective-permute-start(bf16[2,416,128]{2,1,0:T(8,128)(2,1)S(1)} %get-tuple-element.74), channel_id=1, source_target_pairs={{0,1},{1,0},{2,3},{3,2},{4,5},{5,4},{6,7},{7,6},{8,9},{9,8},{10,11... | collective-permute-start | bytes 638984 | tf_op jit(solution)/shard_map/ppermute | solution.py:434
  6.5 8.7 %collective-permute-start.5 = (bf16[2,416,128]{2,1,0:T(8,128)(2,1)S(1)}, bf16[2,416,128]{2,1,0:T(8,128)(2,1)S(1)}, u32[]{:S(2)}, u32[]{:S(2)}) collective-permute-start(bf16[2,416,128]{2,1,0:T(8,128)(2,1)S(1)} %get-tuple-element.75), channel_id=1, source_target_pairs={{1,2},{2,1},{5,6},{6,5},{9,10},{10,9},{13,14},{14,13},{17,18},{18,... | collective-permute-start | bytes 638984 | tf_op jit(solution)/shard_map/ppermute | solution.py:433
  12.0 3.1 %collective-permute-start.2 = (bf16[2,256,128]{2,1,0:T(8,128)(2,1)S(1)}, bf16[2,256,128]{2,1,0:T(8,128)(2,1)S(1)}, u32[]{:S(2)}, u32[]{:S(2)}) collective-permute-start(bf16[2,256,128]{2,1,0:T(8,128)(2,1)S(1)} %get-tuple-element.70), channel_id=1, source_target_pairs={{0,1},{1,0},{2,3},{3,2},{4,5},{5,4},{6,7},{7,6},{8,9},{9,8},{10,11... | collective-permute-start | bytes 393224 | tf_op jit(solution)/shard_map/ppermute | solution.py:434
  12.1 7.4 %collective-permute-start.3 = (bf16[2,256,128]{2,1,0:T(8,128)(2,1)S(1)}, bf16[2,256,128]{2,1,0:T(8,128)(2,1)S(1)}, u32[]{:S(2)}, u32[]{:S(2)}) collective-permute-start(bf16[2,256,128]{2,1,0:T(8,128)(2,1)S(1)} %get-tuple-element.71), channel_id=1, source_target_pairs={{1,2},{2,1},{5,6},{6,5},{9,10},{10,9},{13,14},{14,13},{17,18},{18,... | collective-permute-start | bytes 393224 | tf_op jit(solution)/shard_map/ppermute | solution.py:433
  16.9 10.2 %collective-permute-start.8 = (bf16[2,1024,128]{2,1,0:T(8,128)(2,1)S(1)}, bf16[2,1024,128]{2,1,0:T(8,128)(2,1)S(1)}, u32[]{:S(2)}, u32[]{:S(2)}) collective-permute-start(bf16[2,1024,128]{2,1,0:T(8,128)(2,1)S(1)} %get-tuple-element.82), channel_id=1, source_target_pairs={{0,1},{1,0},{2,3},{3,2},{4,5},{5,4},{6,7},{7,6},{8,9},{9,8},{10,11... | collective-permute-start | bytes 1572872 | tf_op jit(solution)/shard_map/ppermute | solution.py:434
  16.9 10.6 %collective-permute-start.9 = (bf16[2,1024,128]{2,1,0:T(8,128)(2,1)S(1)}, bf16[2,1024,128]{2,1,0:T(8,128)(2,1)S(1)}, u32[]{:S(2)}, u32[]{:S(2)}) collective-permute-start(bf16[2,1024,128]{2,1,0:T(8,128)(2,1)S(1)} %get-tuple-element.83), channel_id=1, source_target_pairs={{1,2},{2,1},{5,6},{6,5},{9,10},{10,9},{13,14},{14,13},{17,18},{18,... | collective-permute-start | bytes 1572872 | tf_op jit(solution)/shard_map/ppermute | solution.py:433
  20.7 1.3 %collective-permute-start.6 = (bf16[2,128,128]{2,1,0:T(8,128)(2,1)S(1)}, bf16[2,128,128]{2,1,0:T(8,128)(2,1)S(1)}, u32[]{:S(2)}, u32[]{:S(2)}) collective-permute-start(bf16[2,128,128]{2,1,0:T(8,128)(2,1)S(1)} %third_rows.1.own), channel_id=1, source_target_pairs={{0,1},{1,0},{2,3},{3,2},{4,5},{5,4},{6,7},{7,6},{8,9},{9,8},{10,11... | collective-permute-start | bytes 196616 | tf_op jit(solution)/shard_map/ppermute | solution.py:437
  22.0 8.9 %collective-permute-start.7 = (bf16[4,128,128]{2,1,0:T(8,128)(2,1)S(1)}, bf16[4,128,128]{2,1,0:T(8,128)(2,1)S(1)}, u32[]{:S(2)}, u32[]{:S(2)}) collective-permute-start(bf16[4,128,128]{2,1,0:T(8,128)(2,1)S(1)} %merge.1.after), channel_id=1, source_target_pairs={{0,4},{3,5},{2,6},{1,7},{4,8},{7,9},{6,10},{5,11},{8,12},{11,13},{... | collective-permute-start | bytes 393224 | tf_op jit(solution)/shard_map/ppermute | solution.py:449
  29.8 1.4 %collective-permute-start.10 = (bf16[256,256]{1,0:T(8,128)(2,1)S(1)}, bf16[256,256]{1,0:T(8,128)(2,1)S(1)}, u32[]{:S(2)}, u32[]{:S(2)}) collective-permute-start(bf16[256,256]{1,0:T(8,128)(2,1)S(1)} %get-tuple-element.88.rest_0_), channel_id=1, source_target_pairs={{0,1},{1,0},{2,3},{3,2},{4,5},{5,4},{6,7},{7,6},{8,9},{9,8},{10,11... | collective-permute-start | bytes 393224 | tf_op jit(solution)/shard_map/ppermute | solution.py:437
  29.8 1.5 %collective-permute-start.11 = (bf16[256,256]{1,0:T(8,128)(2,1)S(1)}, bf16[256,256]{1,0:T(8,128)(2,1)S(1)}, u32[]{:S(2)}, u32[]{:S(2)}) collective-permute-start(bf16[256,256]{1,0:T(8,128)(2,1)S(1)} %get-tuple-element.89.rest_1_), channel_id=1, source_target_pairs={{0,1},{1,0},{2,3},{3,2},{4,5},{5,4},{6,7},{7,6},{8,9},{9,8},{10,11... | collective-permute-start | bytes 393224 | tf_op jit(solution)/shard_map/ppermute | solution.py:437
  30.3 1.3 %collective-permute-start.12 = (bf16[256,256]{1,0:T(8,128)(2,1)S(1)}, bf16[256,256]{1,0:T(8,128)(2,1)S(1)}, u32[]{:S(2)}, u32[]{:S(2)}) collective-permute-start(bf16[256,256]{1,0:T(8,128)(2,1)S(1)} %get-tuple-element.90.rest_2_), channel_id=1, source_target_pairs={{0,1},{1,0},{2,3},{3,2},{4,5},{5,4},{6,7},{7,6},{8,9},{9,8},{10,11... | collective-permute-start | bytes 393224 | tf_op jit(solution)/shard_map/ppermute | solution.py:437
  30.4 1.5 %collective-permute-start.13 = (bf16[256,256]{1,0:T(8,128)(2,1)S(1)}, bf16[256,256]{1,0:T(8,128)(2,1)S(1)}, u32[]{:S(2)}, u32[]{:S(2)}) collective-permute-start(bf16[256,256]{1,0:T(8,128)(2,1)S(1)} %get-tuple-element.91.rest_3_), channel_id=1, source_target_pairs={{0,1},{1,0},{2,3},{3,2},{4,5},{5,4},{6,7},{7,6},{8,9},{9,8},{10,11... | collective-permute-start | bytes 393224 | tf_op jit(solution)/shard_map/ppermute | solution.py:437
  31.9 1.6 %collective-permute-start.15 = (bf16[4,128,128]{2,1,0:T(8,128)(2,1)S(1)}, bf16[4,128,128]{2,1,0:T(8,128)(2,1)S(1)}, u32[]{:S(2)}, u32[]{:S(2)}) collective-permute-start(bf16[4,128,128]{2,1,0:T(8,128)(2,1)S(1)} %collective-permute-done.7.rest_10_.rest_0_), channel_id=1, source_target_pairs={{0,1},{1,0},{2,3},{3,2},{4,5},{5,4},{6,7},{7,6},{8,9},{9,8},{10,11... | collective-permute-start | bytes 393224 | tf_op jit(solution)/shard_map/ppermute | solution.py:437
  32.2 1.3 %collective-permute-start.14 = (bf16[1,2,128,128]{3,2,1,0:T(8,128)(2,1)S(1)}, bf16[1,2,128,128]{3,2,1,0:T(8,128)(2,1)S(1)}, u32[]{:S(2)}, u32[]{:S(2)}) collective-permute-start(bf16[1,2,128,128]{3,2,1,0:T(8,128)(2,1)S(1)} %get-tuple-element.96.rest_8_), channel_id=1, source_target_pairs={{0,1},{1,0},{2,3},{3,2},{4,5},{5,4},{6,7},{7,6},{8,9},{9,8},{10,11... | collective-permute-start | bytes 196616 | tf_op jit(solution)/shard_map/ppermute | solution.py:437
  33.8 10.0 %collective-permute-start.16 = (bf16[4,128,128]{2,1,0:T(8,128)(2,1)S(1)}, bf16[4,128,128]{2,1,0:T(8,128)(2,1)S(1)}, u32[]{:S(2)}, u32[]{:S(2)}) collective-permute-start(bf16[4,128,128]{2,1,0:T(8,128)(2,1)S(1)} %chain.2.after), channel_id=1, source_target_pairs={{0,4},{3,5},{2,6},{1,7},{4,8},{7,9},{6,10},{5,11},{8,12},{11,13},{... | collective-permute-start | bytes 393224 | tf_op jit(solution)/shard_map/ppermute | solution.py:449
  41.5 2.3 %collective-permute-start.17 = (bf16[1,2,128,128]{3,2,1,0:T(8,128)(2,1)S(1)}, bf16[1,2,128,128]{3,2,1,0:T(8,128)(2,1)S(1)}, u32[]{:S(2)}, u32[]{:S(2)}) collective-permute-start(bf16[1,2,128,128]{3,2,1,0:T(8,128)(2,1)S(1)} %get-tuple-element.104.rest_8_), channel_id=1, source_target_pairs={{0,1},{1,0},{2,3},{3,2},{4,5},{5,4},{6,7},{7,6},{8,9},{9,8},{10,11... | collective-permute-start | bytes 196616 | tf_op jit(solution)/shard_map/ppermute | solution.py:437
  43.8 1.3 %collective-permute-start.18 = (bf16[4,128,128]{2,1,0:T(8,128)(2,1)S(1)}, bf16[4,128,128]{2,1,0:T(8,128)(2,1)S(1)}, u32[]{:S(2)}, u32[]{:S(2)}) collective-permute-start(bf16[4,128,128]{2,1,0:T(8,128)(2,1)S(1)} %collective-permute-done.16.rest_10_.rest_2_), channel_id=1, source_target_pairs={{0,1},{1,0},{2,3},{3,2},{4,5},{5,4},{6,7},{7,6},{8,9},{9,8},{10,11... | collective-permute-start | bytes 393224 | tf_op jit(solution)/shard_map/ppermute | solution.py:437
  45.5 8.7 %collective-permute-start.19 = (bf16[4,128,128]{2,1,0:T(8,128)(2,1)S(1)}, bf16[4,128,128]{2,1,0:T(8,128)(2,1)S(1)}, u32[]{:S(2)}, u32[]{:S(2)}) collective-permute-start(bf16[4,128,128]{2,1,0:T(8,128)(2,1)S(1)} %chain.3.rest_11_.after), channel_id=1, source_target_pairs={{0,4},{3,5},{2,6},{1,7},{4,8},{7,9},{6,10},{5,11},{8,12},{11,13},{... | collective-permute-start | bytes 393224 | tf_op jit(solution)/shard_map/ppermute | solution.py:449
  54.2 1.8 %collective-permute-start.20 = (bf16[4,128,128]{2,1,0:T(8,128)(2,1)S(1)}, bf16[4,128,128]{2,1,0:T(8,128)(2,1)S(1)}, u32[]{:S(2)}, u32[]{:S(2)}) collective-permute-start(bf16[4,128,128]{2,1,0:T(8,128)(2,1)S(1)} %collective-permute-done.19.rest_0_), channel_id=1, source_target_pairs={{0,1},{1,0},{2,3},{3,2},{4,5},{5,4},{6,7},{7,6},{8,9},{9,8},{10,11... | collective-permute-start | bytes 393224 | tf_op jit(solution)/shard_map/ppermute | solution.py:437
